TPU v7x, 32 devices: a whole 2x2x4 slice. The times are simulated.
32 devices in a mesh: leaf: 8 (over y, x, core), front: 4 (over z).
Axes of the slice: x: 2, y: 2, z: 4, core: 2. Of those that a mesh axis runs over, the one named last changes fastest.
Arguments:
- rhs: bfloat16 [3, 4096, 256], P(None, ('leaf', 'front')), may hold values from -6 to 6
- inverse_blocks: bfloat16 [4096, 3584], P(('leaf', 'front')), may hold values from -0.1875 to 0.1875
- update_blocks: bfloat16 [4096, 1536], P(('leaf', 'front')), may hold values from -0.1875 to 0.1875
- asm_owner: int32 [2, 4096, 1], P(None, ('leaf', 'front')), may hold values from 0 to 7; in each aligned block of 128 rows (0 to 127, 128 to 255, ..., all dimensions but the last counted through in order) at most 64 rows name the same one
- asm_row: int32 [2, 4096], P(None, ('leaf', 'front')), may hold values from 0 to 127
Outputs:
- solutions: float32 [3, 4096, 256], P(None, ('leaf', 'front'))
Inputs may be any that keep to these rules, and one draw needn't show every extreme that they name: `asm_owner`: among the 128 update rows of one device at one level (aligned blocks of rows), at most 64 name the same owner, and some block reaches 64.
All inputs are finite; a program needn't handle non-finite values.
Results may differ from a plain program's by a relative error of at most 0.03.
Values may be sent and summed in bfloat16 or wider, within the bound.
No kernel may reach another device: no remote copies, remote signals or barrier semaphores. Data moves between devices by JAX's collectives and lax.ppermute only.
A program may use at most 64 MiB of HBM per device.

v0:
```python
import jax
import jax.numpy as jnp
from jax import lax
from jax.sharding import PartitionSpec as P

LEVELS = 3


def swapped(shard, axis, distance):
    return lax.ppermute(shard, axis, [(i, i ^ 1 << distance) for i in range(lax.axis_size(axis))])


def contract_rows(left, right):
    return lax.dot_general(
        left, right, (((0,), (0,)), ((), ())), preferred_element_type=jnp.float32
    )


def shards(rhs, inverse_blocks, update_blocks, asm_owner, asm_row):
    own_rows = rhs.shape[1]
    rhs_cols = rhs.shape[2]
    front_count = lax.axis_size("front")
    leaf_rows = front_count * own_rows
    leaf_id = lax.axis_index("leaf")

    def side_of(bit_index):
        return leaf_id // (1 << bit_index) % 2

    def node_gather(local, pair_bits):
        gathered = lax.all_gather(local, "front", axis=0, tiled=True)
        for bit_index in pair_bits:
            partner = swapped(gathered, "leaf", bit_index)
            gathered = jnp.where(
                side_of(bit_index) == 1,
                jnp.concatenate([partner, gathered], 0),
                jnp.concatenate([gathered, partner], 0),
            )
        return gathered

    def node_reduce(partial_value, pair_bits):
        for bit_index in pair_bits:
            half_rows = partial_value.shape[0] // 2
            upper_half = side_of(bit_index) == 1
            kept = jnp.where(upper_half, partial_value[half_rows:], partial_value[:half_rows])
            handed = jnp.where(upper_half, partial_value[:half_rows], partial_value[half_rows:])
            partial_value = kept + swapped(handed.astype(jnp.bfloat16), "leaf", bit_index).astype(
                handed.dtype
            )
        partial_value = lax.psum_scatter(
            partial_value.astype(jnp.bfloat16), "front", scatter_dimension=0, tiled=True
        ).astype(jnp.float32)
        return partial_value

    assembled = jnp.zeros((own_rows, rhs_cols), jnp.float32)
    solved_all = []
    records = []
    for level_index in range(LEVELS):
        front_rows = leaf_rows << level_index
        column_start = leaf_rows * ((1 << level_index) - 1)
        pair_bits = list(range(level_index))
        pivot_rhs = (rhs[level_index].astype(jnp.float32) - assembled).astype(jnp.bfloat16)
        pivot_node = node_gather(pivot_rhs, pair_bits)
        solved = jnp.dot(
            inverse_blocks[:, column_start : column_start + front_rows],
            pivot_node,
            preferred_element_type=jnp.float32,
        ).astype(jnp.bfloat16)
        solved_all.append(solved)
        if level_index + 1 < LEVELS:
            solved_node = node_gather(solved, pair_bits)
            update = jnp.dot(
                update_blocks[:, column_start : column_start + front_rows],
                solved_node,
                preferred_element_type=jnp.float32,
            ).astype(jnp.bfloat16)
            owner_ids = asm_owner[level_index, :, 0]
            parent_row = asm_row[level_index]
            target_local = owner_ids * own_rows + parent_row
            selector = (target_local[:, None] == jnp.arange(2 * leaf_rows)[None, :]).astype(
                jnp.bfloat16
            )
            records.append(selector)
            assembled = node_reduce(contract_rows(selector, update), [level_index])
    solutions = [None] * LEVELS
    below = None
    for level_index in reversed(range(LEVELS)):
        front_rows = leaf_rows << level_index
        column_start = leaf_rows * ((1 << level_index) - 1)
        down_bits = list(reversed(range(level_index)))
        if level_index + 1 == LEVELS:
            weights = solved_all[level_index]
        else:
            pair_block = node_gather(below, [level_index])
            fetched = jnp.dot(
                records[level_index], pair_block, preferred_element_type=jnp.float32
            ).astype(jnp.bfloat16)
            carried = node_reduce(
                contract_rows(update_blocks[:, column_start : column_start + front_rows], fetched),
                down_bits,
            )
            weights = (solved_all[level_index].astype(jnp.float32) - carried).astype(jnp.bfloat16)
        solution = node_reduce(
            contract_rows(inverse_blocks[:, column_start : column_start + front_rows], weights),
            down_bits,
        )
        solutions[level_index] = solution
        below = solution.astype(jnp.bfloat16)
    return jnp.stack(solutions)


def solution(mesh):
    placed = (
        P(None, ("leaf", "front"), None),
        P(("leaf", "front"), None),
        P(("leaf", "front"), None),
        P(None, ("leaf", "front"), None),
        P(None, ("leaf", "front")),
    )
    return jax.shard_map(
        shards,
        mesh=mesh,
        in_specs=placed,
        out_specs=P(None, ("leaf", "front"), None),
        check_vma=False,
    )
```

profile of v0, /device:TPU:0, one launch (start us, length us, event | category | flops | bytes accessed | tf_op | source)
XLA Modules:
  0.0 321.3 jit_solution(15363279527186912953)
XLA Ops:
  6.5 0.8 slice.90
  7.4 15.6 %all-gather = bf16[1,512,256]{2,1,0:T(8,128)(2,1)S(1)} all-gather(bf16[1,128,256]{2,1,0:T(8,128)(2,1)S(1)} %slice.90), channel_id=2, replica_groups=mesh['leaf'=8,'front'=4] {'front'}, dimensions={1}, use_global_device_ids=true | all-gather | bytes 327680 | tf_op jit(solution)/shard_map/all_gather | solution.py:30
  23.0 1.1 convolution_convert_fusion.8
  24.1 14.4 %all_gather.22 = bf16[512,256]{1,0:T(8,128)(2,1)S(1)} all-gather(bf16[128,256]{1,0:T(8,128)(2,1)S(1)} %convolution_convert_fusion.8), channel_id=1, replica_groups=mesh['leaf'=8,'front'=4] {'front'}, dimensions={0}, use_global_device_ids=true | all-gather | bytes 327680 | tf_op jit(solution)/shard_map/all_gather | solution.py:30
  38.5 0.8 bitcast_add_fusion
  39.3 1.5 fusion.2
  40.8 0.1 select_convert_fusion.5
  40.9 0.1 collective-permute-start
  41.0 1.5 collective-permute-done
  42.5 0.8 add_convert_fusion.4
  43.3 0.0 reduce-scatter.10.cloned.1.call-start
  43.4 20.7 %reduce-scatter.8.cloned.1.call-done = bf16[128,256]{1,0:T(8,128)(2,1)} async-done(((bf16[512,256]{1,0:T(8,128)(2,1)}), bf16[128,256]{1,0:T(8,128)(2,1)}) %reduce-scatter.8.cloned.1.call-update) | async-done | bytes 65552 | tf_op jit(solution)/shard_map/reduce_scatter | solution.py:49
  64.1 0.9 fusion.78
  64.9 13.8 %all_gather.23 = bf16[512,256]{1,0:T(8,128)(2,1)S(1)} all-gather(bf16[128,256]{1,0:T(8,128)(2,1)S(1)} %fusion.78), channel_id=1, replica_groups=mesh['leaf'=8,'front'=4] {'front'}, dimensions={0}, use_global_device_ids=true | all-gather | bytes 327680 | tf_op jit(solution)/shard_map/all_gather | solution.py:30
  78.8 1.5 collective-permute-done.1
  80.3 1.2 fusion.4
  81.5 14.4 %all_gather.24 = bf16[512,256]{1,0:T(8,128)(2,1)S(1)} all-gather(bf16[128,256]{1,0:T(8,128)(2,1)S(1)} %fusion.4), channel_id=1, replica_groups=mesh['leaf'=8,'front'=4] {'front'}, dimensions={0}, use_global_device_ids=true | all-gather | bytes 327680 | tf_op jit(solution)/shard_map/all_gather | solution.py:30
  96.0 1.5 collective-permute-done.2
  97.5 0.8 fusion.3
  98.4 0.1 select_convert_fusion.4
  98.4 1.6 collective-permute-start.3
  100.0 6.8 %collective-permute-done.3 = bf16[512,256]{1,0:T(8,128)(2,1)S(1)} collective-permute-done((bf16[512,256]{1,0:T(8,128)(2,1)S(1)}, bf16[512,256]{1,0:T(8,128)(2,1)S(1)}, u32[]{:S(2)}, u32[]{:S(2)}) %collective-permute-start.3) | collective-permute-done | bytes 262176 | tf_op jit(solution)/shard_map/ppermute | solution.py:10
  106.8 0.8 add_convert_fusion.3
  107.7 0.0 reduce-scatter.12.cloned.1.call-start
  107.7 18.0 %reduce-scatter.10.cloned.1.call-done = bf16[128,256]{1,0:T(8,128)(2,1)} async-done(((bf16[512,256]{1,0:T(8,128)(2,1)}), bf16[128,256]{1,0:T(8,128)(2,1)}) %reduce-scatter.10.cloned.1.call-update) | async-done | bytes 65552 | tf_op jit(solution)/shard_map/reduce_scatter | solution.py:49
  125.7 0.9 fusion.77
  126.6 13.9 %all_gather.25 = bf16[512,256]{1,0:T(8,128)(2,1)S(1)} all-gather(bf16[128,256]{1,0:T(8,128)(2,1)S(1)} %fusion.77), channel_id=1, replica_groups=mesh['leaf'=8,'front'=4] {'front'}, dimensions={0}, use_global_device_ids=true | all-gather | bytes 327680 | tf_op jit(solution)/shard_map/all_gather | solution.py:30
  140.4 1.5 collective-permute-done.4
  142.0 0.2 maximum_select_fusion.8
  142.2 1.6 collective-permute-start.5
  143.8 12.6 %collective-permute-done.5 = bf16[1024,256]{1,0:T(8,128)(2,1)} collective-permute-done((bf16[1024,256]{1,0:T(8,128)(2,1)S(1)}, bf16[1024,256]{1,0:T(8,128)(2,1)}, u32[]{:S(2)}, u32[]{:S(2)}) %collective-permute-start.5) | collective-permute-done | bytes 524320 | tf_op jit(solution)/shard_map/ppermute | solution.py:10
  156.3 3.0 convolution_bitcast_fusion
  159.3 0.1 select_convert_fusion
  159.4 1.6 collective-permute-start.6
  161.0 11.6 %collective-permute-done.6 = bf16[1024,256]{1,0:T(8,128)(2,1)S(1)} collective-permute-done((bf16[1024,256]{1,0:T(8,128)(2,1)S(1)}, bf16[1024,256]{1,0:T(8,128)(2,1)S(1)}, u32[]{:S(2)}, u32[]{:S(2)}) %collective-permute-start.6) | collective-permute-done | bytes 524320 | tf_op jit(solution)/shard_map/ppermute | solution.py:10
  172.6 0.2 convert_add_fusion
  172.8 0.1 select_convert_fusion.3
  172.8 0.1 collective-permute-start.7
  172.9 1.5 collective-permute-done.7
  174.4 0.8 add_convert_fusion.2
  175.3 0.0 reduce-scatter.14.cloned.1.call-start
  175.3 18.2 %reduce-scatter.12.cloned.1.call-done = bf16[128,256]{1,0:T(8,128)(2,1)} async-done(((bf16[512,256]{1,0:T(8,128)(2,1)}), bf16[128,256]{1,0:T(8,128)(2,1)}) %reduce-scatter.12.cloned.1.call-update) | async-done | bytes 65552 | tf_op jit(solution)/shard_map/reduce_scatter | solution.py:49
  193.5 14.1 %all_gather.26 = bf16[512,256]{1,0:T(8,128)(2,1)S(1)} all-gather(bf16[128,256]{1,0:T(8,128)(2,1)} %reduce-scatter.12.cloned.1.call-done), channel_id=1, replica_groups=mesh['leaf'=8,'front'=4] {'front'}, dimensions={0}, use_global_device_ids=true | all-gather | bytes 327680 | tf_op jit(solution)/shard_map/all_gather | solution.py:30
  207.6 1.5 collective-permute-start.8
  209.1 4.9 %collective-permute-done.8 = bf16[512,256]{1,0:T(8,128)(2,1)S(1)} collective-permute-done((bf16[512,256]{1,0:T(8,128)(2,1)S(1)}, bf16[512,256]{1,0:T(8,128)(2,1)S(1)}, u32[]{:S(2)}, u32[]{:S(2)}) %collective-permute-start.8) | collective-permute-done | bytes 262176 | tf_op jit(solution)/shard_map/ppermute | solution.py:10
  214.0 0.7 convolution_bitcast_fusion.2
  214.6 0.1 select_convert_fusion.2
  214.7 0.1 collective-permute-start.9
  214.8 1.5 collective-permute-done.9
  216.3 0.8 add_convert_fusion.1
  217.2 18.3 %reduce-scatter.14.cloned.1.call-done = bf16[128,256]{1,0:T(8,128)(2,1)} async-done(((bf16[512,256]{1,0:T(8,128)(2,1)}), bf16[128,256]{1,0:T(8,128)(2,1)}) %reduce-scatter.14.cloned.1.call-update) | async-done | bytes 65552 | tf_op jit(solution)/shard_map/reduce_scatter | solution.py:49
  235.4 1.3 convolution_bitcast_fusion.1
  236.8 0.1 select_convert_fusion.1
  236.8 0.1 collective-permute-start.10
  236.9 1.5 collective-permute-done.10
  238.4 0.8 add_convert_fusion
  239.3 18.0 %reduce-scatter.16.cloned.1.call-done = bf16[128,256]{1,0:T(8,128)(2,1)} async-done(((bf16[512,256]{1,0:T(8,128)(2,1)}), bf16[128,256]{1,0:T(8,128)(2,1)}) %reduce-scatter.16.cloned.1.call-update) | async-done | bytes 65552 | tf_op jit(solution)/shard_map/reduce_scatter | solution.py:49
  257.3 14.2 %all_gather.27 = bf16[512,256]{1,0:T(8,128)(2,1)S(1)} all-gather(bf16[128,256]{1,0:T(8,128)(2,1)} %reduce-scatter.16.cloned.1.call-done), channel_id=1, replica_groups=mesh['leaf'=8,'front'=4] {'front'}, dimensions={0}, use_global_device_ids=true | all-gather | bytes 327680 | tf_op jit(solution)/shard_map/all_gather | solution.py:30
  271.5 1.5 collective-permute-done.11
  273.1 1.3 fusion
  274.4 18.3 %reduce-scatter.18.cloned.1.call-done = bf16[128,256]{1,0:T(8,128)(2,1)} async-done(((bf16[512,256]{1,0:T(8,128)(2,1)}), bf16[128,256]{1,0:T(8,128)(2,1)}) %reduce-scatter.18.cloned.1.call-update) | async-done | bytes 65552 | tf_op jit(solution)/shard_map/reduce_scatter | solution.py:49
  292.7 1.9 fusion.1
  294.6 18.2 %reduce-scatter.20.cloned.1.call-done = bf16[128,256]{1,0:T(8,128)(2,1)} async-done(((bf16[512,256]{1,0:T(8,128)(2,1)}), bf16[128,256]{1,0:T(8,128)(2,1)}) %reduce-scatter.20.cloned.1.call-update) | async-done | bytes 65552 | tf_op jit(solution)/shard_map/reduce_scatter | solution.py:49
  312.8 1.6 maximum_convert_fusion
  (23 shorter events, 0.3 us)
Async XLA Ops:
  6.5 57.5 %reduce-scatter.8.cloned.1.call-start = ((), (), s32[]{:S(2)}) async-start(), calls=%async_computation.7 | async-start | bytes 327680 | tf_op jit(solution)/shard_map/reduce_scatter | solution.py:49
  38.5 25.5 %copy-start.2 = (bf16[3,128,256]{2,1,0:T(8,128)(2,1)S(1)}, bf16[3,128,256]{2,1,0:T(8,128)(2,1)}, u32[]{:S(2)}) copy-start(bf16[3,128,256]{2,1,0:T(8,128)(2,1)} %param.5) | copy-start | bytes 589828
  40.9 1.6 collective-permute-start
  43.3 54.2 %copy-start.3 = (bf16[128,1536]{1,0:T(8,128)(2,1)S(1)}, bf16[128,1536]{1,0:T(8,128)(2,1)}, u32[]{:S(2)}) copy-start(bf16[128,1536]{1,0:T(8,128)(2,1)} %param.7) | copy-start | bytes 1179652
  43.3 82.4 %reduce-scatter.10.cloned.1.call-start = ((), (), s32[]{:S(2)}) async-start(), calls=%async_computation.8 | async-start | bytes 327680 | tf_op jit(solution)/shard_map/reduce_scatter | solution.py:49
  78.8 1.5 collective-permute-start.1
  96.0 1.5 collective-permute-start.2
  98.4 8.4 %collective-permute-start.3 = (bf16[512,256]{1,0:T(8,128)(2,1)S(1)}, bf16[512,256]{1,0:T(8,128)(2,1)S(1)}, u32[]{:S(2)}, u32[]{:S(2)}) collective-permute-start(bf16[512,256]{1,0:T(8,128)(2,1)S(1)} %select_convert_fusion.4), channel_id=1, source_target_pairs={{0,8},{4,12},{8,0},{12,4},{16,24},{20,28},{24,16},{28,20},{1,9},{5... | collective-permute-start | bytes 786440 | tf_op jit(solution)/shard_map/ppermute | solution.py:10
  107.7 85.8 %reduce-scatter.12.cloned.1.call-start = ((), (), s32[]{:S(2)}) async-start(), calls=%async_computation.9 | async-start | bytes 327680 | tf_op jit(solution)/shard_map/reduce_scatter | solution.py:49
  140.4 1.5 collective-permute-start.4
  142.2 14.1 %collective-permute-start.5 = (bf16[1024,256]{1,0:T(8,128)(2,1)S(1)}, bf16[1024,256]{1,0:T(8,128)(2,1)}, u32[]{:S(2)}, u32[]{:S(2)}) collective-permute-start(bf16[1024,256]{1,0:T(8,128)(2,1)S(1)} %maximum_select_fusion.8), channel_id=1, source_target_pairs={{0,8},{4,12},{8,0},{12,4},{16,24},{20,28},{24,16},{28,20},{1,9},{5... | collective-permute-start | bytes 1572872 | tf_op jit(solution)/shard_map/ppermute | solution.py:10
  159.4 13.2 %collective-permute-start.6 = (bf16[1024,256]{1,0:T(8,128)(2,1)S(1)}, bf16[1024,256]{1,0:T(8,128)(2,1)S(1)}, u32[]{:S(2)}, u32[]{:S(2)}) collective-permute-start(bf16[1024,256]{1,0:T(8,128)(2,1)S(1)} %select_convert_fusion), channel_id=1, source_target_pairs={{0,8},{4,12},{8,0},{12,4},{16,24},{20,28},{24,16},{28,20},{1,9},{5... | collective-permute-start | bytes 1572872 | tf_op jit(solution)/shard_map/ppermute | solution.py:10
  172.8 1.6 collective-permute-start.7
  175.3 60.2 %reduce-scatter.14.cloned.1.call-start = ((), (), s32[]{:S(2)}) async-start(), calls=%async_computation.10 | async-start | bytes 327680 | tf_op jit(solution)/shard_map/reduce_scatter | solution.py:49
  207.6 6.4 %collective-permute-start.8 = (bf16[512,256]{1,0:T(8,128)(2,1)S(1)}, bf16[512,256]{1,0:T(8,128)(2,1)S(1)}, u32[]{:S(2)}, u32[]{:S(2)}) collective-permute-start(bf16[512,256]{1,0:T(8,128)(2,1)S(1)} %all_gather.26), channel_id=1, source_target_pairs={{0,8},{4,12},{8,0},{12,4},{16,24},{20,28},{24,16},{28,20},{1,9},{5... | collective-permute-start | bytes 786440 | tf_op jit(solution)/shard_map/ppermute | solution.py:10
  214.7 1.6 collective-permute-start.9
  217.1 40.2 %reduce-scatter.16.cloned.1.call-start = ((), (), s32[]{:S(2)}) async-start(), calls=%async_computation.11 | async-start | bytes 327680 | tf_op jit(solution)/shard_map/reduce_scatter | solution.py:49
  236.8 1.6 collective-permute-start.10
  239.2 73.6 %copy-start = (bf16[128,256]{1,0:T(8,128)(2,1)S(1)}, bf16[128,256]{1,0:T(8,128)(2,1)}, u32[]{:S(2)}) copy-start(bf16[128,256]{1,0:T(8,128)(2,1)} %reduce-scatter.12.cloned.1.call-done) | copy-start | bytes 196612
  239.2 53.5 %reduce-scatter.18.cloned.1.call-start = ((), (), s32[]{:S(2)}) async-start(), calls=%async_computation.12 | async-start | bytes 327680 | tf_op jit(solution)/shard_map/reduce_scatter | solution.py:49
  257.3 55.5 %copy-start.1 = (bf16[128,256]{1,0:T(8,128)(2,1)S(1)}, bf16[128,256]{1,0:T(8,128)(2,1)}, u32[]{:S(2)}) copy-start(bf16[128,256]{1,0:T(8,128)(2,1)} %reduce-scatter.16.cloned.1.call-done) | copy-start | bytes 196612
  271.5 1.5 collective-permute-start.11
  274.4 38.4 %reduce-scatter.20.cloned.1.call-start = ((), (), s32[]{:S(2)}) async-start(), calls=%async_computation.13 | async-start | bytes 327680 | tf_op jit(solution)/shard_map/reduce_scatter | solution.py:49
Sparse Core Ops, SparseCore 0:
  43.4 20.5 reduce-scatter.7
  107.8 17.8 reduce-scatter.9
  175.4 18.0 reduce-scatter.11
  217.2 18.1 reduce-scatter.13
  239.4 17.8 reduce-scatter.15
  274.5 18.1 reduce-scatter.17
  295.0 17.8 reduce-scatter.19
where the time goes:
time: 322 us; the launch traced here: 321 us
  waiting for transfers between devices  178 us (55%)
  blocking collectives  101 us (31%)
  between operations  13.6 us (4%)
  matrix products  12.9 us (4%)
  other arithmetic  8.8 us (3%)
  starting transfers between devices  6.71 us (2%)
    reduce_scatter x7, waiting for transfers between devices, node_reduce(): lax.psum_scatter(partial_value.astype(jnp.bfloat16), 'front', scatter_dim...  130 us
    all_gather x7, blocking collectives, node_gather(): gathered = lax.all_gather(local, 'front', axis=0, tiled=True)  101 us
    ppermute x12, waiting for transfers between devices, swapped(): lax.ppermute(shard, axis, [(i, i ^ 1 << distance) for i in range(lax.axis...  48.2 us
    dot_general x7, matrix products, contract_rows(): lax.dot_general(left, right, (((0,), (0,)), ((), ())), preferred_element_...  10.5 us
    ppermute x12, starting transfers between devices, swapped(): lax.ppermute(shard, axis, [(i, i ^ 1 << distance) for i in range(lax.axis...  6.46 us
  transfers between devices with their start and end apart: 19, of which 19 were waited for; matrix products, arithmetic and copies ran while one was open for 0% of the time, Pallas kernels for 0%

commit v1 on v0

v1 whole, which is shorter than its diff:
```python
import jax
import jax.numpy as jnp
from jax import lax
from jax.sharding import PartitionSpec as P

LEVELS = 3
BF16 = jnp.bfloat16


def swapped(shard, axis, distance):
    return lax.ppermute(shard, axis, [(i, i ^ 1 << distance) for i in range(lax.axis_size(axis))])


def product(left, right, left_dim, right_dim):
    return lax.dot_general(
        left, right, (((left_dim,), (right_dim,)), ((), ())), preferred_element_type=jnp.float32
    )


def forward(vector, matrix):
    return product(vector, matrix, 1, 1)


def adjoint(vector, matrix):
    return product(vector, matrix, 1, 0)


def ordered(own, other, upper, axis):
    return jnp.where(
        upper == 1,
        jnp.concatenate([other, own], axis),
        jnp.concatenate([own, other], axis),
    )


def part(array, index, count, axis):
    size = array.shape[axis] // count
    return lax.dynamic_slice_in_dim(array, index * size, size, axis)


def shards(rhs, inverse_blocks, update_blocks, asm_owner, asm_row):
    own_rows, rhs_cols = rhs.shape[1:]
    front_count = lax.axis_size("front")
    leaf_rows = front_count * own_rows
    leaf_id = lax.axis_index("leaf")
    front_id = lax.axis_index("front")
    odd = front_id % 2
    side = leaf_id % 2
    wing = leaf_id // 2 % 2
    high_bits = range(1, front_count.bit_length() - 1)

    def high_gather(block, axis):
        for bit in high_bits:
            block = ordered(block, swapped(block, "front", bit), front_id >> bit & 1, axis)
        return block

    inverse0 = inverse_blocks[:, :leaf_rows]
    inverse1 = inverse_blocks[:, leaf_rows : 3 * leaf_rows]
    inverse2 = inverse_blocks[:, 3 * leaf_rows :]

    lists = jnp.concatenate([asm_owner[:, :, 0], asm_row], 0).astype(BF16)
    lists = jnp.pad(lists, ((0, 12), (0, 0)))
    kept = part(rhs, odd, 2, 2).reshape(LEVELS * own_rows, -1)
    handed = part(rhs, 1 - odd, 2, 2).reshape(LEVELS * own_rows, -1)
    lists_wide = jnp.pad(lists, ((0, 0), (0, kept.shape[1] - own_rows)))
    received = swapped(jnp.concatenate([handed, lists_wide], 0), "front", 0)
    kept = jnp.concatenate([kept, lists_wide], 0)
    inverse0_pair = swapped(inverse0, "front", 0)
    update_pair = swapped(update_blocks, "front", 0)
    inverse1_leaf = lax.all_gather(inverse1, "front", axis=0, tiled=True)

    def level_rows(level_index):
        return ordered(
            kept[level_index * own_rows : (level_index + 1) * own_rows],
            received[level_index * own_rows : (level_index + 1) * own_rows],
            odd,
            0,
        )

    rhs0 = high_gather(level_rows(0), 0)
    later = jnp.concatenate(
        [
            level_rows(1).T,
            level_rows(2).T,
            ordered(
                kept[LEVELS * own_rows :, :own_rows], received[LEVELS * own_rows :, :own_rows], odd, 1
            ),
        ],
        0,
    )
    later = high_gather(later, 1)
    half_cols = rhs_cols // 2
    rhs1 = later[:half_cols]
    rhs2 = later[half_cols : 2 * half_cols]
    lists = later[2 * half_cols : 2 * half_cols + 4].astype(jnp.int32)

    def selector(level_index):
        target = lists[level_index : level_index + 1] * own_rows + lists[2 + level_index : 3 + level_index]
        return (jnp.arange(2 * leaf_rows)[:, None] == target).astype(BF16)

    def placed_in(block, upper):
        zeros = jnp.zeros_like(block)
        return ordered(block, zeros, upper, 1)

    def pair_product(vector, own, other):
        return ordered(forward(vector, own), forward(vector, other), odd, 1).astype(BF16)

    solved0 = high_gather(
        ordered(
            product(rhs0, inverse0, 0, 1), product(rhs0, inverse0_pair, 0, 1), odd, 1
        ).astype(BF16),
        1,
    )
    update0 = high_gather(
        pair_product(solved0, update_blocks[:, :leaf_rows], update_pair[:, :leaf_rows]), 1
    )
    select0 = selector(0)
    pivots1 = placed_in(rhs1, side).astype(jnp.float32) - forward(update0, select0)
    pivots1 = (pivots1 + swapped(pivots1.astype(BF16), "leaf", 0).astype(jnp.float32)).astype(BF16)

    solved1 = forward(pivots1, inverse1_leaf).astype(BF16)
    solved1_all = ordered(solved1, swapped(solved1, "leaf", 0), side, 1)
    update1 = high_gather(
        pair_product(solved1_all, update_blocks[:, leaf_rows:], update_pair[:, leaf_rows:]), 1
    )
    select1 = selector(1)
    pivots2 = placed_in(rhs2, wing).astype(jnp.float32) - forward(update1, select1)
    pivots2 = (
        part(pivots2, wing, 2, 0)
        + swapped(part(pivots2, 1 - wing, 2, 0).astype(BF16), "leaf", 1).astype(jnp.float32)
    ).astype(BF16)
    pivots2 = ordered(
        pivots2.reshape(-1, 2, 1, leaf_rows),
        swapped(pivots2, "leaf", 0).reshape(-1, 2, 1, leaf_rows),
        side,
        2,
    ).reshape(-1, 4 * leaf_rows)

    inverse2_wing = swapped(inverse2, "leaf", 1)
    inverse2_all = jnp.concatenate(
        [inverse2, inverse2_wing, swapped(inverse2, "front", 0), swapped(inverse2_wing, "front", 0)], 0
    )
    solved2 = forward(pivots2, inverse2_all).astype(BF16)
    below2 = adjoint(solved2, inverse2_all).reshape(-1, 2, 2, leaf_rows)
    handed2 = lax.dynamic_index_in_dim(below2, 1 - side, 2, False).reshape(-1, 2 * leaf_rows)
    below2 = lax.dynamic_index_in_dim(below2, side, 2, False).reshape(-1, 2 * leaf_rows)
    below2 = below2 + swapped(handed2.astype(BF16), "leaf", 0).astype(jnp.float32)
    for bit in high_bits:
        below2 = below2 + swapped(below2.astype(BF16), "front", bit).astype(jnp.float32)
    below2 = below2.astype(BF16)
    below2 = ordered(below2, swapped(below2, "leaf", 1), wing, 0)

    update1_leaf = lax.all_gather(update_blocks[:, leaf_rows:], "front", axis=0, tiled=True)
    fetched1 = adjoint(below2, select1).astype(BF16)
    carried1 = adjoint(fetched1, update1_leaf)
    carried1 = part(carried1, side, 2, 1) + swapped(
        part(carried1, 1 - side, 2, 1).astype(BF16), "leaf", 0
    ).astype(jnp.float32)
    weights1 = (solved1.astype(jnp.float32) - carried1).astype(BF16)
    below1 = adjoint(weights1, inverse1_leaf)
    below1 = (below1 + swapped(below1.astype(BF16), "leaf", 0).astype(jnp.float32)).astype(BF16)

    level0_leaf = lax.all_gather(
        jnp.concatenate([inverse0, update_blocks[:, :leaf_rows]], 1), "front", axis=0, tiled=True
    )
    fetched0 = adjoint(below1, select0).astype(BF16)
    weights0 = solved0.astype(jnp.float32) - adjoint(fetched0, level0_leaf[:, leaf_rows:])
    below0 = adjoint(weights0.astype(BF16), level0_leaf[:, :leaf_rows])

    def own_columns(block):
        return part(block, front_id, front_count, 1), part(block, front_id ^ 1, front_count, 1)

    def finished(block):
        own, other = own_columns(block)
        other = swapped(other.astype(BF16), "front", 0).astype(jnp.float32)
        return ordered(own.astype(jnp.float32), other, odd, 0).T

    return jnp.stack(
        [finished(below0), finished(part(below1, side, 2, 1)), finished(part(below2, wing, 2, 1))]
    )


def solution(mesh):
    placed = (
        P(None, ("leaf", "front"), None),
        P(("leaf", "front"), None),
        P(("leaf", "front"), None),
        P(None, ("leaf", "front"), None),
        P(None, ("leaf", "front")),
    )
    return jax.shard_map(
        shards,
        mesh=mesh,
        in_specs=placed,
        out_specs=P(None, ("leaf", "front"), None),
        check_vma=False,
    )
```

time: 322 us -> 168 us (0.52)
  blocking collectives: 101 us -> 0 us
  waiting for transfers between devices: 178 us -> 111 us
  starting transfers between devices: 6.71 us -> 18.8 us
  local copies, waits for them, and re-layouts: 0.86 us -> 8.04 us
  other arithmetic: 8.8 us -> 4.1 us
    reduce_scatter x7 -> x0, waiting for transfers between devices: 130 us -> none  [node_reduce(): lax.psum_scatter(partial_value.astype(jnp.bfloat16), 'front', scatter_dim...]
    all_gather x7 -> x0, blocking collectives: 101 us -> none  [node_gather(): gathered = lax.all_gather(local, 'front', axis=0, tiled=True)]
    ppermute x12 -> x23, waiting for transfers between devices: 48.2 us -> 108 us  [swapped(): lax.ppermute(shard, axis, [(i, i ^ 1 << distance) for i in range(lax.axis...]
    ppermute x12 -> x23, starting transfers between devices: 6.46 us -> 18.7 us  [swapped(): lax.ppermute(shard, axis, [(i, i ^ 1 << distance) for i in range(lax.axis...]
    convert_element_type x13 -> x11, other arithmetic: 6.03 us -> 0.24 us  [the longest x1 0.06 us: shards(): (below1 + swapped(below1.astype(BF16), 'leaf', 0).astype(jnp.float32)).as...]
    all_gather x0 -> x3, waiting for transfers between devices: none -> 3.73 us  [the longest x1 3.71 us: shards(): lax.all_gather(jnp.concatenate([inverse0, update_blocks[:, :leaf_rows]],...]
    dot_general x9 -> x14, matrix products: 12.9 us -> 11 us  [product(): lax.dot_general(left, right, (((left_dim,), (right_dim,)), ((), ())), pre...]
  transfers between devices with their start and end apart: 19 -> 26, of which waited for: 19 -> 19; matrix products, arithmetic and copies ran while one was open for 0% -> 10% of each run, Pallas kernels for 0% -> 0%
where the time goes in v1:
time: 168 us; the launch traced here: 167 us
  waiting for transfers between devices  111 us (66%)
  starting transfers between devices  18.8 us (11%)
  between operations  13.8 us (8%)
  matrix products  11 us (7%)
  local copies, waits for them, and re-layouts  8.04 us (5%)
  other arithmetic  4.1 us (2%)
    ppermute x23, waiting for transfers between devices, swapped(): lax.ppermute(shard, axis, [(i, i ^ 1 << distance) for i in range(lax.axis...  108 us
    ppermute x23, starting transfers between devices, swapped(): lax.ppermute(shard, axis, [(i, i ^ 1 << distance) for i in range(lax.axis...  18.7 us
    dot_general x14, matrix products, product(): lax.dot_general(left, right, (((left_dim,), (right_dim,)), ((), ())), pre...  11 us
    all_gather x1, waiting for transfers between devices, shards(): lax.all_gather(jnp.concatenate([inverse0, update_blocks[:, :leaf_rows]],...  3.71 us
  transfers between devices with their start and end apart: 26, of which 19 were waited for; matrix products, arithmetic and copies ran while one was open for 10% of the time, Pallas kernels for 0%

profile of v1, /device:TPU:0, one launch (start us, length us, event | category | flops | bytes accessed | tf_op | source)
XLA Modules:
  0.0 167.2 jit_solution(496003707929651835)
XLA Ops:
  6.5 0.7 convert.8
  7.3 0.7 convert_bitcast_fusion
  7.9 0.9 constant_dynamic-slice_fusion.4
  8.9 3.1 %collective-permute-start = (bf16[400,128]{1,0:T(8,128)(2,1)S(1)}, bf16[400,128]{1,0:T(8,128)(2,1)S(1)}, u32[]{:S(2)}, u32[]{:S(2)}) collective-permute-start(bf16[400,128]{1,0:T(8,128)(2,1)S(1)} %pad_maximum_fusion.7), channel_id=1, source_target_pairs={{0,1},{1,0},{2,3},{3,2},{4,5},{5,4},{6,7},{7,6},{8,9},{9,8},{10,11... | collective-permute-start | bytes 307208 | tf_op jit(solution)/shard_map/ppermute | solution.py:11
  12.0 0.9 slice.83
  13.0 2.0 %collective-permute-start.5 = (bf16[128,1536]{1,0:T(8,128)(2,1)}, bf16[128,1536]{1,0:T(8,128)(2,1)S(1)}, u32[]{:S(2)}, u32[]{:S(2)}) collective-permute-start(bf16[128,1536]{1,0:T(8,128)(2,1)} %param.7), channel_id=1, source_target_pairs={{0,1},{1,0},{2,3},{3,2},{4,5},{5,4},{6,7},{7,6},{8,9},{9,8},{10,11... | collective-permute-start | bytes 1179656 | tf_op jit(solution)/shard_map/ppermute | solution.py:11
  15.0 1.7 slice.97
  16.9 2.7 %collective-permute-start.1 = (bf16[256,128]{1,0:T(8,128)(2,1)S(1)}, bf16[256,128]{1,0:T(8,128)(2,1)S(1)}, u32[]{:S(2)}, u32[]{:S(2)}) collective-permute-start(bf16[256,128]{1,0:T(8,128)(2,1)S(1)} %maximum_select_fusion.14), channel_id=1, source_target_pairs={{0,2},{1,3},{2,0},{3,1},{4,6},{5,7},{6,4},{7,5},{8,10},{9,11},{10,... | collective-permute-start | bytes 196616 | tf_op jit(solution)/shard_map/ppermute | solution.py:11
  19.5 0.1 copy.39
  19.6 0.1 copy.40
  19.8 9.6 %collective-permute-done.1 = bf16[256,128]{1,0:T(8,128)(2,1)S(1)} collective-permute-done((bf16[256,128]{1,0:T(8,128)(2,1)S(1)}, bf16[256,128]{1,0:T(8,128)(2,1)S(1)}, u32[]{:S(2)}, u32[]{:S(2)}) %collective-permute-start.1) | collective-permute-done | bytes 65568 | tf_op jit(solution)/shard_map/ppermute | solution.py:11
  29.5 0.2 fusion.48
  29.6 0.2 fusion.47
  29.9 3.4 %collective-permute-start.3 = (bf16[128,256]{0,1:T(8,128)(2,1)S(1)}, bf16[128,256]{0,1:T(8,128)(2,1)S(1)}, u32[]{:S(2)}, u32[]{:S(2)}) collective-permute-start(bf16[128,256]{0,1:T(8,128)(2,1)S(1)} %fusion.26), channel_id=1, source_target_pairs={{0,2},{1,3},{2,0},{3,1},{4,6},{5,7},{6,4},{7,5},{8,10},{9,11},{10,... | collective-permute-start | bytes 196616 | tf_op jit(solution)/shard_map/ppermute | solution.py:11
  33.4 11.3 %collective-permute-done.3 = bf16[128,256]{0,1:T(8,128)(2,1)S(1)} collective-permute-done((bf16[128,256]{0,1:T(8,128)(2,1)S(1)}, bf16[128,256]{0,1:T(8,128)(2,1)S(1)}, u32[]{:S(2)}, u32[]{:S(2)}) %collective-permute-start.3) | collective-permute-done | bytes 65568 | tf_op jit(solution)/shard_map/ppermute | solution.py:11
  44.8 0.2 fusion.61
  44.9 11.6 %collective-permute-done.4 = bf16[272,256]{0,1:T(8,128)(2,1)S(1)} collective-permute-done((bf16[272,256]{0,1:T(8,128)(2,1)S(1)}, bf16[272,256]{0,1:T(8,128)(2,1)S(1)}, u32[]{:S(2)}, u32[]{:S(2)}) %collective-permute-start.4) | collective-permute-done | bytes 139296 | tf_op jit(solution)/shard_map/ppermute | solution.py:11
  56.6 0.2 copy.41
  56.8 0.2 copy.42
  57.0 0.2 fusion.24
  57.3 5.1 %collective-permute-done.6 = bf16[128,256]{0,1:T(8,128)(2,1)S(1)} collective-permute-done((bf16[128,256]{0,1:T(8,128)(2,1)S(1)}, bf16[128,256]{0,1:T(8,128)(2,1)S(1)}, u32[]{:S(2)}, u32[]{:S(2)}) %collective-permute-start.6) | collective-permute-done | bytes 65568 | tf_op jit(solution)/shard_map/ppermute | solution.py:11
  62.5 0.6 fusion.67
  63.2 1.5 collective-permute-done.7
  64.7 1.7 %convolution_convert_fusion = bf16[128,512]{1,0:T(8,128)(2,1)S(1)} fusion(bf16[512,1024]{1,0:T(8,128)(2,1)} %all-gather.4.cloned.1.call-done, f32[128,1024]{1,0:T(8,128)S(1)} %get-tuple-element.24, bf16[128,1024]{1,0:T(8,128)(2,1)S(1)} %collective-permute-done.7), kind=kOutput, calls=%fused_computation.11 | convolution fusion | flops 134676480 | bytes 1966080 | tf_op jit(solution)/shard_map/dot_general | solution.py:15
  66.4 0.2 collective-permute-start.8
  66.7 1.5 collective-permute-start.12
  68.2 0.2 fusion.20
  68.4 0.2 fusion.46
  68.8 5.3 %collective-permute-done.9 = bf16[128,256]{0,1:T(8,128)(2,1)S(1)} collective-permute-done((bf16[128,256]{0,1:T(8,128)(2,1)S(1)}, bf16[128,256]{0,1:T(8,128)(2,1)S(1)}, u32[]{:S(2)}, u32[]{:S(2)}) %collective-permute-start.9) | collective-permute-done | bytes 65568 | tf_op jit(solution)/shard_map/ppermute | solution.py:11
  74.1 0.6 fusion.5
  74.7 1.2 collective-permute-start.10
  75.9 5.6 %collective-permute-done.12 = bf16[128,2048]{1,0:T(8,128)(2,1)S(1)} collective-permute-done((bf16[128,2048]{1,0:T(8,128)(2,1)S(1)}, bf16[128,2048]{1,0:T(8,128)(2,1)S(1)}, u32[]{:S(2)}, u32[]{:S(2)}) %collective-permute-start.12) | collective-permute-done | bytes 524320 | tf_op jit(solution)/shard_map/ppermute | solution.py:11
  81.5 0.7 slice.100
  82.3 1.4 collective-permute-done.10
  83.9 0.1 reshape.34
  84.0 1.2 collective-permute-done.11
  85.3 1.2 broadcast_select_fusion
  86.5 0.2 select_n.219
  86.7 4.1 %collective-permute-done.13 = bf16[128,2048]{1,0:T(8,128)(2,1)S(1)} collective-permute-done((bf16[128,2048]{1,0:T(8,128)(2,1)S(1)}, bf16[128,2048]{1,0:T(8,128)(2,1)S(1)}, u32[]{:S(2)}, u32[]{:S(2)}) %collective-permute-start.13) | collective-permute-done | bytes 524320 | tf_op jit(solution)/shard_map/ppermute | solution.py:11
  90.8 26.6 %collective-permute-done.14 = bf16[128,2048]{1,0:T(8,128)(2,1)} collective-permute-done((bf16[128,2048]{1,0:T(8,128)(2,1)S(1)}, bf16[128,2048]{1,0:T(8,128)(2,1)}, u32[]{:S(2)}, u32[]{:S(2)}) %collective-permute-start.14) | collective-permute-done | bytes 524320 | tf_op jit(solution)/shard_map/ppermute | solution.py:11
  117.4 2.4 %fusion.10 = f32[64,2048]{1,0:T(8,128)S(1)} fusion(bf16[64,2048]{1,0:T(8,128)(2,1)S(1)} %select_n.219, bf16[128,2048]{1,0:T(8,128)(2,1)} %collective-permute-done.14, bf16[128,2048]{1,0:T(8,128)(2,1)S(1)} %collective-permute-done.13, bf16[128,2048]{1,0:T(8,128)(2,1)S(1)} %collective-permute-done.12, bf16[128,2048]{1,0:T(8,128)(2,1)S(1)} %slice.103), kind=kOutput, calls=%fused_computation.15 | convolution fusion | flops 285245440 | bytes 2883584 | tf_op jit(solution)/shard_map/dot_general | solution.py:15
  119.8 0.4 reshape.31
  120.2 0.2 constant_dynamic-slice_fusion.3
  120.5 0.1 copy.57
  120.7 0.9 dynamic-slice_reduce_fusion
  121.6 0.4 collective-permute-done.15
  122.1 0.6 collective-permute-start.16
  122.7 0.7 pad_maximum_fusion.5
  123.5 7.9 %collective-permute-done.16 = bf16[64,1024]{1,0:T(8,128)(2,1)S(1)} collective-permute-done((bf16[64,1024]{1,0:T(8,128)(2,1)S(1)}, bf16[64,1024]{1,0:T(8,128)(2,1)S(1)}, u32[]{:S(2)}, u32[]{:S(2)}) %collective-permute-start.16) | collective-permute-done | bytes 131104 | tf_op jit(solution)/shard_map/ppermute | solution.py:11
  131.4 0.9 collective-permute-start.17
  132.3 4.6 %collective-permute-done.17 = bf16[64,1024]{1,0:T(8,128)(2,1)S(1)} collective-permute-done((bf16[64,1024]{1,0:T(8,128)(2,1)S(1)}, bf16[64,1024]{1,0:T(8,128)(2,1)S(1)}, u32[]{:S(2)}, u32[]{:S(2)}) %collective-permute-start.17) | collective-permute-done | bytes 131104 | tf_op jit(solution)/shard_map/ppermute | solution.py:11
  137.0 2.0 %fusion.8 = f32[128,1024]{1,0:T(8,128)S(1)} fusion(bf16[512,1024]{1,0:T(8,128)(2,1)} %all-gather.6.cloned.1.call-done, bf16[128,1024]{1,0:T(8,128)(2,1)S(1)} %maximum_select_fusion.1, s32[512]{0:T(512)S(1)} %bitcast.50), kind=kOutput, calls=%fused_computation.12 | convolution fusion | flops 269025280 | bytes 1837056 | tf_op jit(solution)/shard_map/dot_general | solution.py:15
  139.2 1.3 collective-permute-done.18
  140.5 0.3 fusion.68
  140.8 0.2 collective-permute-start.19
  141.2 6.4 %collective-permute-done.22 = bf16[128,128]{1,0:T(8,128)(2,1)S(1)} collective-permute-done((bf16[128,128]{1,0:T(8,128)(2,1)S(1)}, bf16[128,128]{1,0:T(8,128)(2,1)S(1)}, u32[]{:S(2)}, u32[]{:S(2)}) %collective-permute-start.22) | collective-permute-done | bytes 32800 | tf_op jit(solution)/shard_map/ppermute | solution.py:11
  147.7 3.7 %all-gather.8.cloned.1.call-done = bf16[512,1024]{1,0:T(8,128)(2,1)} async-done(((bf16[128,1024]{1,0:T(8,128)(2,1)}), bf16[512,1024]{1,0:T(8,128)(2,1)}) %all-gather.8.cloned.1.call-update) | async-done | bytes 1048592 | tf_op jit(solution)/shard_map/all_gather | solution.py:163
  151.4 1.9 %fusion.9 = f32[128,512]{0,1:T(8,128)S(1)} fusion(bf16[128,1024]{1,0:T(8,128)(2,1)S(1)} %add_convert_fusion, s32[512]{0:T(512)S(1)} %bitcast.48, bf16[512,1024]{1,0:T(8,128)(2,1)} %all-gather.8.cloned.1.call-done), kind=kOutput, calls=%fused_computation.13 | convolution fusion | flops 201916416 | bytes 1050624 | tf_op jit(solution)/shard_map/dot_general | solution.py:15
  153.3 0.3 fusion.17
  153.6 2.0 %collective-permute-start.20 = (bf16[128,128]{1,0:T(8,128)(2,1)S(1)}, bf16[128,128]{1,0:T(8,128)(2,1)S(1)}, u32[]{:S(2)}, u32[]{:S(2)}) collective-permute-start(bf16[128,128]{1,0:T(8,128)(2,1)S(1)} %dynamic-slice_convert_fusion.2), channel_id=1, source_target_pairs={{0,1},{1,0},{2,3},{3,2},{4,5},{5,4},{6,7},{7,6},{8,9},{9,8},{10,11... | collective-permute-start | bytes 98312 | tf_op jit(solution)/shard_map/ppermute | solution.py:11
  155.7 0.2 collective-permute-start.21
  155.9 1.7 %collective-permute-done.20 = bf16[128,128]{1,0:T(8,128)(2,1)S(1)} collective-permute-done((bf16[128,128]{1,0:T(8,128)(2,1)S(1)}, bf16[128,128]{1,0:T(8,128)(2,1)S(1)}, u32[]{:S(2)}, u32[]{:S(2)}) %collective-permute-start.20) | collective-permute-done | bytes 32800 | tf_op jit(solution)/shard_map/ppermute | solution.py:11
  157.6 2.1 %collective-permute-done.21 = bf16[128,128]{1,0:T(8,128)(2,1)S(1)} collective-permute-done((bf16[128,128]{1,0:T(8,128)(2,1)S(1)}, bf16[128,128]{1,0:T(8,128)(2,1)S(1)}, u32[]{:S(2)}, u32[]{:S(2)}) %collective-permute-start.21) | collective-permute-done | bytes 32800 | tf_op jit(solution)/shard_map/ppermute | solution.py:11
  159.7 0.9 copy.50
  (75 shorter events, 2.0 us)
Async XLA Ops:
  6.5 10.2 %copy-start.4 = (bf16[3,128,256]{2,1,0:T(8,128)(2,1)S(1)}, bf16[3,128,256]{2,1,0:T(8,128)(2,1)}, u32[]{:S(2)}) copy-start(bf16[3,128,256]{2,1,0:T(8,128)(2,1)} %param.5) | copy-start | bytes 589828
  6.5 58.2 %all-gather.4.cloned.1.call-start = ((), (), s32[]{:S(2)}) async-start(), calls=%async_computation | async-start | bytes 1310720 | tf_op jit(solution)/shard_map/all_gather | solution.py:70
  8.9 7.9 %collective-permute-start = (bf16[400,128]{1,0:T(8,128)(2,1)S(1)}, bf16[400,128]{1,0:T(8,128)(2,1)S(1)}, u32[]{:S(2)}, u32[]{:S(2)}) collective-permute-start(bf16[400,128]{1,0:T(8,128)(2,1)S(1)} %pad_maximum_fusion.7), channel_id=1, source_target_pairs={{0,1},{1,0},{2,3},{3,2},{4,5},{5,4},{6,7},{7,6},{8,9},{9,8},{10,11... | collective-permute-start | bytes 307208 | tf_op jit(solution)/shard_map/ppermute | solution.py:11
  12.9 16.6 %copy-start.1 = (bf16[128,3584]{1,0:T(8,128)(2,1)S(1)}, bf16[128,3584]{1,0:T(8,128)(2,1)}, u32[]{:S(2)}) copy-start(bf16[128,3584]{1,0:T(8,128)(2,1)} %param.6) | copy-start | bytes 2752516
  12.9 16.8 %collective-permute-start.2 = (bf16[128,512]{1,0:T(8,128)(2,1)S(1)}, bf16[128,512]{1,0:T(8,128)(2,1)S(1)}, u32[]{:S(2)}, u32[]{:S(2)}) collective-permute-start(bf16[128,512]{1,0:T(8,128)(2,1)S(1)} %slice.83), channel_id=1, source_target_pairs={{0,1},{1,0},{2,3},{3,2},{4,5},{5,4},{6,7},{7,6},{8,9},{9,8},{10,11... | collective-permute-start | bytes 393224 | tf_op jit(solution)/shard_map/ppermute | solution.py:11
  13.0 44.0 %collective-permute-start.5 = (bf16[128,1536]{1,0:T(8,128)(2,1)}, bf16[128,1536]{1,0:T(8,128)(2,1)S(1)}, u32[]{:S(2)}, u32[]{:S(2)}) collective-permute-start(bf16[128,1536]{1,0:T(8,128)(2,1)} %param.7), channel_id=1, source_target_pairs={{0,1},{1,0},{2,3},{3,2},{4,5},{5,4},{6,7},{7,6},{8,9},{9,8},{10,11... | collective-permute-start | bytes 1179656 | tf_op jit(solution)/shard_map/ppermute | solution.py:11
  16.7 120.3 %all-gather.6.cloned.1.call-start = ((), (), s32[]{:S(2)}) async-start(), calls=%async_computation.1 | async-start | bytes 1310720 | tf_op jit(solution)/shard_map/all_gather | solution.py:153
  16.9 12.6 %collective-permute-start.1 = (bf16[256,128]{1,0:T(8,128)(2,1)S(1)}, bf16[256,128]{1,0:T(8,128)(2,1)S(1)}, u32[]{:S(2)}, u32[]{:S(2)}) collective-permute-start(bf16[256,128]{1,0:T(8,128)(2,1)S(1)} %maximum_select_fusion.14), channel_id=1, source_target_pairs={{0,2},{1,3},{2,0},{3,1},{4,6},{5,7},{6,4},{7,5},{8,10},{9,11},{10,... | collective-permute-start | bytes 196616 | tf_op jit(solution)/shard_map/ppermute | solution.py:11
  19.8 25.0 %copy-start.2 = (bf16[128,1536]{1,0:T(8,128)(2,1)S(1)}, bf16[128,1536]{1,0:T(8,128)(2,1)}, u32[]{:S(2)}) copy-start(bf16[128,1536]{1,0:T(8,128)(2,1)} %param.7) | copy-start | bytes 1179652
  29.9 14.9 %collective-permute-start.3 = (bf16[128,256]{0,1:T(8,128)(2,1)S(1)}, bf16[128,256]{0,1:T(8,128)(2,1)S(1)}, u32[]{:S(2)}, u32[]{:S(2)}) collective-permute-start(bf16[128,256]{0,1:T(8,128)(2,1)S(1)} %fusion.26), channel_id=1, source_target_pairs={{0,2},{1,3},{2,0},{3,1},{4,6},{5,7},{6,4},{7,5},{8,10},{9,11},{10,... | collective-permute-start | bytes 196616 | tf_op jit(solution)/shard_map/ppermute | solution.py:11
  33.3 23.2 %collective-permute-start.4 = (bf16[272,256]{0,1:T(8,128)(2,1)S(1)}, bf16[272,256]{0,1:T(8,128)(2,1)S(1)}, u32[]{:S(2)}, u32[]{:S(2)}) collective-permute-start(bf16[272,256]{0,1:T(8,128)(2,1)S(1)} %pad_maximum_fusion.6), channel_id=1, source_target_pairs={{0,2},{1,3},{2,0},{3,1},{4,6},{5,7},{6,4},{7,5},{8,10},{9,11},{10,... | collective-permute-start | bytes 417800 | tf_op jit(solution)/shard_map/ppermute | solution.py:11
  57.2 5.2 %collective-permute-start.6 = (bf16[128,256]{0,1:T(8,128)(2,1)S(1)}, bf16[128,256]{0,1:T(8,128)(2,1)S(1)}, u32[]{:S(2)}, u32[]{:S(2)}) collective-permute-start(bf16[128,256]{0,1:T(8,128)(2,1)S(1)} %fusion.27), channel_id=1, source_target_pairs={{0,2},{1,3},{2,0},{3,1},{4,6},{5,7},{6,4},{7,5},{8,10},{9,11},{10,... | collective-permute-start | bytes 196616 | tf_op jit(solution)/shard_map/ppermute | solution.py:11
  63.1 1.6 collective-permute-start.7
  66.4 1.7 %collective-permute-start.8 = (bf16[128,512]{1,0:T(8,128)(2,1)S(1)}, bf16[128,512]{1,0:T(8,128)(2,1)S(1)}, u32[]{:S(2)}, u32[]{:S(2)}) collective-permute-start(bf16[128,512]{1,0:T(8,128)(2,1)S(1)} %convolution_convert_fusion), channel_id=1, source_target_pairs={{0,4},{4,0},{8,12},{12,8},{16,20},{20,16},{24,28},{28,24},{1,5},{5... | collective-permute-start | bytes 393224 | tf_op jit(solution)/shard_map/ppermute | solution.py:11
  66.7 14.8 %collective-permute-start.12 = (bf16[128,2048]{1,0:T(8,128)(2,1)S(1)}, bf16[128,2048]{1,0:T(8,128)(2,1)S(1)}, u32[]{:S(2)}, u32[]{:S(2)}) collective-permute-start(bf16[128,2048]{1,0:T(8,128)(2,1)S(1)} %slice.103), channel_id=1, source_target_pairs={{0,8},{4,12},{8,0},{12,4},{16,24},{20,28},{24,16},{28,20},{1,9},{5... | collective-permute-start | bytes 1572872 | tf_op jit(solution)/shard_map/ppermute | solution.py:11
  68.7 5.4 %collective-permute-start.9 = (bf16[128,256]{0,1:T(8,128)(2,1)S(1)}, bf16[128,256]{0,1:T(8,128)(2,1)S(1)}, u32[]{:S(2)}, u32[]{:S(2)}) collective-permute-start(bf16[128,256]{0,1:T(8,128)(2,1)S(1)} %fusion.33), channel_id=1, source_target_pairs={{0,2},{1,3},{2,0},{3,1},{4,6},{5,7},{6,4},{7,5},{8,10},{9,11},{10,... | collective-permute-start | bytes 196616 | tf_op jit(solution)/shard_map/ppermute | solution.py:11
  74.7 9.0 %collective-permute-start.10 = (bf16[64,1024]{1,0:T(8,128)(2,1)S(1)}, bf16[64,1024]{1,0:T(8,128)(2,1)S(1)}, u32[]{:S(2)}, u32[]{:S(2)}) collective-permute-start(bf16[64,1024]{1,0:T(8,128)(2,1)S(1)} %dynamic-slice_convert_fusion.1), channel_id=1, source_target_pairs={{0,8},{4,12},{8,0},{12,4},{16,24},{20,28},{24,16},{28,20},{1,9},{5... | collective-permute-start | bytes 393224 | tf_op jit(solution)/shard_map/ppermute | solution.py:11
  75.9 14.9 %collective-permute-start.13 = (bf16[128,2048]{1,0:T(8,128)(2,1)S(1)}, bf16[128,2048]{1,0:T(8,128)(2,1)S(1)}, u32[]{:S(2)}, u32[]{:S(2)}) collective-permute-start(bf16[128,2048]{1,0:T(8,128)(2,1)S(1)} %slice.103), channel_id=1, source_target_pairs={{0,1},{1,0},{2,3},{3,2},{4,5},{5,4},{6,7},{7,6},{8,9},{9,8},{10,11... | collective-permute-start | bytes 1572872 | tf_op jit(solution)/shard_map/ppermute | solution.py:11
  81.5 35.9 %collective-permute-start.14 = (bf16[128,2048]{1,0:T(8,128)(2,1)S(1)}, bf16[128,2048]{1,0:T(8,128)(2,1)}, u32[]{:S(2)}, u32[]{:S(2)}) collective-permute-start(bf16[128,2048]{1,0:T(8,128)(2,1)S(1)} %collective-permute-done.12), channel_id=1, source_target_pairs={{0,1},{1,0},{2,3},{3,2},{4,5},{5,4},{6,7},{7,6},{8,9},{9,8},{10,11... | collective-permute-start | bytes 1572872 | tf_op jit(solution)/shard_map/ppermute | solution.py:11
  82.2 69.2 %all-gather.8.cloned.1.call-start = ((), (), s32[]{:S(2)}) async-start(), calls=%async_computation.2 | async-start | bytes 1310720 | tf_op jit(solution)/shard_map/all_gather | solution.py:163
  83.8 1.4 collective-permute-start.11
  120.6 1.4 collective-permute-start.15
  122.1 9.3 %collective-permute-start.16 = (bf16[64,1024]{1,0:T(8,128)(2,1)S(1)}, bf16[64,1024]{1,0:T(8,128)(2,1)S(1)}, u32[]{:S(2)}, u32[]{:S(2)}) collective-permute-start(bf16[64,1024]{1,0:T(8,128)(2,1)S(1)} %fusion.22), channel_id=1, source_target_pairs={{0,2},{1,3},{2,0},{3,1},{4,6},{5,7},{6,4},{7,5},{8,10},{9,11},{10,... | collective-permute-start | bytes 393224 | tf_op jit(solution)/shard_map/ppermute | solution.py:11
  131.4 5.5 %collective-permute-start.17 = (bf16[64,1024]{1,0:T(8,128)(2,1)S(1)}, bf16[64,1024]{1,0:T(8,128)(2,1)S(1)}, u32[]{:S(2)}, u32[]{:S(2)}) collective-permute-start(bf16[64,1024]{1,0:T(8,128)(2,1)S(1)} %add_convert_fusion.3), channel_id=1, source_target_pairs={{0,8},{4,12},{8,0},{12,4},{16,24},{20,28},{24,16},{28,20},{1,9},{5... | collective-permute-start | bytes 393224 | tf_op jit(solution)/shard_map/ppermute | solution.py:11
  136.9 3.5 %copy-start = (bf16[512,1024]{1,0:T(8,128)(2,1)S(1)}, bf16[512,1024]{1,0:T(8,128)(2,1)}, u32[]{:S(2)}) copy-start(bf16[512,1024]{1,0:T(8,128)(2,1)} %all-gather.4.cloned.1.call-done) | copy-start | bytes 3145732
  139.1 1.4 collective-permute-start.18
  140.8 6.8 %collective-permute-start.19 = (bf16[128,1024]{1,0:T(8,128)(2,1)S(1)}, bf16[128,1024]{1,0:T(8,128)(2,1)S(1)}, u32[]{:S(2)}, u32[]{:S(2)}) collective-permute-start(bf16[128,1024]{1,0:T(8,128)(2,1)S(1)} %get-tuple-element.25), channel_id=1, source_target_pairs={{0,4},{4,0},{8,12},{12,8},{16,20},{20,16},{24,28},{28,24},{1,5},{5... | collective-permute-start | bytes 786440 | tf_op jit(solution)/shard_map/ppermute | solution.py:11
  141.1 6.5 %collective-permute-start.22 = (bf16[128,128]{1,0:T(8,128)(2,1)S(1)}, bf16[128,128]{1,0:T(8,128)(2,1)S(1)}, u32[]{:S(2)}, u32[]{:S(2)}) collective-permute-start(bf16[128,128]{1,0:T(8,128)(2,1)S(1)} %get-tuple-element.11), channel_id=1, source_target_pairs={{0,1},{1,0},{2,3},{3,2},{4,5},{5,4},{6,7},{7,6},{8,9},{9,8},{10,11... | collective-permute-start | bytes 98312 | tf_op jit(solution)/shard_map/ppermute | solution.py:11
  151.4 1.9 %copy-start.3 = (bf16[512,1024]{1,0:T(8,128)(2,1)S(1)}, bf16[512,1024]{1,0:T(8,128)(2,1)}, u32[]{:S(2)}) copy-start(bf16[512,1024]{1,0:T(8,128)(2,1)} %all-gather.8.cloned.1.call-done) | copy-start | bytes 3145732
  153.6 4.0 %collective-permute-start.20 = (bf16[128,128]{1,0:T(8,128)(2,1)S(1)}, bf16[128,128]{1,0:T(8,128)(2,1)S(1)}, u32[]{:S(2)}, u32[]{:S(2)}) collective-permute-start(bf16[128,128]{1,0:T(8,128)(2,1)S(1)} %dynamic-slice_convert_fusion.2), channel_id=1, source_target_pairs={{0,1},{1,0},{2,3},{3,2},{4,5},{5,4},{6,7},{7,6},{8,9},{9,8},{10,11... | collective-permute-start | bytes 98312 | tf_op jit(solution)/shard_map/ppermute | solution.py:11
  155.7 4.0 %collective-permute-start.21 = (bf16[128,128]{1,0:T(8,128)(2,1)S(1)}, bf16[128,128]{1,0:T(8,128)(2,1)S(1)}, u32[]{:S(2)}, u32[]{:S(2)}) collective-permute-start(bf16[128,128]{1,0:T(8,128)(2,1)S(1)} %get-tuple-element.9), channel_id=1, source_target_pairs={{0,1},{1,0},{2,3},{3,2},{4,5},{5,4},{6,7},{7,6},{8,9},{9,8},{10,11... | collective-permute-start | bytes 98312 | tf_op jit(solution)/shard_map/ppermute | solution.py:11
Sparse Core Ops, SparseCore 0:
  16.8 40.7 all-gather.3
  82.4 34.6 all-gather.5
  123.6 27.7 all-gather.7

commit v2 on v1

v2 whole, which is shorter than its diff:
```python
import jax
import jax.numpy as jnp
from jax import lax
from jax.sharding import PartitionSpec as P

LEVELS = 3
BF16 = jnp.bfloat16
F32 = jnp.float32


def swapped(shard, axis, distance):
    return lax.ppermute(shard, axis, [(i, i ^ 1 << distance) for i in range(lax.axis_size(axis))])


def product(left, right, left_dim, right_dim):
    return lax.dot_general(
        left, right, (((left_dim,), (right_dim,)), ((), ())), preferred_element_type=F32
    )


def forward(vector, matrix):
    return product(vector, matrix, 1, 1)


def adjoint(vector, matrix):
    return product(vector, matrix, 1, 0)


def ordered(own, other, upper, axis):
    return jnp.where(
        upper == 1,
        jnp.concatenate([other, own], axis),
        jnp.concatenate([own, other], axis),
    )


def after(array, *earlier):
    return lax.optimization_barrier((array, *earlier))[0]


def together(*arrays):
    return lax.optimization_barrier(arrays)


def part(array, index, count, axis):
    size = array.shape[axis] // count
    return lax.dynamic_slice_in_dim(array, index * size, size, axis)


def shards(rhs, inverse_blocks, update_blocks, asm_owner, asm_row):
    own_rows, rhs_cols = rhs.shape[1:]
    front_count = lax.axis_size("front")
    leaf_rows = front_count * own_rows
    half_cols = rhs_cols // 2
    leaf_id = lax.axis_index("leaf")
    front_id = lax.axis_index("front")
    odd = front_id % 2
    side = leaf_id % 2
    wing = leaf_id // 2 % 2
    high_bits = range(1, front_count.bit_length() - 1)

    def high_gather(block, axis):
        for bit in high_bits:
            block = ordered(block, swapped(block, "front", bit), front_id >> bit & 1, axis)
        return block

    def high_scatter(block):
        for bit in reversed(high_bits):
            upper = front_id >> bit & 1
            block = part(block, upper, 2, 1) + swapped(
                part(block, 1 - upper, 2, 1).astype(BF16), "front", bit
            ).astype(F32)
        return block

    def high_sum(block):
        for bit in high_bits:
            block = block + swapped(block.astype(BF16), "front", bit).astype(F32)
        return block

    def side_scatter(block):
        return part(block, side, 2, 1) + swapped(
            part(block, 1 - side, 2, 1).astype(BF16), "leaf", 0
        ).astype(F32)

    def pair_rows(block):
        return part(block, front_id // 2, front_count // 2, 1)

    def pair_forward(vector, own, other):
        return ordered(forward(vector, own), forward(vector, other), odd, 1).astype(BF16)

    def pair_adjoint(vector, own, other):
        return adjoint(part(vector, odd, 2, 1), own) + adjoint(part(vector, 1 - odd, 2, 1), other)

    inverse0 = inverse_blocks[:, :leaf_rows]
    inverse1 = inverse_blocks[:, leaf_rows : 3 * leaf_rows]
    inverse2 = inverse_blocks[:, 3 * leaf_rows :]
    update0 = update_blocks[:, :leaf_rows]
    update1 = update_blocks[:, leaf_rows:]

    rhs0 = ordered(
        part(rhs[0], odd, 2, 1), swapped(part(rhs[0], 1 - odd, 2, 1), "front", 0), odd, 0
    )
    inverse0_pair = swapped(inverse0, "front", 0)
    update0_pair = swapped(after(update0, rhs0), "front", 0)
    wing2 = swapped(after(inverse2, rhs0), "leaf", 1)

    lists = jnp.concatenate([asm_owner[:, :, 0], asm_row], 0).astype(BF16)
    lists = jnp.pad(lists, ((0, 12), (0, half_cols - own_rows)))
    kept = jnp.concatenate([part(rhs[1:], odd, 2, 2).reshape(2 * own_rows, -1), lists], 0)
    handed = jnp.concatenate([part(rhs[1:], 1 - odd, 2, 2).reshape(2 * own_rows, -1), lists], 0)
    received = swapped(after(handed, rhs0), "front", 0)

    rhs0_leaf = high_gather(rhs0, 0)
    rhs0_leaf, inverse0_pair, received = together(rhs0_leaf, inverse0_pair, received)
    solved0_pair = ordered(
        product(rhs0_leaf, inverse0, 0, 1), product(rhs0_leaf, inverse0_pair, 0, 1), odd, 1
    ).astype(BF16)
    inverse1_pair = swapped(after(inverse1, solved0_pair), "front", 0)
    solved0 = high_gather(solved0_pair, 1)
    solved0, update0_pair, inverse1_pair = together(solved0, update0_pair, inverse1_pair)

    def level_rows(index):
        rows = slice(index * own_rows, (index + 1) * own_rows)
        return ordered(kept[rows], received[rows], odd, 0).T

    lists = ordered(
        kept[2 * own_rows :, :own_rows], received[2 * own_rows :, :own_rows], odd, 1
    )
    rhs1 = level_rows(0)
    rhs2 = level_rows(1)
    updated0_pair = pair_forward(solved0, update0, update0_pair)
    update1_pair = swapped(after(update1, updated0_pair), "front", 0)
    updated0 = high_gather(jnp.concatenate([updated0_pair, rhs1, lists], 0), 1)
    updated0, wing2 = together(updated0, wing2)
    lists = updated0[2 * half_cols : 2 * half_cols + 4].astype(jnp.int32)
    rhs1 = updated0[half_cols : 2 * half_cols]
    updated0 = updated0[:half_cols]

    def selector(level_index):
        target = lists[level_index : level_index + 1] * own_rows + lists[2 + level_index : 3 + level_index]
        return (jnp.arange(2 * leaf_rows)[:, None] == target).astype(BF16)

    select0 = selector(0)
    select1 = selector(1)
    pivots1 = ordered(rhs1, jnp.zeros_like(rhs1), side, 1).astype(F32) - forward(updated0, select0)
    pivots1 = (pivots1 + swapped(pivots1.astype(BF16), "leaf", 0).astype(F32)).astype(BF16)

    solved1_pair = pair_forward(pivots1, inverse1, inverse1_pair)
    solved1 = high_gather(solved1_pair, 1)
    solved1, update1_pair = together(solved1, update1_pair)
    solved1 = ordered(solved1, swapped(solved1, "leaf", 0), side, 1)
    updated1_pair = pair_forward(solved1, update1, update1_pair)
    updated1 = high_gather(jnp.concatenate([updated1_pair, rhs2], 0), 1)
    rhs2 = updated1[half_cols:]
    updated1 = updated1[:half_cols]

    def stacked(block):
        return jnp.concatenate([block[:, :leaf_rows], block[:, leaf_rows:]], 0)

    def flat(block):
        cols = block.shape[0] // 2
        return block[:cols], block[cols:]

    pivots2 = ordered(rhs2, jnp.zeros_like(rhs2), wing, 1).astype(F32) - forward(updated1, select1)
    pivots2 = (
        stacked(part(pivots2, wing, 2, 0))
        + swapped(stacked(part(pivots2, 1 - wing, 2, 0)).astype(BF16), "leaf", 1).astype(F32)
    ).astype(BF16)
    pivots2 = jnp.concatenate(
        [
            jnp.concatenate(pieces, 0)
            for pieces in zip(flat(pivots2), flat(swapped(pivots2, "front", 0)))
        ],
        0,
    )
    other2 = swapped(pivots2, "leaf", 0)
    low2 = flat(jnp.where(side == 1, other2, pivots2))
    high2 = flat(jnp.where(side == 1, pivots2, other2))
    pivots2 = jnp.concatenate([low2[0], high2[0], low2[1], high2[1]], 1)
    inverse2_all = jnp.concatenate([inverse2, wing2], 0)
    solved2 = forward(pivots2, inverse2_all).astype(BF16)
    below2 = adjoint(solved2, inverse2_all)
    leaves = [below2[:, i * leaf_rows : (i + 1) * leaf_rows] for i in range(4)]
    low2 = jnp.concatenate([leaves[0], leaves[2]], 0)
    high2 = jnp.concatenate([leaves[1], leaves[3]], 0)
    handed2 = jnp.where(side == 1, low2, high2).astype(BF16)
    below2 = jnp.where(side == 1, high2, low2) + swapped(handed2, "leaf", 0).astype(F32)
    quarter = half_cols // 2
    low2, high2 = flat(below2)
    handed2 = jnp.concatenate([low2[quarter:], high2[quarter:]], 0).astype(BF16)
    below2 = jnp.concatenate([low2[:quarter], high2[:quarter]], 0)
    below2 = below2 + swapped(handed2, "front", 0).astype(F32)
    below2 = high_sum(below2).astype(BF16)
    own2 = flat(below2)
    other2 = flat(swapped(below2, "leaf", 1))
    below2 = jnp.concatenate(
        [ordered(own, other, wing, 0) for own, other in zip(own2, other2)], 1
    )

    fetched1 = adjoint(below2, pair_rows(select1)).astype(BF16)
    carried1 = pair_adjoint(fetched1, update1, update1_pair)
    weights1 = (solved1_pair.astype(F32) - high_scatter(side_scatter(carried1))).astype(BF16)
    below1 = high_sum(side_scatter(pair_adjoint(weights1, inverse1, inverse1_pair))).astype(BF16)
    below1_all = ordered(below1, swapped(below1, "leaf", 0), side, 1)

    fetched0 = adjoint(below1_all, pair_rows(select0)).astype(BF16)
    carried0 = pair_adjoint(fetched0, update0, update0_pair)
    weights0 = (solved0_pair.astype(F32) - high_scatter(carried0)).astype(BF16)
    below0 = high_scatter(pair_adjoint(weights0, inverse0, inverse0_pair))

    def finished(block):
        other = swapped(part(block, 1 - odd, 2, 1).astype(BF16), "front", 0).astype(F32)
        return ordered(part(block, odd, 2, 1).astype(F32), other, odd, 0).T

    return jnp.stack(
        [
            finished(below0),
            finished(pair_rows(below1)),
            finished(pair_rows(part(below2, wing, 2, 1))),
        ]
    )


def solution(mesh):
    placed = (
        P(None, ("leaf", "front"), None),
        P(("leaf", "front"), None),
        P(("leaf", "front"), None),
        P(None, ("leaf", "front"), None),
        P(None, ("leaf", "front")),
    )
    return jax.shard_map(
        shards,
        mesh=mesh,
        in_specs=placed,
        out_specs=P(None, ("leaf", "front"), None),
        check_vma=False,
    )
```

time: 168 us -> 134 us (0.80)
  waiting for transfers between devices: 111 us -> 83.8 us
  between operations: 13.8 us -> 0.87 us
  starting transfers between devices: 18.8 us -> 30.1 us
  local copies, waits for them, and re-layouts: 8.04 us -> 4.81 us
  matrix products: 11 us -> 7.86 us
  other arithmetic: 4.1 us -> 6.05 us
    ppermute x23 -> x31, waiting for transfers between devices: 108 us -> 83.8 us  [swapped(): lax.ppermute(shard, axis, [(i, i ^ 1 << distance) for i in range(lax.axis...]
    ppermute x23 -> x31, starting transfers between devices: 18.7 us -> 30.1 us  [swapped(): lax.ppermute(shard, axis, [(i, i ^ 1 << distance) for i in range(lax.axis...]
    all_gather x3 -> x0, waiting for transfers between devices: 3.73 us -> none  [the longest x1 3.71 us: shards(): lax.all_gather(jnp.concatenate([inverse0, update_blocks[:, :leaf_rows]],...]
    dot_general x14 -> x21, matrix products: 11 us -> 7.86 us  [product(): lax.dot_general(left, right, (((left_dim,), (right_dim,)), ((), ())), pre...]
    slice x6 -> x20, local copies, waits for them, and re-layouts: 0.8 us -> 2.85 us  [the longest x1 0.93 us: shards(): rhs[0]]
  transfers between devices with their start and end apart: 26 -> 31, of which waited for: 19 -> 25; matrix products, arithmetic and copies ran while one was open for 10% -> 6% of each run, Pallas kernels for 0% -> 0%
where the time goes in v2:
time: 134 us
  waiting for transfers between devices  83.8 us (63%)
  starting transfers between devices  30.1 us (22%)
  matrix products  7.86 us (6%)
  other arithmetic  6.05 us (5%)
  local copies, waits for them, and re-layouts  4.81 us (4%)
    ppermute x31, waiting for transfers between devices, swapped(): lax.ppermute(shard, axis, [(i, i ^ 1 << distance) for i in range(lax.axis...  83.8 us
    ppermute x31, starting transfers between devices, swapped(): lax.ppermute(shard, axis, [(i, i ^ 1 << distance) for i in range(lax.axis...  30.1 us
    dot_general x21, matrix products, product(): lax.dot_general(left, right, (((left_dim,), (right_dim,)), ((), ())), pre...  7.86 us
  transfers between devices with their start and end apart: 31, of which 25 were waited for; matrix products, arithmetic and copies ran while one was open for 6% of the time, Pallas kernels for 0%

profile of v2, /device:TPU:0, one launch (start us, length us, event | category | flops | bytes accessed | tf_op | source)
XLA Modules:
  0.0 133.6 jit_solution(2409428564892002727)
XLA Ops:
  0.0 0.9 slice.153
  0.9 3.1 %collective-permute-start = (bf16[128,128]{1,0:T(8,128)(2,1)S(1)}, bf16[128,128]{1,0:T(8,128)(2,1)S(1)}, u32[]{:S(2)}, u32[]{:S(2)}) collective-permute-start(bf16[128,128]{1,0:T(8,128)(2,1)S(1)} %get-tuple-element.73), channel_id=1, source_target_pairs={{0,1},{1,0},{2,3},{3,2},{4,5},{5,4},{6,7},{7,6},{8,9},{9,8},{10,11... | collective-permute-start | bytes 98312 | tf_op jit(solution)/shard_map/ppermute | solution.py:12
  4.0 0.9 slice.154
  5.0 0.9 slice.155
  6.0 0.7 convert.20
  6.7 0.7 convert_bitcast_fusion
  7.5 3.1 %collective-permute-start.1 = (bf16[256,128]{1,0:T(8,128)(2,1)S(1)}, bf16[256,128]{1,0:T(8,128)(2,1)S(1)}, u32[]{:S(2)}, u32[]{:S(2)}) collective-permute-start(bf16[256,128]{1,0:T(8,128)(2,1)S(1)} %maximum_select_fusion.17), channel_id=1, source_target_pairs={{0,2},{1,3},{2,0},{3,1},{4,6},{5,7},{6,4},{7,5},{8,10},{9,11},{10,... | collective-permute-start | bytes 196616 | tf_op jit(solution)/shard_map/ppermute | solution.py:12
  10.7 1.6 %collective-permute-start.3 = (bf16[272,128]{1,0:T(8,128)(2,1)S(1)}, bf16[272,128]{1,0:T(8,128)(2,1)S(1)}, u32[]{:S(2)}, u32[]{:S(2)}) collective-permute-start(bf16[272,128]{1,0:T(8,128)(2,1)S(1)} %pad_maximum_fusion.10), channel_id=1, source_target_pairs={{0,1},{1,0},{2,3},{3,2},{4,5},{5,4},{6,7},{7,6},{8,9},{9,8},{10,11... | collective-permute-start | bytes 208904 | tf_op jit(solution)/shard_map/ppermute | solution.py:12
  12.3 0.4 collective-permute-start.5
  12.8 1.5 %collective-permute-start.8 = (bf16[128,2048]{1,0:T(8,128)(2,1)S(1)}, bf16[128,2048]{1,0:T(8,128)(2,1)}, u32[]{:S(2)}, u32[]{:S(2)}) collective-permute-start(bf16[128,2048]{1,0:T(8,128)(2,1)S(1)} %slice.162), channel_id=1, source_target_pairs={{0,8},{4,12},{8,0},{12,4},{16,24},{20,28},{24,16},{28,20},{1,9},{5... | collective-permute-start | bytes 1572872 | tf_op jit(solution)/shard_map/ppermute | solution.py:12
  14.3 1.5 %collective-permute-done.3 = bf16[272,128]{1,0:T(8,128)(2,1)S(1)} collective-permute-done((bf16[272,128]{1,0:T(8,128)(2,1)S(1)}, bf16[272,128]{1,0:T(8,128)(2,1)S(1)}, u32[]{:S(2)}, u32[]{:S(2)}) %collective-permute-start.3) | collective-permute-done | bytes 69664 | tf_op jit(solution)/shard_map/ppermute | solution.py:12
  16.2 0.3 copy-done.4
  16.4 1.1 collective-permute-start.4
  17.5 1.7 %collective-permute-start.6 = (bf16[128,1024]{1,0:T(8,128)(2,1)S(1)}, bf16[128,1024]{1,0:T(8,128)(2,1)S(1)}, u32[]{:S(2)}, u32[]{:S(2)}) collective-permute-start(bf16[128,1024]{1,0:T(8,128)(2,1)S(1)} %slice.157), channel_id=1, source_target_pairs={{0,1},{1,0},{2,3},{3,2},{4,5},{5,4},{6,7},{7,6},{8,9},{9,8},{10,11... | collective-permute-start | bytes 786440 | tf_op jit(solution)/shard_map/ppermute | solution.py:12
  19.5 2.2 %collective-permute-done.4 = bf16[128,256]{0,1:T(8,128)(2,1)S(1)} collective-permute-done((bf16[128,256]{0,1:T(8,128)(2,1)S(1)}, bf16[128,256]{0,1:T(8,128)(2,1)S(1)}, u32[]{:S(2)}, u32[]{:S(2)}) %collective-permute-start.4) | collective-permute-done | bytes 65568 | tf_op jit(solution)/shard_map/ppermute | solution.py:12
  21.7 2.7 %collective-permute-done.6 = bf16[128,1024]{1,0:T(8,128)(2,1)S(1)} collective-permute-done((bf16[128,1024]{1,0:T(8,128)(2,1)S(1)}, bf16[128,1024]{1,0:T(8,128)(2,1)S(1)}, u32[]{:S(2)}, u32[]{:S(2)}) %collective-permute-start.6) | collective-permute-done | bytes 262176 | tf_op jit(solution)/shard_map/ppermute | solution.py:12
  24.8 2.1 %collective-permute-start.7 = (bf16[272,256]{0,1:T(8,128)(2,1)S(1)}, bf16[272,256]{0,1:T(8,128)(2,1)S(1)}, u32[]{:S(2)}, u32[]{:S(2)}) collective-permute-start(bf16[272,256]{0,1:T(8,128)(2,1)S(1)} %pad_maximum_fusion.6), channel_id=1, source_target_pairs={{0,2},{1,3},{2,0},{3,1},{4,6},{5,7},{6,4},{7,5},{8,10},{9,11},{10,... | collective-permute-start | bytes 417800 | tf_op jit(solution)/shard_map/ppermute | solution.py:12
  27.0 6.6 %collective-permute-done.7 = bf16[272,256]{0,1:T(8,128)(2,1)S(1)} collective-permute-done((bf16[272,256]{0,1:T(8,128)(2,1)S(1)}, bf16[272,256]{0,1:T(8,128)(2,1)S(1)}, u32[]{:S(2)}, u32[]{:S(2)}) %collective-permute-start.7) | collective-permute-done | bytes 139296 | tf_op jit(solution)/shard_map/ppermute | solution.py:12
  33.8 0.4 fusion.23
  34.2 0.5 fusion.105
  34.9 0.5 collective-permute-start.11
  35.4 1.0 collective-permute-done.9
  36.9 2.5 %collective-permute-start.10 = (bf16[128,256]{0,1:T(8,128)(2,1)S(1)}, bf16[128,256]{0,1:T(8,128)(2,1)S(1)}, u32[]{:S(2)}, u32[]{:S(2)}) collective-permute-start(bf16[128,256]{0,1:T(8,128)(2,1)S(1)} %fusion.36), channel_id=1, source_target_pairs={{0,2},{1,3},{2,0},{3,1},{4,6},{5,7},{6,4},{7,5},{8,10},{9,11},{10,... | collective-permute-start | bytes 196616 | tf_op jit(solution)/shard_map/ppermute | solution.py:12
  39.3 3.6 %collective-permute-done.10 = bf16[128,256]{0,1:T(8,128)(2,1)S(1)} collective-permute-done((bf16[128,256]{0,1:T(8,128)(2,1)S(1)}, bf16[128,256]{0,1:T(8,128)(2,1)S(1)}, u32[]{:S(2)}, u32[]{:S(2)}) %collective-permute-start.10) | collective-permute-done | bytes 65568 | tf_op jit(solution)/shard_map/ppermute | solution.py:12
  43.0 2.0 %collective-permute-done.11 = bf16[128,1024]{1,0:T(8,128)(2,1)S(1)} collective-permute-done((bf16[128,1024]{1,0:T(8,128)(2,1)S(1)}, bf16[128,1024]{1,0:T(8,128)(2,1)S(1)}, u32[]{:S(2)}, u32[]{:S(2)}) %collective-permute-start.11) | collective-permute-done | bytes 262176 | tf_op jit(solution)/shard_map/ppermute | solution.py:12
  45.1 1.3 collective-permute-done.12
  46.9 1.5 %collective-permute-start.13 = (bf16[256,256]{0,1:T(8,128)(2,1)S(1)}, bf16[256,256]{0,1:T(8,128)(2,1)S(1)}, u32[]{:S(2)}, u32[]{:S(2)}) collective-permute-start(bf16[256,256]{0,1:T(8,128)(2,1)S(1)} %pad_maximum_fusion.7), channel_id=1, source_target_pairs={{0,2},{1,3},{2,0},{3,1},{4,6},{5,7},{6,4},{7,5},{8,10},{9,11},{10,... | collective-permute-start | bytes 393224 | tf_op jit(solution)/shard_map/ppermute | solution.py:12
  48.5 7.8 %collective-permute-done.13 = bf16[256,256]{0,1:T(8,128)(2,1)S(1)} collective-permute-done((bf16[256,256]{0,1:T(8,128)(2,1)S(1)}, bf16[256,256]{0,1:T(8,128)(2,1)S(1)}, u32[]{:S(2)}, u32[]{:S(2)}) %collective-permute-start.13) | collective-permute-done | bytes 131104 | tf_op jit(solution)/shard_map/ppermute | solution.py:12
  56.4 0.5 convolution_subtract_fusion
  57.2 1.6 %collective-permute-start.14 = (bf16[128,512]{0,1:T(8,128)(2,1)S(1)}, bf16[128,512]{0,1:T(8,128)(2,1)S(1)}, u32[]{:S(2)}, u32[]{:S(2)}) collective-permute-start(bf16[128,512]{0,1:T(8,128)(2,1)S(1)} %pad_maximum_fusion.8), channel_id=1, source_target_pairs={{0,8},{4,12},{8,0},{12,4},{16,24},{20,28},{24,16},{28,20},{1,9},{5... | collective-permute-start | bytes 393224 | tf_op jit(solution)/shard_map/ppermute | solution.py:12
  59.0 3.2 %collective-permute-done.14 = bf16[128,512]{0,1:T(8,128)(2,1)S(1)} collective-permute-done((bf16[128,512]{0,1:T(8,128)(2,1)S(1)}, bf16[128,512]{0,1:T(8,128)(2,1)S(1)}, u32[]{:S(2)}, u32[]{:S(2)}) %collective-permute-start.14) | collective-permute-done | bytes 131104 | tf_op jit(solution)/shard_map/ppermute | solution.py:12
  62.6 4.8 %collective-permute-done.15 = bf16[128,512]{0,1:T(8,128)(2,1)S(1)} collective-permute-done((bf16[128,512]{0,1:T(8,128)(2,1)S(1)}, bf16[128,512]{0,1:T(8,128)(2,1)S(1)}, u32[]{:S(2)}, u32[]{:S(2)}) %collective-permute-start.15) | collective-permute-done | bytes 131104 | tf_op jit(solution)/shard_map/ppermute | solution.py:12
  67.8 1.5 %collective-permute-done.16 = bf16[256,512]{0,1:T(8,128)(2,1)S(1)} collective-permute-done((bf16[256,512]{0,1:T(8,128)(2,1)S(1)}, bf16[256,512]{0,1:T(8,128)(2,1)S(1)}, u32[]{:S(2)}, u32[]{:S(2)}) %collective-permute-start.16) | collective-permute-done | bytes 262176 | tf_op jit(solution)/shard_map/ppermute | solution.py:12
  69.3 0.3 broadcast_select_fusion.1
  69.6 2.6 %fusion = f32[128,2048]{0,1:T(8,128)S(1)} fusion(bf16[128,2048]{1,0:T(8,128)(2,1)} %collective-permute-done.8, bf16[128,2048]{1,0:T(8,128)(2,1)S(1)} %slice.162, bf16[128,512]{0,1:T(8,128)(2,1)S(1)} %get-tuple-element.56, bf16[128,512]{0,1:T(8,128)(2,1)S(1)} %get-tuple-element.54, bf16[128,512]{0,1:T(8,128)(2,1)S(1)} %get-tuple-element.55, ...), kind=kOutput, calls=%fused_computation.11 | convolution fusion | flops 274759680 | bytes 2621440 | tf_op jit(solution)/shard_map/dot_general | solution.py:16
  72.5 1.4 %collective-permute-done.17 = bf16[256,512]{0,1:T(8,128)(2,1)S(1)} collective-permute-done((bf16[256,512]{0,1:T(8,128)(2,1)S(1)}, bf16[256,512]{0,1:T(8,128)(2,1)S(1)}, u32[]{:S(2)}, u32[]{:S(2)}) %collective-permute-start.17) | collective-permute-done | bytes 262176 | tf_op jit(solution)/shard_map/ppermute | solution.py:12
  74.4 5.5 %collective-permute-done.18 = bf16[128,512]{0,1:T(8,128)(2,1)S(1)} collective-permute-done((bf16[128,512]{0,1:T(8,128)(2,1)S(1)}, bf16[128,512]{0,1:T(8,128)(2,1)S(1)}, u32[]{:S(2)}, u32[]{:S(2)}) %collective-permute-start.18) | collective-permute-done | bytes 131104 | tf_op jit(solution)/shard_map/ppermute | solution.py:12
  80.0 1.7 %collective-permute-start.19 = (bf16[128,512]{0,1:T(8,128)(2,1)S(1)}, bf16[128,512]{0,1:T(8,128)(2,1)S(1)}, u32[]{:S(2)}, u32[]{:S(2)}) collective-permute-start(bf16[128,512]{0,1:T(8,128)(2,1)S(1)} %fusion.74), channel_id=1, source_target_pairs={{0,2},{1,3},{2,0},{3,1},{4,6},{5,7},{6,4},{7,5},{8,10},{9,11},{10,... | collective-permute-start | bytes 393224 | tf_op jit(solution)/shard_map/ppermute | solution.py:12
  81.8 0.4 iota_compare_fusion
  82.1 6.4 %collective-permute-done.19 = bf16[128,512]{0,1:T(8,128)(2,1)S(1)} collective-permute-done((bf16[128,512]{0,1:T(8,128)(2,1)S(1)}, bf16[128,512]{0,1:T(8,128)(2,1)S(1)}, u32[]{:S(2)}, u32[]{:S(2)}) %collective-permute-start.19) | collective-permute-done | bytes 131104 | tf_op jit(solution)/shard_map/ppermute | solution.py:12
  88.7 1.6 %collective-permute-start.20 = (bf16[128,512]{0,1:T(8,128)(2,1)S(1)}, bf16[128,512]{0,1:T(8,128)(2,1)S(1)}, u32[]{:S(2)}, u32[]{:S(2)}) collective-permute-start(bf16[128,512]{0,1:T(8,128)(2,1)S(1)} %add_convert_fusion.2), channel_id=1, source_target_pairs={{0,8},{4,12},{8,0},{12,4},{16,24},{20,28},{24,16},{28,20},{1,9},{5... | collective-permute-start | bytes 393224 | tf_op jit(solution)/shard_map/ppermute | solution.py:12
  90.4 3.5 %collective-permute-done.20 = bf16[128,512]{0,1:T(8,128)(2,1)S(1)} collective-permute-done((bf16[128,512]{0,1:T(8,128)(2,1)S(1)}, bf16[128,512]{0,1:T(8,128)(2,1)S(1)}, u32[]{:S(2)}, u32[]{:S(2)}) %collective-permute-start.20) | collective-permute-done | bytes 131104 | tf_op jit(solution)/shard_map/ppermute | solution.py:12
  94.1 0.3 maximum_select_fusion.12
  94.4 0.3 convolution_convert_fusion.1
  94.7 0.3 fusion.58
  95.0 0.3 convolution_add_fusion.1
  95.4 1.3 collective-permute-done.21
  96.9 6.4 %collective-permute-done.22 = bf16[128,256]{0,1:T(8,128)(2,1)S(1)} collective-permute-done((bf16[128,256]{0,1:T(8,128)(2,1)S(1)}, bf16[128,256]{0,1:T(8,128)(2,1)S(1)}, u32[]{:S(2)}, u32[]{:S(2)}) %collective-permute-start.22) | collective-permute-done | bytes 65568 | tf_op jit(solution)/shard_map/ppermute | solution.py:12
  103.4 0.3 fusion.55
  103.7 0.3 convolution_add_fusion
  104.0 1.3 collective-permute-done.23
  105.5 0.3 fusion.46
  105.8 2.3 %collective-permute-start.30 = (bf16[128,128]{0,1:T(8,128)(2,1)S(1)}, bf16[128,128]{0,1:T(8,128)(2,1)S(1)}, u32[]{:S(2)}, u32[]{:S(2)}) collective-permute-start(bf16[128,128]{0,1:T(8,128)(2,1)S(1)} %get-tuple-element.49), channel_id=1, source_target_pairs={{0,1},{1,0},{2,3},{3,2},{4,5},{5,4},{6,7},{7,6},{8,9},{9,8},{10,11... | collective-permute-start | bytes 98312 | tf_op jit(solution)/shard_map/ppermute | solution.py:12
  108.1 5.7 %collective-permute-done.24 = bf16[128,512]{0,1:T(8,128)(2,1)S(1)} collective-permute-done((bf16[128,512]{0,1:T(8,128)(2,1)S(1)}, bf16[128,512]{0,1:T(8,128)(2,1)S(1)}, u32[]{:S(2)}, u32[]{:S(2)}) %collective-permute-start.24) | collective-permute-done | bytes 131104 | tf_op jit(solution)/shard_map/ppermute | solution.py:12
  114.0 0.4 iota_compare_fusion.1
  114.5 0.8 collective-permute-done.25
  115.3 0.3 convolution_convert_fusion
  116.1 2.0 %collective-permute-start.26 = (bf16[128,256]{0,1:T(8,128)(2,1)S(1)}, bf16[128,256]{0,1:T(8,128)(2,1)S(1)}, u32[]{:S(2)}, u32[]{:S(2)}) collective-permute-start(bf16[128,256]{0,1:T(8,128)(2,1)S(1)} %dynamic-slice_convert_fusion.4), channel_id=1, source_target_pairs={{0,2},{1,3},{2,0},{3,1},{4,6},{5,7},{6,4},{7,5},{8,10},{9,11},{10,... | collective-permute-start | bytes 196616 | tf_op jit(solution)/shard_map/ppermute | solution.py:12
  118.1 0.3 collective-permute-done.29
  118.4 4.3 %collective-permute-done.26 = bf16[128,256]{0,1:T(8,128)(2,1)S(1)} collective-permute-done((bf16[128,256]{0,1:T(8,128)(2,1)S(1)}, bf16[128,256]{0,1:T(8,128)(2,1)S(1)}, u32[]{:S(2)}, u32[]{:S(2)}) %collective-permute-start.26) | collective-permute-done | bytes 65568 | tf_op jit(solution)/shard_map/ppermute | solution.py:12
  123.2 0.7 collective-permute-start.27
  123.9 4.7 %collective-permute-done.27 = bf16[128,256]{1,0:T(8,128)(2,1)S(1)} collective-permute-done((bf16[128,256]{1,0:T(8,128)(2,1)S(1)}, bf16[128,256]{1,0:T(8,128)(2,1)S(1)}, u32[]{:S(2)}, u32[]{:S(2)}) %collective-permute-start.27) | collective-permute-done | bytes 65568 | tf_op jit(solution)/shard_map/ppermute | solution.py:12
  128.8 3.9 %collective-permute-done.28 = bf16[128,128]{1,0:T(8,128)(2,1)S(1)} collective-permute-done((bf16[128,128]{1,0:T(8,128)(2,1)S(1)}, bf16[128,128]{1,0:T(8,128)(2,1)S(1)}, u32[]{:S(2)}, u32[]{:S(2)}) %collective-permute-start.28) | collective-permute-done | bytes 32800 | tf_op jit(solution)/shard_map/ppermute | solution.py:12
  132.8 0.8 pad_maximum_fusion.2
  (124 shorter events, 7.3 us)
Async XLA Ops:
  0.0 10.6 %copy-start = (bf16[128,3584]{1,0:T(8,128)(2,1)S(1)}, bf16[128,3584]{1,0:T(8,128)(2,1)}, u32[]{:S(2)}) copy-start(bf16[128,3584]{1,0:T(8,128)(2,1)} %param.6) | copy-start | bytes 2752516
  0.9 6.5 %collective-permute-start = (bf16[128,128]{1,0:T(8,128)(2,1)S(1)}, bf16[128,128]{1,0:T(8,128)(2,1)S(1)}, u32[]{:S(2)}, u32[]{:S(2)}) collective-permute-start(bf16[128,128]{1,0:T(8,128)(2,1)S(1)} %get-tuple-element.73), channel_id=1, source_target_pairs={{0,1},{1,0},{2,3},{3,2},{4,5},{5,4},{6,7},{7,6},{8,9},{9,8},{10,11... | collective-permute-start | bytes 98312 | tf_op jit(solution)/shard_map/ppermute | solution.py:12
  4.9 10.8 %collective-permute-start.2 = (bf16[128,512]{1,0:T(8,128)(2,1)S(1)}, bf16[128,512]{1,0:T(8,128)(2,1)S(1)}, u32[]{:S(2)}, u32[]{:S(2)}) collective-permute-start(bf16[128,512]{1,0:T(8,128)(2,1)S(1)} %slice.154), channel_id=1, source_target_pairs={{0,1},{1,0},{2,3},{3,2},{4,5},{5,4},{6,7},{7,6},{8,9},{9,8},{10,11... | collective-permute-start | bytes 393224 | tf_op jit(solution)/shard_map/ppermute | solution.py:12
  5.9 4.7 %copy-start.1 = (bf16[128,1536]{1,0:T(8,128)(2,1)S(1)}, bf16[128,1536]{1,0:T(8,128)(2,1)}, u32[]{:S(2)}) copy-start(bf16[128,1536]{1,0:T(8,128)(2,1)} %param.7) | copy-start | bytes 1179652
  7.5 6.8 %collective-permute-start.1 = (bf16[256,128]{1,0:T(8,128)(2,1)S(1)}, bf16[256,128]{1,0:T(8,128)(2,1)S(1)}, u32[]{:S(2)}, u32[]{:S(2)}) collective-permute-start(bf16[256,128]{1,0:T(8,128)(2,1)S(1)} %maximum_select_fusion.17), channel_id=1, source_target_pairs={{0,2},{1,3},{2,0},{3,1},{4,6},{5,7},{6,4},{7,5},{8,10},{9,11},{10,... | collective-permute-start | bytes 196616 | tf_op jit(solution)/shard_map/ppermute | solution.py:12
  10.7 5.1 %collective-permute-start.3 = (bf16[272,128]{1,0:T(8,128)(2,1)S(1)}, bf16[272,128]{1,0:T(8,128)(2,1)S(1)}, u32[]{:S(2)}, u32[]{:S(2)}) collective-permute-start(bf16[272,128]{1,0:T(8,128)(2,1)S(1)} %pad_maximum_fusion.10), channel_id=1, source_target_pairs={{0,1},{1,0},{2,3},{3,2},{4,5},{5,4},{6,7},{7,6},{8,9},{9,8},{10,11... | collective-permute-start | bytes 208904 | tf_op jit(solution)/shard_map/ppermute | solution.py:12
  12.3 9.4 %collective-permute-start.5 = (bf16[128,512]{1,0:T(8,128)(2,1)S(1)}, bf16[128,512]{1,0:T(8,128)(2,1)S(1)}, u32[]{:S(2)}, u32[]{:S(2)}) collective-permute-start(bf16[128,512]{1,0:T(8,128)(2,1)S(1)} %slice.156), channel_id=1, source_target_pairs={{0,1},{1,0},{2,3},{3,2},{4,5},{5,4},{6,7},{7,6},{8,9},{9,8},{10,11... | collective-permute-start | bytes 393224 | tf_op jit(solution)/shard_map/ppermute | solution.py:12
  12.8 21.0 %collective-permute-start.8 = (bf16[128,2048]{1,0:T(8,128)(2,1)S(1)}, bf16[128,2048]{1,0:T(8,128)(2,1)}, u32[]{:S(2)}, u32[]{:S(2)}) collective-permute-start(bf16[128,2048]{1,0:T(8,128)(2,1)S(1)} %slice.162), channel_id=1, source_target_pairs={{0,8},{4,12},{8,0},{12,4},{16,24},{20,28},{24,16},{28,20},{1,9},{5... | collective-permute-start | bytes 1572872 | tf_op jit(solution)/shard_map/ppermute | solution.py:12
  15.8 0.7 copy-start.4
  16.4 5.2 %collective-permute-start.4 = (bf16[128,256]{0,1:T(8,128)(2,1)S(1)}, bf16[128,256]{0,1:T(8,128)(2,1)S(1)}, u32[]{:S(2)}, u32[]{:S(2)}) collective-permute-start(bf16[128,256]{0,1:T(8,128)(2,1)S(1)} %fusion.34), channel_id=1, source_target_pairs={{0,2},{1,3},{2,0},{3,1},{4,6},{5,7},{6,4},{7,5},{8,10},{9,11},{10,... | collective-permute-start | bytes 196616 | tf_op jit(solution)/shard_map/ppermute | solution.py:12
  17.5 6.9 %collective-permute-start.6 = (bf16[128,1024]{1,0:T(8,128)(2,1)S(1)}, bf16[128,1024]{1,0:T(8,128)(2,1)S(1)}, u32[]{:S(2)}, u32[]{:S(2)}) collective-permute-start(bf16[128,1024]{1,0:T(8,128)(2,1)S(1)} %slice.157), channel_id=1, source_target_pairs={{0,1},{1,0},{2,3},{3,2},{4,5},{5,4},{6,7},{7,6},{8,9},{9,8},{10,11... | collective-permute-start | bytes 786440 | tf_op jit(solution)/shard_map/ppermute | solution.py:12
  21.7 2.9 %copy-start.6 = (bf16[128,512]{1,0:T(8,128)(2,1)}, bf16[128,512]{1,0:T(8,128)(2,1)S(1)}, u32[]{:S(2)}) copy-start(bf16[128,512]{1,0:T(8,128)(2,1)S(1)} %collective-permute-done.5) | copy-start | bytes 393220
  24.4 12.2 %copy-start.2 = (bf16[128,1024]{1,0:T(8,128)(2,1)}, bf16[128,1024]{1,0:T(8,128)(2,1)S(1)}, u32[]{:S(2)}) copy-start(bf16[128,1024]{1,0:T(8,128)(2,1)S(1)} %collective-permute-done.6) | copy-start | bytes 786436
  24.8 8.7 %collective-permute-start.7 = (bf16[272,256]{0,1:T(8,128)(2,1)S(1)}, bf16[272,256]{0,1:T(8,128)(2,1)S(1)}, u32[]{:S(2)}, u32[]{:S(2)}) collective-permute-start(bf16[272,256]{0,1:T(8,128)(2,1)S(1)} %pad_maximum_fusion.6), channel_id=1, source_target_pairs={{0,2},{1,3},{2,0},{3,1},{4,6},{5,7},{6,4},{7,5},{8,10},{9,11},{10,... | collective-permute-start | bytes 417800 | tf_op jit(solution)/shard_map/ppermute | solution.py:12
  34.8 1.6 %collective-permute-start.9 = (bf16[128,1024]{0,1:T(8,128)(2,1)S(1)}, bf16[128,1024]{0,1:T(8,128)(2,1)S(1)}, u32[]{:S(2)}, u32[]{:S(2)}) collective-permute-start(bf16[128,1024]{0,1:T(8,128)(2,1)S(1)} %get-tuple-element.77), channel_id=1, source_target_pairs={{0,4},{4,0},{8,12},{12,8},{16,20},{20,16},{24,28},{28,24},{1,5},{5... | collective-permute-start | bytes 786440 | tf_op jit(solution)/shard_map/ppermute | solution.py:12
  34.9 10.2 %collective-permute-start.11 = (bf16[128,1024]{1,0:T(8,128)(2,1)S(1)}, bf16[128,1024]{1,0:T(8,128)(2,1)S(1)}, u32[]{:S(2)}, u32[]{:S(2)}) collective-permute-start(bf16[128,1024]{1,0:T(8,128)(2,1)S(1)} %slice.168), channel_id=1, source_target_pairs={{0,1},{1,0},{2,3},{3,2},{4,5},{5,4},{6,7},{7,6},{8,9},{9,8},{10,11... | collective-permute-start | bytes 786440 | tf_op jit(solution)/shard_map/ppermute | solution.py:12
  36.9 6.1 %collective-permute-start.10 = (bf16[128,256]{0,1:T(8,128)(2,1)S(1)}, bf16[128,256]{0,1:T(8,128)(2,1)S(1)}, u32[]{:S(2)}, u32[]{:S(2)}) collective-permute-start(bf16[128,256]{0,1:T(8,128)(2,1)S(1)} %fusion.36), channel_id=1, source_target_pairs={{0,2},{1,3},{2,0},{3,1},{4,6},{5,7},{6,4},{7,5},{8,10},{9,11},{10,... | collective-permute-start | bytes 196616 | tf_op jit(solution)/shard_map/ppermute | solution.py:12
  45.0 1.9 %copy-start.8 = (bf16[128,1024]{1,0:T(8,128)(2,1)}, bf16[128,1024]{1,0:T(8,128)(2,1)S(1)}, u32[]{:S(2)}) copy-start(bf16[128,1024]{1,0:T(8,128)(2,1)S(1)} %collective-permute-done.11) | copy-start | bytes 786436
  45.0 1.3 %collective-permute-start.12 = (bf16[128,512]{0,1:T(8,128)(2,1)S(1)}, bf16[128,512]{0,1:T(8,128)(2,1)S(1)}, u32[]{:S(2)}, u32[]{:S(2)}) collective-permute-start(bf16[128,512]{0,1:T(8,128)(2,1)S(1)} %maximum_select_fusion.10), channel_id=1, source_target_pairs={{0,4},{4,0},{8,12},{12,8},{16,20},{20,16},{24,28},{28,24},{1,5},{5... | collective-permute-start | bytes 393224 | tf_op jit(solution)/shard_map/ppermute | solution.py:12
  46.9 9.3 %collective-permute-start.13 = (bf16[256,256]{0,1:T(8,128)(2,1)S(1)}, bf16[256,256]{0,1:T(8,128)(2,1)S(1)}, u32[]{:S(2)}, u32[]{:S(2)}) collective-permute-start(bf16[256,256]{0,1:T(8,128)(2,1)S(1)} %pad_maximum_fusion.7), channel_id=1, source_target_pairs={{0,2},{1,3},{2,0},{3,1},{4,6},{5,7},{6,4},{7,5},{8,10},{9,11},{10,... | collective-permute-start | bytes 393224 | tf_op jit(solution)/shard_map/ppermute | solution.py:12
  57.2 5.0 %collective-permute-start.14 = (bf16[128,512]{0,1:T(8,128)(2,1)S(1)}, bf16[128,512]{0,1:T(8,128)(2,1)S(1)}, u32[]{:S(2)}, u32[]{:S(2)}) collective-permute-start(bf16[128,512]{0,1:T(8,128)(2,1)S(1)} %pad_maximum_fusion.8), channel_id=1, source_target_pairs={{0,8},{4,12},{8,0},{12,4},{16,24},{20,28},{24,16},{28,20},{1,9},{5... | collective-permute-start | bytes 393224 | tf_op jit(solution)/shard_map/ppermute | solution.py:12
  62.4 5.0 %collective-permute-start.15 = (bf16[128,512]{0,1:T(8,128)(2,1)S(1)}, bf16[128,512]{0,1:T(8,128)(2,1)S(1)}, u32[]{:S(2)}, u32[]{:S(2)}) collective-permute-start(bf16[128,512]{0,1:T(8,128)(2,1)S(1)} %fusion.25), channel_id=1, source_target_pairs={{0,1},{1,0},{2,3},{3,2},{4,5},{5,4},{6,7},{7,6},{8,9},{9,8},{10,11... | collective-permute-start | bytes 393224 | tf_op jit(solution)/shard_map/ppermute | solution.py:12
  67.7 1.6 %collective-permute-start.16 = (bf16[256,512]{0,1:T(8,128)(2,1)S(1)}, bf16[256,512]{0,1:T(8,128)(2,1)S(1)}, u32[]{:S(2)}, u32[]{:S(2)}) collective-permute-start(bf16[256,512]{0,1:T(8,128)(2,1)S(1)} %pad_maximum_fusion.5), channel_id=1, source_target_pairs={{0,4},{4,0},{8,12},{12,8},{16,20},{20,16},{24,28},{28,24},{1,5},{5... | collective-permute-start | bytes 786440 | tf_op jit(solution)/shard_map/ppermute | solution.py:12
  72.3 1.6 %collective-permute-start.17 = (bf16[256,512]{0,1:T(8,128)(2,1)S(1)}, bf16[256,512]{0,1:T(8,128)(2,1)S(1)}, u32[]{:S(2)}, u32[]{:S(2)}) collective-permute-start(bf16[256,512]{0,1:T(8,128)(2,1)S(1)} %select_convert_fusion), channel_id=1, source_target_pairs={{0,4},{4,0},{8,12},{12,8},{16,20},{20,16},{24,28},{28,24},{1,5},{5... | collective-permute-start | bytes 786440 | tf_op jit(solution)/shard_map/ppermute | solution.py:12
  74.3 5.6 %collective-permute-start.18 = (bf16[128,512]{0,1:T(8,128)(2,1)S(1)}, bf16[128,512]{0,1:T(8,128)(2,1)S(1)}, u32[]{:S(2)}, u32[]{:S(2)}) collective-permute-start(bf16[128,512]{0,1:T(8,128)(2,1)S(1)} %pad_maximum_fusion.9), channel_id=1, source_target_pairs={{0,1},{1,0},{2,3},{3,2},{4,5},{5,4},{6,7},{7,6},{8,9},{9,8},{10,11... | collective-permute-start | bytes 393224 | tf_op jit(solution)/shard_map/ppermute | solution.py:12
  80.0 8.5 %collective-permute-start.19 = (bf16[128,512]{0,1:T(8,128)(2,1)S(1)}, bf16[128,512]{0,1:T(8,128)(2,1)S(1)}, u32[]{:S(2)}, u32[]{:S(2)}) collective-permute-start(bf16[128,512]{0,1:T(8,128)(2,1)S(1)} %fusion.74), channel_id=1, source_target_pairs={{0,2},{1,3},{2,0},{3,1},{4,6},{5,7},{6,4},{7,5},{8,10},{9,11},{10,... | collective-permute-start | bytes 393224 | tf_op jit(solution)/shard_map/ppermute | solution.py:12
  88.7 5.3 %collective-permute-start.20 = (bf16[128,512]{0,1:T(8,128)(2,1)S(1)}, bf16[128,512]{0,1:T(8,128)(2,1)S(1)}, u32[]{:S(2)}, u32[]{:S(2)}) collective-permute-start(bf16[128,512]{0,1:T(8,128)(2,1)S(1)} %add_convert_fusion.2), channel_id=1, source_target_pairs={{0,8},{4,12},{8,0},{12,4},{16,24},{20,28},{24,16},{28,20},{1,9},{5... | collective-permute-start | bytes 393224 | tf_op jit(solution)/shard_map/ppermute | solution.py:12
  94.1 1.0 copy-start.9
  95.3 8.3 %copy-start.3 = (bf16[128,1024]{1,0:T(8,128)(2,1)S(1)}, bf16[128,1024]{1,0:T(8,128)(2,1)}, u32[]{:S(2)}) copy-start(bf16[128,1024]{1,0:T(8,128)(2,1)} %copy-done.2) | copy-start | bytes 786436
  95.3 1.4 %collective-permute-start.21 = (bf16[128,512]{0,1:T(8,128)(2,1)S(1)}, bf16[128,512]{0,1:T(8,128)(2,1)S(1)}, u32[]{:S(2)}, u32[]{:S(2)}) collective-permute-start(bf16[128,512]{0,1:T(8,128)(2,1)S(1)} %dynamic-slice_convert_fusion.2), channel_id=1, source_target_pairs={{0,4},{4,0},{8,12},{12,8},{16,20},{20,16},{24,28},{28,24},{1,5},{5... | collective-permute-start | bytes 393224 | tf_op jit(solution)/shard_map/ppermute | solution.py:12
  96.8 6.5 %collective-permute-start.22 = (bf16[128,256]{0,1:T(8,128)(2,1)S(1)}, bf16[128,256]{0,1:T(8,128)(2,1)S(1)}, u32[]{:S(2)}, u32[]{:S(2)}) collective-permute-start(bf16[128,256]{0,1:T(8,128)(2,1)S(1)} %dynamic-slice_convert_fusion.5), channel_id=1, source_target_pairs={{0,2},{1,3},{2,0},{3,1},{4,6},{5,7},{6,4},{7,5},{8,10},{9,11},{10,... | collective-permute-start | bytes 196616 | tf_op jit(solution)/shard_map/ppermute | solution.py:12
  104.0 1.4 %collective-permute-start.23 = (bf16[128,512]{0,1:T(8,128)(2,1)S(1)}, bf16[128,512]{0,1:T(8,128)(2,1)S(1)}, u32[]{:S(2)}, u32[]{:S(2)}) collective-permute-start(bf16[128,512]{0,1:T(8,128)(2,1)S(1)} %dynamic-slice_convert_fusion.1), channel_id=1, source_target_pairs={{0,4},{4,0},{8,12},{12,8},{16,20},{20,16},{24,28},{28,24},{1,5},{5... | collective-permute-start | bytes 393224 | tf_op jit(solution)/shard_map/ppermute | solution.py:12
  105.4 8.4 %collective-permute-start.24 = (bf16[128,512]{0,1:T(8,128)(2,1)S(1)}, bf16[128,512]{0,1:T(8,128)(2,1)S(1)}, u32[]{:S(2)}, u32[]{:S(2)}) collective-permute-start(bf16[128,512]{0,1:T(8,128)(2,1)S(1)} %fusion.32), channel_id=1, source_target_pairs={{0,2},{1,3},{2,0},{3,1},{4,6},{5,7},{6,4},{7,5},{8,10},{9,11},{10,... | collective-permute-start | bytes 393224 | tf_op jit(solution)/shard_map/ppermute | solution.py:12
  105.8 8.5 %collective-permute-start.30 = (bf16[128,128]{0,1:T(8,128)(2,1)S(1)}, bf16[128,128]{0,1:T(8,128)(2,1)S(1)}, u32[]{:S(2)}, u32[]{:S(2)}) collective-permute-start(bf16[128,128]{0,1:T(8,128)(2,1)S(1)} %get-tuple-element.49), channel_id=1, source_target_pairs={{0,1},{1,0},{2,3},{3,2},{4,5},{5,4},{6,7},{7,6},{8,9},{9,8},{10,11... | collective-permute-start | bytes 98312 | tf_op jit(solution)/shard_map/ppermute | solution.py:12
  113.9 1.4 %collective-permute-start.25 = (bf16[128,512]{0,1:T(8,128)(2,1)S(1)}, bf16[128,512]{0,1:T(8,128)(2,1)S(1)}, u32[]{:S(2)}, u32[]{:S(2)}) collective-permute-start(bf16[128,512]{0,1:T(8,128)(2,1)S(1)} %add_convert_fusion.1), channel_id=1, source_target_pairs={{0,4},{4,0},{8,12},{12,8},{16,20},{20,16},{24,28},{28,24},{1,5},{5... | collective-permute-start | bytes 393224 | tf_op jit(solution)/shard_map/ppermute | solution.py:12
  114.3 1.5 %copy-start.7 = (bf16[128,512]{1,0:T(8,128)(2,1)S(1)}, bf16[128,512]{1,0:T(8,128)(2,1)}, u32[]{:S(2)}) copy-start(bf16[128,512]{1,0:T(8,128)(2,1)} %copy-done.6) | copy-start | bytes 393220
  114.4 4.0 %collective-permute-start.29 = (bf16[128,128]{0,1:T(8,128)(2,1)S(1)}, bf16[128,128]{0,1:T(8,128)(2,1)S(1)}, u32[]{:S(2)}, u32[]{:S(2)}) collective-permute-start(bf16[128,128]{0,1:T(8,128)(2,1)S(1)} %get-tuple-element.59), channel_id=1, source_target_pairs={{0,1},{1,0},{2,3},{3,2},{4,5},{5,4},{6,7},{7,6},{8,9},{9,8},{10,11... | collective-permute-start | bytes 98312 | tf_op jit(solution)/shard_map/ppermute | solution.py:12
  115.9 7.1 %copy-start.5 = (bf16[128,512]{1,0:T(8,128)(2,1)S(1)}, bf16[128,512]{1,0:T(8,128)(2,1)}, u32[]{:S(2)}) copy-start(bf16[128,512]{1,0:T(8,128)(2,1)} %copy-done.4) | copy-start | bytes 393220
  116.1 6.5 %collective-permute-start.26 = (bf16[128,256]{0,1:T(8,128)(2,1)S(1)}, bf16[128,256]{0,1:T(8,128)(2,1)S(1)}, u32[]{:S(2)}, u32[]{:S(2)}) collective-permute-start(bf16[128,256]{0,1:T(8,128)(2,1)S(1)} %dynamic-slice_convert_fusion.4), channel_id=1, source_target_pairs={{0,2},{1,3},{2,0},{3,1},{4,6},{5,7},{6,4},{7,5},{8,10},{9,11},{10,... | collective-permute-start | bytes 196616 | tf_op jit(solution)/shard_map/ppermute | solution.py:12
  123.2 5.4 %collective-permute-start.27 = (bf16[128,256]{1,0:T(8,128)(2,1)S(1)}, bf16[128,256]{1,0:T(8,128)(2,1)S(1)}, u32[]{:S(2)}, u32[]{:S(2)}) collective-permute-start(bf16[128,256]{1,0:T(8,128)(2,1)S(1)} %dynamic-slice_convert_fusion.3), channel_id=1, source_target_pairs={{0,2},{1,3},{2,0},{3,1},{4,6},{5,7},{6,4},{7,5},{8,10},{9,11},{10,... | collective-permute-start | bytes 196616 | tf_op jit(solution)/shard_map/ppermute | solution.py:12
  128.7 4.0 %collective-permute-start.28 = (bf16[128,128]{1,0:T(8,128)(2,1)S(1)}, bf16[128,128]{1,0:T(8,128)(2,1)S(1)}, u32[]{:S(2)}, u32[]{:S(2)}) collective-permute-start(bf16[128,128]{1,0:T(8,128)(2,1)S(1)} %dynamic-slice_convert_fusion.6), channel_id=1, source_target_pairs={{0,1},{1,0},{2,3},{3,2},{4,5},{5,4},{6,7},{7,6},{8,9},{9,8},{10,11... | collective-permute-start | bytes 98312 | tf_op jit(solution)/shard_map/ppermute | solution.py:12

commit v3 on v2

v3 whole, which is shorter than its diff:
```python
import jax
import jax.numpy as jnp
from jax import lax
from jax.sharding import PartitionSpec as P

LEVELS = 3
BF16 = jnp.bfloat16
F32 = jnp.float32


def traded(shard, axis, mask):
    return lax.ppermute(shard, axis, [(i, i ^ mask) for i in range(lax.axis_size(axis))])


def product(left, right, left_dim, right_dim):
    return lax.dot_general(
        left, right, (((left_dim,), (right_dim,)), ((), ())), preferred_element_type=F32
    )


def forward(vector, matrix):
    return product(vector, matrix, 1, 1)


def adjoint(vector, matrix):
    return product(vector, matrix, 1, 0)


def ordered(own, other, upper, axis):
    return jnp.where(
        upper == 1,
        jnp.concatenate([other, own], axis),
        jnp.concatenate([own, other], axis),
    )


def after(array, *earlier):
    return lax.optimization_barrier((array, *earlier))[0]


def together(*arrays):
    return lax.optimization_barrier(arrays)


def part(array, index, count, axis):
    size = array.shape[axis] // count
    return lax.dynamic_slice_in_dim(array, index * size, size, axis)


def stacked(block):
    middle = block.shape[1] // 2
    return jnp.concatenate([block[:, :middle], block[:, middle:]], 0)


def flat(block):
    middle = block.shape[0] // 2
    return block[:middle], block[middle:]


def shards(rhs, inverse_blocks, update_blocks, asm_owner, asm_row):
    own_rows, rhs_cols = rhs.shape[1:]
    front_count = lax.axis_size("front")
    leaf_rows = front_count * own_rows
    half_cols = rhs_cols // 2
    quarter = half_cols // 2
    leaf_id = lax.axis_index("leaf")
    front_id = lax.axis_index("front")
    odd = front_id % 2
    side = leaf_id % 2
    wing = leaf_id // 2 % 2
    high_bits = range(1, front_count.bit_length() - 1)

    def high_gather(*blocks):
        for bit in high_bits:
            received = traded(jnp.concatenate(blocks, 1), "front", 1 << bit)
            ends = [sum(b.shape[1] for b in blocks[: i + 1]) for i in range(len(blocks))]
            blocks = [
                ordered(b, received[:, end - b.shape[1] : end], front_id >> bit & 1, 1)
                for b, end in zip(blocks, ends)
            ]
        return blocks[0] if len(blocks) == 1 else blocks

    def high_scatter(block):
        for bit in reversed(high_bits):
            upper = front_id >> bit & 1
            block = part(block, upper, 2, 1).astype(F32) + traded(
                part(block, 1 - upper, 2, 1).astype(BF16), "front", 1 << bit
            ).astype(F32)
        return block

    def side_scatter(block):
        return part(block, side, 2, 1) + traded(
            part(block, 1 - side, 2, 1).astype(BF16), "leaf", 1
        ).astype(F32)

    def pair_forward(vector, own, other):
        return ordered(forward(vector, own), forward(vector, other), odd, 1).astype(BF16)

    def pair_adjoint(vector, own, other):
        return adjoint(part(vector, odd, 2, 1), own) + adjoint(part(vector, 1 - odd, 2, 1), other)

    def high_sum(block):
        for bit in high_bits:
            block = block + traded(block.astype(BF16), "front", 1 << bit).astype(F32)
        return block

    def pair_rows(block):
        return part(block, front_id // 2, front_count // 2, 1)

    def high_pieces(own):
        pieces = [own]
        for bit in high_bits:
            pieces += [traded(piece, "front", 1 << bit) for piece in pieces]
        return pieces

    def in_order(blocks, axis):
        for bit in range(front_count.bit_length() - 1):
            blocks = [
                ordered(blocks[i], blocks[i + 1], front_id >> bit & 1, axis)
                for i in range(0, len(blocks), 2)
            ]
        return blocks[0]

    def leaf_forward(vector, pieces):
        return in_order([forward(vector, piece) for piece in pieces], 1).astype(BF16)

    def leaf_adjoint(vector, pieces):
        return sum(
            adjoint(part(vector, front_id ^ i, front_count, 1), piece)
            for i, piece in enumerate(pieces)
        )

    def alternated(even, odd_ones):
        return [piece for pieces in zip(even, odd_ones) for piece in pieces]

    inverse0 = inverse_blocks[:, :leaf_rows]
    inverse1 = inverse_blocks[:, leaf_rows : 3 * leaf_rows]
    inverse2 = inverse_blocks[:, 3 * leaf_rows :]
    update0 = update_blocks[:, :leaf_rows]
    update1 = update_blocks[:, leaf_rows:]
    inverse0 = lax.optimization_barrier(inverse0)
    inverse1 = lax.optimization_barrier(inverse1)
    inverse2 = lax.optimization_barrier(inverse2)
    update0 = lax.optimization_barrier(update0)
    update1 = lax.optimization_barrier(update1)

    first = jnp.concatenate([inverse0, rhs[0]], 1)
    first_even = high_pieces(first)
    inverse0_near = traded(inverse0, "front", 1)
    count = len(first_even)

    lists = jnp.concatenate([asm_owner[:, :, 0], asm_row], 0).astype(BF16)
    kept = part(rhs[1:], odd, 2, 2).reshape(2 * own_rows, -1)
    handed = part(rhs[1:], 1 - odd, 2, 2).reshape(2 * own_rows, -1)
    received = traded(
        after(jnp.concatenate([handed, lists.reshape(-1, half_cols)], 0), first), "front", 1
    )


    def level_rows(index):
        rows = slice(index * own_rows, (index + 1) * own_rows)
        return ordered(kept[rows], received[rows], odd, 0).T

    def as_block(lists):
        return lists.reshape(-1, half_cols).T

    lists = ordered(lists, received[2 * own_rows :].reshape(4, -1), odd, 1)
    rhs1, rhs2, *lists = high_gather(
        level_rows(0), level_rows(1), *(as_block(lists[i : i + 1]) for i in range(4))
    )
    lists = jnp.concatenate([block.T.reshape(1, -1) for block in lists], 0)

    through = traded(
        jnp.concatenate(
            [part(block[:, leaf_rows:], 1 - odd, 2, 1) for block in first_even]
            + [block[:, :leaf_rows] for block in first_even[1:]],
            1,
        ),
        "front",
        1,
    )
    update0_pair = traded(after(update0, first_even[-1]), "front", 1)
    wing2 = traded(after(inverse2, first), "leaf", 2)
    through, inverse0_near, update0_pair = together(through, inverse0_near, update0_pair)
    rhs0_leaf = in_order(
        alternated(
            [part(block[:, leaf_rows:], odd, 2, 1) for block in first_even],
            [through[:, i * half_cols : (i + 1) * half_cols] for i in range(count)],
        ),
        0,
    )
    inverse0_pieces = alternated(
        [block[:, :leaf_rows] for block in first_even],
        [inverse0_near]
        + [through[:, count * half_cols + i * leaf_rows :][:, :leaf_rows] for i in range(count - 1)],
    )

    solved0 = in_order([product(rhs0_leaf, piece, 0, 1) for piece in inverse0_pieces], 1).astype(BF16)
    updated0_pair = pair_forward(solved0, update0, update0_pair)
    inverse1_pair = traded(after(inverse1, solved0), "front", 1)
    updated0 = high_gather(updated0_pair)
    updated0, inverse1_pair, rhs1, rhs2, lists, wing2 = together(
        updated0, inverse1_pair, rhs1, rhs2, lists, wing2
    )
    update1_pair = traded(after(update1, updated0), "front", 1)

    def selector(level_index):
        numbers = lists.astype(jnp.int32)
        target = numbers[level_index : level_index + 1] * own_rows + numbers[2 + level_index : 3 + level_index]
        return (jnp.arange(2 * leaf_rows)[:, None] == target).astype(BF16)

    select0 = selector(0)
    select1 = selector(1)
    pivots1 = ordered(rhs1, jnp.zeros_like(rhs1), side, 1).astype(F32) - forward(updated0, select0)
    pivots1 = (pivots1 + traded(pivots1.astype(BF16), "leaf", 1).astype(F32)).astype(BF16)

    solved1_pair = pair_forward(pivots1, inverse1, inverse1_pair)
    solved0_late, update0_late = together(solved0, update0, solved1_pair)[:2]
    straight0 = pair_rows(leaf_adjoint(solved0_late, inverse0_pieces))
    both0 = leaf_adjoint(update0_late, inverse0_pieces).astype(BF16)
    both0_pair = leaf_adjoint(update0_pair, inverse0_pieces).astype(BF16)
    solved1 = high_gather(solved1_pair)
    solved1, straight0, both0, both0_pair, update1_pair = together(solved1, straight0, both0, both0_pair, update1_pair)
    solved1 = ordered(solved1, traded(solved1, "leaf", 1), side, 1)
    updated1_pair = pair_forward(solved1, update1, update1_pair)
    updated1 = high_gather(updated1_pair)

    pivots2 = ordered(rhs2, jnp.zeros_like(rhs2), wing, 1).astype(F32) - forward(updated1, select1)
    pivots2 = (
        stacked(part(pivots2, wing, 2, 0))
        + traded(stacked(part(pivots2, 1 - wing, 2, 0)).astype(BF16), "leaf", 2).astype(F32)
    ).astype(BF16)
    pivots2 = jnp.concatenate(
        [
            jnp.concatenate(pieces, 0)
            for pieces in zip(flat(pivots2), flat(traded(pivots2, "front", 1)))
        ],
        0,
    )
    other2 = traded(pivots2, "leaf", 1)
    low2 = flat(jnp.where(side == 1, other2, pivots2))
    high2 = flat(jnp.where(side == 1, pivots2, other2))
    pivots2 = jnp.concatenate([low2[0], high2[0], low2[1], high2[1]], 1)
    below2 = adjoint(forward(pivots2, inverse2).astype(BF16), inverse2) + adjoint(
        forward(pivots2, wing2).astype(BF16), wing2
    )
    leaves = [below2[:, i * leaf_rows : (i + 1) * leaf_rows] for i in range(4)]
    low2 = jnp.concatenate([leaves[0], leaves[2]], 0)
    high2 = jnp.concatenate([leaves[1], leaves[3]], 0)
    handed2 = jnp.where(side == 1, low2, high2).astype(BF16)
    below2 = jnp.where(side == 1, high2, low2) + traded(handed2, "leaf", 1).astype(F32)
    low2, high2 = flat(below2)
    handed2 = jnp.concatenate([low2[quarter:], high2[quarter:]], 0).astype(BF16)
    below2 = jnp.concatenate([low2[:quarter], high2[:quarter]], 0)
    below2 = below2 + traded(handed2, "front", 1).astype(F32)
    below2 = high_sum(below2).astype(BF16)
    own2 = flat(below2)
    other2 = flat(traded(below2, "leaf", 2))
    below2 = jnp.concatenate(
        [ordered(own, other, wing, 0) for own, other in zip(own2, other2)], 1
    )

    fetched1 = adjoint(below2, pair_rows(select1)).astype(BF16)
    carried1 = pair_adjoint(fetched1, update1, update1_pair)
    weights1 = (solved1_pair.astype(F32) - high_scatter(side_scatter(carried1))).astype(BF16)
    below1 = high_sum(side_scatter(pair_adjoint(weights1, inverse1, inverse1_pair))).astype(BF16)
    below1_all = ordered(below1, traded(below1, "leaf", 1), side, 1)

    fetched0 = adjoint(below1_all, pair_rows(select0)).astype(BF16)
    carried0 = pair_adjoint(fetched0, both0, both0_pair)
    upper = jnp.concatenate([pair_rows(below1), pair_rows(part(below2, wing, 2, 1))], 0)
    upper, carried0 = together(upper, carried0)
    upper_other = traded(part(upper, 1 - odd, 2, 1), "front", 1)
    carried0, upper_other = together(high_scatter(carried0), upper_other)
    below0 = straight0 - carried0
    below0_other = traded(part(below0, 1 - odd, 2, 1).astype(BF16), "front", 1)

    def finished(own, other):
        return ordered(own.astype(F32), other.astype(F32), odd, 0).T

    upper = part(upper, odd, 2, 1)
    return jnp.stack(
        [
            finished(part(below0, odd, 2, 1), below0_other),
            finished(upper[:half_cols], upper_other[:half_cols]),
            finished(upper[half_cols:], upper_other[half_cols:]),
        ]
    )


def solution(mesh):
    placed = (
        P(None, ("leaf", "front"), None),
        P(("leaf", "front"), None),
        P(("leaf", "front"), None),
        P(None, ("leaf", "front"), None),
        P(None, ("leaf", "front")),
    )
    return jax.shard_map(
        shards,
        mesh=mesh,
        in_specs=placed,
        out_specs=P(None, ("leaf", "front"), None),
        check_vma=False,
    )
```

time: 134 us -> 128 us (0.955)
  waiting for transfers between devices: 83.8 us -> 70.4 us
  local copies, waits for them, and re-layouts: 4.81 us -> 8.48 us
  matrix products: 7.86 us -> 10.6 us
  starting transfers between devices: 30.1 us -> 32.3 us
  other arithmetic: 6.05 us -> 4.42 us
    ppermute x31 -> x29, waiting for transfers between devices: 83.8 us -> 70.4 us  [traded(): lax.ppermute(shard, axis, [(i, i ^ mask) for i in range(lax.axis_size(axi...]
    dot_general x21 -> x34, matrix products: 7.86 us -> 10.6 us  [product(): lax.dot_general(left, right, (((left_dim,), (right_dim,)), ((), ())), pre...]
    ppermute x31 -> x29, starting transfers between devices: 30.1 us -> 32.3 us  [traded(): lax.ppermute(shard, axis, [(i, i ^ mask) for i in range(lax.axis_size(axi...]
  transfers between devices with their start and end apart: 31 -> 29, of which waited for: 25 -> 24; matrix products, arithmetic and copies ran while one was open for 6% -> 12% of each run, Pallas kernels for 0% -> 0%
where the time goes in v3:
time: 128 us; the launch traced here: 127 us
  waiting for transfers between devices  70.4 us (55%)
  starting transfers between devices  32.3 us (25%)
  matrix products  10.6 us (8%)
  local copies, waits for them, and re-layouts  8.48 us (7%)
  other arithmetic  4.42 us (3%)
    ppermute x29, waiting for transfers between devices, traded(): lax.ppermute(shard, axis, [(i, i ^ mask) for i in range(lax.axis_size(axi...  70.4 us
    ppermute x29, starting transfers between devices, traded(): lax.ppermute(shard, axis, [(i, i ^ mask) for i in range(lax.axis_size(axi...  32.3 us
    dot_general x34, matrix products, product(): lax.dot_general(left, right, (((left_dim,), (right_dim,)), ((), ())), pre...  10.6 us
  transfers between devices with their start and end apart: 29, of which 24 were waited for; matrix products, arithmetic and copies ran while one was open for 12% of the time, Pallas kernels for 0%

profile of v3, /device:TPU:0, one launch (start us, length us, event | category | flops | bytes accessed | tf_op | source)
XLA Modules:
  0.0 127.4 jit_solution(8736761930989796788)
XLA Ops:
  0.0 1.0 slice.197
  1.0 3.1 %collective-permute-start.2 = (bf16[128,512]{1,0:T(8,128)(2,1)S(1)}, bf16[128,512]{1,0:T(8,128)(2,1)S(1)}, u32[]{:S(2)}, u32[]{:S(2)}) collective-permute-start(bf16[128,512]{1,0:T(8,128)(2,1)S(1)} %slice.197), channel_id=1, source_target_pairs={{0,1},{1,0},{2,3},{3,2},{4,5},{5,4},{6,7},{7,6},{8,9},{9,8},{10,11... | collective-permute-start | bytes 393224 | tf_op jit(solution)/shard_map/ppermute | solution.py:12
  4.1 0.8 slice_bitcast_fusion
  5.0 2.7 %collective-permute-start = (bf16[128,768]{1,0:T(8,128)(2,1)S(1)}, bf16[128,768]{1,0:T(8,128)(2,1)S(1)}, u32[]{:S(2)}, u32[]{:S(2)}) collective-permute-start(bf16[128,768]{1,0:T(8,128)(2,1)S(1)} %pad_maximum_fusion.7), channel_id=1, source_target_pairs={{0,2},{1,3},{2,0},{3,1},{4,6},{5,7},{6,4},{7,5},{8,10},{9,11},{10,... | collective-permute-start | bytes 589832 | tf_op jit(solution)/shard_map/ppermute | solution.py:12
  7.6 0.9 slice.205
  9.1 0.5 collective-permute-start.6
  9.7 1.6 %collective-permute-start.8 = (bf16[128,2048]{1,0:T(8,128)(2,1)S(1)}, bf16[128,2048]{1,0:T(8,128)(2,1)S(1)}, u32[]{:S(2)}, u32[]{:S(2)}) collective-permute-start(bf16[128,2048]{1,0:T(8,128)(2,1)S(1)} %slice.223), channel_id=1, source_target_pairs={{0,8},{4,12},{8,0},{12,4},{16,24},{20,28},{24,16},{28,20},{1,9},{5... | collective-permute-start | bytes 1572872 | tf_op jit(solution)/shard_map/ppermute | solution.py:12
  11.3 1.0 slice.204
  12.7 1.9 %collective-permute-done.6 = bf16[260,128]{0,1:T(8,128)(2,1)} collective-permute-done((bf16[260,128]{0,1:T(8,128)(2,1)S(1)}, bf16[260,128]{0,1:T(8,128)(2,1)}, u32[]{:S(2)}, u32[]{:S(2)}) %collective-permute-start.6) | collective-permute-done | bytes 66592 | tf_op jit(solution)/shard_map/ppermute | solution.py:12
  14.6 0.8 slice.261
  15.5 0.8 fusion.124
  17.4 2.2 %collective-permute-start.7 = (bf16[128,520]{1,0:T(8,128)(2,1)S(1)}, bf16[128,520]{1,0:T(8,128)(2,1)S(1)}, u32[]{:S(2)}, u32[]{:S(2)}) collective-permute-start(bf16[128,520]{1,0:T(8,128)(2,1)S(1)} %concatenate.258), channel_id=1, source_target_pairs={{0,2},{1,3},{2,0},{3,1},{4,6},{5,7},{6,4},{7,5},{8,10},{9,11},{10,... | collective-permute-start | bytes 399368 | tf_op jit(solution)/shard_map/ppermute | solution.py:12
  19.8 2.0 %collective-permute-start.3 = (bf16[128,512]{1,0:T(8,128)(2,1)S(1)}, bf16[128,512]{1,0:T(8,128)(2,1)S(1)}, u32[]{:S(2)}, u32[]{:S(2)}) collective-permute-start(bf16[128,512]{1,0:T(8,128)(2,1)S(1)} %slice.200), channel_id=1, source_target_pairs={{0,1},{1,0},{2,3},{3,2},{4,5},{5,4},{6,7},{7,6},{8,9},{9,8},{10,11... | collective-permute-start | bytes 393224 | tf_op jit(solution)/shard_map/ppermute | solution.py:12
  21.8 4.4 %collective-permute-done.7 = bf16[128,520]{1,0:T(8,128)(2,1)S(1)} collective-permute-done((bf16[128,520]{1,0:T(8,128)(2,1)S(1)}, bf16[128,520]{1,0:T(8,128)(2,1)S(1)}, u32[]{:S(2)}, u32[]{:S(2)}) %collective-permute-start.7) | collective-permute-done | bytes 133152 | tf_op jit(solution)/shard_map/ppermute | solution.py:12
  26.8 0.7 maximum_select_fusion.10
  27.6 2.6 %collective-permute-done.3 = bf16[128,512]{1,0:T(8,128)(2,1)S(1)} collective-permute-done((bf16[128,512]{1,0:T(8,128)(2,1)S(1)}, bf16[128,512]{1,0:T(8,128)(2,1)S(1)}, u32[]{:S(2)}, u32[]{:S(2)}) %collective-permute-start.3) | collective-permute-done | bytes 131104 | tf_op jit(solution)/shard_map/ppermute | solution.py:12
  31.3 1.5 %collective-permute-start.5 = (bf16[128,1024]{1,0:T(8,128)(2,1)S(1)}, bf16[128,1024]{1,0:T(8,128)(2,1)S(1)}, u32[]{:S(2)}, u32[]{:S(2)}) collective-permute-start(bf16[128,1024]{1,0:T(8,128)(2,1)S(1)} %slice.204), channel_id=1, source_target_pairs={{0,1},{1,0},{2,3},{3,2},{4,5},{5,4},{6,7},{7,6},{8,9},{9,8},{10,11... | collective-permute-start | bytes 786440 | tf_op jit(solution)/shard_map/ppermute | solution.py:12
  33.0 0.5 collective-permute-start.4
  33.8 4.5 %collective-permute-done.4 = bf16[128,256]{0,1:T(8,128)(2,1)S(1)} collective-permute-done((bf16[128,256]{0,1:T(8,128)(2,1)S(1)}, bf16[128,256]{0,1:T(8,128)(2,1)S(1)}, u32[]{:S(2)}, u32[]{:S(2)}) %collective-permute-start.4) | collective-permute-done | bytes 65568 | tf_op jit(solution)/shard_map/ppermute | solution.py:12
  38.4 1.0 collective-permute-done.5
  39.4 0.6 fusion.125
  40.2 0.8 fusion.3
  41.1 0.9 collective-permute-start.11
  43.6 1.7 %collective-permute-start.10 = (bf16[128,256]{0,1:T(8,128)(2,1)S(1)}, bf16[128,256]{0,1:T(8,128)(2,1)S(1)}, u32[]{:S(2)}, u32[]{:S(2)}) collective-permute-start(bf16[128,256]{0,1:T(8,128)(2,1)S(1)} %fusion.18), channel_id=1, source_target_pairs={{0,2},{1,3},{2,0},{3,1},{4,6},{5,7},{6,4},{7,5},{8,10},{9,11},{10,... | collective-permute-start | bytes 196616 | tf_op jit(solution)/shard_map/ppermute | solution.py:12
  45.4 0.8 fusion.2
  46.5 0.7 dynamic-slice_add_fusion
  47.2 2.4 %collective-permute-done.10 = bf16[128,256]{0,1:T(8,128)(2,1)S(1)} collective-permute-done((bf16[128,256]{0,1:T(8,128)(2,1)S(1)}, bf16[128,256]{0,1:T(8,128)(2,1)S(1)}, u32[]{:S(2)}, u32[]{:S(2)}) %collective-permute-start.10) | collective-permute-done | bytes 65568 | tf_op jit(solution)/shard_map/ppermute | solution.py:12
  49.6 1.5 %collective-permute-done.11 = bf16[128,1024]{1,0:T(8,128)(2,1)S(1)} collective-permute-done((bf16[128,1024]{1,0:T(8,128)(2,1)S(1)}, bf16[128,1024]{1,0:T(8,128)(2,1)S(1)}, u32[]{:S(2)}, u32[]{:S(2)}) %collective-permute-start.11) | collective-permute-done | bytes 262176 | tf_op jit(solution)/shard_map/ppermute | solution.py:12
  51.2 1.3 %collective-permute-done.12 = bf16[128,512]{0,1:T(8,128)(2,1)S(1)} collective-permute-done((bf16[128,512]{0,1:T(8,128)(2,1)S(1)}, bf16[128,512]{0,1:T(8,128)(2,1)S(1)}, u32[]{:S(2)}, u32[]{:S(2)}) %collective-permute-start.12) | collective-permute-done | bytes 131104 | tf_op jit(solution)/shard_map/ppermute | solution.py:12
  53.1 2.0 %collective-permute-start.13 = (bf16[128,256]{0,1:T(8,128)(2,1)S(1)}, bf16[128,256]{0,1:T(8,128)(2,1)S(1)}, u32[]{:S(2)}, u32[]{:S(2)}) collective-permute-start(bf16[128,256]{0,1:T(8,128)(2,1)S(1)} %fusion.19), channel_id=1, source_target_pairs={{0,2},{1,3},{2,0},{3,1},{4,6},{5,7},{6,4},{7,5},{8,10},{9,11},{10,... | collective-permute-start | bytes 196616 | tf_op jit(solution)/shard_map/ppermute | solution.py:12
  55.1 3.2 %collective-permute-done.13 = bf16[128,256]{0,1:T(8,128)(2,1)S(1)} collective-permute-done((bf16[128,256]{0,1:T(8,128)(2,1)S(1)}, bf16[128,256]{0,1:T(8,128)(2,1)S(1)}, u32[]{:S(2)}, u32[]{:S(2)}) %collective-permute-start.13) | collective-permute-done | bytes 65568 | tf_op jit(solution)/shard_map/ppermute | solution.py:12
  58.3 0.6 convolution_subtract_fusion
  59.0 1.6 %collective-permute-start.14 = (bf16[128,512]{1,0:T(8,128)(2,1)S(1)}, bf16[128,512]{1,0:T(8,128)(2,1)S(1)}, u32[]{:S(2)}, u32[]{:S(2)}) collective-permute-start(bf16[128,512]{1,0:T(8,128)(2,1)S(1)} %pad_maximum_fusion.9), channel_id=1, source_target_pairs={{0,8},{4,12},{8,0},{12,4},{16,24},{20,28},{24,16},{28,20},{1,9},{5... | collective-permute-start | bytes 393224 | tf_op jit(solution)/shard_map/ppermute | solution.py:12
  60.6 3.5 %collective-permute-done.14 = bf16[128,512]{1,0:T(8,128)(2,1)S(1)} collective-permute-done((bf16[128,512]{1,0:T(8,128)(2,1)S(1)}, bf16[128,512]{1,0:T(8,128)(2,1)S(1)}, u32[]{:S(2)}, u32[]{:S(2)}) %collective-permute-start.14) | collective-permute-done | bytes 131104 | tf_op jit(solution)/shard_map/ppermute | solution.py:12
  64.1 2.2 %collective-permute-start.15 = (bf16[128,512]{1,0:T(8,128)(2,1)S(1)}, bf16[128,512]{1,0:T(8,128)(2,1)S(1)}, u32[]{:S(2)}, u32[]{:S(2)}) collective-permute-start(bf16[128,512]{1,0:T(8,128)(2,1)S(1)} %fusion.8), channel_id=1, source_target_pairs={{0,1},{1,0},{2,3},{3,2},{4,5},{5,4},{6,7},{7,6},{8,9},{9,8},{10,11... | collective-permute-start | bytes 393224 | tf_op jit(solution)/shard_map/ppermute | solution.py:12
  66.2 2.9 %collective-permute-done.15 = bf16[128,512]{1,0:T(8,128)(2,1)S(1)} collective-permute-done((bf16[128,512]{1,0:T(8,128)(2,1)S(1)}, bf16[128,512]{1,0:T(8,128)(2,1)S(1)}, u32[]{:S(2)}, u32[]{:S(2)}) %collective-permute-start.15) | collective-permute-done | bytes 131104 | tf_op jit(solution)/shard_map/ppermute | solution.py:12
  69.3 1.5 %collective-permute-done.16 = bf16[256,512]{1,0:T(8,128)(2,1)S(1)} collective-permute-done((bf16[256,512]{1,0:T(8,128)(2,1)S(1)}, bf16[256,512]{1,0:T(8,128)(2,1)S(1)}, u32[]{:S(2)}, u32[]{:S(2)}) %collective-permute-start.16) | collective-permute-done | bytes 262176 | tf_op jit(solution)/shard_map/ppermute | solution.py:12
  71.0 0.8 fusion.4
  71.7 0.8 convolution_add_fusion
  72.9 1.4 %collective-permute-done.17 = bf16[256,512]{1,0:T(8,128)(2,1)S(1)} collective-permute-done((bf16[256,512]{1,0:T(8,128)(2,1)S(1)}, bf16[256,512]{1,0:T(8,128)(2,1)S(1)}, u32[]{:S(2)}, u32[]{:S(2)}) %collective-permute-start.17) | collective-permute-done | bytes 262176 | tf_op jit(solution)/shard_map/ppermute | solution.py:12
  74.5 2.1 %collective-permute-start.18 = (bf16[128,512]{1,0:T(8,128)(2,1)S(1)}, bf16[128,512]{1,0:T(8,128)(2,1)S(1)}, u32[]{:S(2)}, u32[]{:S(2)}) collective-permute-start(bf16[128,512]{1,0:T(8,128)(2,1)S(1)} %pad_maximum_fusion.10), channel_id=1, source_target_pairs={{0,1},{1,0},{2,3},{3,2},{4,5},{5,4},{6,7},{7,6},{8,9},{9,8},{10,11... | collective-permute-start | bytes 393224 | tf_op jit(solution)/shard_map/ppermute | solution.py:12
  76.6 3.8 %collective-permute-done.18 = bf16[128,512]{1,0:T(8,128)(2,1)S(1)} collective-permute-done((bf16[128,512]{1,0:T(8,128)(2,1)S(1)}, bf16[128,512]{1,0:T(8,128)(2,1)S(1)}, u32[]{:S(2)}, u32[]{:S(2)}) %collective-permute-start.18) | collective-permute-done | bytes 131104 | tf_op jit(solution)/shard_map/ppermute | solution.py:12
  80.4 1.6 %collective-permute-start.19 = (bf16[128,512]{1,0:T(8,128)(2,1)S(1)}, bf16[128,512]{1,0:T(8,128)(2,1)S(1)}, u32[]{:S(2)}, u32[]{:S(2)}) collective-permute-start(bf16[128,512]{1,0:T(8,128)(2,1)S(1)} %fusion.16), channel_id=1, source_target_pairs={{0,2},{1,3},{2,0},{3,1},{4,6},{5,7},{6,4},{7,5},{8,10},{9,11},{10,... | collective-permute-start | bytes 393224 | tf_op jit(solution)/shard_map/ppermute | solution.py:12
  82.1 0.4 iota_compare_fusion
  82.4 6.8 %collective-permute-done.19 = bf16[128,512]{1,0:T(8,128)(2,1)S(1)} collective-permute-done((bf16[128,512]{1,0:T(8,128)(2,1)S(1)}, bf16[128,512]{1,0:T(8,128)(2,1)S(1)}, u32[]{:S(2)}, u32[]{:S(2)}) %collective-permute-start.19) | collective-permute-done | bytes 131104 | tf_op jit(solution)/shard_map/ppermute | solution.py:12
  89.3 1.6 %collective-permute-start.20 = (bf16[128,512]{1,0:T(8,128)(2,1)S(1)}, bf16[128,512]{1,0:T(8,128)(2,1)S(1)}, u32[]{:S(2)}, u32[]{:S(2)}) collective-permute-start(bf16[128,512]{1,0:T(8,128)(2,1)S(1)} %add_convert_fusion.2), channel_id=1, source_target_pairs={{0,8},{4,12},{8,0},{12,4},{16,24},{20,28},{24,16},{28,20},{1,9},{5... | collective-permute-start | bytes 393224 | tf_op jit(solution)/shard_map/ppermute | solution.py:12
  90.9 3.5 %collective-permute-done.20 = bf16[128,512]{1,0:T(8,128)(2,1)S(1)} collective-permute-done((bf16[128,512]{1,0:T(8,128)(2,1)S(1)}, bf16[128,512]{1,0:T(8,128)(2,1)S(1)}, u32[]{:S(2)}, u32[]{:S(2)}) %collective-permute-start.20) | collective-permute-done | bytes 131104 | tf_op jit(solution)/shard_map/ppermute | solution.py:12
  94.4 0.3 convolution_convert_fusion.1
  94.7 0.3 fusion.49
  95.0 0.3 copy-done.10
  95.3 0.3 convolution_add_fusion.2
  95.7 1.3 %collective-permute-done.21 = bf16[128,512]{0,1:T(8,128)(2,1)S(1)} collective-permute-done((bf16[128,512]{0,1:T(8,128)(2,1)S(1)}, bf16[128,512]{0,1:T(8,128)(2,1)S(1)}, u32[]{:S(2)}, u32[]{:S(2)}) %collective-permute-start.21) | collective-permute-done | bytes 131104 | tf_op jit(solution)/shard_map/ppermute | solution.py:12
  97.2 6.3 %collective-permute-done.22 = bf16[128,256]{0,1:T(8,128)(2,1)S(1)} collective-permute-done((bf16[128,256]{0,1:T(8,128)(2,1)S(1)}, bf16[128,256]{0,1:T(8,128)(2,1)S(1)}, u32[]{:S(2)}, u32[]{:S(2)}) %collective-permute-start.22) | collective-permute-done | bytes 65568 | tf_op jit(solution)/shard_map/ppermute | solution.py:12
  103.8 0.3 convolution_add_fusion.1
  104.2 1.3 %collective-permute-done.23 = bf16[128,512]{0,1:T(8,128)(2,1)S(1)} collective-permute-done((bf16[128,512]{0,1:T(8,128)(2,1)S(1)}, bf16[128,512]{0,1:T(8,128)(2,1)S(1)}, u32[]{:S(2)}, u32[]{:S(2)}) %collective-permute-start.23) | collective-permute-done | bytes 131104 | tf_op jit(solution)/shard_map/ppermute | solution.py:12
  105.6 0.4 iota_compare_fusion.1
  106.3 7.3 %collective-permute-done.24 = bf16[128,512]{0,1:T(8,128)(2,1)S(1)} collective-permute-done((bf16[128,512]{0,1:T(8,128)(2,1)S(1)}, bf16[128,512]{0,1:T(8,128)(2,1)S(1)}, u32[]{:S(2)}, u32[]{:S(2)}) %collective-permute-start.24) | collective-permute-done | bytes 131104 | tf_op jit(solution)/shard_map/ppermute | solution.py:12
  113.8 1.3 %collective-permute-done.25 = bf16[128,512]{0,1:T(8,128)(2,1)S(1)} collective-permute-done((bf16[128,512]{0,1:T(8,128)(2,1)S(1)}, bf16[128,512]{0,1:T(8,128)(2,1)S(1)}, u32[]{:S(2)}, u32[]{:S(2)}) %collective-permute-start.25) | collective-permute-done | bytes 131104 | tf_op jit(solution)/shard_map/ppermute | solution.py:12
  115.1 0.3 convolution_convert_fusion
  116.1 3.0 %collective-permute-start.27 = (bf16[256,128]{0,1:T(8,128)(2,1)S(1)}, bf16[256,128]{0,1:T(8,128)(2,1)S(1)}, u32[]{:S(2)}, u32[]{:S(2)}) collective-permute-start(bf16[256,128]{0,1:T(8,128)(2,1)S(1)} %constant_dynamic-slice_fusion.2), channel_id=1, source_target_pairs={{0,1},{1,0},{2,3},{3,2},{4,5},{5,4},{6,7},{7,6},{8,9},{9,8},{10,11... | collective-permute-start | bytes 196616 | tf_op jit(solution)/shard_map/ppermute | solution.py:12
  119.1 3.3 %collective-permute-done.26 = bf16[128,256]{0,1:T(8,128)(2,1)S(1)} collective-permute-done((bf16[128,256]{0,1:T(8,128)(2,1)S(1)}, bf16[128,256]{0,1:T(8,128)(2,1)S(1)}, u32[]{:S(2)}, u32[]{:S(2)}) %collective-permute-start.26) | collective-permute-done | bytes 65568 | tf_op jit(solution)/shard_map/ppermute | solution.py:12
  122.7 0.8 collective-permute-start.28
  123.5 3.1 %collective-permute-done.28 = bf16[128,128]{0,1:T(8,128)(2,1)S(1)} collective-permute-done((bf16[128,128]{0,1:T(8,128)(2,1)S(1)}, bf16[128,128]{0,1:T(8,128)(2,1)S(1)}, u32[]{:S(2)}, u32[]{:S(2)}) %collective-permute-start.28) | collective-permute-done | bytes 32800 | tf_op jit(solution)/shard_map/ppermute | solution.py:12
  126.7 0.8 pad_maximum_fusion.3
  (174 shorter events, 10.2 us)
Async XLA Ops:
  0.0 9.6 %copy-start.4 = (bf16[128,3584]{1,0:T(8,128)(2,1)S(1)}, bf16[128,3584]{1,0:T(8,128)(2,1)}, u32[]{:S(2)}) copy-start(bf16[128,3584]{1,0:T(8,128)(2,1)} %param.6) | copy-start | bytes 2752516
  0.0 8.7 %copy-start.12 = (s32[2,128,1]{1,2,0:T(1,128)S(1)}, s32[2,128,1]{1,2,0:T(1,128)}, u32[]{:S(2)}) copy-start(s32[2,128,1]{1,2,0:T(1,128)} %param.8) | copy-start | bytes 3076
  0.0 8.8 %copy-start.13 = (s32[2,128]{1,0:T(2,128)S(1)}, s32[2,128]{1,0:T(2,128)}, u32[]{:S(2)}) copy-start(s32[2,128]{1,0:T(2,128)} %param.9) | copy-start | bytes 3076
  1.0 26.5 %collective-permute-start.2 = (bf16[128,512]{1,0:T(8,128)(2,1)S(1)}, bf16[128,512]{1,0:T(8,128)(2,1)S(1)}, u32[]{:S(2)}, u32[]{:S(2)}) collective-permute-start(bf16[128,512]{1,0:T(8,128)(2,1)S(1)} %slice.197), channel_id=1, source_target_pairs={{0,1},{1,0},{2,3},{3,2},{4,5},{5,4},{6,7},{7,6},{8,9},{9,8},{10,11... | collective-permute-start | bytes 393224 | tf_op jit(solution)/shard_map/ppermute | solution.py:12
  5.0 14.7 %collective-permute-start = (bf16[128,768]{1,0:T(8,128)(2,1)S(1)}, bf16[128,768]{1,0:T(8,128)(2,1)S(1)}, u32[]{:S(2)}, u32[]{:S(2)}) collective-permute-start(bf16[128,768]{1,0:T(8,128)(2,1)S(1)} %pad_maximum_fusion.7), channel_id=1, source_target_pairs={{0,2},{1,3},{2,0},{3,1},{4,6},{5,7},{6,4},{7,5},{8,10},{9,11},{10,... | collective-permute-start | bytes 589832 | tf_op jit(solution)/shard_map/ppermute | solution.py:12
  8.7 3.6 %copy-start.8 = (bf16[128,1536]{1,0:T(8,128)(2,1)S(1)}, bf16[128,1536]{1,0:T(8,128)(2,1)}, u32[]{:S(2)}) copy-start(bf16[128,1536]{1,0:T(8,128)(2,1)} %param.7) | copy-start | bytes 1179652
  9.1 5.5 %collective-permute-start.6 = (bf16[260,128]{0,1:T(8,128)(2,1)S(1)}, bf16[260,128]{0,1:T(8,128)(2,1)}, u32[]{:S(2)}, u32[]{:S(2)}) collective-permute-start(bf16[260,128]{0,1:T(8,128)(2,1)S(1)} %pad_maximum_fusion.12), channel_id=1, source_target_pairs={{0,1},{1,0},{2,3},{3,2},{4,5},{5,4},{6,7},{7,6},{8,9},{9,8},{10,11... | collective-permute-start | bytes 199688 | tf_op jit(solution)/shard_map/ppermute | solution.py:12
  9.7 28.7 %collective-permute-start.8 = (bf16[128,2048]{1,0:T(8,128)(2,1)S(1)}, bf16[128,2048]{1,0:T(8,128)(2,1)S(1)}, u32[]{:S(2)}, u32[]{:S(2)}) collective-permute-start(bf16[128,2048]{1,0:T(8,128)(2,1)S(1)} %slice.223), channel_id=1, source_target_pairs={{0,8},{4,12},{8,0},{12,4},{16,24},{20,28},{24,16},{28,20},{1,9},{5... | collective-permute-start | bytes 1572872 | tf_op jit(solution)/shard_map/ppermute | solution.py:12
  12.4 40.2 %copy-start.2 = (bf16[128,1024]{1,0:T(8,128)(2,1)}, bf16[128,1024]{1,0:T(8,128)(2,1)S(1)}, u32[]{:S(2)}) copy-start(bf16[128,1024]{1,0:T(8,128)(2,1)S(1)} %slice.226) | copy-start | bytes 786436
  17.4 8.8 %collective-permute-start.7 = (bf16[128,520]{1,0:T(8,128)(2,1)S(1)}, bf16[128,520]{1,0:T(8,128)(2,1)S(1)}, u32[]{:S(2)}, u32[]{:S(2)}) collective-permute-start(bf16[128,520]{1,0:T(8,128)(2,1)S(1)} %concatenate.258), channel_id=1, source_target_pairs={{0,2},{1,3},{2,0},{3,1},{4,6},{5,7},{6,4},{7,5},{8,10},{9,11},{10,... | collective-permute-start | bytes 399368 | tf_op jit(solution)/shard_map/ppermute | solution.py:12
  19.7 10.5 %collective-permute-start.1 = (bf16[128,768]{1,0:T(8,128)(2,1)S(1)}, bf16[128,768]{1,0:T(8,128)(2,1)S(1)}, u32[]{:S(2)}, u32[]{:S(2)}) collective-permute-start(bf16[128,768]{1,0:T(8,128)(2,1)S(1)} %pad_maximum_fusion.8), channel_id=1, source_target_pairs={{0,1},{1,0},{2,3},{3,2},{4,5},{5,4},{6,7},{7,6},{8,9},{9,8},{10,11... | collective-permute-start | bytes 589832 | tf_op jit(solution)/shard_map/ppermute | solution.py:12
  19.8 10.4 %collective-permute-start.3 = (bf16[128,512]{1,0:T(8,128)(2,1)S(1)}, bf16[128,512]{1,0:T(8,128)(2,1)S(1)}, u32[]{:S(2)}, u32[]{:S(2)}) collective-permute-start(bf16[128,512]{1,0:T(8,128)(2,1)S(1)} %slice.200), channel_id=1, source_target_pairs={{0,1},{1,0},{2,3},{3,2},{4,5},{5,4},{6,7},{7,6},{8,9},{9,8},{10,11... | collective-permute-start | bytes 393224 | tf_op jit(solution)/shard_map/ppermute | solution.py:12
  31.3 8.1 %collective-permute-start.5 = (bf16[128,1024]{1,0:T(8,128)(2,1)S(1)}, bf16[128,1024]{1,0:T(8,128)(2,1)S(1)}, u32[]{:S(2)}, u32[]{:S(2)}) collective-permute-start(bf16[128,1024]{1,0:T(8,128)(2,1)S(1)} %slice.204), channel_id=1, source_target_pairs={{0,1},{1,0},{2,3},{3,2},{4,5},{5,4},{6,7},{7,6},{8,9},{9,8},{10,11... | collective-permute-start | bytes 786440 | tf_op jit(solution)/shard_map/ppermute | solution.py:12
  33.0 5.3 %collective-permute-start.4 = (bf16[128,256]{0,1:T(8,128)(2,1)S(1)}, bf16[128,256]{0,1:T(8,128)(2,1)S(1)}, u32[]{:S(2)}, u32[]{:S(2)}) collective-permute-start(bf16[128,256]{0,1:T(8,128)(2,1)S(1)} %fusion.17), channel_id=1, source_target_pairs={{0,2},{1,3},{2,0},{3,1},{4,6},{5,7},{6,4},{7,5},{8,10},{9,11},{10,... | collective-permute-start | bytes 196616 | tf_op jit(solution)/shard_map/ppermute | solution.py:12
  39.4 2.9 %copy-start = (bf16[128,1024]{1,0:T(8,128)(2,1)}, bf16[128,1024]{1,0:T(8,128)(2,1)S(1)}, u32[]{:S(2)}) copy-start(bf16[128,1024]{1,0:T(8,128)(2,1)S(1)} %collective-permute-done.5) | copy-start | bytes 786436
  40.0 2.0 %collective-permute-start.9 = (bf16[128,1024]{1,0:T(8,128)(2,1)S(1)}, bf16[128,1024]{1,0:T(8,128)(2,1)S(1)}, u32[]{:S(2)}, u32[]{:S(2)}) collective-permute-start(bf16[128,1024]{1,0:T(8,128)(2,1)S(1)} %get-tuple-element.111), channel_id=1, source_target_pairs={{0,4},{4,0},{8,12},{12,8},{16,20},{20,16},{24,28},{28,24},{1,5},{5... | collective-permute-start | bytes 786440 | tf_op jit(solution)/shard_map/ppermute | solution.py:12
  41.1 10.1 %collective-permute-start.11 = (bf16[128,1024]{1,0:T(8,128)(2,1)S(1)}, bf16[128,1024]{1,0:T(8,128)(2,1)S(1)}, u32[]{:S(2)}, u32[]{:S(2)}) collective-permute-start(bf16[128,1024]{1,0:T(8,128)(2,1)S(1)} %slice.226), channel_id=1, source_target_pairs={{0,1},{1,0},{2,3},{3,2},{4,5},{5,4},{6,7},{7,6},{8,9},{9,8},{10,11... | collective-permute-start | bytes 786440 | tf_op jit(solution)/shard_map/ppermute | solution.py:12
  43.6 6.0 %collective-permute-start.10 = (bf16[128,256]{0,1:T(8,128)(2,1)S(1)}, bf16[128,256]{0,1:T(8,128)(2,1)S(1)}, u32[]{:S(2)}, u32[]{:S(2)}) collective-permute-start(bf16[128,256]{0,1:T(8,128)(2,1)S(1)} %fusion.18), channel_id=1, source_target_pairs={{0,2},{1,3},{2,0},{3,1},{4,6},{5,7},{6,4},{7,5},{8,10},{9,11},{10,... | collective-permute-start | bytes 196616 | tf_op jit(solution)/shard_map/ppermute | solution.py:12
  51.2 1.9 %copy-start.9 = (bf16[128,1024]{1,0:T(8,128)(2,1)}, bf16[128,1024]{1,0:T(8,128)(2,1)S(1)}, u32[]{:S(2)}) copy-start(bf16[128,1024]{1,0:T(8,128)(2,1)S(1)} %collective-permute-done.11) | copy-start | bytes 786436
  51.2 1.3 %collective-permute-start.12 = (bf16[128,512]{0,1:T(8,128)(2,1)S(1)}, bf16[128,512]{0,1:T(8,128)(2,1)S(1)}, u32[]{:S(2)}, u32[]{:S(2)}) collective-permute-start(bf16[128,512]{0,1:T(8,128)(2,1)S(1)} %maximum_select_fusion.12), channel_id=1, source_target_pairs={{0,4},{4,0},{8,12},{12,8},{16,20},{20,16},{24,28},{28,24},{1,5},{5... | collective-permute-start | bytes 393224 | tf_op jit(solution)/shard_map/ppermute | solution.py:12
  52.8 5.5 %copy-start.11 = (bf16[128,512]{1,0:T(8,128)(2,1)S(1)}, bf16[128,512]{1,0:T(8,128)(2,1)}, u32[]{:S(2)}) copy-start(bf16[128,512]{1,0:T(8,128)(2,1)} %maximum_select_fusion.10) | copy-start | bytes 393220
  53.1 5.2 %collective-permute-start.13 = (bf16[128,256]{0,1:T(8,128)(2,1)S(1)}, bf16[128,256]{0,1:T(8,128)(2,1)S(1)}, u32[]{:S(2)}, u32[]{:S(2)}) collective-permute-start(bf16[128,256]{0,1:T(8,128)(2,1)S(1)} %fusion.19), channel_id=1, source_target_pairs={{0,2},{1,3},{2,0},{3,1},{4,6},{5,7},{6,4},{7,5},{8,10},{9,11},{10,... | collective-permute-start | bytes 196616 | tf_op jit(solution)/shard_map/ppermute | solution.py:12
  59.0 5.0 %collective-permute-start.14 = (bf16[128,512]{1,0:T(8,128)(2,1)S(1)}, bf16[128,512]{1,0:T(8,128)(2,1)S(1)}, u32[]{:S(2)}, u32[]{:S(2)}) collective-permute-start(bf16[128,512]{1,0:T(8,128)(2,1)S(1)} %pad_maximum_fusion.9), channel_id=1, source_target_pairs={{0,8},{4,12},{8,0},{12,4},{16,24},{20,28},{24,16},{28,20},{1,9},{5... | collective-permute-start | bytes 393224 | tf_op jit(solution)/shard_map/ppermute | solution.py:12
  64.1 5.1 %collective-permute-start.15 = (bf16[128,512]{1,0:T(8,128)(2,1)S(1)}, bf16[128,512]{1,0:T(8,128)(2,1)S(1)}, u32[]{:S(2)}, u32[]{:S(2)}) collective-permute-start(bf16[128,512]{1,0:T(8,128)(2,1)S(1)} %fusion.8), channel_id=1, source_target_pairs={{0,1},{1,0},{2,3},{3,2},{4,5},{5,4},{6,7},{7,6},{8,9},{9,8},{10,11... | collective-permute-start | bytes 393224 | tf_op jit(solution)/shard_map/ppermute | solution.py:12
  69.2 1.6 %collective-permute-start.16 = (bf16[256,512]{1,0:T(8,128)(2,1)S(1)}, bf16[256,512]{1,0:T(8,128)(2,1)S(1)}, u32[]{:S(2)}, u32[]{:S(2)}) collective-permute-start(bf16[256,512]{1,0:T(8,128)(2,1)S(1)} %pad_maximum_fusion.6), channel_id=1, source_target_pairs={{0,4},{4,0},{8,12},{12,8},{16,20},{20,16},{24,28},{28,24},{1,5},{5... | collective-permute-start | bytes 786440 | tf_op jit(solution)/shard_map/ppermute | solution.py:12
  72.7 1.6 %collective-permute-start.17 = (bf16[256,512]{1,0:T(8,128)(2,1)S(1)}, bf16[256,512]{1,0:T(8,128)(2,1)S(1)}, u32[]{:S(2)}, u32[]{:S(2)}) collective-permute-start(bf16[256,512]{1,0:T(8,128)(2,1)S(1)} %select_convert_fusion), channel_id=1, source_target_pairs={{0,4},{4,0},{8,12},{12,8},{16,20},{20,16},{24,28},{28,24},{1,5},{5... | collective-permute-start | bytes 786440 | tf_op jit(solution)/shard_map/ppermute | solution.py:12
  74.5 5.9 %collective-permute-start.18 = (bf16[128,512]{1,0:T(8,128)(2,1)S(1)}, bf16[128,512]{1,0:T(8,128)(2,1)S(1)}, u32[]{:S(2)}, u32[]{:S(2)}) collective-permute-start(bf16[128,512]{1,0:T(8,128)(2,1)S(1)} %pad_maximum_fusion.10), channel_id=1, source_target_pairs={{0,1},{1,0},{2,3},{3,2},{4,5},{5,4},{6,7},{7,6},{8,9},{9,8},{10,11... | collective-permute-start | bytes 393224 | tf_op jit(solution)/shard_map/ppermute | solution.py:12
  80.4 8.8 %collective-permute-start.19 = (bf16[128,512]{1,0:T(8,128)(2,1)S(1)}, bf16[128,512]{1,0:T(8,128)(2,1)S(1)}, u32[]{:S(2)}, u32[]{:S(2)}) collective-permute-start(bf16[128,512]{1,0:T(8,128)(2,1)S(1)} %fusion.16), channel_id=1, source_target_pairs={{0,2},{1,3},{2,0},{3,1},{4,6},{5,7},{6,4},{7,5},{8,10},{9,11},{10,... | collective-permute-start | bytes 393224 | tf_op jit(solution)/shard_map/ppermute | solution.py:12
  89.3 5.5 %copy-start.3 = (bf16[128,1024]{1,0:T(8,128)(2,1)S(1)}, bf16[128,1024]{1,0:T(8,128)(2,1)}, u32[]{:S(2)}) copy-start(bf16[128,1024]{1,0:T(8,128)(2,1)} %copy-done.2) | copy-start | bytes 786436
  89.3 5.0 %collective-permute-start.20 = (bf16[128,512]{1,0:T(8,128)(2,1)S(1)}, bf16[128,512]{1,0:T(8,128)(2,1)S(1)}, u32[]{:S(2)}, u32[]{:S(2)}) collective-permute-start(bf16[128,512]{1,0:T(8,128)(2,1)S(1)} %add_convert_fusion.2), channel_id=1, source_target_pairs={{0,8},{4,12},{8,0},{12,4},{16,24},{20,28},{24,16},{28,20},{1,9},{5... | collective-permute-start | bytes 393224 | tf_op jit(solution)/shard_map/ppermute | solution.py:12
  94.4 1.0 copy-start.10
  95.6 8.2 %copy-start.1 = (bf16[128,1024]{1,0:T(8,128)(2,1)S(1)}, bf16[128,1024]{1,0:T(8,128)(2,1)}, u32[]{:S(2)}) copy-start(bf16[128,1024]{1,0:T(8,128)(2,1)} %copy-done) | copy-start | bytes 786436
  95.7 1.4 %collective-permute-start.21 = (bf16[128,512]{0,1:T(8,128)(2,1)S(1)}, bf16[128,512]{0,1:T(8,128)(2,1)S(1)}, u32[]{:S(2)}, u32[]{:S(2)}) collective-permute-start(bf16[128,512]{0,1:T(8,128)(2,1)S(1)} %dynamic-slice_convert_fusion.1), channel_id=1, source_target_pairs={{0,4},{4,0},{8,12},{12,8},{16,20},{20,16},{24,28},{28,24},{1,5},{5... | collective-permute-start | bytes 393224 | tf_op jit(solution)/shard_map/ppermute | solution.py:12
  97.1 6.3 %collective-permute-start.22 = (bf16[128,256]{0,1:T(8,128)(2,1)S(1)}, bf16[128,256]{0,1:T(8,128)(2,1)S(1)}, u32[]{:S(2)}, u32[]{:S(2)}) collective-permute-start(bf16[128,256]{0,1:T(8,128)(2,1)S(1)} %dynamic-slice_convert_fusion.4), channel_id=1, source_target_pairs={{0,2},{1,3},{2,0},{3,1},{4,6},{5,7},{6,4},{7,5},{8,10},{9,11},{10,... | collective-permute-start | bytes 196616 | tf_op jit(solution)/shard_map/ppermute | solution.py:12
  104.1 1.4 %collective-permute-start.23 = (bf16[128,512]{0,1:T(8,128)(2,1)S(1)}, bf16[128,512]{0,1:T(8,128)(2,1)S(1)}, u32[]{:S(2)}, u32[]{:S(2)}) collective-permute-start(bf16[128,512]{0,1:T(8,128)(2,1)S(1)} %dynamic-slice_convert_fusion), channel_id=1, source_target_pairs={{0,4},{4,0},{8,12},{12,8},{16,20},{20,16},{24,28},{28,24},{1,5},{5... | collective-permute-start | bytes 393224 | tf_op jit(solution)/shard_map/ppermute | solution.py:12
  105.5 8.0 %collective-permute-start.24 = (bf16[128,512]{0,1:T(8,128)(2,1)S(1)}, bf16[128,512]{0,1:T(8,128)(2,1)S(1)}, u32[]{:S(2)}, u32[]{:S(2)}) collective-permute-start(bf16[128,512]{0,1:T(8,128)(2,1)S(1)} %fusion.15), channel_id=1, source_target_pairs={{0,2},{1,3},{2,0},{3,1},{4,6},{5,7},{6,4},{7,5},{8,10},{9,11},{10,... | collective-permute-start | bytes 393224 | tf_op jit(solution)/shard_map/ppermute | solution.py:12
  113.6 1.8 %copy-start.6 = (bf16[128,512]{1,0:T(8,128)(2,1)S(1)}, bf16[128,512]{1,0:T(8,128)(2,1)}, u32[]{:S(2)}) copy-start(bf16[128,512]{1,0:T(8,128)(2,1)} %fusion.3) | copy-start | bytes 393220
  113.7 1.4 %collective-permute-start.25 = (bf16[128,512]{0,1:T(8,128)(2,1)S(1)}, bf16[128,512]{0,1:T(8,128)(2,1)S(1)}, u32[]{:S(2)}, u32[]{:S(2)}) collective-permute-start(bf16[128,512]{0,1:T(8,128)(2,1)S(1)} %add_convert_fusion.1), channel_id=1, source_target_pairs={{0,4},{4,0},{8,12},{12,8},{16,20},{20,16},{24,28},{28,24},{1,5},{5... | collective-permute-start | bytes 393224 | tf_op jit(solution)/shard_map/ppermute | solution.py:12
  113.8 1.9 %copy-start.7 = (bf16[128,512]{1,0:T(8,128)(2,1)S(1)}, bf16[128,512]{1,0:T(8,128)(2,1)}, u32[]{:S(2)}) copy-start(bf16[128,512]{1,0:T(8,128)(2,1)} %fusion.2) | copy-start | bytes 393220
  115.4 7.2 %copy-start.5 = (f32[128,256]{0,1:T(8,128)S(1)}, f32[128,256]{0,1:T(8,128)}, u32[]{:S(2)}) copy-start(f32[128,256]{0,1:T(8,128)} %dynamic-slice_add_fusion) | copy-start | bytes 393220
  116.0 6.4 %collective-permute-start.26 = (bf16[128,256]{0,1:T(8,128)(2,1)S(1)}, bf16[128,256]{0,1:T(8,128)(2,1)S(1)}, u32[]{:S(2)}, u32[]{:S(2)}) collective-permute-start(bf16[128,256]{0,1:T(8,128)(2,1)S(1)} %dynamic-slice_convert_fusion.3), channel_id=1, source_target_pairs={{0,2},{1,3},{2,0},{3,1},{4,6},{5,7},{6,4},{7,5},{8,10},{9,11},{10,... | collective-permute-start | bytes 196616 | tf_op jit(solution)/shard_map/ppermute | solution.py:12
  116.1 6.6 %collective-permute-start.27 = (bf16[256,128]{0,1:T(8,128)(2,1)S(1)}, bf16[256,128]{0,1:T(8,128)(2,1)S(1)}, u32[]{:S(2)}, u32[]{:S(2)}) collective-permute-start(bf16[256,128]{0,1:T(8,128)(2,1)S(1)} %constant_dynamic-slice_fusion.2), channel_id=1, source_target_pairs={{0,1},{1,0},{2,3},{3,2},{4,5},{5,4},{6,7},{7,6},{8,9},{9,8},{10,11... | collective-permute-start | bytes 196616 | tf_op jit(solution)/shard_map/ppermute | solution.py:12
  122.7 4.0 %collective-permute-start.28 = (bf16[128,128]{0,1:T(8,128)(2,1)S(1)}, bf16[128,128]{0,1:T(8,128)(2,1)S(1)}, u32[]{:S(2)}, u32[]{:S(2)}) collective-permute-start(bf16[128,128]{0,1:T(8,128)(2,1)S(1)} %dynamic-slice_convert_fusion.5), channel_id=1, source_target_pairs={{0,1},{1,0},{2,3},{3,2},{4,5},{5,4},{6,7},{7,6},{8,9},{9,8},{10,11... | collective-permute-start | bytes 98312 | tf_op jit(solution)/shard_map/ppermute | solution.py:12

commit v4 on v3

--- a/solution.py
+++ b/solution.py
@@ -144,65 +144,40 @@
     update0 = lax.optimization_barrier(update0)
     update1 = lax.optimization_barrier(update1)
 
-    first = jnp.concatenate([inverse0, rhs[0]], 1)
-    first_even = high_pieces(first)
-    inverse0_near = traded(inverse0, "front", 1)
-    count = len(first_even)
-
     lists = jnp.concatenate([asm_owner[:, :, 0], asm_row], 0).astype(BF16)
-    kept = part(rhs[1:], odd, 2, 2).reshape(2 * own_rows, -1)
-    handed = part(rhs[1:], 1 - odd, 2, 2).reshape(2 * own_rows, -1)
-    received = traded(
-        after(jnp.concatenate([handed, lists.reshape(-1, half_cols)], 0), first), "front", 1
-    )
-
-
-    def level_rows(index):
-        rows = slice(index * own_rows, (index + 1) * own_rows)
-        return ordered(kept[rows], received[rows], odd, 0).T
-
-    def as_block(lists):
-        return lists.reshape(-1, half_cols).T
-
-    lists = ordered(lists, received[2 * own_rows :].reshape(4, -1), odd, 1)
-    rhs1, rhs2, *lists = high_gather(
-        level_rows(0), level_rows(1), *(as_block(lists[i : i + 1]) for i in range(4))
-    )
-    lists = jnp.concatenate([block.T.reshape(1, -1) for block in lists], 0)
-
-    through = traded(
-        jnp.concatenate(
-            [part(block[:, leaf_rows:], 1 - odd, 2, 1) for block in first_even]
-            + [block[:, :leaf_rows] for block in first_even[1:]],
-            1,
-        ),
-        "front",
-        1,
-    )
-    update0_pair = traded(after(update0, first_even[-1]), "front", 1)
-    wing2 = traded(after(inverse2, first), "leaf", 2)
-    through, inverse0_near, update0_pair = together(through, inverse0_near, update0_pair)
-    rhs0_leaf = in_order(
-        alternated(
-            [part(block[:, leaf_rows:], odd, 2, 1) for block in first_even],
-            [through[:, i * half_cols : (i + 1) * half_cols] for i in range(count)],
-        ),
-        0,
-    )
-    inverse0_pieces = alternated(
-        [block[:, :leaf_rows] for block in first_even],
-        [inverse0_near]
-        + [through[:, count * half_cols + i * leaf_rows :][:, :leaf_rows] for i in range(count - 1)],
-    )
-
-    solved0 = in_order([product(rhs0_leaf, piece, 0, 1) for piece in inverse0_pieces], 1).astype(BF16)
+    lists = jnp.pad(lists, ((0, 4), (0, leaf_rows + LEVELS * half_cols - own_rows)))
+
+    def parcel(half):
+        columns = [part(rhs[level], half, 2, 1) for level in range(LEVELS)]
+        return jnp.concatenate([jnp.concatenate([inverse0, *columns], 1), lists], 0)
+
+    kept, handed = parcel(odd), parcel(1 - odd)
+    parcels = [kept] + [
+        traded(handed if mask % 2 else kept, "front", mask) for mask in range(1, front_count)
+    ]
+    update0_pair = traded(after(update0, handed), "front", 1)
+    inverse1_pair = traded(after(inverse1, handed), "front", 1)
+    *parcels, update0_pair = together(*parcels, update0_pair)
+    inverse0_pieces = [block[:own_rows, :leaf_rows] for block in parcels]
+    rhs0, rhs1, rhs2 = (
+        in_order(
+            [
+                block[:own_rows, leaf_rows + level * half_cols : leaf_rows + (level + 1) * half_cols]
+                for block in parcels
+            ],
+            0,
+        )
+        for level in range(LEVELS)
+    )
+    rhs1, rhs2 = rhs1.T, rhs2.T
+    lists = in_order([block[own_rows : own_rows + 4, :own_rows] for block in parcels], 1)
+
+    solved0 = in_order([product(rhs0, piece, 0, 1) for piece in inverse0_pieces], 1).astype(BF16)
     updated0_pair = pair_forward(solved0, update0, update0_pair)
-    inverse1_pair = traded(after(inverse1, solved0), "front", 1)
+    update1_pair = traded(after(update1, solved0), "front", 1)
     updated0 = high_gather(updated0_pair)
-    updated0, inverse1_pair, rhs1, rhs2, lists, wing2 = together(
-        updated0, inverse1_pair, rhs1, rhs2, lists, wing2
-    )
-    update1_pair = traded(after(update1, updated0), "front", 1)
+    updated0, inverse1_pair = together(updated0, inverse1_pair)
+    wing2 = traded(after(inverse2, solved0), "leaf", 2)
 
     def selector(level_index):
         numbers = lists.astype(jnp.int32)
@@ -220,7 +195,9 @@
     both0 = leaf_adjoint(update0_late, inverse0_pieces).astype(BF16)
     both0_pair = leaf_adjoint(update0_pair, inverse0_pieces).astype(BF16)
     solved1 = high_gather(solved1_pair)
-    solved1, straight0, both0, both0_pair, update1_pair = together(solved1, straight0, both0, both0_pair, update1_pair)
+    solved1, straight0, both0, both0_pair, update1_pair, wing2 = together(
+        solved1, straight0, both0, both0_pair, update1_pair, wing2
+    )
     solved1 = ordered(solved1, traded(solved1, "leaf", 1), side, 1)
     updated1_pair = pair_forward(solved1, update1, update1_pair)
     updated1 = high_gather(updated1_pair)

time: 128 us -> 124 us (0.969)
  starting transfers between devices: 32.3 us -> 28 us
  local copies, waits for them, and re-layouts: 8.48 us -> 5.15 us
  waiting for transfers between devices: 70.4 us -> 73.1 us
  other arithmetic: 4.42 us -> 6.11 us
    ppermute x29 -> x27, starting transfers between devices: 32.3 us -> 28 us  [traded(): lax.ppermute(shard, axis, [(i, i ^ mask) for i in range(lax.axis_size(axi...]
    ppermute x29 -> x27, waiting for transfers between devices: 70.4 us -> 73.1 us  [traded(): lax.ppermute(shard, axis, [(i, i ^ mask) for i in range(lax.axis_size(axi...]
    slice x15 -> x9, local copies, waits for them, and re-layouts: 2.98 us -> 1.06 us  [the longest x1 0.97 us: parcel(): columns = [part(rhs[level], half, 2, 1) for level in range(LEVELS)]]
  transfers between devices with their start and end apart: 29 -> 27, of which waited for: 24 -> 22; matrix products, arithmetic and copies ran while one was open for 12% -> 8% of each run, Pallas kernels for 0% -> 0%
where the time goes in v4:
time: 124 us
  waiting for transfers between devices  73.1 us (59%)
  starting transfers between devices  28 us (23%)
  matrix products  10.5 us (8%)
  other arithmetic  6.11 us (5%)
  local copies, waits for them, and re-layouts  5.15 us (4%)
    ppermute x27, waiting for transfers between devices, traded(): lax.ppermute(shard, axis, [(i, i ^ mask) for i in range(lax.axis_size(axi...  73.1 us
    ppermute x27, starting transfers between devices, traded(): lax.ppermute(shard, axis, [(i, i ^ mask) for i in range(lax.axis_size(axi...  28 us
    dot_general x34, matrix products, product(): lax.dot_general(left, right, (((left_dim,), (right_dim,)), ((), ())), pre...  10.5 us
  transfers between devices with their start and end apart: 27, of which 22 were waited for; matrix products, arithmetic and copies ran while one was open for 8% of the time, Pallas kernels for 0%

profile of v4, /device:TPU:0, one launch (start us, length us, event | category | flops | bytes accessed | tf_op | source)
XLA Modules:
  0.0 124.0 jit_solution(6070900113160031613)
XLA Ops:
  0.0 1.0 fusion.132
  1.0 0.7 convert.20
  1.7 0.7 convert_bitcast_fusion
  2.5 3.1 %collective-permute-start = (bf16[136,896]{1,0:T(8,128)(2,1)S(1)}, bf16[136,896]{1,0:T(8,128)(2,1)S(1)}, u32[]{:S(2)}, u32[]{:S(2)}) collective-permute-start(bf16[136,896]{1,0:T(8,128)(2,1)S(1)} %get-tuple-element.86), channel_id=1, source_target_pairs={{0,1},{1,0},{2,3},{3,2},{4,5},{5,4},{6,7},{7,6},{8,9},{9,8},{10,11... | collective-permute-start | bytes 731144 | tf_op jit(solution)/shard_map/ppermute | solution.py:12
  5.6 2.6 %collective-permute-start.1 = (bf16[136,896]{1,0:T(8,128)(2,1)S(1)}, bf16[136,896]{1,0:T(8,128)(2,1)S(1)}, u32[]{:S(2)}, u32[]{:S(2)}) collective-permute-start(bf16[136,896]{1,0:T(8,128)(2,1)S(1)} %get-tuple-element.32), channel_id=1, source_target_pairs={{0,2},{1,3},{2,0},{3,1},{4,6},{5,7},{6,4},{7,5},{8,10},{9,11},{10,... | collective-permute-start | bytes 731144 | tf_op jit(solution)/shard_map/ppermute | solution.py:12
  8.2 1.0 collective-permute-start.3
  9.1 1.0 slice.210
  10.1 1.2 collective-permute-start.5
  11.3 1.1 slice.218
  12.5 12.8 %collective-permute-done.3 = bf16[128,512]{1,0:T(8,128)(2,1)S(1)} collective-permute-done((bf16[128,512]{1,0:T(8,128)(2,1)S(1)}, bf16[128,512]{1,0:T(8,128)(2,1)S(1)}, u32[]{:S(2)}, u32[]{:S(2)}) %collective-permute-start.3) | collective-permute-done | bytes 131104 | tf_op jit(solution)/shard_map/ppermute | solution.py:12
  25.3 0.5 collective-permute-done.1
  27.6 5.3 %collective-permute-start.4 = (bf16[128,256]{0,1:T(8,128)(2,1)S(1)}, bf16[128,256]{0,1:T(8,128)(2,1)S(1)}, u32[]{:S(2)}, u32[]{:S(2)}) collective-permute-start(bf16[128,256]{0,1:T(8,128)(2,1)S(1)} %fusion.18), channel_id=1, source_target_pairs={{0,2},{1,3},{2,0},{3,1},{4,6},{5,7},{6,4},{7,5},{8,10},{9,11},{10,... | collective-permute-start | bytes 196616 | tf_op jit(solution)/shard_map/ppermute | solution.py:12
  32.9 1.5 %collective-permute-start.9 = (bf16[128,2048]{1,0:T(8,128)(2,1)S(1)}, bf16[128,2048]{1,0:T(8,128)(2,1)S(1)}, u32[]{:S(2)}, u32[]{:S(2)}) collective-permute-start(bf16[128,2048]{1,0:T(8,128)(2,1)S(1)} %slice.218), channel_id=1, source_target_pairs={{0,8},{4,12},{8,0},{12,4},{16,24},{20,28},{24,16},{28,20},{1,9},{5... | collective-permute-start | bytes 1572872 | tf_op jit(solution)/shard_map/ppermute | solution.py:12
  34.7 0.7 collective-permute-done.4
  35.5 0.5 fusion.137
  36.2 0.8 fusion.1
  37.1 0.5 collective-permute-done.6
  37.6 0.2 fusion.120
  37.8 0.3 fusion.119
  38.4 0.4 copy-done.7
  39.0 3.5 %collective-permute-start.7 = (bf16[128,256]{0,1:T(8,128)(2,1)S(1)}, bf16[128,256]{0,1:T(8,128)(2,1)S(1)}, u32[]{:S(2)}, u32[]{:S(2)}) collective-permute-start(bf16[128,256]{0,1:T(8,128)(2,1)S(1)} %fusion.20), channel_id=1, source_target_pairs={{0,2},{1,3},{2,0},{3,1},{4,6},{5,7},{6,4},{7,5},{8,10},{9,11},{10,... | collective-permute-start | bytes 196616 | tf_op jit(solution)/shard_map/ppermute | solution.py:12
  43.0 0.8 fusion
  44.3 0.7 dynamic-slice_add_fusion
  45.0 1.2 %collective-permute-done.7 = bf16[128,256]{0,1:T(8,128)(2,1)S(1)} collective-permute-done((bf16[128,256]{0,1:T(8,128)(2,1)S(1)}, bf16[128,256]{0,1:T(8,128)(2,1)S(1)}, u32[]{:S(2)}, u32[]{:S(2)}) %collective-permute-start.7) | collective-permute-done | bytes 65568 | tf_op jit(solution)/shard_map/ppermute | solution.py:12
  46.4 1.3 %collective-permute-done.10 = bf16[128,512]{0,1:T(8,128)(2,1)S(1)} collective-permute-done((bf16[128,512]{0,1:T(8,128)(2,1)S(1)}, bf16[128,512]{0,1:T(8,128)(2,1)S(1)}, u32[]{:S(2)}, u32[]{:S(2)}) %collective-permute-start.10) | collective-permute-done | bytes 131104 | tf_op jit(solution)/shard_map/ppermute | solution.py:12
  47.7 0.2 fusion.60
  48.0 0.2 fusion.59
  48.3 1.4 %collective-permute-start.11 = (bf16[128,256]{0,1:T(8,128)(2,1)S(1)}, bf16[128,256]{0,1:T(8,128)(2,1)S(1)}, u32[]{:S(2)}, u32[]{:S(2)}) collective-permute-start(bf16[128,256]{0,1:T(8,128)(2,1)S(1)} %fusion.22), channel_id=1, source_target_pairs={{0,2},{1,3},{2,0},{3,1},{4,6},{5,7},{6,4},{7,5},{8,10},{9,11},{10,... | collective-permute-start | bytes 196616 | tf_op jit(solution)/shard_map/ppermute | solution.py:12
  49.7 4.8 %collective-permute-done.11 = bf16[128,256]{0,1:T(8,128)(2,1)S(1)} collective-permute-done((bf16[128,256]{0,1:T(8,128)(2,1)S(1)}, bf16[128,256]{0,1:T(8,128)(2,1)S(1)}, u32[]{:S(2)}, u32[]{:S(2)}) %collective-permute-start.11) | collective-permute-done | bytes 65568 | tf_op jit(solution)/shard_map/ppermute | solution.py:12
  54.5 0.5 convolution_subtract_fusion
  55.3 1.6 %collective-permute-start.12 = (bf16[128,512]{0,1:T(8,128)(2,1)S(1)}, bf16[128,512]{0,1:T(8,128)(2,1)S(1)}, u32[]{:S(2)}, u32[]{:S(2)}) collective-permute-start(bf16[128,512]{0,1:T(8,128)(2,1)S(1)} %pad_maximum_fusion.11), channel_id=1, source_target_pairs={{0,8},{4,12},{8,0},{12,4},{16,24},{20,28},{24,16},{28,20},{1,9},{5... | collective-permute-start | bytes 393224 | tf_op jit(solution)/shard_map/ppermute | solution.py:12
  57.2 3.6 %collective-permute-done.12 = bf16[128,512]{0,1:T(8,128)(2,1)S(1)} collective-permute-done((bf16[128,512]{0,1:T(8,128)(2,1)S(1)}, bf16[128,512]{0,1:T(8,128)(2,1)S(1)}, u32[]{:S(2)}, u32[]{:S(2)}) %collective-permute-start.12) | collective-permute-done | bytes 131104 | tf_op jit(solution)/shard_map/ppermute | solution.py:12
  61.1 4.8 %collective-permute-done.13 = bf16[128,512]{0,1:T(8,128)(2,1)S(1)} collective-permute-done((bf16[128,512]{0,1:T(8,128)(2,1)S(1)}, bf16[128,512]{0,1:T(8,128)(2,1)S(1)}, u32[]{:S(2)}, u32[]{:S(2)}) %collective-permute-start.13) | collective-permute-done | bytes 131104 | tf_op jit(solution)/shard_map/ppermute | solution.py:12
  66.3 1.5 %collective-permute-done.14 = bf16[256,512]{0,1:T(8,128)(2,1)S(1)} collective-permute-done((bf16[256,512]{0,1:T(8,128)(2,1)S(1)}, bf16[256,512]{0,1:T(8,128)(2,1)S(1)}, u32[]{:S(2)}, u32[]{:S(2)}) %collective-permute-start.14) | collective-permute-done | bytes 262176 | tf_op jit(solution)/shard_map/ppermute | solution.py:12
  67.9 0.3 broadcast_select_fusion.1
  68.2 0.8 fusion.2
  69.0 0.8 convolution_add_fusion
  70.2 1.4 %collective-permute-done.15 = bf16[256,512]{0,1:T(8,128)(2,1)S(1)} collective-permute-done((bf16[256,512]{0,1:T(8,128)(2,1)S(1)}, bf16[256,512]{0,1:T(8,128)(2,1)S(1)}, u32[]{:S(2)}, u32[]{:S(2)}) %collective-permute-start.15) | collective-permute-done | bytes 262176 | tf_op jit(solution)/shard_map/ppermute | solution.py:12
  72.1 5.5 %collective-permute-done.16 = bf16[128,512]{0,1:T(8,128)(2,1)S(1)} collective-permute-done((bf16[128,512]{0,1:T(8,128)(2,1)S(1)}, bf16[128,512]{0,1:T(8,128)(2,1)S(1)}, u32[]{:S(2)}, u32[]{:S(2)}) %collective-permute-start.16) | collective-permute-done | bytes 131104 | tf_op jit(solution)/shard_map/ppermute | solution.py:12
  77.8 0.4 iota_compare_fusion
  78.2 8.0 %collective-permute-done.17 = bf16[128,512]{0,1:T(8,128)(2,1)S(1)} collective-permute-done((bf16[128,512]{0,1:T(8,128)(2,1)S(1)}, bf16[128,512]{0,1:T(8,128)(2,1)S(1)}, u32[]{:S(2)}, u32[]{:S(2)}) %collective-permute-start.17) | collective-permute-done | bytes 131104 | tf_op jit(solution)/shard_map/ppermute | solution.py:12
  86.3 1.6 %collective-permute-start.18 = (bf16[128,512]{0,1:T(8,128)(2,1)S(1)}, bf16[128,512]{0,1:T(8,128)(2,1)S(1)}, u32[]{:S(2)}, u32[]{:S(2)}) collective-permute-start(bf16[128,512]{0,1:T(8,128)(2,1)S(1)} %add_convert_fusion.2), channel_id=1, source_target_pairs={{0,8},{4,12},{8,0},{12,4},{16,24},{20,28},{24,16},{28,20},{1,9},{5... | collective-permute-start | bytes 393224 | tf_op jit(solution)/shard_map/ppermute | solution.py:12
  88.1 3.7 %collective-permute-done.18 = bf16[128,512]{0,1:T(8,128)(2,1)S(1)} collective-permute-done((bf16[128,512]{0,1:T(8,128)(2,1)S(1)}, bf16[128,512]{0,1:T(8,128)(2,1)S(1)}, u32[]{:S(2)}, u32[]{:S(2)}) %collective-permute-start.18) | collective-permute-done | bytes 131104 | tf_op jit(solution)/shard_map/ppermute | solution.py:12
  92.2 0.3 convolution_convert_fusion.1
  92.5 0.3 fusion.68
  93.0 0.3 convolution_add_fusion.2
  93.4 1.3 %collective-permute-done.19 = bf16[128,512]{0,1:T(8,128)(2,1)S(1)} collective-permute-done((bf16[128,512]{0,1:T(8,128)(2,1)S(1)}, bf16[128,512]{0,1:T(8,128)(2,1)S(1)}, u32[]{:S(2)}, u32[]{:S(2)}) %collective-permute-start.19) | collective-permute-done | bytes 131104 | tf_op jit(solution)/shard_map/ppermute | solution.py:12
  94.9 5.2 %collective-permute-done.20 = bf16[128,256]{0,1:T(8,128)(2,1)S(1)} collective-permute-done((bf16[128,256]{0,1:T(8,128)(2,1)S(1)}, bf16[128,256]{0,1:T(8,128)(2,1)S(1)}, u32[]{:S(2)}, u32[]{:S(2)}) %collective-permute-start.20) | collective-permute-done | bytes 65568 | tf_op jit(solution)/shard_map/ppermute | solution.py:12
  100.0 0.3 fusion.65
  100.3 0.3 convolution_add_fusion.1
  100.8 1.3 %collective-permute-done.21 = bf16[128,512]{0,1:T(8,128)(2,1)S(1)} collective-permute-done((bf16[128,512]{0,1:T(8,128)(2,1)S(1)}, bf16[128,512]{0,1:T(8,128)(2,1)S(1)}, u32[]{:S(2)}, u32[]{:S(2)}) %collective-permute-start.21) | collective-permute-done | bytes 131104 | tf_op jit(solution)/shard_map/ppermute | solution.py:12
  102.1 0.3 collective-permute-start.22
  102.4 0.4 iota_compare_fusion.1
  102.8 0.3 fusion.58
  103.1 7.0 %collective-permute-done.22 = bf16[128,512]{0,1:T(8,128)(2,1)S(1)} collective-permute-done((bf16[128,512]{0,1:T(8,128)(2,1)S(1)}, bf16[128,512]{0,1:T(8,128)(2,1)S(1)}, u32[]{:S(2)}, u32[]{:S(2)}) %collective-permute-start.22) | collective-permute-done | bytes 131104 | tf_op jit(solution)/shard_map/ppermute | solution.py:12
  110.3 1.3 %collective-permute-done.23 = bf16[128,512]{0,1:T(8,128)(2,1)S(1)} collective-permute-done((bf16[128,512]{0,1:T(8,128)(2,1)S(1)}, bf16[128,512]{0,1:T(8,128)(2,1)S(1)}, u32[]{:S(2)}, u32[]{:S(2)}) %collective-permute-start.23) | collective-permute-done | bytes 131104 | tf_op jit(solution)/shard_map/ppermute | solution.py:12
  111.6 0.3 convolution_convert_fusion
  111.9 0.2 fusion.61
  112.2 0.2 convolution_add_fusion.3
  112.6 3.0 %collective-permute-start.25 = (bf16[256,128]{0,1:T(8,128)(2,1)S(1)}, bf16[256,128]{0,1:T(8,128)(2,1)S(1)}, u32[]{:S(2)}, u32[]{:S(2)}) collective-permute-start(bf16[256,128]{0,1:T(8,128)(2,1)S(1)} %constant_dynamic-slice_fusion.1), channel_id=1, source_target_pairs={{0,1},{1,0},{2,3},{3,2},{4,5},{5,4},{6,7},{7,6},{8,9},{9,8},{10,11... | collective-permute-start | bytes 196616 | tf_op jit(solution)/shard_map/ppermute | solution.py:12
  115.6 3.3 %collective-permute-done.24 = bf16[128,256]{0,1:T(8,128)(2,1)S(1)} collective-permute-done((bf16[128,256]{0,1:T(8,128)(2,1)S(1)}, bf16[128,256]{0,1:T(8,128)(2,1)S(1)}, u32[]{:S(2)}, u32[]{:S(2)}) %collective-permute-start.24) | collective-permute-done | bytes 65568 | tf_op jit(solution)/shard_map/ppermute | solution.py:12
  119.2 0.8 collective-permute-start.26
  120.1 3.1 %collective-permute-done.26 = bf16[128,128]{0,1:T(8,128)(2,1)S(1)} collective-permute-done((bf16[128,128]{0,1:T(8,128)(2,1)S(1)}, bf16[128,128]{0,1:T(8,128)(2,1)S(1)}, u32[]{:S(2)}, u32[]{:S(2)}) %collective-permute-start.26) | collective-permute-done | bytes 32800 | tf_op jit(solution)/shard_map/ppermute | solution.py:12
  123.2 0.8 pad_maximum_fusion.3
  (142 shorter events, 7.9 us)
Async XLA Ops:
  0.0 2.4 %slice-start = ((bf16[128,3584]{1,0:T(8,128)(2,1)}), bf16[128,512]{1,0:T(8,128)(2,1)S(1)}, s32[]{:S(2)}) async-start(bf16[128,3584]{1,0:T(8,128)(2,1)} %param.6), calls=%async_computation | async-start | bytes 262144 | tf_op jit(solution)/shard_map/slice | solution.py:136
  0.0 8.2 %copy-start.11 = (bf16[128,1536]{1,0:T(8,128)(2,1)S(1)}, bf16[128,1536]{1,0:T(8,128)(2,1)}, u32[]{:S(2)}) copy-start(bf16[128,1536]{1,0:T(8,128)(2,1)} %param.7) | copy-start | bytes 1179652
  2.5 22.8 %collective-permute-start = (bf16[136,896]{1,0:T(8,128)(2,1)S(1)}, bf16[136,896]{1,0:T(8,128)(2,1)S(1)}, u32[]{:S(2)}, u32[]{:S(2)}) collective-permute-start(bf16[136,896]{1,0:T(8,128)(2,1)S(1)} %get-tuple-element.86), channel_id=1, source_target_pairs={{0,1},{1,0},{2,3},{3,2},{4,5},{5,4},{6,7},{7,6},{8,9},{9,8},{10,11... | collective-permute-start | bytes 731144 | tf_op jit(solution)/shard_map/ppermute | solution.py:12
  5.6 20.2 %collective-permute-start.1 = (bf16[136,896]{1,0:T(8,128)(2,1)S(1)}, bf16[136,896]{1,0:T(8,128)(2,1)S(1)}, u32[]{:S(2)}, u32[]{:S(2)}) collective-permute-start(bf16[136,896]{1,0:T(8,128)(2,1)S(1)} %get-tuple-element.32), channel_id=1, source_target_pairs={{0,2},{1,3},{2,0},{3,1},{4,6},{5,7},{6,4},{7,5},{8,10},{9,11},{10,... | collective-permute-start | bytes 731144 | tf_op jit(solution)/shard_map/ppermute | solution.py:12
  8.2 17.6 %collective-permute-start.2 = (bf16[136,896]{1,0:T(8,128)(2,1)S(1)}, bf16[136,896]{1,0:T(8,128)(2,1)S(1)}, u32[]{:S(2)}, u32[]{:S(2)}) collective-permute-start(bf16[136,896]{1,0:T(8,128)(2,1)S(1)} %get-tuple-element.86), channel_id=1, source_target_pairs={{0,3},{1,2},{2,1},{3,0},{4,7},{5,6},{6,5},{7,4},{8,11},{9,10},{10,... | collective-permute-start | bytes 731144 | tf_op jit(solution)/shard_map/ppermute | solution.py:12
  8.2 17.1 %collective-permute-start.3 = (bf16[128,512]{1,0:T(8,128)(2,1)S(1)}, bf16[128,512]{1,0:T(8,128)(2,1)S(1)}, u32[]{:S(2)}, u32[]{:S(2)}) collective-permute-start(bf16[128,512]{1,0:T(8,128)(2,1)S(1)} %slice.197), channel_id=1, source_target_pairs={{0,1},{1,0},{2,3},{3,2},{4,5},{5,4},{6,7},{7,6},{8,9},{9,8},{10,11... | collective-permute-start | bytes 393224 | tf_op jit(solution)/shard_map/ppermute | solution.py:12
  10.1 25.3 %collective-permute-start.5 = (bf16[128,1024]{1,0:T(8,128)(2,1)S(1)}, bf16[128,1024]{1,0:T(8,128)(2,1)S(1)}, u32[]{:S(2)}, u32[]{:S(2)}) collective-permute-start(bf16[128,1024]{1,0:T(8,128)(2,1)S(1)} %slice.210), channel_id=1, source_target_pairs={{0,1},{1,0},{2,3},{3,2},{4,5},{5,4},{6,7},{7,6},{8,9},{9,8},{10,11... | collective-permute-start | bytes 786440 | tf_op jit(solution)/shard_map/ppermute | solution.py:12
  12.4 35.3 %copy-start.2 = (bf16[128,1024]{1,0:T(8,128)(2,1)}, bf16[128,1024]{1,0:T(8,128)(2,1)S(1)}, u32[]{:S(2)}) copy-start(bf16[128,1024]{1,0:T(8,128)(2,1)S(1)} %slice.217) | copy-start | bytes 786436
  25.3 2.0 %copy-start.6 = (bf16[136,896]{1,0:T(8,128)(2,1)}, bf16[136,896]{1,0:T(8,128)(2,1)S(1)}, u32[]{:S(2)}) copy-start(bf16[136,896]{1,0:T(8,128)(2,1)S(1)} %collective-permute-done) | copy-start | bytes 731140
  25.8 0.7 copy-start.4
  27.6 7.8 %collective-permute-start.4 = (bf16[128,256]{0,1:T(8,128)(2,1)S(1)}, bf16[128,256]{0,1:T(8,128)(2,1)S(1)}, u32[]{:S(2)}, u32[]{:S(2)}) collective-permute-start(bf16[128,256]{0,1:T(8,128)(2,1)S(1)} %fusion.18), channel_id=1, source_target_pairs={{0,2},{1,3},{2,0},{3,1},{4,6},{5,7},{6,4},{7,5},{8,10},{9,11},{10,... | collective-permute-start | bytes 196616 | tf_op jit(solution)/shard_map/ppermute | solution.py:12
  32.9 13.4 %collective-permute-start.9 = (bf16[128,2048]{1,0:T(8,128)(2,1)S(1)}, bf16[128,2048]{1,0:T(8,128)(2,1)S(1)}, u32[]{:S(2)}, u32[]{:S(2)}) collective-permute-start(bf16[128,2048]{1,0:T(8,128)(2,1)S(1)} %slice.218), channel_id=1, source_target_pairs={{0,8},{4,12},{8,0},{12,4},{16,24},{20,28},{24,16},{28,20},{1,9},{5... | collective-permute-start | bytes 1572872 | tf_op jit(solution)/shard_map/ppermute | solution.py:12
  34.4 11.9 %collective-permute-start.8 = (bf16[128,1024]{1,0:T(8,128)(2,1)S(1)}, bf16[128,1024]{1,0:T(8,128)(2,1)S(1)}, u32[]{:S(2)}, u32[]{:S(2)}) collective-permute-start(bf16[128,1024]{1,0:T(8,128)(2,1)S(1)} %slice.217), channel_id=1, source_target_pairs={{0,1},{1,0},{2,3},{3,2},{4,5},{5,4},{6,7},{7,6},{8,9},{9,8},{10,11... | collective-permute-start | bytes 786440 | tf_op jit(solution)/shard_map/ppermute | solution.py:12
  34.6 1.4 %copy-start.5 = (bf16[136,896]{1,0:T(8,128)(2,1)S(1)}, bf16[136,896]{1,0:T(8,128)(2,1)}, u32[]{:S(2)}) copy-start(bf16[136,896]{1,0:T(8,128)(2,1)} %copy-done.4) | copy-start | bytes 731140
  35.5 2.4 %copy-start = (bf16[128,1024]{1,0:T(8,128)(2,1)}, bf16[128,1024]{1,0:T(8,128)(2,1)S(1)}, u32[]{:S(2)}) copy-start(bf16[128,1024]{1,0:T(8,128)(2,1)S(1)} %collective-permute-done.5) | copy-start | bytes 786436
  36.0 1.6 %collective-permute-start.6 = (bf16[128,1024]{0,1:T(8,128)(2,1)S(1)}, bf16[128,1024]{0,1:T(8,128)(2,1)S(1)}, u32[]{:S(2)}, u32[]{:S(2)}) collective-permute-start(bf16[128,1024]{0,1:T(8,128)(2,1)S(1)} %get-tuple-element.108), channel_id=1, source_target_pairs={{0,4},{4,0},{8,12},{12,8},{16,20},{20,16},{24,28},{28,24},{1,5},{5... | collective-permute-start | bytes 786440 | tf_op jit(solution)/shard_map/ppermute | solution.py:12
  37.8 0.9 copy-start.7
  39.0 7.2 %collective-permute-start.7 = (bf16[128,256]{0,1:T(8,128)(2,1)S(1)}, bf16[128,256]{0,1:T(8,128)(2,1)S(1)}, u32[]{:S(2)}, u32[]{:S(2)}) collective-permute-start(bf16[128,256]{0,1:T(8,128)(2,1)S(1)} %fusion.20), channel_id=1, source_target_pairs={{0,2},{1,3},{2,0},{3,1},{4,6},{5,7},{6,4},{7,5},{8,10},{9,11},{10,... | collective-permute-start | bytes 196616 | tf_op jit(solution)/shard_map/ppermute | solution.py:12
  46.3 1.9 %copy-start.12 = (bf16[128,1024]{1,0:T(8,128)(2,1)}, bf16[128,1024]{1,0:T(8,128)(2,1)S(1)}, u32[]{:S(2)}) copy-start(bf16[128,1024]{1,0:T(8,128)(2,1)S(1)} %collective-permute-done.8) | copy-start | bytes 786436
  46.3 1.4 %collective-permute-start.10 = (bf16[128,512]{0,1:T(8,128)(2,1)S(1)}, bf16[128,512]{0,1:T(8,128)(2,1)S(1)}, u32[]{:S(2)}, u32[]{:S(2)}) collective-permute-start(bf16[128,512]{0,1:T(8,128)(2,1)S(1)} %maximum_select_fusion.11), channel_id=1, source_target_pairs={{0,4},{4,0},{8,12},{12,8},{16,20},{20,16},{24,28},{28,24},{1,5},{5... | collective-permute-start | bytes 393224 | tf_op jit(solution)/shard_map/ppermute | solution.py:12
  48.3 6.3 %collective-permute-start.11 = (bf16[128,256]{0,1:T(8,128)(2,1)S(1)}, bf16[128,256]{0,1:T(8,128)(2,1)S(1)}, u32[]{:S(2)}, u32[]{:S(2)}) collective-permute-start(bf16[128,256]{0,1:T(8,128)(2,1)S(1)} %fusion.22), channel_id=1, source_target_pairs={{0,2},{1,3},{2,0},{3,1},{4,6},{5,7},{6,4},{7,5},{8,10},{9,11},{10,... | collective-permute-start | bytes 196616 | tf_op jit(solution)/shard_map/ppermute | solution.py:12
  55.3 5.5 %collective-permute-start.12 = (bf16[128,512]{0,1:T(8,128)(2,1)S(1)}, bf16[128,512]{0,1:T(8,128)(2,1)S(1)}, u32[]{:S(2)}, u32[]{:S(2)}) collective-permute-start(bf16[128,512]{0,1:T(8,128)(2,1)S(1)} %pad_maximum_fusion.11), channel_id=1, source_target_pairs={{0,8},{4,12},{8,0},{12,4},{16,24},{20,28},{24,16},{28,20},{1,9},{5... | collective-permute-start | bytes 393224 | tf_op jit(solution)/shard_map/ppermute | solution.py:12
  60.9 5.0 %collective-permute-start.13 = (bf16[128,512]{0,1:T(8,128)(2,1)S(1)}, bf16[128,512]{0,1:T(8,128)(2,1)S(1)}, u32[]{:S(2)}, u32[]{:S(2)}) collective-permute-start(bf16[128,512]{0,1:T(8,128)(2,1)S(1)} %fusion.6), channel_id=1, source_target_pairs={{0,1},{1,0},{2,3},{3,2},{4,5},{5,4},{6,7},{7,6},{8,9},{9,8},{10,11... | collective-permute-start | bytes 393224 | tf_op jit(solution)/shard_map/ppermute | solution.py:12
  66.3 1.6 %collective-permute-start.14 = (bf16[256,512]{0,1:T(8,128)(2,1)S(1)}, bf16[256,512]{0,1:T(8,128)(2,1)S(1)}, u32[]{:S(2)}, u32[]{:S(2)}) collective-permute-start(bf16[256,512]{0,1:T(8,128)(2,1)S(1)} %pad_maximum_fusion.10), channel_id=1, source_target_pairs={{0,4},{4,0},{8,12},{12,8},{16,20},{20,16},{24,28},{28,24},{1,5},{5... | collective-permute-start | bytes 786440 | tf_op jit(solution)/shard_map/ppermute | solution.py:12
  70.0 1.6 %collective-permute-start.15 = (bf16[256,512]{0,1:T(8,128)(2,1)S(1)}, bf16[256,512]{0,1:T(8,128)(2,1)S(1)}, u32[]{:S(2)}, u32[]{:S(2)}) collective-permute-start(bf16[256,512]{0,1:T(8,128)(2,1)S(1)} %select_convert_fusion), channel_id=1, source_target_pairs={{0,4},{4,0},{8,12},{12,8},{16,20},{20,16},{24,28},{28,24},{1,5},{5... | collective-permute-start | bytes 786440 | tf_op jit(solution)/shard_map/ppermute | solution.py:12
  72.0 5.6 %collective-permute-start.16 = (bf16[128,512]{0,1:T(8,128)(2,1)S(1)}, bf16[128,512]{0,1:T(8,128)(2,1)S(1)}, u32[]{:S(2)}, u32[]{:S(2)}) collective-permute-start(bf16[128,512]{0,1:T(8,128)(2,1)S(1)} %pad_maximum_fusion.12), channel_id=1, source_target_pairs={{0,1},{1,0},{2,3},{3,2},{4,5},{5,4},{6,7},{7,6},{8,9},{9,8},{10,11... | collective-permute-start | bytes 393224 | tf_op jit(solution)/shard_map/ppermute | solution.py:12
  77.7 8.5 %collective-permute-start.17 = (bf16[128,512]{0,1:T(8,128)(2,1)S(1)}, bf16[128,512]{0,1:T(8,128)(2,1)S(1)}, u32[]{:S(2)}, u32[]{:S(2)}) collective-permute-start(bf16[128,512]{0,1:T(8,128)(2,1)S(1)} %fusion.109), channel_id=1, source_target_pairs={{0,2},{1,3},{2,0},{3,1},{4,6},{5,7},{6,4},{7,5},{8,10},{9,11},{10,... | collective-permute-start | bytes 393224 | tf_op jit(solution)/shard_map/ppermute | solution.py:12
  86.3 5.4 %collective-permute-start.18 = (bf16[128,512]{0,1:T(8,128)(2,1)S(1)}, bf16[128,512]{0,1:T(8,128)(2,1)S(1)}, u32[]{:S(2)}, u32[]{:S(2)}) collective-permute-start(bf16[128,512]{0,1:T(8,128)(2,1)S(1)} %add_convert_fusion.2), channel_id=1, source_target_pairs={{0,8},{4,12},{8,0},{12,4},{16,24},{20,28},{24,16},{28,20},{1,9},{5... | collective-permute-start | bytes 393224 | tf_op jit(solution)/shard_map/ppermute | solution.py:12
  88.1 4.4 %copy-start.3 = (bf16[128,1024]{1,0:T(8,128)(2,1)S(1)}, bf16[128,1024]{1,0:T(8,128)(2,1)}, u32[]{:S(2)}) copy-start(bf16[128,1024]{1,0:T(8,128)(2,1)} %copy-done.2) | copy-start | bytes 786436
  92.0 1.0 copy-start.13
  93.3 7.1 %copy-start.1 = (bf16[128,1024]{1,0:T(8,128)(2,1)S(1)}, bf16[128,1024]{1,0:T(8,128)(2,1)}, u32[]{:S(2)}) copy-start(bf16[128,1024]{1,0:T(8,128)(2,1)} %copy-done) | copy-start | bytes 786436
  93.3 1.4 %collective-permute-start.19 = (bf16[128,512]{0,1:T(8,128)(2,1)S(1)}, bf16[128,512]{0,1:T(8,128)(2,1)S(1)}, u32[]{:S(2)}, u32[]{:S(2)}) collective-permute-start(bf16[128,512]{0,1:T(8,128)(2,1)S(1)} %dynamic-slice_convert_fusion.2), channel_id=1, source_target_pairs={{0,4},{4,0},{8,12},{12,8},{16,20},{20,16},{24,28},{28,24},{1,5},{5... | collective-permute-start | bytes 393224 | tf_op jit(solution)/shard_map/ppermute | solution.py:12
  94.8 5.2 %collective-permute-start.20 = (bf16[128,256]{0,1:T(8,128)(2,1)S(1)}, bf16[128,256]{0,1:T(8,128)(2,1)S(1)}, u32[]{:S(2)}, u32[]{:S(2)}) collective-permute-start(bf16[128,256]{0,1:T(8,128)(2,1)S(1)} %dynamic-slice_convert_fusion.4), channel_id=1, source_target_pairs={{0,2},{1,3},{2,0},{3,1},{4,6},{5,7},{6,4},{7,5},{8,10},{9,11},{10,... | collective-permute-start | bytes 196616 | tf_op jit(solution)/shard_map/ppermute | solution.py:12
  100.7 1.4 %collective-permute-start.21 = (bf16[128,512]{0,1:T(8,128)(2,1)S(1)}, bf16[128,512]{0,1:T(8,128)(2,1)S(1)}, u32[]{:S(2)}, u32[]{:S(2)}) collective-permute-start(bf16[128,512]{0,1:T(8,128)(2,1)S(1)} %dynamic-slice_convert_fusion.1), channel_id=1, source_target_pairs={{0,4},{4,0},{8,12},{12,8},{16,20},{20,16},{24,28},{28,24},{1,5},{5... | collective-permute-start | bytes 393224 | tf_op jit(solution)/shard_map/ppermute | solution.py:12
  102.1 8.0 %collective-permute-start.22 = (bf16[128,512]{0,1:T(8,128)(2,1)S(1)}, bf16[128,512]{0,1:T(8,128)(2,1)S(1)}, u32[]{:S(2)}, u32[]{:S(2)}) collective-permute-start(bf16[128,512]{0,1:T(8,128)(2,1)S(1)} %fusion.17), channel_id=1, source_target_pairs={{0,2},{1,3},{2,0},{3,1},{4,6},{5,7},{6,4},{7,5},{8,10},{9,11},{10,... | collective-permute-start | bytes 393224 | tf_op jit(solution)/shard_map/ppermute | solution.py:12
  110.2 1.8 %copy-start.8 = (bf16[128,512]{1,0:T(8,128)(2,1)S(1)}, bf16[128,512]{1,0:T(8,128)(2,1)}, u32[]{:S(2)}) copy-start(bf16[128,512]{1,0:T(8,128)(2,1)} %fusion.1) | copy-start | bytes 393220
  110.2 1.4 %collective-permute-start.23 = (bf16[128,512]{0,1:T(8,128)(2,1)S(1)}, bf16[128,512]{0,1:T(8,128)(2,1)S(1)}, u32[]{:S(2)}, u32[]{:S(2)}) collective-permute-start(bf16[128,512]{0,1:T(8,128)(2,1)S(1)} %add_convert_fusion.1), channel_id=1, source_target_pairs={{0,4},{4,0},{8,12},{12,8},{16,20},{20,16},{24,28},{28,24},{1,5},{5... | collective-permute-start | bytes 393224 | tf_op jit(solution)/shard_map/ppermute | solution.py:12
  110.3 1.9 %copy-start.10 = (bf16[128,512]{1,0:T(8,128)(2,1)S(1)}, bf16[128,512]{1,0:T(8,128)(2,1)}, u32[]{:S(2)}) copy-start(bf16[128,512]{1,0:T(8,128)(2,1)} %fusion) | copy-start | bytes 393220
  111.9 7.2 %copy-start.9 = (f32[128,256]{0,1:T(8,128)S(1)}, f32[128,256]{0,1:T(8,128)}, u32[]{:S(2)}) copy-start(f32[128,256]{0,1:T(8,128)} %dynamic-slice_add_fusion) | copy-start | bytes 393220
  112.5 6.5 %collective-permute-start.24 = (bf16[128,256]{0,1:T(8,128)(2,1)S(1)}, bf16[128,256]{0,1:T(8,128)(2,1)S(1)}, u32[]{:S(2)}, u32[]{:S(2)}) collective-permute-start(bf16[128,256]{0,1:T(8,128)(2,1)S(1)} %dynamic-slice_convert_fusion.3), channel_id=1, source_target_pairs={{0,2},{1,3},{2,0},{3,1},{4,6},{5,7},{6,4},{7,5},{8,10},{9,11},{10,... | collective-permute-start | bytes 196616 | tf_op jit(solution)/shard_map/ppermute | solution.py:12
  112.6 6.6 %collective-permute-start.25 = (bf16[256,128]{0,1:T(8,128)(2,1)S(1)}, bf16[256,128]{0,1:T(8,128)(2,1)S(1)}, u32[]{:S(2)}, u32[]{:S(2)}) collective-permute-start(bf16[256,128]{0,1:T(8,128)(2,1)S(1)} %constant_dynamic-slice_fusion.1), channel_id=1, source_target_pairs={{0,1},{1,0},{2,3},{3,2},{4,5},{5,4},{6,7},{7,6},{8,9},{9,8},{10,11... | collective-permute-start | bytes 196616 | tf_op jit(solution)/shard_map/ppermute | solution.py:12
  119.2 4.0 %collective-permute-start.26 = (bf16[128,128]{0,1:T(8,128)(2,1)S(1)}, bf16[128,128]{0,1:T(8,128)(2,1)S(1)}, u32[]{:S(2)}, u32[]{:S(2)}) collective-permute-start(bf16[128,128]{0,1:T(8,128)(2,1)S(1)} %dynamic-slice_convert_fusion.5), channel_id=1, source_target_pairs={{0,1},{1,0},{2,3},{3,2},{4,5},{5,4},{6,7},{7,6},{8,9},{9,8},{10,11... | collective-permute-start | bytes 98312 | tf_op jit(solution)/shard_map/ppermute | solution.py:12

commit v5 on v4

--- a/solution.py
+++ b/solution.py
@@ -138,69 +138,78 @@
     inverse2 = inverse_blocks[:, 3 * leaf_rows :]
     update0 = update_blocks[:, :leaf_rows]
     update1 = update_blocks[:, leaf_rows:]
-    inverse0 = lax.optimization_barrier(inverse0)
-    inverse1 = lax.optimization_barrier(inverse1)
-    inverse2 = lax.optimization_barrier(inverse2)
-    update0 = lax.optimization_barrier(update0)
-    update1 = lax.optimization_barrier(update1)
+    inverse0, inverse1, inverse2, update0, update1 = together(
+        inverse0, inverse1, inverse2, update0, update1
+    )
 
     lists = jnp.concatenate([asm_owner[:, :, 0], asm_row], 0).astype(BF16)
-    lists = jnp.pad(lists, ((0, 4), (0, leaf_rows + LEVELS * half_cols - own_rows)))
-
-    def parcel(half):
+    lists = jnp.pad(lists, ((0, 4), (0, 2 * own_rows + LEVELS * half_cols - own_rows)))
+
+    def parcel(mask):
+        half = odd if mask % 2 == 0 else 1 - odd
         columns = [part(rhs[level], half, 2, 1) for level in range(LEVELS)]
-        return jnp.concatenate([jnp.concatenate([inverse0, *columns], 1), lists], 0)
-
-    kept, handed = parcel(odd), parcel(1 - odd)
-    parcels = [kept] + [
-        traded(handed if mask % 2 else kept, "front", mask) for mask in range(1, front_count)
+        updates = part(update0, (front_id ^ mask) // 2, front_count // 2, 1)
+        return jnp.concatenate([jnp.concatenate([updates, *columns], 1), lists], 0)
+
+    parcels = {0: parcel(0)}
+    for mask in sorted(range(1, front_count), key=lambda mask: (mask + 1) % front_count):
+        parcels[mask] = traded(parcel(mask), "front", mask)
+    parcels = [parcels[mask] for mask in range(front_count)]
+    inverse0_pair = traded(inverse0, "front", 1)
+    cores2 = [
+        jnp.concatenate(
+            [inverse2[:, (2 * other + core) * leaf_rows :][:, :leaf_rows] for other in range(2)], 1
+        )
+        for core in range(2)
     ]
-    update0_pair = traded(after(update0, handed), "front", 1)
-    inverse1_pair = traded(after(inverse1, handed), "front", 1)
-    *parcels, update0_pair = together(*parcels, update0_pair)
-    inverse0_pieces = [block[:own_rows, :leaf_rows] for block in parcels]
-    rhs0, rhs1, rhs2 = (
-        in_order(
+    handed2 = jnp.where(side == 1, cores2[0], cores2[1])
+    block2 = jnp.where(side == 1, cores2[1], cores2[0])
+    block2 = jnp.concatenate([block2, traded(handed2, "leaf", 1)], 0)
+    wing2 = traded(block2, "leaf", 2)
+    inverse1_pair = traded(after(inverse1, inverse0_pair), "front", 1)
+    *parcels, block2, inverse0_pair = together(*parcels, block2, inverse0_pair)
+    update0_columns = in_order([block[:own_rows, : 2 * own_rows] for block in parcels], 0)
+
+    def level_rows(blocks, level):
+        return in_order(
             [
-                block[:own_rows, leaf_rows + level * half_cols : leaf_rows + (level + 1) * half_cols]
-                for block in parcels
+                block[:own_rows, 2 * own_rows + level * half_cols :][:, :half_cols]
+                for block in blocks
             ],
             0,
         )
-        for level in range(LEVELS)
-    )
-    rhs1, rhs2 = rhs1.T, rhs2.T
+
+    rhs0 = level_rows(parcels, 0)
+
+    solved0_pair = ordered(
+        product(rhs0, inverse0, 0, 1), product(rhs0, inverse0_pair, 0, 1), odd, 1
+    ).astype(BF16)
+    update1_pair = traded(after(update1, solved0_pair), "front", 1)
+    updated0 = forward(solved0_pair, update0_columns)
+    parcels = together(*parcels, updated0)[:-1]
+    rhs1, rhs2 = level_rows(parcels, 1).T, level_rows(parcels, 2).T
     lists = in_order([block[own_rows : own_rows + 4, :own_rows] for block in parcels], 1)
-
-    solved0 = in_order([product(rhs0, piece, 0, 1) for piece in inverse0_pieces], 1).astype(BF16)
-    updated0_pair = pair_forward(solved0, update0, update0_pair)
-    update1_pair = traded(after(update1, solved0), "front", 1)
-    updated0 = high_gather(updated0_pair)
+    lists_wing = traded(jnp.pad(lists, ((0, 12), (0, 0))), "leaf", 2)[:4]
+    updated0 = high_sum(updated0).astype(BF16)
     updated0, inverse1_pair = together(updated0, inverse1_pair)
-    wing2 = traded(after(inverse2, solved0), "leaf", 2)
-
-    def selector(level_index):
+
+    def selector(lists, level_index):
         numbers = lists.astype(jnp.int32)
         target = numbers[level_index : level_index + 1] * own_rows + numbers[2 + level_index : 3 + level_index]
         return (jnp.arange(2 * leaf_rows)[:, None] == target).astype(BF16)
 
-    select0 = selector(0)
-    select1 = selector(1)
+    select0 = selector(lists, 0)
+    select1 = selector(lists, 1)
     pivots1 = ordered(rhs1, jnp.zeros_like(rhs1), side, 1).astype(F32) - forward(updated0, select0)
     pivots1 = (pivots1 + traded(pivots1.astype(BF16), "leaf", 1).astype(F32)).astype(BF16)
 
     solved1_pair = pair_forward(pivots1, inverse1, inverse1_pair)
-    solved0_late, update0_late = together(solved0, update0, solved1_pair)[:2]
-    straight0 = pair_rows(leaf_adjoint(solved0_late, inverse0_pieces))
-    both0 = leaf_adjoint(update0_late, inverse0_pieces).astype(BF16)
-    both0_pair = leaf_adjoint(update0_pair, inverse0_pieces).astype(BF16)
     solved1 = high_gather(solved1_pair)
-    solved1, straight0, both0, both0_pair, update1_pair, wing2 = together(
-        solved1, straight0, both0, both0_pair, update1_pair, wing2
-    )
+    solved1, update1_pair = together(solved1, update1_pair)
     solved1 = ordered(solved1, traded(solved1, "leaf", 1), side, 1)
     updated1_pair = pair_forward(solved1, update1, update1_pair)
     updated1 = high_gather(updated1_pair)
+    updated1, wing2 = together(updated1, wing2)
 
     pivots2 = ordered(rhs2, jnp.zeros_like(rhs2), wing, 1).astype(F32) - forward(updated1, select1)
     pivots2 = (
@@ -214,43 +223,53 @@
         ],
         0,
     )
-    other2 = traded(pivots2, "leaf", 1)
-    low2 = flat(jnp.where(side == 1, other2, pivots2))
-    high2 = flat(jnp.where(side == 1, pivots2, other2))
-    pivots2 = jnp.concatenate([low2[0], high2[0], low2[1], high2[1]], 1)
-    below2 = adjoint(forward(pivots2, inverse2).astype(BF16), inverse2) + adjoint(
-        forward(pivots2, wing2).astype(BF16), wing2
-    )
-    leaves = [below2[:, i * leaf_rows : (i + 1) * leaf_rows] for i in range(4)]
-    low2 = jnp.concatenate([leaves[0], leaves[2]], 0)
-    high2 = jnp.concatenate([leaves[1], leaves[3]], 0)
-    handed2 = jnp.where(side == 1, low2, high2).astype(BF16)
-    below2 = jnp.where(side == 1, high2, low2) + traded(handed2, "leaf", 1).astype(F32)
+    pivots2 = jnp.concatenate(flat(pivots2), 1)
+    solved2 = [forward(pivots2, block2), forward(pivots2, wing2)]
+    received = traded(jnp.concatenate(solved2, 1).astype(BF16), "leaf", 1)
+    below2 = 0.0
+    for index, block in enumerate((block2, wing2)):
+        other = received[:, 2 * index * own_rows :][:, : 2 * own_rows]
+        other = jnp.concatenate([other[:, own_rows:], other[:, :own_rows]], 1)
+        below2 += adjoint((solved2[index] + other.astype(F32)).astype(BF16), block)
+    handed2 = stacked(below2[quarter:].astype(BF16))
+    below2 = stacked(below2[:quarter])
+    below2 = (below2 + traded(handed2, "front", 1).astype(F32)).astype(BF16)
+
+    def wing_gather(own, other):
+        other = traded(stacked(other.astype(BF16)), "leaf", 2)
+        return ordered(own.astype(BF16), jnp.concatenate(flat(other), 1), wing, 0)
+
+    both2 = jnp.concatenate(flat(below2), 1)
+    fetched1 = jnp.concatenate(
+        [adjoint(both2, select1), adjoint(both2, selector(lists_wing, 1))], 0
+    )
+    fetched1 = high_scatter(fetched1)
+    below2 = high_scatter(after(below2, fetched1))
+    fetched1 = wing_gather(*flat(fetched1))
+    carried1 = pair_adjoint(fetched1, update1, update1_pair)
+    carried1 = side_scatter(carried1)
+    carried1, below2 = together(carried1, below2)
     low2, high2 = flat(below2)
-    handed2 = jnp.concatenate([low2[quarter:], high2[quarter:]], 0).astype(BF16)
-    below2 = jnp.concatenate([low2[:quarter], high2[:quarter]], 0)
-    below2 = below2 + traded(handed2, "front", 1).astype(F32)
-    below2 = high_sum(below2).astype(BF16)
-    own2 = flat(below2)
-    other2 = flat(traded(below2, "leaf", 2))
-    below2 = jnp.concatenate(
-        [ordered(own, other, wing, 0) for own, other in zip(own2, other2)], 1
-    )
-
-    fetched1 = adjoint(below2, pair_rows(select1)).astype(BF16)
-    carried1 = pair_adjoint(fetched1, update1, update1_pair)
-    weights1 = (solved1_pair.astype(F32) - high_scatter(side_scatter(carried1))).astype(BF16)
+    solution2 = wing_gather(jnp.where(wing == 1, high2, low2), jnp.where(wing == 1, low2, high2))
+    carried1, solution2 = together(high_scatter(carried1), solution2)
+    weights1 = (solved1_pair.astype(F32) - carried1).astype(BF16)
     below1 = high_sum(side_scatter(pair_adjoint(weights1, inverse1, inverse1_pair))).astype(BF16)
     below1_all = ordered(below1, traded(below1, "leaf", 1), side, 1)
 
-    fetched0 = adjoint(below1_all, pair_rows(select0)).astype(BF16)
-    carried0 = pair_adjoint(fetched0, both0, both0_pair)
-    upper = jnp.concatenate([pair_rows(below1), pair_rows(part(below2, wing, 2, 1))], 0)
-    upper, carried0 = together(upper, carried0)
+    fetched0 = adjoint(below1_all, select0).astype(BF16)
+    weights0 = (solved0_pair.astype(F32) - adjoint(fetched0, update0_columns)).astype(BF16)
+    below0 = pair_adjoint(weights0, inverse0, inverse0_pair)
+    upper = jnp.concatenate([pair_rows(below1), solution2], 0)
+    upper, below0 = together(upper, below0)
     upper_other = traded(part(upper, 1 - odd, 2, 1), "front", 1)
-    carried0, upper_other = together(high_scatter(carried0), upper_other)
-    below0 = straight0 - carried0
-    below0_other = traded(part(below0, 1 - odd, 2, 1).astype(BF16), "front", 1)
+    shares = [
+        traded(part(below0, front_id ^ mask, front_count, 1).astype(BF16), "front", mask)
+        for mask in range(1, front_count)
+    ]
+    upper_other, *shares = together(upper_other, *shares)
+    sums = [part(below0, front_id, front_count, 1), 0.0]
+    for mask, share in enumerate(shares):
+        sums[(mask + 1) % 2] += share.astype(F32)
 
     def finished(own, other):
         return ordered(own.astype(F32), other.astype(F32), odd, 0).T
@@ -258,7 +277,7 @@
     upper = part(upper, odd, 2, 1)
     return jnp.stack(
         [
-            finished(part(below0, odd, 2, 1), below0_other),
+            finished(*sums),
             finished(upper[:half_cols], upper_other[:half_cols]),
             finished(upper[half_cols:], upper_other[half_cols:]),
         ]

time: 124 us -> 117 us (0.944)
  other arithmetic: 6.11 us -> 2.92 us
  matrix products: 10.5 us -> 7.71 us
    dot_general x34 -> x22, matrix products: 10.5 us -> 7.71 us  [product(): lax.dot_general(left, right, (((left_dim,), (right_dim,)), ((), ())), pre...]
    ppermute x27 -> x31, waiting for transfers between devices: 73.1 us -> 74.2 us  [traded(): lax.ppermute(shard, axis, [(i, i ^ mask) for i in range(lax.axis_size(axi...]
    ppermute x27 -> x31, starting transfers between devices: 28 us -> 27.2 us  [traded(): lax.ppermute(shard, axis, [(i, i ^ mask) for i in range(lax.axis_size(axi...]
  transfers between devices with their start and end apart: 27 -> 31, of which waited for: 22 -> 23; matrix products, arithmetic and copies ran while one was open for 8% -> 4% of each run, Pallas kernels for 0% -> 0%
where the time goes in v5:
time: 117 us
  waiting for transfers between devices  74.2 us (63%)
  starting transfers between devices  27.2 us (23%)
  matrix products  7.71 us (7%)
  local copies, waits for them, and re-layouts  4.19 us (4%)
  other arithmetic  2.92 us (2%)
    ppermute x31, waiting for transfers between devices, traded(): lax.ppermute(shard, axis, [(i, i ^ mask) for i in range(lax.axis_size(axi...  74.2 us
    ppermute x31, starting transfers between devices, traded(): lax.ppermute(shard, axis, [(i, i ^ mask) for i in range(lax.axis_size(axi...  27.2 us
    dot_general x22, matrix products, product(): lax.dot_general(left, right, (((left_dim,), (right_dim,)), ((), ())), pre...  7.71 us
  transfers between devices with their start and end apart: 31, of which 23 were waited for; matrix products, arithmetic and copies ran while one was open for 4% of the time, Pallas kernels for 0%

profile of v5, /device:TPU:0, one launch (start us, length us, event | category | flops | bytes accessed | tf_op | source)
XLA Modules:
  0.0 117.2 jit_solution(9283529796510428501)
XLA Ops:
  0.0 1.2 %copy-done = bf16[128,3584]{1,0:T(8,128)(2,1)S(1)} copy-done((bf16[128,3584]{1,0:T(8,128)(2,1)S(1)}, bf16[128,3584]{1,0:T(8,128)(2,1)}, u32[]{:S(2)}) %copy-start) | copy-done | bytes 917528
  1.3 0.9 slice-done
  2.2 0.3 copy.34
  2.7 0.5 collective-permute-start.3
  3.7 3.1 %collective-permute-start = (bf16[136,640]{1,0:T(8,128)(2,1)S(1)}, bf16[136,640]{1,0:T(8,128)(2,1)S(1)}, u32[]{:S(2)}, u32[]{:S(2)}) collective-permute-start(bf16[136,640]{1,0:T(8,128)(2,1)S(1)} %get-tuple-element.120), channel_id=1, source_target_pairs={{0,1},{1,0},{2,3},{3,2},{4,5},{5,4},{6,7},{7,6},{8,9},{9,8},{10,11... | collective-permute-start | bytes 522248 | tf_op jit(solution)/shard_map/ppermute | solution.py:12
  6.8 2.5 %collective-permute-start.2 = (bf16[136,640]{1,0:T(8,128)(2,1)S(1)}, bf16[136,640]{1,0:T(8,128)(2,1)S(1)}, u32[]{:S(2)}, u32[]{:S(2)}) collective-permute-start(bf16[136,640]{1,0:T(8,128)(2,1)S(1)} %get-tuple-element.119), channel_id=1, source_target_pairs={{0,3},{1,2},{2,1},{3,0},{4,7},{5,6},{6,5},{7,4},{8,11},{9,10},{10,... | collective-permute-start | bytes 522248 | tf_op jit(solution)/shard_map/ppermute | solution.py:12
  9.3 0.7 collective-permute-start.4
  10.0 1.3 %collective-permute-start.1 = (bf16[136,640]{1,0:T(8,128)(2,1)S(1)}, bf16[136,640]{1,0:T(8,128)(2,1)S(1)}, u32[]{:S(2)}, u32[]{:S(2)}) collective-permute-start(bf16[136,640]{1,0:T(8,128)(2,1)S(1)} %get-tuple-element.121), channel_id=1, source_target_pairs={{0,2},{1,3},{2,0},{3,1},{4,6},{5,7},{6,4},{7,5},{8,10},{9,11},{10,... | collective-permute-start | bytes 522248 | tf_op jit(solution)/shard_map/ppermute | solution.py:12
  11.3 9.0 %collective-permute-done.4 = bf16[128,512]{1,0:T(8,128)(2,1)S(1)} collective-permute-done((bf16[128,512]{1,0:T(8,128)(2,1)S(1)}, bf16[128,512]{1,0:T(8,128)(2,1)S(1)}, u32[]{:S(2)}, u32[]{:S(2)}) %collective-permute-start.4) | collective-permute-done | bytes 131104 | tf_op jit(solution)/shard_map/ppermute | solution.py:12
  20.3 0.4 collective-permute-start.6
  20.8 3.8 %collective-permute-done.1 = bf16[136,640]{1,0:T(8,128)(2,1)S(1)} collective-permute-done((bf16[136,640]{1,0:T(8,128)(2,1)S(1)}, bf16[136,640]{1,0:T(8,128)(2,1)S(1)}, u32[]{:S(2)}, u32[]{:S(2)}) %collective-permute-start.1) | collective-permute-done | bytes 174112 | tf_op jit(solution)/shard_map/ppermute | solution.py:12
  25.6 0.9 collective-permute-start.5
  26.6 6.8 %collective-permute-done.5 = bf16[128,512]{1,0:T(8,128)(2,1)S(1)} collective-permute-done((bf16[128,512]{1,0:T(8,128)(2,1)S(1)}, bf16[128,512]{1,0:T(8,128)(2,1)S(1)}, u32[]{:S(2)}, u32[]{:S(2)}) %collective-permute-start.5) | collective-permute-done | bytes 131104 | tf_op jit(solution)/shard_map/ppermute | solution.py:12
  33.5 0.5 fusion.111
  34.1 1.4 %collective-permute-done.7 = bf16[128,1024]{0,1:T(8,128)(2,1)S(1)} collective-permute-done((bf16[128,1024]{0,1:T(8,128)(2,1)S(1)}, bf16[128,1024]{0,1:T(8,128)(2,1)S(1)}, u32[]{:S(2)}, u32[]{:S(2)}) %collective-permute-start.7) | collective-permute-done | bytes 262176 | tf_op jit(solution)/shard_map/ppermute | solution.py:12
  36.0 1.4 %collective-permute-start.8 = (bf16[128,256]{0,1:T(8,128)(2,1)S(1)}, bf16[128,256]{0,1:T(8,128)(2,1)S(1)}, u32[]{:S(2)}, u32[]{:S(2)}) collective-permute-start(bf16[128,256]{0,1:T(8,128)(2,1)S(1)} %fusion.38), channel_id=1, source_target_pairs={{0,2},{1,3},{2,0},{3,1},{4,6},{5,7},{6,4},{7,5},{8,10},{9,11},{10,... | collective-permute-start | bytes 196616 | tf_op jit(solution)/shard_map/ppermute | solution.py:12
  37.5 1.5 %collective-permute-start.12 = (bf16[256,1024]{0,1:T(8,128)(2,1)S(1)}, bf16[256,1024]{0,1:T(8,128)(2,1)S(1)}, u32[]{:S(2)}, u32[]{:S(2)}) collective-permute-start(bf16[256,1024]{0,1:T(8,128)(2,1)S(1)} %pad_maximum_fusion), channel_id=1, source_target_pairs={{0,8},{4,12},{8,0},{12,4},{16,24},{20,28},{24,16},{28,20},{1,9},{5... | collective-permute-start | bytes 1572872 | tf_op jit(solution)/shard_map/ppermute | solution.py:12
  39.0 0.6 collective-permute-start.17
  39.5 2.4 %collective-permute-done.8 = bf16[128,256]{0,1:T(8,128)(2,1)S(1)} collective-permute-done((bf16[128,256]{0,1:T(8,128)(2,1)S(1)}, bf16[128,256]{0,1:T(8,128)(2,1)S(1)}, u32[]{:S(2)}, u32[]{:S(2)}) %collective-permute-start.8) | collective-permute-done | bytes 65568 | tf_op jit(solution)/shard_map/ppermute | solution.py:12
  42.0 2.2 %collective-permute-done.9 = bf16[128,1024]{1,0:T(8,128)(2,1)S(1)} collective-permute-done((bf16[128,1024]{1,0:T(8,128)(2,1)S(1)}, bf16[128,1024]{1,0:T(8,128)(2,1)S(1)}, u32[]{:S(2)}, u32[]{:S(2)}) %collective-permute-start.9) | collective-permute-done | bytes 262176 | tf_op jit(solution)/shard_map/ppermute | solution.py:12
  44.2 1.3 %collective-permute-done.10 = bf16[128,512]{0,1:T(8,128)(2,1)S(1)} collective-permute-done((bf16[128,512]{0,1:T(8,128)(2,1)S(1)}, bf16[128,512]{0,1:T(8,128)(2,1)S(1)}, u32[]{:S(2)}, u32[]{:S(2)}) %collective-permute-start.10) | collective-permute-done | bytes 131104 | tf_op jit(solution)/shard_map/ppermute | solution.py:12
  45.5 0.2 fusion.53
  45.8 0.2 fusion.52
  46.0 1.3 %collective-permute-start.11 = (bf16[128,256]{0,1:T(8,128)(2,1)S(1)}, bf16[128,256]{0,1:T(8,128)(2,1)S(1)}, u32[]{:S(2)}, u32[]{:S(2)}) collective-permute-start(bf16[128,256]{0,1:T(8,128)(2,1)S(1)} %fusion.40), channel_id=1, source_target_pairs={{0,2},{1,3},{2,0},{3,1},{4,6},{5,7},{6,4},{7,5},{8,10},{9,11},{10,... | collective-permute-start | bytes 196616 | tf_op jit(solution)/shard_map/ppermute | solution.py:12
  47.4 5.1 %collective-permute-done.11 = bf16[128,256]{0,1:T(8,128)(2,1)S(1)} collective-permute-done((bf16[128,256]{0,1:T(8,128)(2,1)S(1)}, bf16[128,256]{0,1:T(8,128)(2,1)S(1)}, u32[]{:S(2)}, u32[]{:S(2)}) %collective-permute-start.11) | collective-permute-done | bytes 65568 | tf_op jit(solution)/shard_map/ppermute | solution.py:12
  52.6 0.5 fusion.6
  53.4 1.6 %collective-permute-start.13 = (bf16[128,512]{0,1:T(8,128)(2,1)S(1)}, bf16[128,512]{0,1:T(8,128)(2,1)S(1)}, u32[]{:S(2)}, u32[]{:S(2)}) collective-permute-start(bf16[128,512]{0,1:T(8,128)(2,1)S(1)} %pad_maximum_fusion.23), channel_id=1, source_target_pairs={{0,8},{4,12},{8,0},{12,4},{16,24},{20,28},{24,16},{28,20},{1,9},{5... | collective-permute-start | bytes 393224 | tf_op jit(solution)/shard_map/ppermute | solution.py:12
  55.1 3.3 %collective-permute-done.13 = bf16[128,512]{0,1:T(8,128)(2,1)S(1)} collective-permute-done((bf16[128,512]{0,1:T(8,128)(2,1)S(1)}, bf16[128,512]{0,1:T(8,128)(2,1)S(1)}, u32[]{:S(2)}, u32[]{:S(2)}) %collective-permute-start.13) | collective-permute-done | bytes 131104 | tf_op jit(solution)/shard_map/ppermute | solution.py:12
  58.6 0.3 collective-permute-start.14
  58.9 4.7 %collective-permute-done.14 = bf16[128,512]{0,1:T(8,128)(2,1)S(1)} collective-permute-done((bf16[128,512]{0,1:T(8,128)(2,1)S(1)}, bf16[128,512]{0,1:T(8,128)(2,1)S(1)}, u32[]{:S(2)}, u32[]{:S(2)}) %collective-permute-start.14) | collective-permute-done | bytes 131104 | tf_op jit(solution)/shard_map/ppermute | solution.py:12
  63.7 0.4 fusion.113
  64.1 0.4 fusion.112
  64.6 1.3 %collective-permute-done.15 = bf16[128,512]{1,0:T(8,128)(2,1)S(1)} collective-permute-done((bf16[128,512]{1,0:T(8,128)(2,1)S(1)}, bf16[128,512]{1,0:T(8,128)(2,1)S(1)}, u32[]{:S(2)}, u32[]{:S(2)}) %collective-permute-start.15) | collective-permute-done | bytes 131104 | tf_op jit(solution)/shard_map/ppermute | solution.py:12
  65.9 0.3 fusion.44
  66.2 0.3 fusion.114
  66.8 0.2 collective-permute-start.16
  67.1 5.3 %collective-permute-done.16 = bf16[128,512]{0,1:T(8,128)(2,1)S(1)} collective-permute-done((bf16[128,512]{0,1:T(8,128)(2,1)S(1)}, bf16[128,512]{0,1:T(8,128)(2,1)S(1)}, u32[]{:S(2)}, u32[]{:S(2)}) %collective-permute-start.16) | collective-permute-done | bytes 131104 | tf_op jit(solution)/shard_map/ppermute | solution.py:12
  72.7 0.7 fusion
  73.4 0.7 fusion.4
  74.2 1.5 %collective-permute-start.18 = (bf16[128,256]{0,1:T(8,128)(2,1)S(1)}, bf16[128,256]{0,1:T(8,128)(2,1)S(1)}, u32[]{:S(2)}, u32[]{:S(2)}) collective-permute-start(bf16[128,256]{0,1:T(8,128)(2,1)S(1)} %fusion.33), channel_id=1, source_target_pairs={{0,2},{1,3},{2,0},{3,1},{4,6},{5,7},{6,4},{7,5},{8,10},{9,11},{10,... | collective-permute-start | bytes 196616 | tf_op jit(solution)/shard_map/ppermute | solution.py:12
  75.7 4.2 %collective-permute-done.18 = bf16[128,256]{0,1:T(8,128)(2,1)S(1)} collective-permute-done((bf16[128,256]{0,1:T(8,128)(2,1)S(1)}, bf16[128,256]{0,1:T(8,128)(2,1)S(1)}, u32[]{:S(2)}, u32[]{:S(2)}) %collective-permute-start.18) | collective-permute-done | bytes 65568 | tf_op jit(solution)/shard_map/ppermute | solution.py:12
  80.2 1.5 %collective-permute-start.19 = (bf16[128,128]{0,1:T(8,128)(2,1)S(1)}, bf16[128,128]{0,1:T(8,128)(2,1)S(1)}, u32[]{:S(2)}, u32[]{:S(2)}) collective-permute-start(bf16[128,128]{0,1:T(8,128)(2,1)S(1)} %pad_maximum_fusion.27), channel_id=1, source_target_pairs={{0,8},{4,12},{8,0},{12,4},{16,24},{20,28},{24,16},{28,20},{1,9},{5... | collective-permute-start | bytes 98312 | tf_op jit(solution)/shard_map/ppermute | solution.py:12
  81.7 1.1 collective-permute-start.21
  82.8 1.4 %collective-permute-done.19 = bf16[128,128]{0,1:T(8,128)(2,1)S(1)} collective-permute-done((bf16[128,128]{0,1:T(8,128)(2,1)S(1)}, bf16[128,128]{0,1:T(8,128)(2,1)S(1)}, u32[]{:S(2)}, u32[]{:S(2)}) %collective-permute-start.19) | collective-permute-done | bytes 32800 | tf_op jit(solution)/shard_map/ppermute | solution.py:12
  84.4 0.3 fusion.61
  84.7 0.3 convolution_add_fusion.1
  85.1 2.3 %collective-permute-done.21 = bf16[128,256]{0,1:T(8,128)(2,1)S(1)} collective-permute-done((bf16[128,256]{0,1:T(8,128)(2,1)S(1)}, bf16[128,256]{0,1:T(8,128)(2,1)S(1)}, u32[]{:S(2)}, u32[]{:S(2)}) %collective-permute-start.21) | collective-permute-done | bytes 65568 | tf_op jit(solution)/shard_map/ppermute | solution.py:12
  87.6 0.6 collective-permute-start.23
  88.2 1.1 collective-permute-start.22
  89.3 2.3 %collective-permute-done.23 = bf16[128,128]{0,1:T(8,128)(2,1)S(1)} collective-permute-done((bf16[128,128]{0,1:T(8,128)(2,1)S(1)}, bf16[128,128]{0,1:T(8,128)(2,1)S(1)}, u32[]{:S(2)}, u32[]{:S(2)}) %collective-permute-start.23) | collective-permute-done | bytes 32800 | tf_op jit(solution)/shard_map/ppermute | solution.py:12
  91.8 2.6 %collective-permute-done.22 = bf16[128,256]{0,1:T(8,128)(2,1)S(1)} collective-permute-done((bf16[128,256]{0,1:T(8,128)(2,1)S(1)}, bf16[128,256]{0,1:T(8,128)(2,1)S(1)}, u32[]{:S(2)}, u32[]{:S(2)}) %collective-permute-start.22) | collective-permute-done | bytes 65568 | tf_op jit(solution)/shard_map/ppermute | solution.py:12
  94.4 0.3 fusion.58
  94.7 0.3 convolution_add_fusion
  95.1 1.3 %collective-permute-done.24 = bf16[128,512]{0,1:T(8,128)(2,1)S(1)} collective-permute-done((bf16[128,512]{0,1:T(8,128)(2,1)S(1)}, bf16[128,512]{0,1:T(8,128)(2,1)S(1)}, u32[]{:S(2)}, u32[]{:S(2)}) %collective-permute-start.24) | collective-permute-done | bytes 131104 | tf_op jit(solution)/shard_map/ppermute | solution.py:12
  96.7 8.5 %collective-permute-done.25 = bf16[128,512]{0,1:T(8,128)(2,1)S(1)} collective-permute-done((bf16[128,512]{0,1:T(8,128)(2,1)S(1)}, bf16[128,512]{0,1:T(8,128)(2,1)S(1)}, u32[]{:S(2)}, u32[]{:S(2)}) %collective-permute-start.25) | collective-permute-done | bytes 131104 | tf_op jit(solution)/shard_map/ppermute | solution.py:12
  105.4 1.3 %collective-permute-done.26 = bf16[128,512]{0,1:T(8,128)(2,1)S(1)} collective-permute-done((bf16[128,512]{0,1:T(8,128)(2,1)S(1)}, bf16[128,512]{0,1:T(8,128)(2,1)S(1)}, u32[]{:S(2)}, u32[]{:S(2)}) %collective-permute-start.26) | collective-permute-done | bytes 131104 | tf_op jit(solution)/shard_map/ppermute | solution.py:12
  106.7 0.8 fusion.10
  108.1 2.1 %collective-permute-start.28 = (bf16[128,128]{0,1:T(8,128)(2,1)S(1)}, bf16[128,128]{0,1:T(8,128)(2,1)S(1)}, u32[]{:S(2)}, u32[]{:S(2)}) collective-permute-start(bf16[128,128]{0,1:T(8,128)(2,1)S(1)} %get-tuple-element.87), channel_id=1, source_target_pairs={{0,1},{1,0},{2,3},{3,2},{4,5},{5,4},{6,7},{7,6},{8,9},{9,8},{10,11... | collective-permute-start | bytes 98312 | tf_op jit(solution)/shard_map/ppermute | solution.py:12
  110.2 0.5 collective-permute-start.29
  110.6 2.0 %collective-permute-start.30 = (bf16[128,128]{0,1:T(8,128)(2,1)S(1)}, bf16[128,128]{0,1:T(8,128)(2,1)S(1)}, u32[]{:S(2)}, u32[]{:S(2)}) collective-permute-start(bf16[128,128]{0,1:T(8,128)(2,1)S(1)} %get-tuple-element.85), channel_id=1, source_target_pairs={{0,3},{1,2},{2,1},{3,0},{4,7},{5,6},{6,5},{7,4},{8,11},{9,10},{10,... | collective-permute-start | bytes 98312 | tf_op jit(solution)/shard_map/ppermute | solution.py:12
  112.6 0.3 collective-permute-done.28
  112.9 2.4 %collective-permute-done.29 = bf16[128,128]{0,1:T(8,128)(2,1)S(1)} collective-permute-done((bf16[128,128]{0,1:T(8,128)(2,1)S(1)}, bf16[128,128]{0,1:T(8,128)(2,1)S(1)}, u32[]{:S(2)}, u32[]{:S(2)}) %collective-permute-start.29) | collective-permute-done | bytes 32800 | tf_op jit(solution)/shard_map/ppermute | solution.py:12
  115.3 1.0 collective-permute-done.30
  116.5 0.8 pad_maximum_fusion.1
  (148 shorter events, 6.2 us)
Async XLA Ops:
  0.0 1.2 %copy-start = (bf16[128,3584]{1,0:T(8,128)(2,1)S(1)}, bf16[128,3584]{1,0:T(8,128)(2,1)}, u32[]{:S(2)}) copy-start(bf16[128,3584]{1,0:T(8,128)(2,1)} %param.6) | copy-start | bytes 2752516
  0.0 1.3 %copy-start.1 = (bf16[128,1536]{1,0:T(8,128)(2,1)S(1)}, bf16[128,1536]{1,0:T(8,128)(2,1)}, u32[]{:S(2)}) copy-start(bf16[128,1536]{1,0:T(8,128)(2,1)} %param.7) | copy-start | bytes 1179652
  1.2 1.1 slice-start
  2.5 0.9 copy-start.2
  2.6 0.9 copy-start.9
  2.6 0.9 copy-start.10
  2.6 1.0 slice-start.1
  2.7 18.0 %collective-permute-start.3 = (bf16[128,1024]{0,1:T(8,128)(2,1)S(1)}, bf16[128,1024]{0,1:T(8,128)(2,1)S(1)}, u32[]{:S(2)}, u32[]{:S(2)}) collective-permute-start(bf16[128,1024]{0,1:T(8,128)(2,1)S(1)} %get-tuple-element.80), channel_id=1, source_target_pairs={{0,4},{4,0},{8,12},{12,8},{16,20},{20,16},{24,28},{28,24},{1,5},{5... | collective-permute-start | bytes 786440 | tf_op jit(solution)/shard_map/ppermute | solution.py:12
  3.7 17.0 %collective-permute-start = (bf16[136,640]{1,0:T(8,128)(2,1)S(1)}, bf16[136,640]{1,0:T(8,128)(2,1)S(1)}, u32[]{:S(2)}, u32[]{:S(2)}) collective-permute-start(bf16[136,640]{1,0:T(8,128)(2,1)S(1)} %get-tuple-element.120), channel_id=1, source_target_pairs={{0,1},{1,0},{2,3},{3,2},{4,5},{5,4},{6,7},{7,6},{8,9},{9,8},{10,11... | collective-permute-start | bytes 522248 | tf_op jit(solution)/shard_map/ppermute | solution.py:12
  6.8 14.0 %collective-permute-start.2 = (bf16[136,640]{1,0:T(8,128)(2,1)S(1)}, bf16[136,640]{1,0:T(8,128)(2,1)S(1)}, u32[]{:S(2)}, u32[]{:S(2)}) collective-permute-start(bf16[136,640]{1,0:T(8,128)(2,1)S(1)} %get-tuple-element.119), channel_id=1, source_target_pairs={{0,3},{1,2},{2,1},{3,0},{4,7},{5,6},{6,5},{7,4},{8,11},{9,10},{10,... | collective-permute-start | bytes 522248 | tf_op jit(solution)/shard_map/ppermute | solution.py:12
  9.3 11.0 %collective-permute-start.4 = (bf16[128,512]{1,0:T(8,128)(2,1)S(1)}, bf16[128,512]{1,0:T(8,128)(2,1)S(1)}, u32[]{:S(2)}, u32[]{:S(2)}) collective-permute-start(bf16[128,512]{1,0:T(8,128)(2,1)S(1)} %slice.265), channel_id=1, source_target_pairs={{0,1},{1,0},{2,3},{3,2},{4,5},{5,4},{6,7},{7,6},{8,9},{9,8},{10,11... | collective-permute-start | bytes 393224 | tf_op jit(solution)/shard_map/ppermute | solution.py:12
  10.0 14.6 %collective-permute-start.1 = (bf16[136,640]{1,0:T(8,128)(2,1)S(1)}, bf16[136,640]{1,0:T(8,128)(2,1)S(1)}, u32[]{:S(2)}, u32[]{:S(2)}) collective-permute-start(bf16[136,640]{1,0:T(8,128)(2,1)S(1)} %get-tuple-element.121), channel_id=1, source_target_pairs={{0,2},{1,3},{2,0},{3,1},{4,6},{5,7},{6,4},{7,5},{8,10},{9,11},{10,... | collective-permute-start | bytes 522248 | tf_op jit(solution)/shard_map/ppermute | solution.py:12
  20.3 4.7 %copy-start.5 = (bf16[128,512]{1,0:T(8,128)(2,1)}, bf16[128,512]{1,0:T(8,128)(2,1)S(1)}, u32[]{:S(2)}) copy-start(bf16[128,512]{1,0:T(8,128)(2,1)S(1)} %collective-permute-done.4) | copy-start | bytes 393220
  20.3 13.2 %collective-permute-start.6 = (bf16[128,1024]{1,0:T(8,128)(2,1)S(1)}, bf16[128,1024]{1,0:T(8,128)(2,1)S(1)}, u32[]{:S(2)}, u32[]{:S(2)}) collective-permute-start(bf16[128,1024]{1,0:T(8,128)(2,1)S(1)} %slice.266), channel_id=1, source_target_pairs={{0,1},{1,0},{2,3},{3,2},{4,5},{5,4},{6,7},{7,6},{8,9},{9,8},{10,11... | collective-permute-start | bytes 786440 | tf_op jit(solution)/shard_map/ppermute | solution.py:12
  25.2 1.3 %copy-start.3 = (bf16[256,256]{1,0:T(8,128)(2,1)}, bf16[256,256]{1,0:T(8,128)(2,1)S(1)}, u32[]{:S(2)}) copy-start(bf16[256,256]{1,0:T(8,128)(2,1)S(1)} %maximum_select_fusion.8) | copy-start | bytes 393220
  25.2 1.3 %copy-start.7 = (bf16[128,256]{0,1:T(8,128)(2,1)}, bf16[128,256]{0,1:T(8,128)(2,1)S(1)}, u32[]{:S(2)}) copy-start(bf16[128,256]{0,1:T(8,128)(2,1)S(1)} %fusion.36) | copy-start | bytes 196612
  25.6 7.8 %collective-permute-start.5 = (bf16[128,512]{1,0:T(8,128)(2,1)S(1)}, bf16[128,512]{1,0:T(8,128)(2,1)S(1)}, u32[]{:S(2)}, u32[]{:S(2)}) collective-permute-start(bf16[128,512]{1,0:T(8,128)(2,1)S(1)} %get-tuple-element.143), channel_id=1, source_target_pairs={{0,2},{1,3},{2,0},{3,1},{4,6},{5,7},{6,4},{7,5},{8,10},{9,11},{10,... | collective-permute-start | bytes 393224 | tf_op jit(solution)/shard_map/ppermute | solution.py:12
  34.0 1.6 %collective-permute-start.7 = (bf16[128,1024]{0,1:T(8,128)(2,1)S(1)}, bf16[128,1024]{0,1:T(8,128)(2,1)S(1)}, u32[]{:S(2)}, u32[]{:S(2)}) collective-permute-start(bf16[128,1024]{0,1:T(8,128)(2,1)S(1)} %get-tuple-element.145), channel_id=1, source_target_pairs={{0,4},{4,0},{8,12},{12,8},{16,20},{20,16},{24,28},{28,24},{1,5},{5... | collective-permute-start | bytes 786440 | tf_op jit(solution)/shard_map/ppermute | solution.py:12
  34.0 10.1 %collective-permute-start.9 = (bf16[128,1024]{1,0:T(8,128)(2,1)S(1)}, bf16[128,1024]{1,0:T(8,128)(2,1)S(1)}, u32[]{:S(2)}, u32[]{:S(2)}) collective-permute-start(bf16[128,1024]{1,0:T(8,128)(2,1)S(1)} %slice.269), channel_id=1, source_target_pairs={{0,1},{1,0},{2,3},{3,2},{4,5},{5,4},{6,7},{7,6},{8,9},{9,8},{10,11... | collective-permute-start | bytes 786440 | tf_op jit(solution)/shard_map/ppermute | solution.py:12
  36.0 5.9 %collective-permute-start.8 = (bf16[128,256]{0,1:T(8,128)(2,1)S(1)}, bf16[128,256]{0,1:T(8,128)(2,1)S(1)}, u32[]{:S(2)}, u32[]{:S(2)}) collective-permute-start(bf16[128,256]{0,1:T(8,128)(2,1)S(1)} %fusion.38), channel_id=1, source_target_pairs={{0,2},{1,3},{2,0},{3,1},{4,6},{5,7},{6,4},{7,5},{8,10},{9,11},{10,... | collective-permute-start | bytes 196616 | tf_op jit(solution)/shard_map/ppermute | solution.py:12
  37.5 15.1 %collective-permute-start.12 = (bf16[256,1024]{0,1:T(8,128)(2,1)S(1)}, bf16[256,1024]{0,1:T(8,128)(2,1)S(1)}, u32[]{:S(2)}, u32[]{:S(2)}) collective-permute-start(bf16[256,1024]{0,1:T(8,128)(2,1)S(1)} %pad_maximum_fusion), channel_id=1, source_target_pairs={{0,8},{4,12},{8,0},{12,4},{16,24},{20,28},{24,16},{28,20},{1,9},{5... | collective-permute-start | bytes 1572872 | tf_op jit(solution)/shard_map/ppermute | solution.py:12
  39.0 16.0 %collective-permute-start.17 = (bf16[16,512]{1,0:T(8,128)(2,1)S(1)}, bf16[16,512]{1,0:T(8,128)(2,1)S(1)}, u32[]{:S(2)}, u32[]{:S(2)}) collective-permute-start(bf16[16,512]{1,0:T(8,128)(2,1)S(1)} %pad.13), channel_id=1, source_target_pairs={{0,8},{4,12},{8,0},{12,4},{16,24},{20,28},{24,16},{28,20},{1,9},{5... | collective-permute-start | bytes 49160 | tf_op jit(solution)/shard_map/ppermute | solution.py:12
  44.2 1.3 %collective-permute-start.10 = (bf16[128,512]{0,1:T(8,128)(2,1)S(1)}, bf16[128,512]{0,1:T(8,128)(2,1)S(1)}, u32[]{:S(2)}, u32[]{:S(2)}) collective-permute-start(bf16[128,512]{0,1:T(8,128)(2,1)S(1)} %maximum_select_fusion.12), channel_id=1, source_target_pairs={{0,4},{4,0},{8,12},{12,8},{16,20},{20,16},{24,28},{28,24},{1,5},{5... | collective-permute-start | bytes 393224 | tf_op jit(solution)/shard_map/ppermute | solution.py:12
  46.0 6.5 %collective-permute-start.11 = (bf16[128,256]{0,1:T(8,128)(2,1)S(1)}, bf16[128,256]{0,1:T(8,128)(2,1)S(1)}, u32[]{:S(2)}, u32[]{:S(2)}) collective-permute-start(bf16[128,256]{0,1:T(8,128)(2,1)S(1)} %fusion.40), channel_id=1, source_target_pairs={{0,2},{1,3},{2,0},{3,1},{4,6},{5,7},{6,4},{7,5},{8,10},{9,11},{10,... | collective-permute-start | bytes 196616 | tf_op jit(solution)/shard_map/ppermute | solution.py:12
  53.4 5.0 %collective-permute-start.13 = (bf16[128,512]{0,1:T(8,128)(2,1)S(1)}, bf16[128,512]{0,1:T(8,128)(2,1)S(1)}, u32[]{:S(2)}, u32[]{:S(2)}) collective-permute-start(bf16[128,512]{0,1:T(8,128)(2,1)S(1)} %pad_maximum_fusion.23), channel_id=1, source_target_pairs={{0,8},{4,12},{8,0},{12,4},{16,24},{20,28},{24,16},{28,20},{1,9},{5... | collective-permute-start | bytes 393224 | tf_op jit(solution)/shard_map/ppermute | solution.py:12
  58.6 5.0 %collective-permute-start.14 = (bf16[128,512]{0,1:T(8,128)(2,1)S(1)}, bf16[128,512]{0,1:T(8,128)(2,1)S(1)}, u32[]{:S(2)}, u32[]{:S(2)}) collective-permute-start(bf16[128,512]{0,1:T(8,128)(2,1)S(1)} %fusion.17), channel_id=1, source_target_pairs={{0,1},{1,0},{2,3},{3,2},{4,5},{5,4},{6,7},{7,6},{8,9},{9,8},{10,11... | collective-permute-start | bytes 393224 | tf_op jit(solution)/shard_map/ppermute | solution.py:12
  64.5 1.4 %collective-permute-start.15 = (bf16[128,512]{1,0:T(8,128)(2,1)S(1)}, bf16[128,512]{1,0:T(8,128)(2,1)S(1)}, u32[]{:S(2)}, u32[]{:S(2)}) collective-permute-start(bf16[128,512]{1,0:T(8,128)(2,1)S(1)} %pad_maximum_fusion.24), channel_id=1, source_target_pairs={{0,4},{4,0},{8,12},{12,8},{16,20},{20,16},{24,28},{28,24},{1,5},{5... | collective-permute-start | bytes 393224 | tf_op jit(solution)/shard_map/ppermute | solution.py:12
  66.8 5.6 %collective-permute-start.16 = (bf16[128,512]{0,1:T(8,128)(2,1)S(1)}, bf16[128,512]{0,1:T(8,128)(2,1)S(1)}, u32[]{:S(2)}, u32[]{:S(2)}) collective-permute-start(bf16[128,512]{0,1:T(8,128)(2,1)S(1)} %pad_maximum_fusion.25), channel_id=1, source_target_pairs={{0,1},{1,0},{2,3},{3,2},{4,5},{5,4},{6,7},{7,6},{8,9},{9,8},{10,11... | collective-permute-start | bytes 393224 | tf_op jit(solution)/shard_map/ppermute | solution.py:12
  74.2 5.7 %collective-permute-start.18 = (bf16[128,256]{0,1:T(8,128)(2,1)S(1)}, bf16[128,256]{0,1:T(8,128)(2,1)S(1)}, u32[]{:S(2)}, u32[]{:S(2)}) collective-permute-start(bf16[128,256]{0,1:T(8,128)(2,1)S(1)} %fusion.33), channel_id=1, source_target_pairs={{0,2},{1,3},{2,0},{3,1},{4,6},{5,7},{6,4},{7,5},{8,10},{9,11},{10,... | collective-permute-start | bytes 196616 | tf_op jit(solution)/shard_map/ppermute | solution.py:12
  80.2 4.0 %collective-permute-start.19 = (bf16[128,128]{0,1:T(8,128)(2,1)S(1)}, bf16[128,128]{0,1:T(8,128)(2,1)S(1)}, u32[]{:S(2)}, u32[]{:S(2)}) collective-permute-start(bf16[128,128]{0,1:T(8,128)(2,1)S(1)} %pad_maximum_fusion.27), channel_id=1, source_target_pairs={{0,8},{4,12},{8,0},{12,4},{16,24},{20,28},{24,16},{28,20},{1,9},{5... | collective-permute-start | bytes 98312 | tf_op jit(solution)/shard_map/ppermute | solution.py:12
  81.7 5.6 %collective-permute-start.21 = (bf16[128,256]{0,1:T(8,128)(2,1)S(1)}, bf16[128,256]{0,1:T(8,128)(2,1)S(1)}, u32[]{:S(2)}, u32[]{:S(2)}) collective-permute-start(bf16[128,256]{0,1:T(8,128)(2,1)S(1)} %constant_dynamic-slice_fusion.3), channel_id=1, source_target_pairs={{0,2},{1,3},{2,0},{3,1},{4,6},{5,7},{6,4},{7,5},{8,10},{9,11},{10,... | collective-permute-start | bytes 196616 | tf_op jit(solution)/shard_map/ppermute | solution.py:12
  85.0 2.4 %collective-permute-start.20 = (bf16[128,512]{0,1:T(8,128)(2,1)S(1)}, bf16[128,512]{0,1:T(8,128)(2,1)S(1)}, u32[]{:S(2)}, u32[]{:S(2)}) collective-permute-start(bf16[128,512]{0,1:T(8,128)(2,1)S(1)} %dynamic-slice_convert_fusion.2), channel_id=1, source_target_pairs={{0,4},{4,0},{8,12},{12,8},{16,20},{20,16},{24,28},{28,24},{1,5},{5... | collective-permute-start | bytes 393224 | tf_op jit(solution)/shard_map/ppermute | solution.py:12
  87.6 4.0 %collective-permute-start.23 = (bf16[128,128]{0,1:T(8,128)(2,1)S(1)}, bf16[128,128]{0,1:T(8,128)(2,1)S(1)}, u32[]{:S(2)}, u32[]{:S(2)}) collective-permute-start(bf16[128,128]{0,1:T(8,128)(2,1)S(1)} %pad_maximum_fusion.28), channel_id=1, source_target_pairs={{0,8},{4,12},{8,0},{12,4},{16,24},{20,28},{24,16},{28,20},{1,9},{5... | collective-permute-start | bytes 98312 | tf_op jit(solution)/shard_map/ppermute | solution.py:12
  88.2 6.2 %collective-permute-start.22 = (bf16[128,256]{0,1:T(8,128)(2,1)S(1)}, bf16[128,256]{0,1:T(8,128)(2,1)S(1)}, u32[]{:S(2)}, u32[]{:S(2)}) collective-permute-start(bf16[128,256]{0,1:T(8,128)(2,1)S(1)} %dynamic-slice_convert_fusion.3), channel_id=1, source_target_pairs={{0,2},{1,3},{2,0},{3,1},{4,6},{5,7},{6,4},{7,5},{8,10},{9,11},{10,... | collective-permute-start | bytes 196616 | tf_op jit(solution)/shard_map/ppermute | solution.py:12
  95.0 11.6 %copy-start.4 = (bf16[256,256]{1,0:T(8,128)(2,1)S(1)}, bf16[256,256]{1,0:T(8,128)(2,1)}, u32[]{:S(2)}) copy-start(bf16[256,256]{1,0:T(8,128)(2,1)} %copy-done.3) | copy-start | bytes 393220
  95.0 11.6 %copy-start.8 = (bf16[128,256]{0,1:T(8,128)(2,1)S(1)}, bf16[128,256]{0,1:T(8,128)(2,1)}, u32[]{:S(2)}) copy-start(bf16[128,256]{0,1:T(8,128)(2,1)} %copy-done.7) | copy-start | bytes 196612
  95.1 1.4 %collective-permute-start.24 = (bf16[128,512]{0,1:T(8,128)(2,1)S(1)}, bf16[128,512]{0,1:T(8,128)(2,1)S(1)}, u32[]{:S(2)}, u32[]{:S(2)}) collective-permute-start(bf16[128,512]{0,1:T(8,128)(2,1)S(1)} %dynamic-slice_convert_fusion.1), channel_id=1, source_target_pairs={{0,4},{4,0},{8,12},{12,8},{16,20},{20,16},{24,28},{28,24},{1,5},{5... | collective-permute-start | bytes 393224 | tf_op jit(solution)/shard_map/ppermute | solution.py:12
  96.5 8.7 %collective-permute-start.25 = (bf16[128,512]{0,1:T(8,128)(2,1)S(1)}, bf16[128,512]{0,1:T(8,128)(2,1)S(1)}, u32[]{:S(2)}, u32[]{:S(2)}) collective-permute-start(bf16[128,512]{0,1:T(8,128)(2,1)S(1)} %fusion.31), channel_id=1, source_target_pairs={{0,2},{1,3},{2,0},{3,1},{4,6},{5,7},{6,4},{7,5},{8,10},{9,11},{10,... | collective-permute-start | bytes 393224 | tf_op jit(solution)/shard_map/ppermute | solution.py:12
  105.2 1.4 %collective-permute-start.26 = (bf16[128,512]{0,1:T(8,128)(2,1)S(1)}, bf16[128,512]{0,1:T(8,128)(2,1)S(1)}, u32[]{:S(2)}, u32[]{:S(2)}) collective-permute-start(bf16[128,512]{0,1:T(8,128)(2,1)S(1)} %add_convert_fusion.1), channel_id=1, source_target_pairs={{0,4},{4,0},{8,12},{12,8},{16,20},{20,16},{24,28},{28,24},{1,5},{5... | collective-permute-start | bytes 393224 | tf_op jit(solution)/shard_map/ppermute | solution.py:12
  105.4 2.3 %copy-start.6 = (bf16[128,512]{1,0:T(8,128)(2,1)S(1)}, bf16[128,512]{1,0:T(8,128)(2,1)}, u32[]{:S(2)}) copy-start(bf16[128,512]{1,0:T(8,128)(2,1)} %copy-done.5) | copy-start | bytes 393220
  108.0 8.3 %collective-permute-start.27 = (bf16[256,128]{0,1:T(8,128)(2,1)S(1)}, bf16[256,128]{0,1:T(8,128)(2,1)S(1)}, u32[]{:S(2)}, u32[]{:S(2)}) collective-permute-start(bf16[256,128]{0,1:T(8,128)(2,1)S(1)} %constant_dynamic-slice_fusion.1), channel_id=1, source_target_pairs={{0,1},{1,0},{2,3},{3,2},{4,5},{5,4},{6,7},{7,6},{8,9},{9,8},{10,11... | collective-permute-start | bytes 196616 | tf_op jit(solution)/shard_map/ppermute | solution.py:12
  108.1 4.8 %collective-permute-start.28 = (bf16[128,128]{0,1:T(8,128)(2,1)S(1)}, bf16[128,128]{0,1:T(8,128)(2,1)S(1)}, u32[]{:S(2)}, u32[]{:S(2)}) collective-permute-start(bf16[128,128]{0,1:T(8,128)(2,1)S(1)} %get-tuple-element.87), channel_id=1, source_target_pairs={{0,1},{1,0},{2,3},{3,2},{4,5},{5,4},{6,7},{7,6},{8,9},{9,8},{10,11... | collective-permute-start | bytes 98312 | tf_op jit(solution)/shard_map/ppermute | solution.py:12
  110.2 5.1 %collective-permute-start.29 = (bf16[128,128]{0,1:T(8,128)(2,1)S(1)}, bf16[128,128]{0,1:T(8,128)(2,1)S(1)}, u32[]{:S(2)}, u32[]{:S(2)}) collective-permute-start(bf16[128,128]{0,1:T(8,128)(2,1)S(1)} %get-tuple-element.86), channel_id=1, source_target_pairs={{0,2},{1,3},{2,0},{3,1},{4,6},{5,7},{6,4},{7,5},{8,10},{9,11},{10,... | collective-permute-start | bytes 98312 | tf_op jit(solution)/shard_map/ppermute | solution.py:12
  110.6 5.7 %collective-permute-start.30 = (bf16[128,128]{0,1:T(8,128)(2,1)S(1)}, bf16[128,128]{0,1:T(8,128)(2,1)S(1)}, u32[]{:S(2)}, u32[]{:S(2)}) collective-permute-start(bf16[128,128]{0,1:T(8,128)(2,1)S(1)} %get-tuple-element.85), channel_id=1, source_target_pairs={{0,3},{1,2},{2,1},{3,0},{4,7},{5,6},{6,5},{7,4},{8,11},{9,10},{10,... | collective-permute-start | bytes 98312 | tf_op jit(solution)/shard_map/ppermute | solution.py:12

commit v6 on v5

--- a/solution.py
+++ b/solution.py
@@ -1,6 +1,7 @@
 import jax
 import jax.numpy as jnp
 from jax import lax
+from jax.experimental.layout import Layout, with_layout_constraint
 from jax.sharding import PartitionSpec as P
 
 LEVELS = 3
@@ -32,6 +33,10 @@
         jnp.concatenate([other, own], axis),
         jnp.concatenate([own, other], axis),
     )
+
+
+def by_rows(array):
+    return with_layout_constraint(array, Layout(major_to_minor=(0, 1)))
 
 
 def after(array, *earlier):
@@ -149,12 +154,20 @@
         half = odd if mask % 2 == 0 else 1 - odd
         columns = [part(rhs[level], half, 2, 1) for level in range(LEVELS)]
         updates = part(update0, (front_id ^ mask) // 2, front_count // 2, 1)
-        return jnp.concatenate([jnp.concatenate([updates, *columns], 1), lists], 0)
+        return by_rows(jnp.concatenate([jnp.concatenate([updates, *columns], 1), lists], 0))
 
     parcels = {0: parcel(0)}
     for mask in sorted(range(1, front_count), key=lambda mask: (mask + 1) % front_count):
         parcels[mask] = traded(parcel(mask), "front", mask)
     parcels = [parcels[mask] for mask in range(front_count)]
+    cores1 = [update1[:, :leaf_rows], update1[:, leaf_rows:]]
+    handed1 = jnp.where(side == 1, cores1[0], cores1[1])
+    block1 = jnp.where(side == 1, cores1[1], cores1[0])
+    block1 = jnp.concatenate([block1, traded(handed1, "leaf", 1)], 0)
+
+    def pair_columns(mask):
+        return part(block1, (front_id ^ mask) // 2, front_count // 2, 1)
+
     inverse0_pair = traded(inverse0, "front", 1)
     cores2 = [
         jnp.concatenate(
@@ -167,7 +180,11 @@
     block2 = jnp.concatenate([block2, traded(handed2, "leaf", 1)], 0)
     wing2 = traded(block2, "leaf", 2)
     inverse1_pair = traded(after(inverse1, inverse0_pair), "front", 1)
+    columns1 = [pair_columns(0)] + [
+        traded(pair_columns(mask), "front", mask) for mask in range(2, front_count, 2)
+    ]
     *parcels, block2, inverse0_pair = together(*parcels, block2, inverse0_pair)
+    parcels = [by_rows(block) for block in parcels]
     update0_columns = in_order([block[:own_rows, : 2 * own_rows] for block in parcels], 0)
 
     def level_rows(blocks, level):
@@ -184,12 +201,20 @@
     solved0_pair = ordered(
         product(rhs0, inverse0, 0, 1), product(rhs0, inverse0_pair, 0, 1), odd, 1
     ).astype(BF16)
-    update1_pair = traded(after(update1, solved0_pair), "front", 1)
     updated0 = forward(solved0_pair, update0_columns)
     parcels = together(*parcels, updated0)[:-1]
     rhs1, rhs2 = level_rows(parcels, 1).T, level_rows(parcels, 2).T
     lists = in_order([block[own_rows : own_rows + 4, :own_rows] for block in parcels], 1)
-    lists_wing = traded(jnp.pad(lists, ((0, 12), (0, 0))), "leaf", 2)[:4]
+    columns1_near = traded(jnp.concatenate(columns1, 0), "front", 1)
+    columns1 = alternated(
+        columns1,
+        [
+            columns1_near[2 * i * own_rows : 2 * (i + 1) * own_rows]
+            for i in range(len(columns1))
+        ],
+    )
+    columns1_side = in_order([block[own_rows:] for block in columns1], 0)
+    columns1 = in_order([block[:own_rows] for block in columns1], 0)
     updated0 = high_sum(updated0).astype(BF16)
     updated0, inverse1_pair = together(updated0, inverse1_pair)
 
@@ -204,11 +229,9 @@
     pivots1 = (pivots1 + traded(pivots1.astype(BF16), "leaf", 1).astype(F32)).astype(BF16)
 
     solved1_pair = pair_forward(pivots1, inverse1, inverse1_pair)
-    solved1 = high_gather(solved1_pair)
-    solved1, update1_pair = together(solved1, update1_pair)
-    solved1 = ordered(solved1, traded(solved1, "leaf", 1), side, 1)
-    updated1_pair = pair_forward(solved1, update1, update1_pair)
-    updated1 = high_gather(updated1_pair)
+    updated1 = forward(solved1_pair, columns1_side).astype(BF16)
+    updated1 = forward(solved1_pair, columns1) + traded(updated1, "leaf", 1).astype(F32)
+    updated1 = high_sum(updated1).astype(BF16)
     updated1, wing2 = together(updated1, wing2)
 
     pivots2 = ordered(rhs2, jnp.zeros_like(rhs2), wing, 1).astype(F32) - forward(updated1, select1)
@@ -233,25 +256,16 @@
         below2 += adjoint((solved2[index] + other.astype(F32)).astype(BF16), block)
     handed2 = stacked(below2[quarter:].astype(BF16))
     below2 = stacked(below2[:quarter])
-    below2 = (below2 + traded(handed2, "front", 1).astype(F32)).astype(BF16)
-
-    def wing_gather(own, other):
-        other = traded(stacked(other.astype(BF16)), "leaf", 2)
-        return ordered(own.astype(BF16), jnp.concatenate(flat(other), 1), wing, 0)
-
-    both2 = jnp.concatenate(flat(below2), 1)
-    fetched1 = jnp.concatenate(
-        [adjoint(both2, select1), adjoint(both2, selector(lists_wing, 1))], 0
-    )
-    fetched1 = high_scatter(fetched1)
-    below2 = high_scatter(after(below2, fetched1))
-    fetched1 = wing_gather(*flat(fetched1))
-    carried1 = pair_adjoint(fetched1, update1, update1_pair)
-    carried1 = side_scatter(carried1)
-    carried1, below2 = together(carried1, below2)
-    low2, high2 = flat(below2)
-    solution2 = wing_gather(jnp.where(wing == 1, high2, low2), jnp.where(wing == 1, low2, high2))
-    carried1, solution2 = together(high_scatter(carried1), solution2)
+    below2 = below2 + traded(handed2, "front", 1).astype(F32)
+    below2 = high_sum(below2).astype(BF16)
+    own2 = flat(below2)
+    other2 = flat(traded(below2, "leaf", 2))
+    below2 = jnp.concatenate(
+        [ordered(own, other, wing, 0) for own, other in zip(own2, other2)], 1
+    )
+
+    fetched1 = adjoint(below2, select1).astype(BF16)
+    carried1 = adjoint(traded(fetched1, "leaf", 1), columns1_side) + adjoint(fetched1, columns1)
     weights1 = (solved1_pair.astype(F32) - carried1).astype(BF16)
     below1 = high_sum(side_scatter(pair_adjoint(weights1, inverse1, inverse1_pair))).astype(BF16)
     below1_all = ordered(below1, traded(below1, "leaf", 1), side, 1)
@@ -259,7 +273,7 @@
     fetched0 = adjoint(below1_all, select0).astype(BF16)
     weights0 = (solved0_pair.astype(F32) - adjoint(fetched0, update0_columns)).astype(BF16)
     below0 = pair_adjoint(weights0, inverse0, inverse0_pair)
-    upper = jnp.concatenate([pair_rows(below1), solution2], 0)
+    upper = jnp.concatenate([pair_rows(below1), pair_rows(part(below2, wing, 2, 1))], 0)
     upper, below0 = together(upper, below0)
     upper_other = traded(part(upper, 1 - odd, 2, 1), "front", 1)
     shares = [

time: 117 us -> 114 us (0.974)
  waiting for transfers between devices: 74.2 us -> 68.1 us
  starting transfers between devices: 27.2 us -> 29.1 us
  other arithmetic: 2.92 us -> 4.57 us
    ppermute x31 -> x28, waiting for transfers between devices: 74.2 us -> 68.1 us  [traded(): lax.ppermute(shard, axis, [(i, i ^ mask) for i in range(lax.axis_size(axi...]
    ppermute x31 -> x28, starting transfers between devices: 27.2 us -> 29.1 us  [traded(): lax.ppermute(shard, axis, [(i, i ^ mask) for i in range(lax.axis_size(axi...]
    concatenate x3 -> x6, other arithmetic: 0.08 us -> 1.25 us  [the longest x1 0.89 us: shards(): block1 = jnp.concatenate([block1, traded(handed1, 'leaf', 1)], 0)]
    dot_general x22 -> x21, matrix products: 7.71 us -> 6.77 us  [product(): lax.dot_general(left, right, (((left_dim,), (right_dim,)), ((), ())), pre...]
  transfers between devices with their start and end apart: 31 -> 28, of which waited for: 23 -> 22; matrix products, arithmetic and copies ran while one was open for 4% -> 5% of each run, Pallas kernels for 0% -> 0%
where the time goes in v6:
time: 114 us
  waiting for transfers between devices  68.1 us (60%)
  starting transfers between devices  29.1 us (26%)
  matrix products  6.77 us (6%)
  other arithmetic  4.57 us (4%)
  local copies, waits for them, and re-layouts  4.56 us (4%)
    ppermute x28, waiting for transfers between devices, traded(): lax.ppermute(shard, axis, [(i, i ^ mask) for i in range(lax.axis_size(axi...  68.1 us
    ppermute x28, starting transfers between devices, traded(): lax.ppermute(shard, axis, [(i, i ^ mask) for i in range(lax.axis_size(axi...  29.1 us
    dot_general x21, matrix products, product(): lax.dot_general(left, right, (((left_dim,), (right_dim,)), ((), ())), pre...  6.77 us
  transfers between devices with their start and end apart: 28, of which 22 were waited for; matrix products, arithmetic and copies ran while one was open for 5% of the time, Pallas kernels for 0%

profile of v6, /device:TPU:0, one launch (start us, length us, event | category | flops | bytes accessed | tf_op | source)
XLA Modules:
  0.0 114.0 jit_solution(10997327114285131858)
XLA Ops:
  0.0 1.2 %copy-done = bf16[128,3584]{1,0:T(8,128)(2,1)S(1)} copy-done((bf16[128,3584]{1,0:T(8,128)(2,1)S(1)}, bf16[128,3584]{1,0:T(8,128)(2,1)}, u32[]{:S(2)}) %copy-start) | copy-done | bytes 917528
  1.3 0.9 slice-done
  2.2 0.3 copy.30
  2.7 0.4 slice-done.2
  3.2 3.1 %collective-permute-start = (bf16[136,640]{1,0:T(8,128)(2,1)S(1)}, bf16[136,640]{1,0:T(8,128)(2,1)S(1)}, u32[]{:S(2)}, u32[]{:S(2)}) collective-permute-start(bf16[136,640]{1,0:T(8,128)(2,1)S(1)} %get-tuple-element.116), channel_id=1, source_target_pairs={{0,1},{1,0},{2,3},{3,2},{4,5},{5,4},{6,7},{7,6},{8,9},{9,8},{10,11... | collective-permute-start | bytes 522248 | tf_op jit(solution)/shard_map/ppermute | solution.py:13
  6.3 2.5 %collective-permute-start.2 = (bf16[136,640]{1,0:T(8,128)(2,1)S(1)}, bf16[136,640]{1,0:T(8,128)(2,1)S(1)}, u32[]{:S(2)}, u32[]{:S(2)}) collective-permute-start(bf16[136,640]{1,0:T(8,128)(2,1)S(1)} %get-tuple-element.115), channel_id=1, source_target_pairs={{0,3},{1,2},{2,1},{3,0},{4,7},{5,6},{6,5},{7,4},{8,11},{9,10},{10,... | collective-permute-start | bytes 522248 | tf_op jit(solution)/shard_map/ppermute | solution.py:13
  9.0 0.7 broadcast_select_fusion.2
  9.8 0.6 collective-permute-start.3
  10.4 1.0 collective-permute-done.8
  11.3 1.8 %collective-permute-start.4 = (bf16[128,512]{1,0:T(8,128)(2,1)S(1)}, bf16[128,512]{1,0:T(8,128)(2,1)S(1)}, u32[]{:S(2)}, u32[]{:S(2)}) collective-permute-start(bf16[128,512]{1,0:T(8,128)(2,1)S(1)} %slice.260), channel_id=1, source_target_pairs={{0,1},{1,0},{2,3},{3,2},{4,5},{5,4},{6,7},{7,6},{8,9},{9,8},{10,11... | collective-permute-start | bytes 393224 | tf_op jit(solution)/shard_map/ppermute | solution.py:13
  13.1 0.9 fusion.33
  14.1 6.2 %collective-permute-done.4 = bf16[128,512]{1,0:T(8,128)(2,1)S(1)} collective-permute-done((bf16[128,512]{1,0:T(8,128)(2,1)S(1)}, bf16[128,512]{1,0:T(8,128)(2,1)S(1)}, u32[]{:S(2)}, u32[]{:S(2)}) %collective-permute-start.4) | collective-permute-done | bytes 131104 | tf_op jit(solution)/shard_map/ppermute | solution.py:13
  20.3 3.5 %collective-permute-start.9 = (bf16[256,256]{1,0:T(8,128)(2,1)S(1)}, bf16[256,256]{1,0:T(8,128)(2,1)S(1)}, u32[]{:S(2)}, u32[]{:S(2)}) collective-permute-start(bf16[256,256]{1,0:T(8,128)(2,1)S(1)} %get-tuple-element.78), channel_id=1, source_target_pairs={{0,2},{1,3},{2,0},{3,1},{4,6},{5,7},{6,4},{7,5},{8,10},{9,11},{10,... | collective-permute-start | bytes 393224 | tf_op jit(solution)/shard_map/ppermute | solution.py:13
  23.9 2.4 %collective-permute-done.1 = bf16[136,640]{1,0:T(8,128)(2,1)S(1)} collective-permute-done((bf16[136,640]{1,0:T(8,128)(2,1)S(1)}, bf16[136,640]{1,0:T(8,128)(2,1)S(1)}, u32[]{:S(2)}, u32[]{:S(2)}) %collective-permute-start.1) | collective-permute-done | bytes 174112 | tf_op jit(solution)/shard_map/ppermute | solution.py:13
  26.9 0.2 fusion.107
  27.2 0.3 copy-done.2
  27.6 1.5 %collective-permute-start.13 = (bf16[256,1024]{0,1:T(8,128)(2,1)S(1)}, bf16[256,1024]{0,1:T(8,128)(2,1)S(1)}, u32[]{:S(2)}, u32[]{:S(2)}) collective-permute-start(bf16[256,1024]{0,1:T(8,128)(2,1)S(1)} %pad_maximum_fusion), channel_id=1, source_target_pairs={{0,8},{4,12},{8,0},{12,4},{16,24},{20,28},{24,16},{28,20},{1,9},{5... | collective-permute-start | bytes 1572872 | tf_op jit(solution)/shard_map/ppermute | solution.py:13
  29.1 0.8 collective-permute-done.9
  29.9 0.3 collective-permute-start.10
  30.2 3.3 %collective-permute-start.5 = (bf16[128,512]{1,0:T(8,128)(2,1)S(1)}, bf16[128,512]{1,0:T(8,128)(2,1)S(1)}, u32[]{:S(2)}, u32[]{:S(2)}) collective-permute-start(bf16[128,512]{1,0:T(8,128)(2,1)S(1)} %get-tuple-element.129), channel_id=1, source_target_pairs={{0,2},{1,3},{2,0},{3,1},{4,6},{5,7},{6,4},{7,5},{8,10},{9,11},{10,... | collective-permute-start | bytes 393224 | tf_op jit(solution)/shard_map/ppermute | solution.py:13
  33.6 6.2 %collective-permute-done.5 = bf16[128,512]{1,0:T(8,128)(2,1)S(1)} collective-permute-done((bf16[128,512]{1,0:T(8,128)(2,1)S(1)}, bf16[128,512]{1,0:T(8,128)(2,1)S(1)}, u32[]{:S(2)}, u32[]{:S(2)}) %collective-permute-start.5) | collective-permute-done | bytes 131104 | tf_op jit(solution)/shard_map/ppermute | solution.py:13
  39.8 0.5 fusion.108
  40.4 1.0 collective-permute-done.10
  41.6 0.4 collective-permute-done.7
  41.9 0.2 fusion.87
  42.2 0.2 fusion.86
  42.4 0.2 convolution_convert_fusion
  43.0 1.1 collective-permute-done.11
  44.1 0.2 fusion.31
  44.3 3.4 %collective-permute-start.12 = (bf16[128,512]{1,0:T(8,128)(2,1)S(1)}, bf16[128,512]{1,0:T(8,128)(2,1)S(1)}, u32[]{:S(2)}, u32[]{:S(2)}) collective-permute-start(bf16[128,512]{1,0:T(8,128)(2,1)S(1)} %get-tuple-element.133), channel_id=1, source_target_pairs={{0,2},{1,3},{2,0},{3,1},{4,6},{5,7},{6,4},{7,5},{8,10},{9,11},{10,... | collective-permute-start | bytes 393224 | tf_op jit(solution)/shard_map/ppermute | solution.py:13
  47.8 6.6 %collective-permute-done.12 = bf16[128,512]{1,0:T(8,128)(2,1)S(1)} collective-permute-done((bf16[128,512]{1,0:T(8,128)(2,1)S(1)}, bf16[128,512]{1,0:T(8,128)(2,1)S(1)}, u32[]{:S(2)}, u32[]{:S(2)}) %collective-permute-start.12) | collective-permute-done | bytes 131104 | tf_op jit(solution)/shard_map/ppermute | solution.py:13
  54.4 0.5 fusion.5
  55.2 1.6 %collective-permute-start.14 = (bf16[128,512]{0,1:T(8,128)(2,1)S(1)}, bf16[128,512]{0,1:T(8,128)(2,1)S(1)}, u32[]{:S(2)}, u32[]{:S(2)}) collective-permute-start(bf16[128,512]{0,1:T(8,128)(2,1)S(1)} %pad_maximum_fusion.23), channel_id=1, source_target_pairs={{0,8},{4,12},{8,0},{12,4},{16,24},{20,28},{24,16},{28,20},{1,9},{5... | collective-permute-start | bytes 393224 | tf_op jit(solution)/shard_map/ppermute | solution.py:13
  57.0 3.3 %collective-permute-done.14 = bf16[128,512]{0,1:T(8,128)(2,1)S(1)} collective-permute-done((bf16[128,512]{0,1:T(8,128)(2,1)S(1)}, bf16[128,512]{0,1:T(8,128)(2,1)S(1)}, u32[]{:S(2)}, u32[]{:S(2)}) %collective-permute-start.14) | collective-permute-done | bytes 131104 | tf_op jit(solution)/shard_map/ppermute | solution.py:13
  60.7 4.8 %collective-permute-done.15 = bf16[128,512]{0,1:T(8,128)(2,1)S(1)} collective-permute-done((bf16[128,512]{0,1:T(8,128)(2,1)S(1)}, bf16[128,512]{0,1:T(8,128)(2,1)S(1)}, u32[]{:S(2)}, u32[]{:S(2)}) %collective-permute-start.15) | collective-permute-done | bytes 131104 | tf_op jit(solution)/shard_map/ppermute | solution.py:13
  65.6 0.4 fusion.110
  66.0 0.4 fusion.109
  66.5 1.3 %collective-permute-done.16 = bf16[128,512]{1,0:T(8,128)(2,1)S(1)} collective-permute-done((bf16[128,512]{1,0:T(8,128)(2,1)S(1)}, bf16[128,512]{1,0:T(8,128)(2,1)S(1)}, u32[]{:S(2)}, u32[]{:S(2)}) %collective-permute-start.16) | collective-permute-done | bytes 131104 | tf_op jit(solution)/shard_map/ppermute | solution.py:13
  67.9 0.3 fusion.42
  68.1 0.3 fusion.111
  68.8 5.5 %collective-permute-done.17 = bf16[128,512]{0,1:T(8,128)(2,1)S(1)} collective-permute-done((bf16[128,512]{0,1:T(8,128)(2,1)S(1)}, bf16[128,512]{0,1:T(8,128)(2,1)S(1)}, u32[]{:S(2)}, u32[]{:S(2)}) %collective-permute-start.17) | collective-permute-done | bytes 131104 | tf_op jit(solution)/shard_map/ppermute | solution.py:13
  74.6 8.4 %collective-permute-done.18 = bf16[128,512]{0,1:T(8,128)(2,1)S(1)} collective-permute-done((bf16[128,512]{0,1:T(8,128)(2,1)S(1)}, bf16[128,512]{0,1:T(8,128)(2,1)S(1)}, u32[]{:S(2)}, u32[]{:S(2)}) %collective-permute-start.18) | collective-permute-done | bytes 131104 | tf_op jit(solution)/shard_map/ppermute | solution.py:13
  83.1 1.6 %collective-permute-start.19 = (bf16[128,512]{0,1:T(8,128)(2,1)S(1)}, bf16[128,512]{0,1:T(8,128)(2,1)S(1)}, u32[]{:S(2)}, u32[]{:S(2)}) collective-permute-start(bf16[128,512]{0,1:T(8,128)(2,1)S(1)} %add_convert_fusion.2), channel_id=1, source_target_pairs={{0,8},{4,12},{8,0},{12,4},{16,24},{20,28},{24,16},{28,20},{1,9},{5... | collective-permute-start | bytes 393224 | tf_op jit(solution)/shard_map/ppermute | solution.py:13
  84.8 3.8 %collective-permute-done.19 = bf16[128,512]{0,1:T(8,128)(2,1)S(1)} collective-permute-done((bf16[128,512]{0,1:T(8,128)(2,1)S(1)}, bf16[128,512]{0,1:T(8,128)(2,1)S(1)}, u32[]{:S(2)}, u32[]{:S(2)}) %collective-permute-start.19) | collective-permute-done | bytes 131104 | tf_op jit(solution)/shard_map/ppermute | solution.py:13
  89.0 0.5 fusion.7
  89.6 0.3 fusion.51
  89.9 1.1 collective-permute-done.20
  90.9 0.3 fusion.11
  91.2 0.3 fusion.57
  91.5 0.3 convolution_add_fusion
  91.8 0.2 collective-permute-start.21
  92.0 1.2 %collective-permute-done.21 = bf16[128,512]{0,1:T(8,128)(2,1)S(1)} collective-permute-done((bf16[128,512]{0,1:T(8,128)(2,1)S(1)}, bf16[128,512]{0,1:T(8,128)(2,1)S(1)}, u32[]{:S(2)}, u32[]{:S(2)}) %collective-permute-start.21) | collective-permute-done | bytes 131104 | tf_op jit(solution)/shard_map/ppermute | solution.py:13
  93.4 0.3 fusion.43
  93.7 7.5 %collective-permute-done.22 = bf16[128,512]{0,1:T(8,128)(2,1)S(1)} collective-permute-done((bf16[128,512]{0,1:T(8,128)(2,1)S(1)}, bf16[128,512]{0,1:T(8,128)(2,1)S(1)}, u32[]{:S(2)}, u32[]{:S(2)}) %collective-permute-start.22) | collective-permute-done | bytes 131104 | tf_op jit(solution)/shard_map/ppermute | solution.py:13
  101.4 1.3 %collective-permute-done.23 = bf16[128,512]{0,1:T(8,128)(2,1)S(1)} collective-permute-done((bf16[128,512]{0,1:T(8,128)(2,1)S(1)}, bf16[128,512]{0,1:T(8,128)(2,1)S(1)}, u32[]{:S(2)}, u32[]{:S(2)}) %collective-permute-start.23) | collective-permute-done | bytes 131104 | tf_op jit(solution)/shard_map/ppermute | solution.py:13
  102.7 0.8 fusion.12
  103.5 0.2 fusion.54
  103.7 0.2 convolution_add_fusion.2
  104.1 2.1 %collective-permute-start.25 = (bf16[128,128]{0,1:T(8,128)(2,1)S(1)}, bf16[128,128]{0,1:T(8,128)(2,1)S(1)}, u32[]{:S(2)}, u32[]{:S(2)}) collective-permute-start(bf16[128,128]{0,1:T(8,128)(2,1)S(1)} %get-tuple-element.69), channel_id=1, source_target_pairs={{0,1},{1,0},{2,3},{3,2},{4,5},{5,4},{6,7},{7,6},{8,9},{9,8},{10,11... | collective-permute-start | bytes 98312 | tf_op jit(solution)/shard_map/ppermute | solution.py:13
  106.2 1.2 %collective-permute-start.26 = (bf16[128,128]{0,1:T(8,128)(2,1)S(1)}, bf16[128,128]{0,1:T(8,128)(2,1)S(1)}, u32[]{:S(2)}, u32[]{:S(2)}) collective-permute-start(bf16[128,128]{0,1:T(8,128)(2,1)S(1)} %get-tuple-element.68), channel_id=1, source_target_pairs={{0,2},{1,3},{2,0},{3,1},{4,6},{5,7},{6,4},{7,5},{8,10},{9,11},{10,... | collective-permute-start | bytes 98312 | tf_op jit(solution)/shard_map/ppermute | solution.py:13
  107.4 1.4 %collective-permute-start.27 = (bf16[128,128]{0,1:T(8,128)(2,1)S(1)}, bf16[128,128]{0,1:T(8,128)(2,1)S(1)}, u32[]{:S(2)}, u32[]{:S(2)}) collective-permute-start(bf16[128,128]{0,1:T(8,128)(2,1)S(1)} %get-tuple-element.67), channel_id=1, source_target_pairs={{0,3},{1,2},{2,1},{3,0},{4,7},{5,6},{6,5},{7,4},{8,11},{9,10},{10,... | collective-permute-start | bytes 98312 | tf_op jit(solution)/shard_map/ppermute | solution.py:13
  108.9 3.1 %collective-permute-done.26 = bf16[128,128]{0,1:T(8,128)(2,1)S(1)} collective-permute-done((bf16[128,128]{0,1:T(8,128)(2,1)S(1)}, bf16[128,128]{0,1:T(8,128)(2,1)S(1)}, u32[]{:S(2)}, u32[]{:S(2)}) %collective-permute-start.26) | collective-permute-done | bytes 32800 | tf_op jit(solution)/shard_map/ppermute | solution.py:13
  112.0 1.1 collective-permute-done.27
  113.2 0.8 pad_maximum_fusion.1
  (129 shorter events, 5.0 us)
Async XLA Ops:
  0.0 1.2 %copy-start = (bf16[128,3584]{1,0:T(8,128)(2,1)S(1)}, bf16[128,3584]{1,0:T(8,128)(2,1)}, u32[]{:S(2)}) copy-start(bf16[128,3584]{1,0:T(8,128)(2,1)} %param.6) | copy-start | bytes 2752516
  1.2 1.0 slice-start
  1.2 1.3 %copy-start.1 = (bf16[3,128,256]{2,1,0:T(8,128)(2,1)S(1)}, bf16[3,128,256]{2,1,0:T(8,128)(2,1)}, u32[]{:S(2)}) copy-start(bf16[3,128,256]{2,1,0:T(8,128)(2,1)} %param.5) | copy-start | bytes 589828
  1.2 1.3 %copy-start.8 = (s32[2,128]{1,0:T(2,128)S(1)}, s32[2,128]{1,0:T(2,128)}, u32[]{:S(2)}) copy-start(s32[2,128]{1,0:T(2,128)} %param.9) | copy-start | bytes 3076
  1.3 1.3 %copy-start.9 = (s32[2,128,1]{1,2,0:T(1,128)S(1)}, s32[2,128,1]{1,2,0:T(1,128)}, u32[]{:S(2)}) copy-start(s32[2,128,1]{1,2,0:T(1,128)} %param.8) | copy-start | bytes 3076
  2.2 0.9 slice-start.2
  2.7 6.3 %slice-start.1 = ((bf16[128,1536]{1,0:T(8,128)(2,1)}), bf16[128,1024]{1,0:T(8,128)(2,1)S(1)}, s32[]{:S(2)}) async-start(bf16[128,1536]{1,0:T(8,128)(2,1)} %param.7), calls=%async_computation.1 | async-start | bytes 524288 | tf_op jit(solution)/shard_map/slice | solution.py:145
  3.2 20.7 %collective-permute-start = (bf16[136,640]{1,0:T(8,128)(2,1)S(1)}, bf16[136,640]{1,0:T(8,128)(2,1)S(1)}, u32[]{:S(2)}, u32[]{:S(2)}) collective-permute-start(bf16[136,640]{1,0:T(8,128)(2,1)S(1)} %get-tuple-element.116), channel_id=1, source_target_pairs={{0,1},{1,0},{2,3},{3,2},{4,5},{5,4},{6,7},{7,6},{8,9},{9,8},{10,11... | collective-permute-start | bytes 522248 | tf_op jit(solution)/shard_map/ppermute | solution.py:13
  6.3 17.6 %collective-permute-start.2 = (bf16[136,640]{1,0:T(8,128)(2,1)S(1)}, bf16[136,640]{1,0:T(8,128)(2,1)S(1)}, u32[]{:S(2)}, u32[]{:S(2)}) collective-permute-start(bf16[136,640]{1,0:T(8,128)(2,1)S(1)} %get-tuple-element.115), channel_id=1, source_target_pairs={{0,3},{1,2},{2,1},{3,0},{4,7},{5,6},{6,5},{7,4},{8,11},{9,10},{10,... | collective-permute-start | bytes 522248 | tf_op jit(solution)/shard_map/ppermute | solution.py:13
  8.8 17.5 %collective-permute-start.1 = (bf16[136,640]{1,0:T(8,128)(2,1)S(1)}, bf16[136,640]{1,0:T(8,128)(2,1)S(1)}, u32[]{:S(2)}, u32[]{:S(2)}) collective-permute-start(bf16[136,640]{1,0:T(8,128)(2,1)S(1)} %get-tuple-element.117), channel_id=1, source_target_pairs={{0,2},{1,3},{2,0},{3,1},{4,6},{5,7},{6,4},{7,5},{8,10},{9,11},{10,... | collective-permute-start | bytes 522248 | tf_op jit(solution)/shard_map/ppermute | solution.py:13
  9.7 1.7 %collective-permute-start.8 = (bf16[128,512]{1,0:T(8,128)(2,1)}, bf16[128,512]{1,0:T(8,128)(2,1)}, u32[]{:S(2)}, u32[]{:S(2)}) collective-permute-start(bf16[128,512]{1,0:T(8,128)(2,1)} %get-tuple-element.80), channel_id=1, source_target_pairs={{0,4},{4,0},{8,12},{12,8},{16,20},{20,16},{24,28},{28,24},{1,5},{5... | collective-permute-start | bytes 393224 | tf_op jit(solution)/shard_map/ppermute | solution.py:13
  9.8 14.0 %collective-permute-start.3 = (bf16[128,1024]{0,1:T(8,128)(2,1)S(1)}, bf16[128,1024]{0,1:T(8,128)(2,1)S(1)}, u32[]{:S(2)}, u32[]{:S(2)}) collective-permute-start(bf16[128,1024]{0,1:T(8,128)(2,1)S(1)} %get-tuple-element.62), channel_id=1, source_target_pairs={{0,4},{4,0},{8,12},{12,8},{16,20},{20,16},{24,28},{28,24},{1,5},{5... | collective-permute-start | bytes 786440 | tf_op jit(solution)/shard_map/ppermute | solution.py:13
  11.3 8.9 %collective-permute-start.4 = (bf16[128,512]{1,0:T(8,128)(2,1)S(1)}, bf16[128,512]{1,0:T(8,128)(2,1)S(1)}, u32[]{:S(2)}, u32[]{:S(2)}) collective-permute-start(bf16[128,512]{1,0:T(8,128)(2,1)S(1)} %slice.260), channel_id=1, source_target_pairs={{0,1},{1,0},{2,3},{3,2},{4,5},{5,4},{6,7},{7,6},{8,9},{9,8},{10,11... | collective-permute-start | bytes 393224 | tf_op jit(solution)/shard_map/ppermute | solution.py:13
  20.3 6.4 %copy-start.6 = (bf16[128,512]{1,0:T(8,128)(2,1)}, bf16[128,512]{1,0:T(8,128)(2,1)S(1)}, u32[]{:S(2)}) copy-start(bf16[128,512]{1,0:T(8,128)(2,1)S(1)} %collective-permute-done.4) | copy-start | bytes 393220
  20.3 9.6 %collective-permute-start.9 = (bf16[256,256]{1,0:T(8,128)(2,1)S(1)}, bf16[256,256]{1,0:T(8,128)(2,1)S(1)}, u32[]{:S(2)}, u32[]{:S(2)}) collective-permute-start(bf16[256,256]{1,0:T(8,128)(2,1)S(1)} %get-tuple-element.78), channel_id=1, source_target_pairs={{0,2},{1,3},{2,0},{3,1},{4,6},{5,7},{6,4},{7,5},{8,10},{9,11},{10,... | collective-permute-start | bytes 393224 | tf_op jit(solution)/shard_map/ppermute | solution.py:13
  23.8 16.0 %collective-permute-start.6 = (bf16[128,1024]{1,0:T(8,128)(2,1)S(1)}, bf16[128,1024]{1,0:T(8,128)(2,1)S(1)}, u32[]{:S(2)}, u32[]{:S(2)}) collective-permute-start(bf16[128,1024]{1,0:T(8,128)(2,1)S(1)} %slice.261), channel_id=1, source_target_pairs={{0,1},{1,0},{2,3},{3,2},{4,5},{5,4},{6,7},{7,6},{8,9},{9,8},{10,11... | collective-permute-start | bytes 786440 | tf_op jit(solution)/shard_map/ppermute | solution.py:13
  26.9 0.6 copy-start.2
  26.9 0.7 copy-start.4
  27.6 26.9 %collective-permute-start.13 = (bf16[256,1024]{0,1:T(8,128)(2,1)S(1)}, bf16[256,1024]{0,1:T(8,128)(2,1)S(1)}, u32[]{:S(2)}, u32[]{:S(2)}) collective-permute-start(bf16[256,1024]{0,1:T(8,128)(2,1)S(1)} %pad_maximum_fusion), channel_id=1, source_target_pairs={{0,8},{4,12},{8,0},{12,4},{16,24},{20,28},{24,16},{28,20},{1,9},{5... | collective-permute-start | bytes 1572872 | tf_op jit(solution)/shard_map/ppermute | solution.py:13
  29.9 11.5 %collective-permute-start.10 = (bf16[512,256]{1,0:T(8,128)(2,1)S(1)}, bf16[512,256]{1,0:T(8,128)(2,1)S(1)}, u32[]{:S(2)}, u32[]{:S(2)}) collective-permute-start(bf16[512,256]{1,0:T(8,128)(2,1)S(1)} %pad_maximum_fusion.10), channel_id=1, source_target_pairs={{0,1},{1,0},{2,3},{3,2},{4,5},{5,4},{6,7},{7,6},{8,9},{9,8},{10,11... | collective-permute-start | bytes 786440 | tf_op jit(solution)/shard_map/ppermute | solution.py:13
  30.2 9.6 %collective-permute-start.5 = (bf16[128,512]{1,0:T(8,128)(2,1)S(1)}, bf16[128,512]{1,0:T(8,128)(2,1)S(1)}, u32[]{:S(2)}, u32[]{:S(2)}) collective-permute-start(bf16[128,512]{1,0:T(8,128)(2,1)S(1)} %get-tuple-element.129), channel_id=1, source_target_pairs={{0,2},{1,3},{2,0},{3,1},{4,6},{5,7},{6,4},{7,5},{8,10},{9,11},{10,... | collective-permute-start | bytes 393224 | tf_op jit(solution)/shard_map/ppermute | solution.py:13
  40.3 1.6 %collective-permute-start.7 = (bf16[128,1024]{0,1:T(8,128)(2,1)S(1)}, bf16[128,1024]{0,1:T(8,128)(2,1)S(1)}, u32[]{:S(2)}, u32[]{:S(2)}) collective-permute-start(bf16[128,1024]{0,1:T(8,128)(2,1)S(1)} %get-tuple-element.131), channel_id=1, source_target_pairs={{0,4},{4,0},{8,12},{12,8},{16,20},{20,16},{24,28},{28,24},{1,5},{5... | collective-permute-start | bytes 786440 | tf_op jit(solution)/shard_map/ppermute | solution.py:13
  42.7 1.4 %collective-permute-start.11 = (bf16[128,512]{1,0:T(8,128)(2,1)S(1)}, bf16[128,512]{1,0:T(8,128)(2,1)S(1)}, u32[]{:S(2)}, u32[]{:S(2)}) collective-permute-start(bf16[128,512]{1,0:T(8,128)(2,1)S(1)} %convolution_convert_fusion), channel_id=1, source_target_pairs={{0,4},{4,0},{8,12},{12,8},{16,20},{20,16},{24,28},{28,24},{1,5},{5... | collective-permute-start | bytes 393224 | tf_op jit(solution)/shard_map/ppermute | solution.py:13
  44.3 10.1 %collective-permute-start.12 = (bf16[128,512]{1,0:T(8,128)(2,1)S(1)}, bf16[128,512]{1,0:T(8,128)(2,1)S(1)}, u32[]{:S(2)}, u32[]{:S(2)}) collective-permute-start(bf16[128,512]{1,0:T(8,128)(2,1)S(1)} %get-tuple-element.133), channel_id=1, source_target_pairs={{0,2},{1,3},{2,0},{3,1},{4,6},{5,7},{6,4},{7,5},{8,10},{9,11},{10,... | collective-permute-start | bytes 393224 | tf_op jit(solution)/shard_map/ppermute | solution.py:13
  55.2 5.1 %collective-permute-start.14 = (bf16[128,512]{0,1:T(8,128)(2,1)S(1)}, bf16[128,512]{0,1:T(8,128)(2,1)S(1)}, u32[]{:S(2)}, u32[]{:S(2)}) collective-permute-start(bf16[128,512]{0,1:T(8,128)(2,1)S(1)} %pad_maximum_fusion.23), channel_id=1, source_target_pairs={{0,8},{4,12},{8,0},{12,4},{16,24},{20,28},{24,16},{28,20},{1,9},{5... | collective-permute-start | bytes 393224 | tf_op jit(solution)/shard_map/ppermute | solution.py:13
  60.5 5.0 %collective-permute-start.15 = (bf16[128,512]{0,1:T(8,128)(2,1)S(1)}, bf16[128,512]{0,1:T(8,128)(2,1)S(1)}, u32[]{:S(2)}, u32[]{:S(2)}) collective-permute-start(bf16[128,512]{0,1:T(8,128)(2,1)S(1)} %fusion.18), channel_id=1, source_target_pairs={{0,1},{1,0},{2,3},{3,2},{4,5},{5,4},{6,7},{7,6},{8,9},{9,8},{10,11... | collective-permute-start | bytes 393224 | tf_op jit(solution)/shard_map/ppermute | solution.py:13
  66.4 1.4 %collective-permute-start.16 = (bf16[128,512]{1,0:T(8,128)(2,1)S(1)}, bf16[128,512]{1,0:T(8,128)(2,1)S(1)}, u32[]{:S(2)}, u32[]{:S(2)}) collective-permute-start(bf16[128,512]{1,0:T(8,128)(2,1)S(1)} %pad_maximum_fusion.24), channel_id=1, source_target_pairs={{0,4},{4,0},{8,12},{12,8},{16,20},{20,16},{24,28},{28,24},{1,5},{5... | collective-permute-start | bytes 393224 | tf_op jit(solution)/shard_map/ppermute | solution.py:13
  68.7 5.6 %collective-permute-start.17 = (bf16[128,512]{0,1:T(8,128)(2,1)S(1)}, bf16[128,512]{0,1:T(8,128)(2,1)S(1)}, u32[]{:S(2)}, u32[]{:S(2)}) collective-permute-start(bf16[128,512]{0,1:T(8,128)(2,1)S(1)} %pad_maximum_fusion.25), channel_id=1, source_target_pairs={{0,1},{1,0},{2,3},{3,2},{4,5},{5,4},{6,7},{7,6},{8,9},{9,8},{10,11... | collective-permute-start | bytes 393224 | tf_op jit(solution)/shard_map/ppermute | solution.py:13
  74.5 8.5 %collective-permute-start.18 = (bf16[128,512]{0,1:T(8,128)(2,1)S(1)}, bf16[128,512]{0,1:T(8,128)(2,1)S(1)}, u32[]{:S(2)}, u32[]{:S(2)}) collective-permute-start(bf16[128,512]{0,1:T(8,128)(2,1)S(1)} %fusion.72), channel_id=1, source_target_pairs={{0,2},{1,3},{2,0},{3,1},{4,6},{5,7},{6,4},{7,5},{8,10},{9,11},{10,... | collective-permute-start | bytes 393224 | tf_op jit(solution)/shard_map/ppermute | solution.py:13
  83.1 5.4 %collective-permute-start.19 = (bf16[128,512]{0,1:T(8,128)(2,1)S(1)}, bf16[128,512]{0,1:T(8,128)(2,1)S(1)}, u32[]{:S(2)}, u32[]{:S(2)}) collective-permute-start(bf16[128,512]{0,1:T(8,128)(2,1)S(1)} %add_convert_fusion.2), channel_id=1, source_target_pairs={{0,8},{4,12},{8,0},{12,4},{16,24},{20,28},{24,16},{28,20},{1,9},{5... | collective-permute-start | bytes 393224 | tf_op jit(solution)/shard_map/ppermute | solution.py:13
  89.5 1.4 %collective-permute-start.20 = (bf16[128,512]{1,0:T(8,128)(2,1)S(1)}, bf16[128,512]{1,0:T(8,128)(2,1)S(1)}, u32[]{:S(2)}, u32[]{:S(2)}) collective-permute-start(bf16[128,512]{1,0:T(8,128)(2,1)S(1)} %fusion.7), channel_id=1, source_target_pairs={{0,4},{4,0},{8,12},{12,8},{16,20},{20,16},{24,28},{28,24},{1,5},{5... | collective-permute-start | bytes 393224 | tf_op jit(solution)/shard_map/ppermute | solution.py:13
  91.8 1.4 %collective-permute-start.21 = (bf16[128,512]{0,1:T(8,128)(2,1)S(1)}, bf16[128,512]{0,1:T(8,128)(2,1)S(1)}, u32[]{:S(2)}, u32[]{:S(2)}) collective-permute-start(bf16[128,512]{0,1:T(8,128)(2,1)S(1)} %dynamic-slice_convert_fusion.1), channel_id=1, source_target_pairs={{0,4},{4,0},{8,12},{12,8},{16,20},{20,16},{24,28},{28,24},{1,5},{5... | collective-permute-start | bytes 393224 | tf_op jit(solution)/shard_map/ppermute | solution.py:13
  92.0 10.6 %copy-start.3 = (bf16[256,256]{1,0:T(8,128)(2,1)S(1)}, bf16[256,256]{1,0:T(8,128)(2,1)}, u32[]{:S(2)}) copy-start(bf16[256,256]{1,0:T(8,128)(2,1)} %copy-done.2) | copy-start | bytes 393220
  92.0 10.6 %copy-start.5 = (bf16[256,256]{1,0:T(8,128)(2,1)S(1)}, bf16[256,256]{1,0:T(8,128)(2,1)}, u32[]{:S(2)}) copy-start(bf16[256,256]{1,0:T(8,128)(2,1)} %copy-done.4) | copy-start | bytes 393220
  93.3 7.9 %collective-permute-start.22 = (bf16[128,512]{0,1:T(8,128)(2,1)S(1)}, bf16[128,512]{0,1:T(8,128)(2,1)S(1)}, u32[]{:S(2)}, u32[]{:S(2)}) collective-permute-start(bf16[128,512]{0,1:T(8,128)(2,1)S(1)} %fusion.32), channel_id=1, source_target_pairs={{0,2},{1,3},{2,0},{3,1},{4,6},{5,7},{6,4},{7,5},{8,10},{9,11},{10,... | collective-permute-start | bytes 393224 | tf_op jit(solution)/shard_map/ppermute | solution.py:13
  101.2 1.4 %collective-permute-start.23 = (bf16[128,512]{0,1:T(8,128)(2,1)S(1)}, bf16[128,512]{0,1:T(8,128)(2,1)S(1)}, u32[]{:S(2)}, u32[]{:S(2)}) collective-permute-start(bf16[128,512]{0,1:T(8,128)(2,1)S(1)} %add_convert_fusion.1), channel_id=1, source_target_pairs={{0,4},{4,0},{8,12},{12,8},{16,20},{20,16},{24,28},{28,24},{1,5},{5... | collective-permute-start | bytes 393224 | tf_op jit(solution)/shard_map/ppermute | solution.py:13
  101.4 2.3 %copy-start.7 = (bf16[128,512]{1,0:T(8,128)(2,1)S(1)}, bf16[128,512]{1,0:T(8,128)(2,1)}, u32[]{:S(2)}) copy-start(bf16[128,512]{1,0:T(8,128)(2,1)} %copy-done.6) | copy-start | bytes 393220
  104.0 9.1 %collective-permute-start.24 = (bf16[256,128]{0,1:T(8,128)(2,1)S(1)}, bf16[256,128]{0,1:T(8,128)(2,1)S(1)}, u32[]{:S(2)}, u32[]{:S(2)}) collective-permute-start(bf16[256,128]{0,1:T(8,128)(2,1)S(1)} %constant_dynamic-slice_fusion.1), channel_id=1, source_target_pairs={{0,1},{1,0},{2,3},{3,2},{4,5},{5,4},{6,7},{7,6},{8,9},{9,8},{10,11... | collective-permute-start | bytes 196616 | tf_op jit(solution)/shard_map/ppermute | solution.py:13
  104.1 4.8 %collective-permute-start.25 = (bf16[128,128]{0,1:T(8,128)(2,1)S(1)}, bf16[128,128]{0,1:T(8,128)(2,1)S(1)}, u32[]{:S(2)}, u32[]{:S(2)}) collective-permute-start(bf16[128,128]{0,1:T(8,128)(2,1)S(1)} %get-tuple-element.69), channel_id=1, source_target_pairs={{0,1},{1,0},{2,3},{3,2},{4,5},{5,4},{6,7},{7,6},{8,9},{9,8},{10,11... | collective-permute-start | bytes 98312 | tf_op jit(solution)/shard_map/ppermute | solution.py:13
  106.2 5.8 %collective-permute-start.26 = (bf16[128,128]{0,1:T(8,128)(2,1)S(1)}, bf16[128,128]{0,1:T(8,128)(2,1)S(1)}, u32[]{:S(2)}, u32[]{:S(2)}) collective-permute-start(bf16[128,128]{0,1:T(8,128)(2,1)S(1)} %get-tuple-element.68), channel_id=1, source_target_pairs={{0,2},{1,3},{2,0},{3,1},{4,6},{5,7},{6,4},{7,5},{8,10},{9,11},{10,... | collective-permute-start | bytes 98312 | tf_op jit(solution)/shard_map/ppermute | solution.py:13
  107.4 5.7 %collective-permute-start.27 = (bf16[128,128]{0,1:T(8,128)(2,1)S(1)}, bf16[128,128]{0,1:T(8,128)(2,1)S(1)}, u32[]{:S(2)}, u32[]{:S(2)}) collective-permute-start(bf16[128,128]{0,1:T(8,128)(2,1)S(1)} %get-tuple-element.67), channel_id=1, source_target_pairs={{0,3},{1,2},{2,1},{3,0},{4,7},{5,6},{6,5},{7,4},{8,11},{9,10},{10,... | collective-permute-start | bytes 98312 | tf_op jit(solution)/shard_map/ppermute | solution.py:13

commit v7 on v6

--- a/solution.py
+++ b/solution.py
@@ -169,21 +169,11 @@
         return part(block1, (front_id ^ mask) // 2, front_count // 2, 1)
 
     inverse0_pair = traded(inverse0, "front", 1)
-    cores2 = [
-        jnp.concatenate(
-            [inverse2[:, (2 * other + core) * leaf_rows :][:, :leaf_rows] for other in range(2)], 1
-        )
-        for core in range(2)
-    ]
-    handed2 = jnp.where(side == 1, cores2[0], cores2[1])
-    block2 = jnp.where(side == 1, cores2[1], cores2[0])
-    block2 = jnp.concatenate([block2, traded(handed2, "leaf", 1)], 0)
-    wing2 = traded(block2, "leaf", 2)
     inverse1_pair = traded(after(inverse1, inverse0_pair), "front", 1)
     columns1 = [pair_columns(0)] + [
         traded(pair_columns(mask), "front", mask) for mask in range(2, front_count, 2)
     ]
-    *parcels, block2, inverse0_pair = together(*parcels, block2, inverse0_pair)
+    *parcels, inverse0_pair = together(*parcels, inverse0_pair)
     parcels = [by_rows(block) for block in parcels]
     update0_columns = in_order([block[:own_rows, : 2 * own_rows] for block in parcels], 0)
 
@@ -202,10 +192,20 @@
         product(rhs0, inverse0, 0, 1), product(rhs0, inverse0_pair, 0, 1), odd, 1
     ).astype(BF16)
     updated0 = forward(solved0_pair, update0_columns)
+    cores2 = [
+        jnp.concatenate(
+            [inverse2[:, (2 * other + core) * leaf_rows :][:, :leaf_rows] for other in range(2)], 1
+        )
+        for core in range(2)
+    ]
+    cores2 = together(*cores2, solved0_pair)[:2]
+    handed2 = jnp.where(side == 1, cores2[0], cores2[1])
+    block2 = jnp.where(side == 1, cores2[1], cores2[0])
+    block2 = jnp.concatenate([block2, traded(handed2, "leaf", 1)], 0)
     parcels = together(*parcels, updated0)[:-1]
     rhs1, rhs2 = level_rows(parcels, 1).T, level_rows(parcels, 2).T
     lists = in_order([block[own_rows : own_rows + 4, :own_rows] for block in parcels], 1)
-    columns1_near = traded(jnp.concatenate(columns1, 0), "front", 1)
+    columns1_near = traded(after(jnp.concatenate(columns1, 0), updated0), "front", 1)
     columns1 = alternated(
         columns1,
         [
@@ -217,6 +217,7 @@
     columns1 = in_order([block[:own_rows] for block in columns1], 0)
     updated0 = high_sum(updated0).astype(BF16)
     updated0, inverse1_pair = together(updated0, inverse1_pair)
+    wing2 = traded(after(block2, updated0), "leaf", 2)
 
     def selector(lists, level_index):
         numbers = lists.astype(jnp.int32)
@@ -267,10 +268,11 @@
     fetched1 = adjoint(below2, select1).astype(BF16)
     carried1 = adjoint(traded(fetched1, "leaf", 1), columns1_side) + adjoint(fetched1, columns1)
     weights1 = (solved1_pair.astype(F32) - carried1).astype(BF16)
+    select0_late = lax.optimization_barrier(selector(after(lists, weights1), 0))
     below1 = high_sum(side_scatter(pair_adjoint(weights1, inverse1, inverse1_pair))).astype(BF16)
     below1_all = ordered(below1, traded(below1, "leaf", 1), side, 1)
 
-    fetched0 = adjoint(below1_all, select0).astype(BF16)
+    fetched0 = adjoint(below1_all, select0_late).astype(BF16)
     weights0 = (solved0_pair.astype(F32) - adjoint(fetched0, update0_columns)).astype(BF16)
     below0 = pair_adjoint(weights0, inverse0, inverse0_pair)
     upper = jnp.concatenate([pair_rows(below1), pair_rows(part(below2, wing, 2, 1))], 0)

time: 114 us -> 111 us (0.974)
  waiting for transfers between devices: 68.1 us -> 62.9 us
  starting transfers between devices: 29.1 us -> 33 us
  other arithmetic: 4.57 us -> 3.38 us
    ppermute x28, waiting for transfers between devices: 68.1 us -> 62.9 us  [traded(): lax.ppermute(shard, axis, [(i, i ^ mask) for i in range(lax.axis_size(axi...]
    ppermute x28, starting transfers between devices: 29.1 us -> 33 us  [traded(): lax.ppermute(shard, axis, [(i, i ^ mask) for i in range(lax.axis_size(axi...]
    unnamed x20 -> x6, local copies, waits for them, and re-layouts: 1.58 us -> 0.02 us
  transfers between devices with their start and end apart: 28 -> 28, of which waited for: 22 -> 19; matrix products, arithmetic and copies ran while one was open for 5% -> 4% of each run, Pallas kernels for 0% -> 0%
where the time goes in v7:
time: 111 us
  waiting for transfers between devices  62.9 us (57%)
  starting transfers between devices  33 us (30%)
  matrix products  6.5 us (6%)
  local copies, waits for them, and re-layouts  4.37 us (4%)
  other arithmetic  3.38 us (3%)
  between operations  1.12 us (1%)
    ppermute x28, waiting for transfers between devices, traded(): lax.ppermute(shard, axis, [(i, i ^ mask) for i in range(lax.axis_size(axi...  62.9 us
    ppermute x28, starting transfers between devices, traded(): lax.ppermute(shard, axis, [(i, i ^ mask) for i in range(lax.axis_size(axi...  33 us
    dot_general x21, matrix products, product(): lax.dot_general(left, right, (((left_dim,), (right_dim,)), ((), ())), pre...  6.5 us
  transfers between devices with their start and end apart: 28, of which 19 were waited for; matrix products, arithmetic and copies ran while one was open for 4% of the time, Pallas kernels for 0%

profile of v7, /device:TPU:0, one launch (start us, length us, event | category | flops | bytes accessed | tf_op | source)
XLA Modules:
  0.0 111.3 jit_solution(6766243516331546444)
XLA Ops:
  0.0 0.9 slice.266
  0.9 1.0 slice.267
  2.1 0.9 slice-done
  2.9 0.3 copy.30
  3.5 3.1 %collective-permute-start = (bf16[136,640]{1,0:T(8,128)(2,1)S(1)}, bf16[136,640]{1,0:T(8,128)(2,1)S(1)}, u32[]{:S(2)}, u32[]{:S(2)}) collective-permute-start(bf16[136,640]{1,0:T(8,128)(2,1)S(1)} %get-tuple-element.126), channel_id=1, source_target_pairs={{0,1},{1,0},{2,3},{3,2},{4,5},{5,4},{6,7},{7,6},{8,9},{9,8},{10,11... | collective-permute-start | bytes 522248 | tf_op jit(solution)/shard_map/ppermute | solution.py:13
  6.6 2.7 %collective-permute-start.1 = (bf16[136,640]{1,0:T(8,128)(2,1)S(1)}, bf16[136,640]{1,0:T(8,128)(2,1)S(1)}, u32[]{:S(2)}, u32[]{:S(2)}) collective-permute-start(bf16[136,640]{1,0:T(8,128)(2,1)S(1)} %get-tuple-element.127), channel_id=1, source_target_pairs={{0,2},{1,3},{2,0},{3,1},{4,6},{5,7},{6,4},{7,5},{8,10},{9,11},{10,... | collective-permute-start | bytes 522248 | tf_op jit(solution)/shard_map/ppermute | solution.py:13
  9.3 0.9 collective-permute-start.3
  10.4 10.2 %collective-permute-done.3 = bf16[128,512]{1,0:T(8,128)(2,1)S(1)} collective-permute-done((bf16[128,512]{1,0:T(8,128)(2,1)S(1)}, bf16[128,512]{1,0:T(8,128)(2,1)S(1)}, u32[]{:S(2)}, u32[]{:S(2)}) %collective-permute-start.3) | collective-permute-done | bytes 131104 | tf_op jit(solution)/shard_map/ppermute | solution.py:13
  20.6 2.5 %collective-permute-start.5 = (bf16[128,1024]{1,0:T(8,128)(2,1)S(1)}, bf16[128,1024]{1,0:T(8,128)(2,1)S(1)}, u32[]{:S(2)}, u32[]{:S(2)}) collective-permute-start(bf16[128,1024]{1,0:T(8,128)(2,1)S(1)} %slice.267), channel_id=1, source_target_pairs={{0,1},{1,0},{2,3},{3,2},{4,5},{5,4},{6,7},{7,6},{8,9},{9,8},{10,11... | collective-permute-start | bytes 786440 | tf_op jit(solution)/shard_map/ppermute | solution.py:13
  23.1 2.6 %collective-permute-start.8 = (bf16[256,256]{1,0:T(8,128)(2,1)S(1)}, bf16[256,256]{1,0:T(8,128)(2,1)S(1)}, u32[]{:S(2)}, u32[]{:S(2)}) collective-permute-start(bf16[256,256]{1,0:T(8,128)(2,1)S(1)} %get-tuple-element.88), channel_id=1, source_target_pairs={{0,2},{1,3},{2,0},{3,1},{4,6},{5,7},{6,4},{7,5},{8,10},{9,11},{10,... | collective-permute-start | bytes 393224 | tf_op jit(solution)/shard_map/ppermute | solution.py:13
  25.9 0.2 fusion.55
  26.4 0.2 fusion.101
  26.7 0.6 collective-permute-start.4
  27.6 4.5 %collective-permute-done.8 = bf16[256,256]{1,0:T(8,128)(2,1)S(1)} collective-permute-done((bf16[256,256]{1,0:T(8,128)(2,1)S(1)}, bf16[256,256]{1,0:T(8,128)(2,1)S(1)}, u32[]{:S(2)}, u32[]{:S(2)}) %collective-permute-start.8) | collective-permute-done | bytes 131104 | tf_op jit(solution)/shard_map/ppermute | solution.py:13
  32.2 4.1 %collective-permute-start.9 = (bf16[512,256]{1,0:T(8,128)(2,1)S(1)}, bf16[512,256]{1,0:T(8,128)(2,1)S(1)}, u32[]{:S(2)}, u32[]{:S(2)}) collective-permute-start(bf16[512,256]{1,0:T(8,128)(2,1)S(1)} %pad_maximum_fusion.8), channel_id=1, source_target_pairs={{0,1},{1,0},{2,3},{3,2},{4,5},{5,4},{6,7},{7,6},{8,9},{9,8},{10,11... | collective-permute-start | bytes 786440 | tf_op jit(solution)/shard_map/ppermute | solution.py:13
  36.4 0.5 fusion.102
  37.1 1.5 %collective-permute-start.13 = (bf16[256,1024]{0,1:T(8,128)(2,1)S(1)}, bf16[256,1024]{0,1:T(8,128)(2,1)S(1)}, u32[]{:S(2)}, u32[]{:S(2)}) collective-permute-start(bf16[256,1024]{0,1:T(8,128)(2,1)S(1)} %pad_maximum_fusion), channel_id=1, source_target_pairs={{0,8},{4,12},{8,0},{12,4},{16,24},{20,28},{24,16},{28,20},{1,9},{5... | collective-permute-start | bytes 1572872 | tf_op jit(solution)/shard_map/ppermute | solution.py:13
  38.7 2.0 %collective-permute-done.9 = bf16[512,256]{1,0:T(8,128)(2,1)S(1)} collective-permute-done((bf16[512,256]{1,0:T(8,128)(2,1)S(1)}, bf16[512,256]{1,0:T(8,128)(2,1)S(1)}, u32[]{:S(2)}, u32[]{:S(2)}) %collective-permute-start.9) | collective-permute-done | bytes 262176 | tf_op jit(solution)/shard_map/ppermute | solution.py:13
  40.7 0.2 fusion.80
  41.0 0.2 fusion.79
  41.2 0.2 convolution_convert_fusion.1
  41.6 1.3 %collective-permute-done.10 = bf16[128,512]{1,0:T(8,128)(2,1)S(1)} collective-permute-done((bf16[128,512]{1,0:T(8,128)(2,1)S(1)}, bf16[128,512]{1,0:T(8,128)(2,1)S(1)}, u32[]{:S(2)}, u32[]{:S(2)}) %collective-permute-start.10) | collective-permute-done | bytes 131104 | tf_op jit(solution)/shard_map/ppermute | solution.py:13
  42.9 0.2 fusion.26
  43.1 2.0 %collective-permute-start.11 = (bf16[128,512]{1,0:T(8,128)(2,1)S(1)}, bf16[128,512]{1,0:T(8,128)(2,1)S(1)}, u32[]{:S(2)}, u32[]{:S(2)}) collective-permute-start(bf16[128,512]{1,0:T(8,128)(2,1)S(1)} %get-tuple-element.143), channel_id=1, source_target_pairs={{0,2},{1,3},{2,0},{3,1},{4,6},{5,7},{6,4},{7,5},{8,10},{9,11},{10,... | collective-permute-start | bytes 393224 | tf_op jit(solution)/shard_map/ppermute | solution.py:13
  45.1 7.3 %collective-permute-done.11 = bf16[128,512]{1,0:T(8,128)(2,1)S(1)} collective-permute-done((bf16[128,512]{1,0:T(8,128)(2,1)S(1)}, bf16[128,512]{1,0:T(8,128)(2,1)S(1)}, u32[]{:S(2)}, u32[]{:S(2)}) %collective-permute-start.11) | collective-permute-done | bytes 131104 | tf_op jit(solution)/shard_map/ppermute | solution.py:13
  52.5 0.5 fusion.5
  53.3 1.6 %collective-permute-start.14 = (bf16[128,512]{0,1:T(8,128)(2,1)S(1)}, bf16[128,512]{0,1:T(8,128)(2,1)S(1)}, u32[]{:S(2)}, u32[]{:S(2)}) collective-permute-start(bf16[128,512]{0,1:T(8,128)(2,1)S(1)} %pad_maximum_fusion.23), channel_id=1, source_target_pairs={{0,8},{4,12},{8,0},{12,4},{16,24},{20,28},{24,16},{28,20},{1,9},{5... | collective-permute-start | bytes 393224 | tf_op jit(solution)/shard_map/ppermute | solution.py:13
  54.8 0.2 constant_dynamic-slice_fusion
  55.0 3.3 %collective-permute-done.14 = bf16[128,512]{0,1:T(8,128)(2,1)S(1)} collective-permute-done((bf16[128,512]{0,1:T(8,128)(2,1)S(1)}, bf16[128,512]{0,1:T(8,128)(2,1)S(1)}, u32[]{:S(2)}, u32[]{:S(2)}) %collective-permute-start.14) | collective-permute-done | bytes 131104 | tf_op jit(solution)/shard_map/ppermute | solution.py:13
  58.4 1.8 %collective-permute-start.15 = (bf16[128,512]{0,1:T(8,128)(2,1)S(1)}, bf16[128,512]{0,1:T(8,128)(2,1)S(1)}, u32[]{:S(2)}, u32[]{:S(2)}) collective-permute-start(bf16[128,512]{0,1:T(8,128)(2,1)S(1)} %fusion.13), channel_id=1, source_target_pairs={{0,1},{1,0},{2,3},{3,2},{4,5},{5,4},{6,7},{7,6},{8,9},{9,8},{10,11... | collective-permute-start | bytes 393224 | tf_op jit(solution)/shard_map/ppermute | solution.py:13
  60.3 3.1 %collective-permute-done.15 = bf16[128,512]{0,1:T(8,128)(2,1)S(1)} collective-permute-done((bf16[128,512]{0,1:T(8,128)(2,1)S(1)}, bf16[128,512]{0,1:T(8,128)(2,1)S(1)}, u32[]{:S(2)}, u32[]{:S(2)}) %collective-permute-start.15) | collective-permute-done | bytes 131104 | tf_op jit(solution)/shard_map/ppermute | solution.py:13
  63.6 0.4 fusion.103
  64.0 0.4 fusion.104
  64.5 1.3 %collective-permute-done.16 = bf16[128,512]{1,0:T(8,128)(2,1)S(1)} collective-permute-done((bf16[128,512]{1,0:T(8,128)(2,1)S(1)}, bf16[128,512]{1,0:T(8,128)(2,1)S(1)}, u32[]{:S(2)}, u32[]{:S(2)}) %collective-permute-start.16) | collective-permute-done | bytes 131104 | tf_op jit(solution)/shard_map/ppermute | solution.py:13
  65.8 0.3 fusion.37
  66.1 0.3 fusion.105
  66.7 1.8 %collective-permute-start.17 = (bf16[128,512]{0,1:T(8,128)(2,1)S(1)}, bf16[128,512]{0,1:T(8,128)(2,1)S(1)}, u32[]{:S(2)}, u32[]{:S(2)}) collective-permute-start(bf16[128,512]{0,1:T(8,128)(2,1)S(1)} %pad_maximum_fusion.25), channel_id=1, source_target_pairs={{0,1},{1,0},{2,3},{3,2},{4,5},{5,4},{6,7},{7,6},{8,9},{9,8},{10,11... | collective-permute-start | bytes 393224 | tf_op jit(solution)/shard_map/ppermute | solution.py:13
  68.5 3.8 %collective-permute-done.17 = bf16[128,512]{0,1:T(8,128)(2,1)S(1)} collective-permute-done((bf16[128,512]{0,1:T(8,128)(2,1)S(1)}, bf16[128,512]{0,1:T(8,128)(2,1)S(1)}, u32[]{:S(2)}, u32[]{:S(2)}) %collective-permute-start.17) | collective-permute-done | bytes 131104 | tf_op jit(solution)/shard_map/ppermute | solution.py:13
  72.5 0.9 collective-permute-start.18
  73.4 7.6 %collective-permute-done.18 = bf16[128,512]{0,1:T(8,128)(2,1)S(1)} collective-permute-done((bf16[128,512]{0,1:T(8,128)(2,1)S(1)}, bf16[128,512]{0,1:T(8,128)(2,1)S(1)}, u32[]{:S(2)}, u32[]{:S(2)}) %collective-permute-start.18) | collective-permute-done | bytes 131104 | tf_op jit(solution)/shard_map/ppermute | solution.py:13
  81.1 1.6 %collective-permute-start.19 = (bf16[128,512]{0,1:T(8,128)(2,1)S(1)}, bf16[128,512]{0,1:T(8,128)(2,1)S(1)}, u32[]{:S(2)}, u32[]{:S(2)}) collective-permute-start(bf16[128,512]{0,1:T(8,128)(2,1)S(1)} %add_convert_fusion.2), channel_id=1, source_target_pairs={{0,8},{4,12},{8,0},{12,4},{16,24},{20,28},{24,16},{28,20},{1,9},{5... | collective-permute-start | bytes 393224 | tf_op jit(solution)/shard_map/ppermute | solution.py:13
  82.8 3.4 %collective-permute-done.19 = bf16[128,512]{0,1:T(8,128)(2,1)S(1)} collective-permute-done((bf16[128,512]{0,1:T(8,128)(2,1)S(1)}, bf16[128,512]{0,1:T(8,128)(2,1)S(1)}, u32[]{:S(2)}, u32[]{:S(2)}) %collective-permute-start.19) | collective-permute-done | bytes 131104 | tf_op jit(solution)/shard_map/ppermute | solution.py:13
  86.6 0.5 fusion.6
  87.2 0.3 fusion.46
  87.5 0.3 fusion.38
  87.7 0.8 collective-permute-done.20
  88.5 0.3 fusion.8
  88.8 0.3 fusion.52
  89.1 0.3 convolution_add_fusion
  89.4 0.2 collective-permute-start.21
  89.6 1.2 %collective-permute-done.21 = bf16[128,512]{0,1:T(8,128)(2,1)S(1)} collective-permute-done((bf16[128,512]{0,1:T(8,128)(2,1)S(1)}, bf16[128,512]{0,1:T(8,128)(2,1)S(1)}, u32[]{:S(2)}, u32[]{:S(2)}) %collective-permute-start.21) | collective-permute-done | bytes 131104 | tf_op jit(solution)/shard_map/ppermute | solution.py:13
  90.9 0.4 fusion.3
  91.3 8.3 %collective-permute-done.22 = bf16[128,512]{0,1:T(8,128)(2,1)S(1)} collective-permute-done((bf16[128,512]{0,1:T(8,128)(2,1)S(1)}, bf16[128,512]{0,1:T(8,128)(2,1)S(1)}, u32[]{:S(2)}, u32[]{:S(2)}) %collective-permute-start.22) | collective-permute-done | bytes 131104 | tf_op jit(solution)/shard_map/ppermute | solution.py:13
  99.8 1.3 %collective-permute-done.23 = bf16[128,512]{0,1:T(8,128)(2,1)S(1)} collective-permute-done((bf16[128,512]{0,1:T(8,128)(2,1)S(1)}, bf16[128,512]{0,1:T(8,128)(2,1)S(1)}, u32[]{:S(2)}, u32[]{:S(2)}) %collective-permute-start.23) | collective-permute-done | bytes 131104 | tf_op jit(solution)/shard_map/ppermute | solution.py:13
  101.1 0.5 fusion.9
  101.6 0.2 fusion.49
  101.8 0.2 convolution_add_fusion.2
  102.2 2.1 %collective-permute-start.25 = (bf16[128,128]{0,1:T(8,128)(2,1)S(1)}, bf16[128,128]{0,1:T(8,128)(2,1)S(1)}, u32[]{:S(2)}, u32[]{:S(2)}) collective-permute-start(bf16[128,128]{0,1:T(8,128)(2,1)S(1)} %get-tuple-element.79), channel_id=1, source_target_pairs={{0,1},{1,0},{2,3},{3,2},{4,5},{5,4},{6,7},{7,6},{8,9},{9,8},{10,11... | collective-permute-start | bytes 98312 | tf_op jit(solution)/shard_map/ppermute | solution.py:13
  104.3 0.4 collective-permute-start.26
  104.7 2.1 %collective-permute-start.27 = (bf16[128,128]{0,1:T(8,128)(2,1)S(1)}, bf16[128,128]{0,1:T(8,128)(2,1)S(1)}, u32[]{:S(2)}, u32[]{:S(2)}) collective-permute-start(bf16[128,128]{0,1:T(8,128)(2,1)S(1)} %get-tuple-element.77), channel_id=1, source_target_pairs={{0,3},{1,2},{2,1},{3,0},{4,7},{5,6},{6,5},{7,4},{8,11},{9,10},{10,... | collective-permute-start | bytes 98312 | tf_op jit(solution)/shard_map/ppermute | solution.py:13
  106.7 0.3 collective-permute-done.25
  107.0 2.3 %collective-permute-done.26 = bf16[128,128]{0,1:T(8,128)(2,1)S(1)} collective-permute-done((bf16[128,128]{0,1:T(8,128)(2,1)S(1)}, bf16[128,128]{0,1:T(8,128)(2,1)S(1)}, u32[]{:S(2)}, u32[]{:S(2)}) %collective-permute-start.26) | collective-permute-done | bytes 32800 | tf_op jit(solution)/shard_map/ppermute | solution.py:13
  109.4 1.0 collective-permute-done.27
  110.5 0.8 pad_maximum_fusion.1
  (122 shorter events, 4.1 us)
Async XLA Ops:
  1.9 1.0 slice-start
  1.9 1.3 %copy-start.1 = (s32[2,128]{1,0:T(2,128)S(1)}, s32[2,128]{1,0:T(2,128)}, u32[]{:S(2)}) copy-start(s32[2,128]{1,0:T(2,128)} %param.9) | copy-start | bytes 3076
  1.9 1.3 %copy-start.2 = (s32[2,128,1]{1,2,0:T(1,128)S(1)}, s32[2,128,1]{1,2,0:T(1,128)}, u32[]{:S(2)}) copy-start(s32[2,128,1]{1,2,0:T(1,128)} %param.8) | copy-start | bytes 3076
  1.9 1.3 %copy-start = (bf16[3,128,256]{2,1,0:T(8,128)(2,1)S(1)}, bf16[3,128,256]{2,1,0:T(8,128)(2,1)}, u32[]{:S(2)}) copy-start(bf16[3,128,256]{2,1,0:T(8,128)(2,1)} %param.5) | copy-start | bytes 589828
  1.9 1.5 %slice-start.1 = ((bf16[128,1536]{1,0:T(8,128)(2,1)}), bf16[128,512]{1,0:T(8,128)(2,1)S(1)}, s32[]{:S(2)}) async-start(bf16[128,1536]{1,0:T(8,128)(2,1)} %param.7), calls=%async_computation.1 | async-start | bytes 262144 | tf_op jit(solution)/shard_map/slice | solution.py:144
  3.3 6.9 %slice-start.2 = ((bf16[128,1536]{1,0:T(8,128)(2,1)}), bf16[128,1024]{1,0:T(8,128)(2,1)S(1)}, s32[]{:S(2)}) async-start(bf16[128,1536]{1,0:T(8,128)(2,1)} %param.7), calls=%async_computation.2 | async-start | bytes 524288 | tf_op jit(solution)/shard_map/slice | solution.py:145
  3.5 22.2 %collective-permute-start = (bf16[136,640]{1,0:T(8,128)(2,1)S(1)}, bf16[136,640]{1,0:T(8,128)(2,1)S(1)}, u32[]{:S(2)}, u32[]{:S(2)}) collective-permute-start(bf16[136,640]{1,0:T(8,128)(2,1)S(1)} %get-tuple-element.126), channel_id=1, source_target_pairs={{0,1},{1,0},{2,3},{3,2},{4,5},{5,4},{6,7},{7,6},{8,9},{9,8},{10,11... | collective-permute-start | bytes 522248 | tf_op jit(solution)/shard_map/ppermute | solution.py:13
  6.6 19.1 %collective-permute-start.1 = (bf16[136,640]{1,0:T(8,128)(2,1)S(1)}, bf16[136,640]{1,0:T(8,128)(2,1)S(1)}, u32[]{:S(2)}, u32[]{:S(2)}) collective-permute-start(bf16[136,640]{1,0:T(8,128)(2,1)S(1)} %get-tuple-element.127), channel_id=1, source_target_pairs={{0,2},{1,3},{2,0},{3,1},{4,6},{5,7},{6,4},{7,5},{8,10},{9,11},{10,... | collective-permute-start | bytes 522248 | tf_op jit(solution)/shard_map/ppermute | solution.py:13
  9.3 16.5 %collective-permute-start.2 = (bf16[136,640]{1,0:T(8,128)(2,1)S(1)}, bf16[136,640]{1,0:T(8,128)(2,1)S(1)}, u32[]{:S(2)}, u32[]{:S(2)}) collective-permute-start(bf16[136,640]{1,0:T(8,128)(2,1)S(1)} %get-tuple-element.125), channel_id=1, source_target_pairs={{0,3},{1,2},{2,1},{3,0},{4,7},{5,6},{6,5},{7,4},{8,11},{9,10},{10,... | collective-permute-start | bytes 522248 | tf_op jit(solution)/shard_map/ppermute | solution.py:13
  9.3 11.3 %collective-permute-start.3 = (bf16[128,512]{1,0:T(8,128)(2,1)S(1)}, bf16[128,512]{1,0:T(8,128)(2,1)S(1)}, u32[]{:S(2)}, u32[]{:S(2)}) collective-permute-start(bf16[128,512]{1,0:T(8,128)(2,1)S(1)} %slice.266), channel_id=1, source_target_pairs={{0,1},{1,0},{2,3},{3,2},{4,5},{5,4},{6,7},{7,6},{8,9},{9,8},{10,11... | collective-permute-start | bytes 393224 | tf_op jit(solution)/shard_map/ppermute | solution.py:13
  10.2 12.9 %collective-permute-start.7 = (bf16[128,512]{1,0:T(8,128)(2,1)S(1)}, bf16[128,512]{1,0:T(8,128)(2,1)S(1)}, u32[]{:S(2)}, u32[]{:S(2)}) collective-permute-start(bf16[128,512]{1,0:T(8,128)(2,1)S(1)} %get-tuple-element.90), channel_id=1, source_target_pairs={{0,4},{4,0},{8,12},{12,8},{16,20},{20,16},{24,28},{28,24},{1,5},{5... | collective-permute-start | bytes 393224 | tf_op jit(solution)/shard_map/ppermute | solution.py:13
  20.6 15.9 %collective-permute-start.5 = (bf16[128,1024]{1,0:T(8,128)(2,1)S(1)}, bf16[128,1024]{1,0:T(8,128)(2,1)S(1)}, u32[]{:S(2)}, u32[]{:S(2)}) collective-permute-start(bf16[128,1024]{1,0:T(8,128)(2,1)S(1)} %slice.267), channel_id=1, source_target_pairs={{0,1},{1,0},{2,3},{3,2},{4,5},{5,4},{6,7},{7,6},{8,9},{9,8},{10,11... | collective-permute-start | bytes 786440 | tf_op jit(solution)/shard_map/ppermute | solution.py:13
  23.1 9.1 %collective-permute-start.8 = (bf16[256,256]{1,0:T(8,128)(2,1)S(1)}, bf16[256,256]{1,0:T(8,128)(2,1)S(1)}, u32[]{:S(2)}, u32[]{:S(2)}) collective-permute-start(bf16[256,256]{1,0:T(8,128)(2,1)S(1)} %get-tuple-element.88), channel_id=1, source_target_pairs={{0,2},{1,3},{2,0},{3,1},{4,6},{5,7},{6,4},{7,5},{8,10},{9,11},{10,... | collective-permute-start | bytes 393224 | tf_op jit(solution)/shard_map/ppermute | solution.py:13
  26.7 9.7 %collective-permute-start.4 = (bf16[128,512]{1,0:T(8,128)(2,1)S(1)}, bf16[128,512]{1,0:T(8,128)(2,1)S(1)}, u32[]{:S(2)}, u32[]{:S(2)}) collective-permute-start(bf16[128,512]{1,0:T(8,128)(2,1)S(1)} %get-tuple-element.139), channel_id=1, source_target_pairs={{0,2},{1,3},{2,0},{3,1},{4,6},{5,7},{6,4},{7,5},{8,10},{9,11},{10,... | collective-permute-start | bytes 393224 | tf_op jit(solution)/shard_map/ppermute | solution.py:13
  27.4 9.6 %collective-permute-start.12 = (bf16[128,1024]{0,1:T(8,128)(2,1)S(1)}, bf16[128,1024]{0,1:T(8,128)(2,1)S(1)}, u32[]{:S(2)}, u32[]{:S(2)}) collective-permute-start(bf16[128,1024]{0,1:T(8,128)(2,1)S(1)} %get-tuple-element.72), channel_id=1, source_target_pairs={{0,4},{4,0},{8,12},{12,8},{16,20},{20,16},{24,28},{28,24},{1,5},{5... | collective-permute-start | bytes 786440 | tf_op jit(solution)/shard_map/ppermute | solution.py:13
  32.2 8.4 %collective-permute-start.9 = (bf16[512,256]{1,0:T(8,128)(2,1)S(1)}, bf16[512,256]{1,0:T(8,128)(2,1)S(1)}, u32[]{:S(2)}, u32[]{:S(2)}) collective-permute-start(bf16[512,256]{1,0:T(8,128)(2,1)S(1)} %pad_maximum_fusion.8), channel_id=1, source_target_pairs={{0,1},{1,0},{2,3},{3,2},{4,5},{5,4},{6,7},{7,6},{8,9},{9,8},{10,11... | collective-permute-start | bytes 786440 | tf_op jit(solution)/shard_map/ppermute | solution.py:13
  37.0 3.8 %collective-permute-start.6 = (bf16[128,1024]{0,1:T(8,128)(2,1)S(1)}, bf16[128,1024]{0,1:T(8,128)(2,1)S(1)}, u32[]{:S(2)}, u32[]{:S(2)}) collective-permute-start(bf16[128,1024]{0,1:T(8,128)(2,1)S(1)} %get-tuple-element.141), channel_id=1, source_target_pairs={{0,4},{4,0},{8,12},{12,8},{16,20},{20,16},{24,28},{28,24},{1,5},{5... | collective-permute-start | bytes 786440 | tf_op jit(solution)/shard_map/ppermute | solution.py:13
  37.1 15.4 %collective-permute-start.13 = (bf16[256,1024]{0,1:T(8,128)(2,1)S(1)}, bf16[256,1024]{0,1:T(8,128)(2,1)S(1)}, u32[]{:S(2)}, u32[]{:S(2)}) collective-permute-start(bf16[256,1024]{0,1:T(8,128)(2,1)S(1)} %pad_maximum_fusion), channel_id=1, source_target_pairs={{0,8},{4,12},{8,0},{12,4},{16,24},{20,28},{24,16},{28,20},{1,9},{5... | collective-permute-start | bytes 1572872 | tf_op jit(solution)/shard_map/ppermute | solution.py:13
  41.5 1.4 %collective-permute-start.10 = (bf16[128,512]{1,0:T(8,128)(2,1)S(1)}, bf16[128,512]{1,0:T(8,128)(2,1)S(1)}, u32[]{:S(2)}, u32[]{:S(2)}) collective-permute-start(bf16[128,512]{1,0:T(8,128)(2,1)S(1)} %convolution_convert_fusion.1), channel_id=1, source_target_pairs={{0,4},{4,0},{8,12},{12,8},{16,20},{20,16},{24,28},{28,24},{1,5},{5... | collective-permute-start | bytes 393224 | tf_op jit(solution)/shard_map/ppermute | solution.py:13
  43.1 9.3 %collective-permute-start.11 = (bf16[128,512]{1,0:T(8,128)(2,1)S(1)}, bf16[128,512]{1,0:T(8,128)(2,1)S(1)}, u32[]{:S(2)}, u32[]{:S(2)}) collective-permute-start(bf16[128,512]{1,0:T(8,128)(2,1)S(1)} %get-tuple-element.143), channel_id=1, source_target_pairs={{0,2},{1,3},{2,0},{3,1},{4,6},{5,7},{6,4},{7,5},{8,10},{9,11},{10,... | collective-permute-start | bytes 393224 | tf_op jit(solution)/shard_map/ppermute | solution.py:13
  53.3 5.0 %collective-permute-start.14 = (bf16[128,512]{0,1:T(8,128)(2,1)S(1)}, bf16[128,512]{0,1:T(8,128)(2,1)S(1)}, u32[]{:S(2)}, u32[]{:S(2)}) collective-permute-start(bf16[128,512]{0,1:T(8,128)(2,1)S(1)} %pad_maximum_fusion.23), channel_id=1, source_target_pairs={{0,8},{4,12},{8,0},{12,4},{16,24},{20,28},{24,16},{28,20},{1,9},{5... | collective-permute-start | bytes 393224 | tf_op jit(solution)/shard_map/ppermute | solution.py:13
  58.4 5.0 %collective-permute-start.15 = (bf16[128,512]{0,1:T(8,128)(2,1)S(1)}, bf16[128,512]{0,1:T(8,128)(2,1)S(1)}, u32[]{:S(2)}, u32[]{:S(2)}) collective-permute-start(bf16[128,512]{0,1:T(8,128)(2,1)S(1)} %fusion.13), channel_id=1, source_target_pairs={{0,1},{1,0},{2,3},{3,2},{4,5},{5,4},{6,7},{7,6},{8,9},{9,8},{10,11... | collective-permute-start | bytes 393224 | tf_op jit(solution)/shard_map/ppermute | solution.py:13
  64.4 1.4 %collective-permute-start.16 = (bf16[128,512]{1,0:T(8,128)(2,1)S(1)}, bf16[128,512]{1,0:T(8,128)(2,1)S(1)}, u32[]{:S(2)}, u32[]{:S(2)}) collective-permute-start(bf16[128,512]{1,0:T(8,128)(2,1)S(1)} %pad_maximum_fusion.24), channel_id=1, source_target_pairs={{0,4},{4,0},{8,12},{12,8},{16,20},{20,16},{24,28},{28,24},{1,5},{5... | collective-permute-start | bytes 393224 | tf_op jit(solution)/shard_map/ppermute | solution.py:13
  66.7 5.6 %collective-permute-start.17 = (bf16[128,512]{0,1:T(8,128)(2,1)S(1)}, bf16[128,512]{0,1:T(8,128)(2,1)S(1)}, u32[]{:S(2)}, u32[]{:S(2)}) collective-permute-start(bf16[128,512]{0,1:T(8,128)(2,1)S(1)} %pad_maximum_fusion.25), channel_id=1, source_target_pairs={{0,1},{1,0},{2,3},{3,2},{4,5},{5,4},{6,7},{7,6},{8,9},{9,8},{10,11... | collective-permute-start | bytes 393224 | tf_op jit(solution)/shard_map/ppermute | solution.py:13
  72.5 8.5 %collective-permute-start.18 = (bf16[128,512]{0,1:T(8,128)(2,1)S(1)}, bf16[128,512]{0,1:T(8,128)(2,1)S(1)}, u32[]{:S(2)}, u32[]{:S(2)}) collective-permute-start(bf16[128,512]{0,1:T(8,128)(2,1)S(1)} %fusion.66), channel_id=1, source_target_pairs={{0,2},{1,3},{2,0},{3,1},{4,6},{5,7},{6,4},{7,5},{8,10},{9,11},{10,... | collective-permute-start | bytes 393224 | tf_op jit(solution)/shard_map/ppermute | solution.py:13
  81.1 5.0 %collective-permute-start.19 = (bf16[128,512]{0,1:T(8,128)(2,1)S(1)}, bf16[128,512]{0,1:T(8,128)(2,1)S(1)}, u32[]{:S(2)}, u32[]{:S(2)}) collective-permute-start(bf16[128,512]{0,1:T(8,128)(2,1)S(1)} %add_convert_fusion.2), channel_id=1, source_target_pairs={{0,8},{4,12},{8,0},{12,4},{16,24},{20,28},{24,16},{28,20},{1,9},{5... | collective-permute-start | bytes 393224 | tf_op jit(solution)/shard_map/ppermute | solution.py:13
  87.1 1.4 %collective-permute-start.20 = (bf16[128,512]{1,0:T(8,128)(2,1)S(1)}, bf16[128,512]{1,0:T(8,128)(2,1)S(1)}, u32[]{:S(2)}, u32[]{:S(2)}) collective-permute-start(bf16[128,512]{1,0:T(8,128)(2,1)S(1)} %fusion.6), channel_id=1, source_target_pairs={{0,4},{4,0},{8,12},{12,8},{16,20},{20,16},{24,28},{28,24},{1,5},{5... | collective-permute-start | bytes 393224 | tf_op jit(solution)/shard_map/ppermute | solution.py:13
  89.4 1.4 %collective-permute-start.21 = (bf16[128,512]{0,1:T(8,128)(2,1)S(1)}, bf16[128,512]{0,1:T(8,128)(2,1)S(1)}, u32[]{:S(2)}, u32[]{:S(2)}) collective-permute-start(bf16[128,512]{0,1:T(8,128)(2,1)S(1)} %dynamic-slice_convert_fusion.1), channel_id=1, source_target_pairs={{0,4},{4,0},{8,12},{12,8},{16,20},{20,16},{24,28},{28,24},{1,5},{5... | collective-permute-start | bytes 393224 | tf_op jit(solution)/shard_map/ppermute | solution.py:13
  90.8 8.8 %collective-permute-start.22 = (bf16[128,512]{0,1:T(8,128)(2,1)S(1)}, bf16[128,512]{0,1:T(8,128)(2,1)S(1)}, u32[]{:S(2)}, u32[]{:S(2)}) collective-permute-start(bf16[128,512]{0,1:T(8,128)(2,1)S(1)} %fusion.27), channel_id=1, source_target_pairs={{0,2},{1,3},{2,0},{3,1},{4,6},{5,7},{6,4},{7,5},{8,10},{9,11},{10,... | collective-permute-start | bytes 393224 | tf_op jit(solution)/shard_map/ppermute | solution.py:13
  99.7 1.4 %collective-permute-start.23 = (bf16[128,512]{0,1:T(8,128)(2,1)S(1)}, bf16[128,512]{0,1:T(8,128)(2,1)S(1)}, u32[]{:S(2)}, u32[]{:S(2)}) collective-permute-start(bf16[128,512]{0,1:T(8,128)(2,1)S(1)} %add_convert_fusion.1), channel_id=1, source_target_pairs={{0,4},{4,0},{8,12},{12,8},{16,20},{20,16},{24,28},{28,24},{1,5},{5... | collective-permute-start | bytes 393224 | tf_op jit(solution)/shard_map/ppermute | solution.py:13
  102.1 8.3 %collective-permute-start.24 = (bf16[256,128]{0,1:T(8,128)(2,1)S(1)}, bf16[256,128]{0,1:T(8,128)(2,1)S(1)}, u32[]{:S(2)}, u32[]{:S(2)}) collective-permute-start(bf16[256,128]{0,1:T(8,128)(2,1)S(1)} %constant_dynamic-slice_fusion.1), channel_id=1, source_target_pairs={{0,1},{1,0},{2,3},{3,2},{4,5},{5,4},{6,7},{7,6},{8,9},{9,8},{10,11... | collective-permute-start | bytes 196616 | tf_op jit(solution)/shard_map/ppermute | solution.py:13
  102.2 4.8 %collective-permute-start.25 = (bf16[128,128]{0,1:T(8,128)(2,1)S(1)}, bf16[128,128]{0,1:T(8,128)(2,1)S(1)}, u32[]{:S(2)}, u32[]{:S(2)}) collective-permute-start(bf16[128,128]{0,1:T(8,128)(2,1)S(1)} %get-tuple-element.79), channel_id=1, source_target_pairs={{0,1},{1,0},{2,3},{3,2},{4,5},{5,4},{6,7},{7,6},{8,9},{9,8},{10,11... | collective-permute-start | bytes 98312 | tf_op jit(solution)/shard_map/ppermute | solution.py:13
  104.3 5.1 %collective-permute-start.26 = (bf16[128,128]{0,1:T(8,128)(2,1)S(1)}, bf16[128,128]{0,1:T(8,128)(2,1)S(1)}, u32[]{:S(2)}, u32[]{:S(2)}) collective-permute-start(bf16[128,128]{0,1:T(8,128)(2,1)S(1)} %get-tuple-element.78), channel_id=1, source_target_pairs={{0,2},{1,3},{2,0},{3,1},{4,6},{5,7},{6,4},{7,5},{8,10},{9,11},{10,... | collective-permute-start | bytes 98312 | tf_op jit(solution)/shard_map/ppermute | solution.py:13
  104.7 5.7 %collective-permute-start.27 = (bf16[128,128]{0,1:T(8,128)(2,1)S(1)}, bf16[128,128]{0,1:T(8,128)(2,1)S(1)}, u32[]{:S(2)}, u32[]{:S(2)}) collective-permute-start(bf16[128,128]{0,1:T(8,128)(2,1)S(1)} %get-tuple-element.77), channel_id=1, source_target_pairs={{0,3},{1,2},{2,1},{3,0},{4,7},{5,6},{6,5},{7,4},{8,11},{9,10},{10,... | collective-permute-start | bytes 98312 | tf_op jit(solution)/shard_map/ppermute | solution.py:13

commit v8 on v7

--- a/solution.py
+++ b/solution.py
@@ -75,24 +75,6 @@
     wing = leaf_id // 2 % 2
     high_bits = range(1, front_count.bit_length() - 1)
 
-    def high_gather(*blocks):
-        for bit in high_bits:
-            received = traded(jnp.concatenate(blocks, 1), "front", 1 << bit)
-            ends = [sum(b.shape[1] for b in blocks[: i + 1]) for i in range(len(blocks))]
-            blocks = [
-                ordered(b, received[:, end - b.shape[1] : end], front_id >> bit & 1, 1)
-                for b, end in zip(blocks, ends)
-            ]
-        return blocks[0] if len(blocks) == 1 else blocks
-
-    def high_scatter(block):
-        for bit in reversed(high_bits):
-            upper = front_id >> bit & 1
-            block = part(block, upper, 2, 1).astype(F32) + traded(
-                part(block, 1 - upper, 2, 1).astype(BF16), "front", 1 << bit
-            ).astype(F32)
-        return block
-
     def side_scatter(block):
         return part(block, side, 2, 1) + traded(
             part(block, 1 - side, 2, 1).astype(BF16), "leaf", 1
@@ -111,12 +93,6 @@
 
     def pair_rows(block):
         return part(block, front_id // 2, front_count // 2, 1)
-
-    def high_pieces(own):
-        pieces = [own]
-        for bit in high_bits:
-            pieces += [traded(piece, "front", 1 << bit) for piece in pieces]
-        return pieces
 
     def in_order(blocks, axis):
         for bit in range(front_count.bit_length() - 1):
@@ -126,15 +102,6 @@
             ]
         return blocks[0]
 
-    def leaf_forward(vector, pieces):
-        return in_order([forward(vector, piece) for piece in pieces], 1).astype(BF16)
-
-    def leaf_adjoint(vector, pieces):
-        return sum(
-            adjoint(part(vector, front_id ^ i, front_count, 1), piece)
-            for i, piece in enumerate(pieces)
-        )
-
     def alternated(even, odd_ones):
         return [piece for pieces in zip(even, odd_ones) for piece in pieces]
 
@@ -143,9 +110,8 @@
     inverse2 = inverse_blocks[:, 3 * leaf_rows :]
     update0 = update_blocks[:, :leaf_rows]
     update1 = update_blocks[:, leaf_rows:]
-    inverse0, inverse1, inverse2, update0, update1 = together(
-        inverse0, inverse1, inverse2, update0, update1
-    )
+    update0, inverse0, inverse1 = together(update0, inverse0, inverse1)
+    inverse2, update1 = together(inverse2, update1)
 
     lists = jnp.concatenate([asm_owner[:, :, 0], asm_row], 0).astype(BF16)
     lists = jnp.pad(lists, ((0, 4), (0, 2 * own_rows + LEVELS * half_cols - own_rows)))
@@ -169,7 +135,7 @@
         return part(block1, (front_id ^ mask) // 2, front_count // 2, 1)
 
     inverse0_pair = traded(inverse0, "front", 1)
-    inverse1_pair = traded(after(inverse1, inverse0_pair), "front", 1)
+    inverse1_pair = traded(after(inverse1, inverse0_pair, block1), "front", 1)
     columns1 = [pair_columns(0)] + [
         traded(pair_columns(mask), "front", mask) for mask in range(2, front_count, 2)
     ]
@@ -258,6 +224,7 @@
     handed2 = stacked(below2[quarter:].astype(BF16))
     below2 = stacked(below2[:quarter])
     below2 = below2 + traded(handed2, "front", 1).astype(F32)
+    select1_late = lax.optimization_barrier(selector(after(lists, below2), 1))
     below2 = high_sum(below2).astype(BF16)
     own2 = flat(below2)
     other2 = flat(traded(below2, "leaf", 2))
@@ -265,7 +232,7 @@
         [ordered(own, other, wing, 0) for own, other in zip(own2, other2)], 1
     )
 
-    fetched1 = adjoint(below2, select1).astype(BF16)
+    fetched1 = adjoint(below2, select1_late).astype(BF16)
     carried1 = adjoint(traded(fetched1, "leaf", 1), columns1_side) + adjoint(fetched1, columns1)
     weights1 = (solved1_pair.astype(F32) - carried1).astype(BF16)
     select0_late = lax.optimization_barrier(selector(after(lists, weights1), 0))

time: 111 us -> 110 us (level)
  waiting for transfers between devices: 62.9 us -> 61.4 us
    ppermute x28, waiting for transfers between devices: 62.9 us -> 61.4 us  [traded(): lax.ppermute(shard, axis, [(i, i ^ mask) for i in range(lax.axis_size(axi...]
  transfers between devices with their start and end apart: 28 -> 28, of which waited for: 19 -> 19; matrix products, arithmetic and copies ran while one was open for 4% -> 5% of each run, Pallas kernels for 0% -> 0%
where the time goes in v8:
time: 110 us
  waiting for transfers between devices  61.4 us (56%)
  starting transfers between devices  33.1 us (30%)
  matrix products  6.29 us (6%)
  local copies, waits for them, and re-layouts  4.22 us (4%)
  other arithmetic  3.72 us (3%)
  between operations  1.18 us (1%)
    ppermute x28, waiting for transfers between devices, traded(): lax.ppermute(shard, axis, [(i, i ^ mask) for i in range(lax.axis_size(axi...  61.4 us
    ppermute x28, starting transfers between devices, traded(): lax.ppermute(shard, axis, [(i, i ^ mask) for i in range(lax.axis_size(axi...  33.1 us
    dot_general x21, matrix products, product(): lax.dot_general(left, right, (((left_dim,), (right_dim,)), ((), ())), pre...  6.29 us
  transfers between devices with their start and end apart: 28, of which 19 were waited for; matrix products, arithmetic and copies ran while one was open for 5% of the time, Pallas kernels for 0%

profile of v8, /device:TPU:0, one launch (start us, length us, event | category | flops | bytes accessed | tf_op | source)
XLA Modules:
  0.0 109.9 jit_solution(17887415146266376298)
XLA Ops:
  0.0 1.0 slice.273
  1.0 1.0 slice.274
  2.3 3.1 %collective-permute-start = (bf16[136,640]{1,0:T(8,128)(2,1)S(1)}, bf16[136,640]{1,0:T(8,128)(2,1)S(1)}, u32[]{:S(2)}, u32[]{:S(2)}) collective-permute-start(bf16[136,640]{1,0:T(8,128)(2,1)S(1)} %get-tuple-element.130), channel_id=1, source_target_pairs={{0,1},{1,0},{2,3},{3,2},{4,5},{5,4},{6,7},{7,6},{8,9},{9,8},{10,11... | collective-permute-start | bytes 522248 | tf_op jit(solution)/shard_map/ppermute | solution.py:13
  5.5 2.7 %collective-permute-start.1 = (bf16[136,640]{1,0:T(8,128)(2,1)S(1)}, bf16[136,640]{1,0:T(8,128)(2,1)S(1)}, u32[]{:S(2)}, u32[]{:S(2)}) collective-permute-start(bf16[136,640]{1,0:T(8,128)(2,1)S(1)} %get-tuple-element.131), channel_id=1, source_target_pairs={{0,2},{1,3},{2,0},{3,1},{4,6},{5,7},{6,4},{7,5},{8,10},{9,11},{10,... | collective-permute-start | bytes 522248 | tf_op jit(solution)/shard_map/ppermute | solution.py:13
  8.2 0.9 collective-permute-start.3
  9.1 0.3 copy.30
  9.3 0.7 slice-done.2
  10.3 9.2 %collective-permute-done.3 = bf16[128,512]{1,0:T(8,128)(2,1)S(1)} collective-permute-done((bf16[128,512]{1,0:T(8,128)(2,1)S(1)}, bf16[128,512]{1,0:T(8,128)(2,1)S(1)}, u32[]{:S(2)}, u32[]{:S(2)}) %collective-permute-start.3) | collective-permute-done | bytes 131104 | tf_op jit(solution)/shard_map/ppermute | solution.py:13
  19.5 2.5 %collective-permute-start.6 = (bf16[128,1024]{1,0:T(8,128)(2,1)S(1)}, bf16[128,1024]{1,0:T(8,128)(2,1)S(1)}, u32[]{:S(2)}, u32[]{:S(2)}) collective-permute-start(bf16[128,1024]{1,0:T(8,128)(2,1)S(1)} %slice.274), channel_id=1, source_target_pairs={{0,1},{1,0},{2,3},{3,2},{4,5},{5,4},{6,7},{7,6},{8,9},{9,8},{10,11... | collective-permute-start | bytes 786440 | tf_op jit(solution)/shard_map/ppermute | solution.py:13
  22.0 2.6 %collective-permute-start.8 = (bf16[256,256]{1,0:T(8,128)(2,1)S(1)}, bf16[256,256]{1,0:T(8,128)(2,1)S(1)}, u32[]{:S(2)}, u32[]{:S(2)}) collective-permute-start(bf16[256,256]{1,0:T(8,128)(2,1)S(1)} %get-tuple-element.92), channel_id=1, source_target_pairs={{0,2},{1,3},{2,0},{3,1},{4,6},{5,7},{6,4},{7,5},{8,10},{9,11},{10,... | collective-permute-start | bytes 393224 | tf_op jit(solution)/shard_map/ppermute | solution.py:13
  25.3 0.2 fusion.99
  25.6 0.6 collective-permute-start.4
  26.5 4.5 %collective-permute-done.8 = bf16[256,256]{1,0:T(8,128)(2,1)S(1)} collective-permute-done((bf16[256,256]{1,0:T(8,128)(2,1)S(1)}, bf16[256,256]{1,0:T(8,128)(2,1)S(1)}, u32[]{:S(2)}, u32[]{:S(2)}) %collective-permute-start.8) | collective-permute-done | bytes 131104 | tf_op jit(solution)/shard_map/ppermute | solution.py:13
  31.1 4.1 %collective-permute-start.9 = (bf16[512,256]{1,0:T(8,128)(2,1)S(1)}, bf16[512,256]{1,0:T(8,128)(2,1)S(1)}, u32[]{:S(2)}, u32[]{:S(2)}) collective-permute-start(bf16[512,256]{1,0:T(8,128)(2,1)S(1)} %pad_maximum_fusion.9), channel_id=1, source_target_pairs={{0,1},{1,0},{2,3},{3,2},{4,5},{5,4},{6,7},{7,6},{8,9},{9,8},{10,11... | collective-permute-start | bytes 786440 | tf_op jit(solution)/shard_map/ppermute | solution.py:13
  35.3 0.5 fusion.100
  36.0 1.6 %collective-permute-start.13 = (bf16[256,1024]{0,1:T(8,128)(2,1)S(1)}, bf16[256,1024]{0,1:T(8,128)(2,1)S(1)}, u32[]{:S(2)}, u32[]{:S(2)}) collective-permute-start(bf16[256,1024]{0,1:T(8,128)(2,1)S(1)} %pad_maximum_fusion), channel_id=1, source_target_pairs={{0,8},{4,12},{8,0},{12,4},{16,24},{20,28},{24,16},{28,20},{1,9},{5... | collective-permute-start | bytes 1572872 | tf_op jit(solution)/shard_map/ppermute | solution.py:13
  37.5 2.0 %collective-permute-done.9 = bf16[512,256]{1,0:T(8,128)(2,1)S(1)} collective-permute-done((bf16[512,256]{1,0:T(8,128)(2,1)S(1)}, bf16[512,256]{1,0:T(8,128)(2,1)S(1)}, u32[]{:S(2)}, u32[]{:S(2)}) %collective-permute-start.9) | collective-permute-done | bytes 262176 | tf_op jit(solution)/shard_map/ppermute | solution.py:13
  39.6 0.2 fusion.77
  39.8 0.2 fusion.76
  40.1 0.2 convolution_convert_fusion.2
  40.5 1.3 %collective-permute-done.10 = bf16[128,512]{1,0:T(8,128)(2,1)S(1)} collective-permute-done((bf16[128,512]{1,0:T(8,128)(2,1)S(1)}, bf16[128,512]{1,0:T(8,128)(2,1)S(1)}, u32[]{:S(2)}, u32[]{:S(2)}) %collective-permute-start.10) | collective-permute-done | bytes 131104 | tf_op jit(solution)/shard_map/ppermute | solution.py:13
  41.8 0.2 fusion.24
  42.0 2.0 %collective-permute-start.11 = (bf16[128,512]{1,0:T(8,128)(2,1)S(1)}, bf16[128,512]{1,0:T(8,128)(2,1)S(1)}, u32[]{:S(2)}, u32[]{:S(2)}) collective-permute-start(bf16[128,512]{1,0:T(8,128)(2,1)S(1)} %get-tuple-element.147), channel_id=1, source_target_pairs={{0,2},{1,3},{2,0},{3,1},{4,6},{5,7},{6,4},{7,5},{8,10},{9,11},{10,... | collective-permute-start | bytes 393224 | tf_op jit(solution)/shard_map/ppermute | solution.py:13
  44.1 7.3 %collective-permute-done.11 = bf16[128,512]{1,0:T(8,128)(2,1)S(1)} collective-permute-done((bf16[128,512]{1,0:T(8,128)(2,1)S(1)}, bf16[128,512]{1,0:T(8,128)(2,1)S(1)}, u32[]{:S(2)}, u32[]{:S(2)}) %collective-permute-start.11) | collective-permute-done | bytes 131104 | tf_op jit(solution)/shard_map/ppermute | solution.py:13
  51.4 0.5 fusion.4
  52.2 1.6 %collective-permute-start.14 = (bf16[128,512]{0,1:T(8,128)(2,1)S(1)}, bf16[128,512]{0,1:T(8,128)(2,1)S(1)}, u32[]{:S(2)}, u32[]{:S(2)}) collective-permute-start(bf16[128,512]{0,1:T(8,128)(2,1)S(1)} %pad_maximum_fusion.24), channel_id=1, source_target_pairs={{0,8},{4,12},{8,0},{12,4},{16,24},{20,28},{24,16},{28,20},{1,9},{5... | collective-permute-start | bytes 393224 | tf_op jit(solution)/shard_map/ppermute | solution.py:13
  53.7 0.2 constant_dynamic-slice_fusion
  53.9 3.3 %collective-permute-done.14 = bf16[128,512]{0,1:T(8,128)(2,1)S(1)} collective-permute-done((bf16[128,512]{0,1:T(8,128)(2,1)S(1)}, bf16[128,512]{0,1:T(8,128)(2,1)S(1)}, u32[]{:S(2)}, u32[]{:S(2)}) %collective-permute-start.14) | collective-permute-done | bytes 131104 | tf_op jit(solution)/shard_map/ppermute | solution.py:13
  57.3 1.8 %collective-permute-start.15 = (bf16[128,512]{0,1:T(8,128)(2,1)S(1)}, bf16[128,512]{0,1:T(8,128)(2,1)S(1)}, u32[]{:S(2)}, u32[]{:S(2)}) collective-permute-start(bf16[128,512]{0,1:T(8,128)(2,1)S(1)} %fusion.11), channel_id=1, source_target_pairs={{0,1},{1,0},{2,3},{3,2},{4,5},{5,4},{6,7},{7,6},{8,9},{9,8},{10,11... | collective-permute-start | bytes 393224 | tf_op jit(solution)/shard_map/ppermute | solution.py:13
  59.2 3.1 %collective-permute-done.15 = bf16[128,512]{0,1:T(8,128)(2,1)S(1)} collective-permute-done((bf16[128,512]{0,1:T(8,128)(2,1)S(1)}, bf16[128,512]{0,1:T(8,128)(2,1)S(1)}, u32[]{:S(2)}, u32[]{:S(2)}) %collective-permute-start.15) | collective-permute-done | bytes 131104 | tf_op jit(solution)/shard_map/ppermute | solution.py:13
  62.5 0.4 fusion.101
  62.9 0.4 fusion.102
  63.4 1.3 %collective-permute-done.16 = bf16[128,512]{1,0:T(8,128)(2,1)S(1)} collective-permute-done((bf16[128,512]{1,0:T(8,128)(2,1)S(1)}, bf16[128,512]{1,0:T(8,128)(2,1)S(1)}, u32[]{:S(2)}, u32[]{:S(2)}) %collective-permute-start.16) | collective-permute-done | bytes 131104 | tf_op jit(solution)/shard_map/ppermute | solution.py:13
  64.7 0.3 fusion.35
  65.0 0.3 fusion.103
  65.6 1.8 %collective-permute-start.17 = (bf16[128,512]{0,1:T(8,128)(2,1)S(1)}, bf16[128,512]{0,1:T(8,128)(2,1)S(1)}, u32[]{:S(2)}, u32[]{:S(2)}) collective-permute-start(bf16[128,512]{0,1:T(8,128)(2,1)S(1)} %pad_maximum_fusion.26), channel_id=1, source_target_pairs={{0,1},{1,0},{2,3},{3,2},{4,5},{5,4},{6,7},{7,6},{8,9},{9,8},{10,11... | collective-permute-start | bytes 393224 | tf_op jit(solution)/shard_map/ppermute | solution.py:13
  67.4 3.8 %collective-permute-done.17 = bf16[128,512]{0,1:T(8,128)(2,1)S(1)} collective-permute-done((bf16[128,512]{0,1:T(8,128)(2,1)S(1)}, bf16[128,512]{0,1:T(8,128)(2,1)S(1)}, u32[]{:S(2)}, u32[]{:S(2)}) %collective-permute-start.17) | collective-permute-done | bytes 131104 | tf_op jit(solution)/shard_map/ppermute | solution.py:13
  71.3 0.9 collective-permute-start.18
  72.3 0.4 fusion.2
  72.7 7.1 %collective-permute-done.18 = bf16[128,512]{0,1:T(8,128)(2,1)S(1)} collective-permute-done((bf16[128,512]{0,1:T(8,128)(2,1)S(1)}, bf16[128,512]{0,1:T(8,128)(2,1)S(1)}, u32[]{:S(2)}, u32[]{:S(2)}) %collective-permute-start.18) | collective-permute-done | bytes 131104 | tf_op jit(solution)/shard_map/ppermute | solution.py:13
  79.9 1.6 %collective-permute-start.19 = (bf16[128,512]{0,1:T(8,128)(2,1)S(1)}, bf16[128,512]{0,1:T(8,128)(2,1)S(1)}, u32[]{:S(2)}, u32[]{:S(2)}) collective-permute-start(bf16[128,512]{0,1:T(8,128)(2,1)S(1)} %add_convert_fusion.2), channel_id=1, source_target_pairs={{0,8},{4,12},{8,0},{12,4},{16,24},{20,28},{24,16},{28,20},{1,9},{5... | collective-permute-start | bytes 393224 | tf_op jit(solution)/shard_map/ppermute | solution.py:13
  81.5 3.3 %collective-permute-done.19 = bf16[128,512]{0,1:T(8,128)(2,1)S(1)} collective-permute-done((bf16[128,512]{0,1:T(8,128)(2,1)S(1)}, bf16[128,512]{0,1:T(8,128)(2,1)S(1)}, u32[]{:S(2)}, u32[]{:S(2)}) %collective-permute-start.19) | collective-permute-done | bytes 131104 | tf_op jit(solution)/shard_map/ppermute | solution.py:13
  85.3 0.4 convolution_convert_fusion.1
  85.8 0.3 fusion.44
  86.0 0.3 fusion.36
  86.3 0.8 collective-permute-done.20
  87.1 0.3 fusion.7
  87.4 0.3 fusion.50
  87.7 0.3 convolution_add_fusion
  88.0 0.2 collective-permute-start.21
  88.2 1.2 %collective-permute-done.21 = bf16[128,512]{0,1:T(8,128)(2,1)S(1)} collective-permute-done((bf16[128,512]{0,1:T(8,128)(2,1)S(1)}, bf16[128,512]{0,1:T(8,128)(2,1)S(1)}, u32[]{:S(2)}, u32[]{:S(2)}) %collective-permute-start.21) | collective-permute-done | bytes 131104 | tf_op jit(solution)/shard_map/ppermute | solution.py:13
  89.5 0.4 fusion.3
  90.0 8.2 %collective-permute-done.22 = bf16[128,512]{0,1:T(8,128)(2,1)S(1)} collective-permute-done((bf16[128,512]{0,1:T(8,128)(2,1)S(1)}, bf16[128,512]{0,1:T(8,128)(2,1)S(1)}, u32[]{:S(2)}, u32[]{:S(2)}) %collective-permute-start.22) | collective-permute-done | bytes 131104 | tf_op jit(solution)/shard_map/ppermute | solution.py:13
  98.4 1.3 %collective-permute-done.23 = bf16[128,512]{0,1:T(8,128)(2,1)S(1)} collective-permute-done((bf16[128,512]{0,1:T(8,128)(2,1)S(1)}, bf16[128,512]{0,1:T(8,128)(2,1)S(1)}, u32[]{:S(2)}, u32[]{:S(2)}) %collective-permute-start.23) | collective-permute-done | bytes 131104 | tf_op jit(solution)/shard_map/ppermute | solution.py:13
  99.7 0.5 fusion.8
  100.2 0.2 fusion.47
  100.4 0.2 convolution_add_fusion.2
  100.8 2.1 %collective-permute-start.25 = (bf16[128,128]{0,1:T(8,128)(2,1)S(1)}, bf16[128,128]{0,1:T(8,128)(2,1)S(1)}, u32[]{:S(2)}, u32[]{:S(2)}) collective-permute-start(bf16[128,128]{0,1:T(8,128)(2,1)S(1)} %get-tuple-element.83), channel_id=1, source_target_pairs={{0,1},{1,0},{2,3},{3,2},{4,5},{5,4},{6,7},{7,6},{8,9},{9,8},{10,11... | collective-permute-start | bytes 98312 | tf_op jit(solution)/shard_map/ppermute | solution.py:13
  102.9 0.4 collective-permute-start.26
  103.3 2.1 %collective-permute-start.27 = (bf16[128,128]{0,1:T(8,128)(2,1)S(1)}, bf16[128,128]{0,1:T(8,128)(2,1)S(1)}, u32[]{:S(2)}, u32[]{:S(2)}) collective-permute-start(bf16[128,128]{0,1:T(8,128)(2,1)S(1)} %get-tuple-element.81), channel_id=1, source_target_pairs={{0,3},{1,2},{2,1},{3,0},{4,7},{5,6},{6,5},{7,4},{8,11},{9,10},{10,... | collective-permute-start | bytes 98312 | tf_op jit(solution)/shard_map/ppermute | solution.py:13
  105.3 0.3 collective-permute-done.25
  105.6 2.3 %collective-permute-done.26 = bf16[128,128]{0,1:T(8,128)(2,1)S(1)} collective-permute-done((bf16[128,128]{0,1:T(8,128)(2,1)S(1)}, bf16[128,128]{0,1:T(8,128)(2,1)S(1)}, u32[]{:S(2)}, u32[]{:S(2)}) %collective-permute-start.26) | collective-permute-done | bytes 32800 | tf_op jit(solution)/shard_map/ppermute | solution.py:13
  108.0 1.0 collective-permute-done.27
  109.1 0.8 pad_maximum_fusion.1
  (133 shorter events, 4.1 us)
Async XLA Ops:
  0.0 2.3 %slice-start.1 = ((bf16[128,1536]{1,0:T(8,128)(2,1)}), bf16[128,512]{1,0:T(8,128)(2,1)S(1)}, s32[]{:S(2)}) async-start(bf16[128,1536]{1,0:T(8,128)(2,1)} %param.7), calls=%async_computation.1 | async-start | bytes 262144 | tf_op jit(solution)/shard_map/slice | solution.py:111
  0.0 2.1 %copy-start.5 = (s32[2,128]{1,0:T(2,128)S(1)}, s32[2,128]{1,0:T(2,128)}, u32[]{:S(2)}) copy-start(s32[2,128]{1,0:T(2,128)} %param.9) | copy-start | bytes 3076
  0.0 2.1 %copy-start.6 = (s32[2,128,1]{1,2,0:T(1,128)S(1)}, s32[2,128,1]{1,2,0:T(1,128)}, u32[]{:S(2)}) copy-start(s32[2,128,1]{1,2,0:T(1,128)} %param.8) | copy-start | bytes 3076
  0.0 2.1 %copy-start = (bf16[3,128,256]{2,1,0:T(8,128)(2,1)S(1)}, bf16[3,128,256]{2,1,0:T(8,128)(2,1)}, u32[]{:S(2)}) copy-start(bf16[3,128,256]{2,1,0:T(8,128)(2,1)} %param.5) | copy-start | bytes 589828
  2.3 22.3 %collective-permute-start = (bf16[136,640]{1,0:T(8,128)(2,1)S(1)}, bf16[136,640]{1,0:T(8,128)(2,1)S(1)}, u32[]{:S(2)}, u32[]{:S(2)}) collective-permute-start(bf16[136,640]{1,0:T(8,128)(2,1)S(1)} %get-tuple-element.130), channel_id=1, source_target_pairs={{0,1},{1,0},{2,3},{3,2},{4,5},{5,4},{6,7},{7,6},{8,9},{9,8},{10,11... | collective-permute-start | bytes 522248 | tf_op jit(solution)/shard_map/ppermute | solution.py:13
  5.5 3.6 %slice-start = ((bf16[128,3584]{1,0:T(8,128)(2,1)}), bf16[128,2048]{1,0:T(8,128)(2,1)S(1)}, s32[]{:S(2)}) async-start(bf16[128,3584]{1,0:T(8,128)(2,1)} %param.6), calls=%async_computation | async-start | bytes 1048576 | tf_op jit(solution)/shard_map/slice | solution.py:110
  5.5 19.1 %collective-permute-start.1 = (bf16[136,640]{1,0:T(8,128)(2,1)S(1)}, bf16[136,640]{1,0:T(8,128)(2,1)S(1)}, u32[]{:S(2)}, u32[]{:S(2)}) collective-permute-start(bf16[136,640]{1,0:T(8,128)(2,1)S(1)} %get-tuple-element.131), channel_id=1, source_target_pairs={{0,2},{1,3},{2,0},{3,1},{4,6},{5,7},{6,4},{7,5},{8,10},{9,11},{10,... | collective-permute-start | bytes 522248 | tf_op jit(solution)/shard_map/ppermute | solution.py:13
  8.2 16.5 %collective-permute-start.2 = (bf16[136,640]{1,0:T(8,128)(2,1)S(1)}, bf16[136,640]{1,0:T(8,128)(2,1)S(1)}, u32[]{:S(2)}, u32[]{:S(2)}) collective-permute-start(bf16[136,640]{1,0:T(8,128)(2,1)S(1)} %get-tuple-element.129), channel_id=1, source_target_pairs={{0,3},{1,2},{2,1},{3,0},{4,7},{5,6},{6,5},{7,4},{8,11},{9,10},{10,... | collective-permute-start | bytes 522248 | tf_op jit(solution)/shard_map/ppermute | solution.py:13
  8.2 11.3 %collective-permute-start.3 = (bf16[128,512]{1,0:T(8,128)(2,1)S(1)}, bf16[128,512]{1,0:T(8,128)(2,1)S(1)}, u32[]{:S(2)}, u32[]{:S(2)}) collective-permute-start(bf16[128,512]{1,0:T(8,128)(2,1)S(1)} %slice.273), channel_id=1, source_target_pairs={{0,1},{1,0},{2,3},{3,2},{4,5},{5,4},{6,7},{7,6},{8,9},{9,8},{10,11... | collective-permute-start | bytes 393224 | tf_op jit(solution)/shard_map/ppermute | solution.py:13
  9.1 0.9 slice-start.2
  10.0 11.9 %collective-permute-start.5 = (bf16[128,512]{1,0:T(8,128)(2,1)S(1)}, bf16[128,512]{1,0:T(8,128)(2,1)S(1)}, u32[]{:S(2)}, u32[]{:S(2)}) collective-permute-start(bf16[128,512]{1,0:T(8,128)(2,1)S(1)} %get-tuple-element.94), channel_id=1, source_target_pairs={{0,4},{4,0},{8,12},{12,8},{16,20},{20,16},{24,28},{28,24},{1,5},{5... | collective-permute-start | bytes 393224 | tf_op jit(solution)/shard_map/ppermute | solution.py:13
  19.5 15.8 %collective-permute-start.6 = (bf16[128,1024]{1,0:T(8,128)(2,1)S(1)}, bf16[128,1024]{1,0:T(8,128)(2,1)S(1)}, u32[]{:S(2)}, u32[]{:S(2)}) collective-permute-start(bf16[128,1024]{1,0:T(8,128)(2,1)S(1)} %slice.274), channel_id=1, source_target_pairs={{0,1},{1,0},{2,3},{3,2},{4,5},{5,4},{6,7},{7,6},{8,9},{9,8},{10,11... | collective-permute-start | bytes 786440 | tf_op jit(solution)/shard_map/ppermute | solution.py:13
  22.0 9.1 %collective-permute-start.8 = (bf16[256,256]{1,0:T(8,128)(2,1)S(1)}, bf16[256,256]{1,0:T(8,128)(2,1)S(1)}, u32[]{:S(2)}, u32[]{:S(2)}) collective-permute-start(bf16[256,256]{1,0:T(8,128)(2,1)S(1)} %get-tuple-element.92), channel_id=1, source_target_pairs={{0,2},{1,3},{2,0},{3,1},{4,6},{5,7},{6,4},{7,5},{8,10},{9,11},{10,... | collective-permute-start | bytes 393224 | tf_op jit(solution)/shard_map/ppermute | solution.py:13
  25.3 1.1 copy-start.1
  25.6 9.7 %collective-permute-start.4 = (bf16[128,512]{1,0:T(8,128)(2,1)S(1)}, bf16[128,512]{1,0:T(8,128)(2,1)S(1)}, u32[]{:S(2)}, u32[]{:S(2)}) collective-permute-start(bf16[128,512]{1,0:T(8,128)(2,1)S(1)} %get-tuple-element.143), channel_id=1, source_target_pairs={{0,2},{1,3},{2,0},{3,1},{4,6},{5,7},{6,4},{7,5},{8,10},{9,11},{10,... | collective-permute-start | bytes 393224 | tf_op jit(solution)/shard_map/ppermute | solution.py:13
  26.3 9.6 %collective-permute-start.12 = (bf16[128,1024]{0,1:T(8,128)(2,1)S(1)}, bf16[128,1024]{0,1:T(8,128)(2,1)S(1)}, u32[]{:S(2)}, u32[]{:S(2)}) collective-permute-start(bf16[128,1024]{0,1:T(8,128)(2,1)S(1)} %get-tuple-element.76), channel_id=1, source_target_pairs={{0,4},{4,0},{8,12},{12,8},{16,20},{20,16},{24,28},{28,24},{1,5},{5... | collective-permute-start | bytes 786440 | tf_op jit(solution)/shard_map/ppermute | solution.py:13
  31.1 8.4 %collective-permute-start.9 = (bf16[512,256]{1,0:T(8,128)(2,1)S(1)}, bf16[512,256]{1,0:T(8,128)(2,1)S(1)}, u32[]{:S(2)}, u32[]{:S(2)}) collective-permute-start(bf16[512,256]{1,0:T(8,128)(2,1)S(1)} %pad_maximum_fusion.9), channel_id=1, source_target_pairs={{0,1},{1,0},{2,3},{3,2},{4,5},{5,4},{6,7},{7,6},{8,9},{9,8},{10,11... | collective-permute-start | bytes 786440 | tf_op jit(solution)/shard_map/ppermute | solution.py:13
  35.8 3.8 %collective-permute-start.7 = (bf16[128,1024]{0,1:T(8,128)(2,1)S(1)}, bf16[128,1024]{0,1:T(8,128)(2,1)S(1)}, u32[]{:S(2)}, u32[]{:S(2)}) collective-permute-start(bf16[128,1024]{0,1:T(8,128)(2,1)S(1)} %get-tuple-element.145), channel_id=1, source_target_pairs={{0,4},{4,0},{8,12},{12,8},{16,20},{20,16},{24,28},{28,24},{1,5},{5... | collective-permute-start | bytes 786440 | tf_op jit(solution)/shard_map/ppermute | solution.py:13
  36.0 15.4 %collective-permute-start.13 = (bf16[256,1024]{0,1:T(8,128)(2,1)S(1)}, bf16[256,1024]{0,1:T(8,128)(2,1)S(1)}, u32[]{:S(2)}, u32[]{:S(2)}) collective-permute-start(bf16[256,1024]{0,1:T(8,128)(2,1)S(1)} %pad_maximum_fusion), channel_id=1, source_target_pairs={{0,8},{4,12},{8,0},{12,4},{16,24},{20,28},{24,16},{28,20},{1,9},{5... | collective-permute-start | bytes 1572872 | tf_op jit(solution)/shard_map/ppermute | solution.py:13
  40.1 1.9 %copy-start.3 = (bf16[128,256]{0,1:T(8,128)(2,1)}, bf16[128,256]{0,1:T(8,128)(2,1)S(1)}, u32[]{:S(2)}) copy-start(bf16[128,256]{0,1:T(8,128)(2,1)S(1)} %fusion.30) | copy-start | bytes 196612
  40.3 1.4 %collective-permute-start.10 = (bf16[128,512]{1,0:T(8,128)(2,1)S(1)}, bf16[128,512]{1,0:T(8,128)(2,1)S(1)}, u32[]{:S(2)}, u32[]{:S(2)}) collective-permute-start(bf16[128,512]{1,0:T(8,128)(2,1)S(1)} %convolution_convert_fusion.2), channel_id=1, source_target_pairs={{0,4},{4,0},{8,12},{12,8},{16,20},{20,16},{24,28},{28,24},{1,5},{5... | collective-permute-start | bytes 393224 | tf_op jit(solution)/shard_map/ppermute | solution.py:13
  42.0 9.3 %collective-permute-start.11 = (bf16[128,512]{1,0:T(8,128)(2,1)S(1)}, bf16[128,512]{1,0:T(8,128)(2,1)S(1)}, u32[]{:S(2)}, u32[]{:S(2)}) collective-permute-start(bf16[128,512]{1,0:T(8,128)(2,1)S(1)} %get-tuple-element.147), channel_id=1, source_target_pairs={{0,2},{1,3},{2,0},{3,1},{4,6},{5,7},{6,4},{7,5},{8,10},{9,11},{10,... | collective-permute-start | bytes 393224 | tf_op jit(solution)/shard_map/ppermute | solution.py:13
  52.2 5.0 %collective-permute-start.14 = (bf16[128,512]{0,1:T(8,128)(2,1)S(1)}, bf16[128,512]{0,1:T(8,128)(2,1)S(1)}, u32[]{:S(2)}, u32[]{:S(2)}) collective-permute-start(bf16[128,512]{0,1:T(8,128)(2,1)S(1)} %pad_maximum_fusion.24), channel_id=1, source_target_pairs={{0,8},{4,12},{8,0},{12,4},{16,24},{20,28},{24,16},{28,20},{1,9},{5... | collective-permute-start | bytes 393224 | tf_op jit(solution)/shard_map/ppermute | solution.py:13
  57.3 5.0 %collective-permute-start.15 = (bf16[128,512]{0,1:T(8,128)(2,1)S(1)}, bf16[128,512]{0,1:T(8,128)(2,1)S(1)}, u32[]{:S(2)}, u32[]{:S(2)}) collective-permute-start(bf16[128,512]{0,1:T(8,128)(2,1)S(1)} %fusion.11), channel_id=1, source_target_pairs={{0,1},{1,0},{2,3},{3,2},{4,5},{5,4},{6,7},{7,6},{8,9},{9,8},{10,11... | collective-permute-start | bytes 393224 | tf_op jit(solution)/shard_map/ppermute | solution.py:13
  63.3 1.4 %collective-permute-start.16 = (bf16[128,512]{1,0:T(8,128)(2,1)S(1)}, bf16[128,512]{1,0:T(8,128)(2,1)S(1)}, u32[]{:S(2)}, u32[]{:S(2)}) collective-permute-start(bf16[128,512]{1,0:T(8,128)(2,1)S(1)} %pad_maximum_fusion.25), channel_id=1, source_target_pairs={{0,4},{4,0},{8,12},{12,8},{16,20},{20,16},{24,28},{28,24},{1,5},{5... | collective-permute-start | bytes 393224 | tf_op jit(solution)/shard_map/ppermute | solution.py:13
  65.6 5.6 %collective-permute-start.17 = (bf16[128,512]{0,1:T(8,128)(2,1)S(1)}, bf16[128,512]{0,1:T(8,128)(2,1)S(1)}, u32[]{:S(2)}, u32[]{:S(2)}) collective-permute-start(bf16[128,512]{0,1:T(8,128)(2,1)S(1)} %pad_maximum_fusion.26), channel_id=1, source_target_pairs={{0,1},{1,0},{2,3},{3,2},{4,5},{5,4},{6,7},{7,6},{8,9},{9,8},{10,11... | collective-permute-start | bytes 393224 | tf_op jit(solution)/shard_map/ppermute | solution.py:13
  71.3 8.5 %collective-permute-start.18 = (bf16[128,512]{0,1:T(8,128)(2,1)S(1)}, bf16[128,512]{0,1:T(8,128)(2,1)S(1)}, u32[]{:S(2)}, u32[]{:S(2)}) collective-permute-start(bf16[128,512]{0,1:T(8,128)(2,1)S(1)} %get-tuple-element.67), channel_id=1, source_target_pairs={{0,2},{1,3},{2,0},{3,1},{4,6},{5,7},{6,4},{7,5},{8,10},{9,11},{10,... | collective-permute-start | bytes 393224 | tf_op jit(solution)/shard_map/ppermute | solution.py:13
  79.9 5.0 %collective-permute-start.19 = (bf16[128,512]{0,1:T(8,128)(2,1)S(1)}, bf16[128,512]{0,1:T(8,128)(2,1)S(1)}, u32[]{:S(2)}, u32[]{:S(2)}) collective-permute-start(bf16[128,512]{0,1:T(8,128)(2,1)S(1)} %add_convert_fusion.2), channel_id=1, source_target_pairs={{0,8},{4,12},{8,0},{12,4},{16,24},{20,28},{24,16},{28,20},{1,9},{5... | collective-permute-start | bytes 393224 | tf_op jit(solution)/shard_map/ppermute | solution.py:13
  85.7 1.4 %copy-start.4 = (bf16[128,256]{0,1:T(8,128)(2,1)S(1)}, bf16[128,256]{0,1:T(8,128)(2,1)}, u32[]{:S(2)}) copy-start(bf16[128,256]{0,1:T(8,128)(2,1)} %copy-done.3) | copy-start | bytes 196612
  85.7 1.4 %collective-permute-start.20 = (bf16[128,512]{1,0:T(8,128)(2,1)S(1)}, bf16[128,512]{1,0:T(8,128)(2,1)S(1)}, u32[]{:S(2)}, u32[]{:S(2)}) collective-permute-start(bf16[128,512]{1,0:T(8,128)(2,1)S(1)} %convolution_convert_fusion.1), channel_id=1, source_target_pairs={{0,4},{4,0},{8,12},{12,8},{16,20},{20,16},{24,28},{28,24},{1,5},{5... | collective-permute-start | bytes 393224 | tf_op jit(solution)/shard_map/ppermute | solution.py:13
  88.0 1.4 %collective-permute-start.21 = (bf16[128,512]{0,1:T(8,128)(2,1)S(1)}, bf16[128,512]{0,1:T(8,128)(2,1)S(1)}, u32[]{:S(2)}, u32[]{:S(2)}) collective-permute-start(bf16[128,512]{0,1:T(8,128)(2,1)S(1)} %dynamic-slice_convert_fusion.1), channel_id=1, source_target_pairs={{0,4},{4,0},{8,12},{12,8},{16,20},{20,16},{24,28},{28,24},{1,5},{5... | collective-permute-start | bytes 393224 | tf_op jit(solution)/shard_map/ppermute | solution.py:13
  89.4 8.8 %collective-permute-start.22 = (bf16[128,512]{0,1:T(8,128)(2,1)S(1)}, bf16[128,512]{0,1:T(8,128)(2,1)S(1)}, u32[]{:S(2)}, u32[]{:S(2)}) collective-permute-start(bf16[128,512]{0,1:T(8,128)(2,1)S(1)} %fusion.25), channel_id=1, source_target_pairs={{0,2},{1,3},{2,0},{3,1},{4,6},{5,7},{6,4},{7,5},{8,10},{9,11},{10,... | collective-permute-start | bytes 393224 | tf_op jit(solution)/shard_map/ppermute | solution.py:13
  89.5 10.1 %copy-start.2 = (bf16[128,256]{0,1:T(8,128)(2,1)S(1)}, bf16[128,256]{0,1:T(8,128)(2,1)}, u32[]{:S(2)}) copy-start(bf16[128,256]{0,1:T(8,128)(2,1)} %copy-done.1) | copy-start | bytes 196612
  98.2 1.4 %collective-permute-start.23 = (bf16[128,512]{0,1:T(8,128)(2,1)S(1)}, bf16[128,512]{0,1:T(8,128)(2,1)S(1)}, u32[]{:S(2)}, u32[]{:S(2)}) collective-permute-start(bf16[128,512]{0,1:T(8,128)(2,1)S(1)} %add_convert_fusion.1), channel_id=1, source_target_pairs={{0,4},{4,0},{8,12},{12,8},{16,20},{20,16},{24,28},{28,24},{1,5},{5... | collective-permute-start | bytes 393224 | tf_op jit(solution)/shard_map/ppermute | solution.py:13
  100.7 8.3 %collective-permute-start.24 = (bf16[256,128]{0,1:T(8,128)(2,1)S(1)}, bf16[256,128]{0,1:T(8,128)(2,1)S(1)}, u32[]{:S(2)}, u32[]{:S(2)}) collective-permute-start(bf16[256,128]{0,1:T(8,128)(2,1)S(1)} %constant_dynamic-slice_fusion.1), channel_id=1, source_target_pairs={{0,1},{1,0},{2,3},{3,2},{4,5},{5,4},{6,7},{7,6},{8,9},{9,8},{10,11... | collective-permute-start | bytes 196616 | tf_op jit(solution)/shard_map/ppermute | solution.py:13
  100.8 4.8 %collective-permute-start.25 = (bf16[128,128]{0,1:T(8,128)(2,1)S(1)}, bf16[128,128]{0,1:T(8,128)(2,1)S(1)}, u32[]{:S(2)}, u32[]{:S(2)}) collective-permute-start(bf16[128,128]{0,1:T(8,128)(2,1)S(1)} %get-tuple-element.83), channel_id=1, source_target_pairs={{0,1},{1,0},{2,3},{3,2},{4,5},{5,4},{6,7},{7,6},{8,9},{9,8},{10,11... | collective-permute-start | bytes 98312 | tf_op jit(solution)/shard_map/ppermute | solution.py:13
  102.9 5.1 %collective-permute-start.26 = (bf16[128,128]{0,1:T(8,128)(2,1)S(1)}, bf16[128,128]{0,1:T(8,128)(2,1)S(1)}, u32[]{:S(2)}, u32[]{:S(2)}) collective-permute-start(bf16[128,128]{0,1:T(8,128)(2,1)S(1)} %get-tuple-element.82), channel_id=1, source_target_pairs={{0,2},{1,3},{2,0},{3,1},{4,6},{5,7},{6,4},{7,5},{8,10},{9,11},{10,... | collective-permute-start | bytes 98312 | tf_op jit(solution)/shard_map/ppermute | solution.py:13
  103.3 5.7 %collective-permute-start.27 = (bf16[128,128]{0,1:T(8,128)(2,1)S(1)}, bf16[128,128]{0,1:T(8,128)(2,1)S(1)}, u32[]{:S(2)}, u32[]{:S(2)}) collective-permute-start(bf16[128,128]{0,1:T(8,128)(2,1)S(1)} %get-tuple-element.81), channel_id=1, source_target_pairs={{0,3},{1,2},{2,1},{3,0},{4,7},{5,6},{6,5},{7,4},{8,11},{9,10},{10,... | collective-permute-start | bytes 98312 | tf_op jit(solution)/shard_map/ppermute | solution.py:13

commit v9 on v8

--- a/solution.py
+++ b/solution.py
@@ -123,7 +123,7 @@
         return by_rows(jnp.concatenate([jnp.concatenate([updates, *columns], 1), lists], 0))
 
     parcels = {0: parcel(0)}
-    for mask in sorted(range(1, front_count), key=lambda mask: (mask + 1) % front_count):
+    for mask in sorted(range(1, front_count), key=lambda mask: (mask + 2) % front_count):
         parcels[mask] = traded(parcel(mask), "front", mask)
     parcels = [parcels[mask] for mask in range(front_count)]
     cores1 = [update1[:, :leaf_rows], update1[:, leaf_rows:]]

time: 110 us -> 110 us (level)
  no operation moved by 1% of the time
where the time goes in v9:
time: 110 us
  waiting for transfers between devices  61.4 us (56%)
  starting transfers between devices  33.1 us (30%)
  matrix products  6.29 us (6%)
  local copies, waits for them, and re-layouts  4.22 us (4%)
  other arithmetic  3.72 us (3%)
  between operations  1.18 us (1%)
    ppermute x28, waiting for transfers between devices, traded(): lax.ppermute(shard, axis, [(i, i ^ mask) for i in range(lax.axis_size(axi...  61.4 us
    ppermute x28, starting transfers between devices, traded(): lax.ppermute(shard, axis, [(i, i ^ mask) for i in range(lax.axis_size(axi...  33.1 us
    dot_general x21, matrix products, product(): lax.dot_general(left, right, (((left_dim,), (right_dim,)), ((), ())), pre...  6.29 us
  transfers between devices with their start and end apart: 28, of which 19 were waited for; matrix products, arithmetic and copies ran while one was open for 5% of the time, Pallas kernels for 0%

profile of v9, /device:TPU:0, one launch (start us, length us, event | category | flops | bytes accessed | tf_op | source)
XLA Modules:
  0.0 109.9 jit_solution(17887415146266376298)
XLA Ops:
  0.0 1.0 slice.273
  1.0 1.0 slice.274
  2.3 3.1 %collective-permute-start = (bf16[136,640]{1,0:T(8,128)(2,1)S(1)}, bf16[136,640]{1,0:T(8,128)(2,1)S(1)}, u32[]{:S(2)}, u32[]{:S(2)}) collective-permute-start(bf16[136,640]{1,0:T(8,128)(2,1)S(1)} %get-tuple-element.130), channel_id=1, source_target_pairs={{0,1},{1,0},{2,3},{3,2},{4,5},{5,4},{6,7},{7,6},{8,9},{9,8},{10,11... | collective-permute-start | bytes 522248 | tf_op jit(solution)/shard_map/ppermute | solution.py:13
  5.5 2.7 %collective-permute-start.1 = (bf16[136,640]{1,0:T(8,128)(2,1)S(1)}, bf16[136,640]{1,0:T(8,128)(2,1)S(1)}, u32[]{:S(2)}, u32[]{:S(2)}) collective-permute-start(bf16[136,640]{1,0:T(8,128)(2,1)S(1)} %get-tuple-element.131), channel_id=1, source_target_pairs={{0,2},{1,3},{2,0},{3,1},{4,6},{5,7},{6,4},{7,5},{8,10},{9,11},{10,... | collective-permute-start | bytes 522248 | tf_op jit(solution)/shard_map/ppermute | solution.py:13
  8.2 0.9 collective-permute-start.3
  9.1 0.3 copy.30
  9.3 0.7 slice-done.2
  10.3 9.2 %collective-permute-done.3 = bf16[128,512]{1,0:T(8,128)(2,1)S(1)} collective-permute-done((bf16[128,512]{1,0:T(8,128)(2,1)S(1)}, bf16[128,512]{1,0:T(8,128)(2,1)S(1)}, u32[]{:S(2)}, u32[]{:S(2)}) %collective-permute-start.3) | collective-permute-done | bytes 131104 | tf_op jit(solution)/shard_map/ppermute | solution.py:13
  19.5 2.5 %collective-permute-start.6 = (bf16[128,1024]{1,0:T(8,128)(2,1)S(1)}, bf16[128,1024]{1,0:T(8,128)(2,1)S(1)}, u32[]{:S(2)}, u32[]{:S(2)}) collective-permute-start(bf16[128,1024]{1,0:T(8,128)(2,1)S(1)} %slice.274), channel_id=1, source_target_pairs={{0,1},{1,0},{2,3},{3,2},{4,5},{5,4},{6,7},{7,6},{8,9},{9,8},{10,11... | collective-permute-start | bytes 786440 | tf_op jit(solution)/shard_map/ppermute | solution.py:13
  22.0 2.6 %collective-permute-start.8 = (bf16[256,256]{1,0:T(8,128)(2,1)S(1)}, bf16[256,256]{1,0:T(8,128)(2,1)S(1)}, u32[]{:S(2)}, u32[]{:S(2)}) collective-permute-start(bf16[256,256]{1,0:T(8,128)(2,1)S(1)} %get-tuple-element.92), channel_id=1, source_target_pairs={{0,2},{1,3},{2,0},{3,1},{4,6},{5,7},{6,4},{7,5},{8,10},{9,11},{10,... | collective-permute-start | bytes 393224 | tf_op jit(solution)/shard_map/ppermute | solution.py:13
  25.3 0.2 fusion.99
  25.6 0.6 collective-permute-start.4
  26.5 4.5 %collective-permute-done.8 = bf16[256,256]{1,0:T(8,128)(2,1)S(1)} collective-permute-done((bf16[256,256]{1,0:T(8,128)(2,1)S(1)}, bf16[256,256]{1,0:T(8,128)(2,1)S(1)}, u32[]{:S(2)}, u32[]{:S(2)}) %collective-permute-start.8) | collective-permute-done | bytes 131104 | tf_op jit(solution)/shard_map/ppermute | solution.py:13
  31.1 4.1 %collective-permute-start.9 = (bf16[512,256]{1,0:T(8,128)(2,1)S(1)}, bf16[512,256]{1,0:T(8,128)(2,1)S(1)}, u32[]{:S(2)}, u32[]{:S(2)}) collective-permute-start(bf16[512,256]{1,0:T(8,128)(2,1)S(1)} %pad_maximum_fusion.9), channel_id=1, source_target_pairs={{0,1},{1,0},{2,3},{3,2},{4,5},{5,4},{6,7},{7,6},{8,9},{9,8},{10,11... | collective-permute-start | bytes 786440 | tf_op jit(solution)/shard_map/ppermute | solution.py:13
  35.3 0.5 fusion.100
  36.0 1.6 %collective-permute-start.13 = (bf16[256,1024]{0,1:T(8,128)(2,1)S(1)}, bf16[256,1024]{0,1:T(8,128)(2,1)S(1)}, u32[]{:S(2)}, u32[]{:S(2)}) collective-permute-start(bf16[256,1024]{0,1:T(8,128)(2,1)S(1)} %pad_maximum_fusion), channel_id=1, source_target_pairs={{0,8},{4,12},{8,0},{12,4},{16,24},{20,28},{24,16},{28,20},{1,9},{5... | collective-permute-start | bytes 1572872 | tf_op jit(solution)/shard_map/ppermute | solution.py:13
  37.5 2.0 %collective-permute-done.9 = bf16[512,256]{1,0:T(8,128)(2,1)S(1)} collective-permute-done((bf16[512,256]{1,0:T(8,128)(2,1)S(1)}, bf16[512,256]{1,0:T(8,128)(2,1)S(1)}, u32[]{:S(2)}, u32[]{:S(2)}) %collective-permute-start.9) | collective-permute-done | bytes 262176 | tf_op jit(solution)/shard_map/ppermute | solution.py:13
  39.6 0.2 fusion.77
  39.8 0.2 fusion.76
  40.1 0.2 convolution_convert_fusion.2
  40.5 1.3 %collective-permute-done.10 = bf16[128,512]{1,0:T(8,128)(2,1)S(1)} collective-permute-done((bf16[128,512]{1,0:T(8,128)(2,1)S(1)}, bf16[128,512]{1,0:T(8,128)(2,1)S(1)}, u32[]{:S(2)}, u32[]{:S(2)}) %collective-permute-start.10) | collective-permute-done | bytes 131104 | tf_op jit(solution)/shard_map/ppermute | solution.py:13
  41.8 0.2 fusion.24
  42.0 2.0 %collective-permute-start.11 = (bf16[128,512]{1,0:T(8,128)(2,1)S(1)}, bf16[128,512]{1,0:T(8,128)(2,1)S(1)}, u32[]{:S(2)}, u32[]{:S(2)}) collective-permute-start(bf16[128,512]{1,0:T(8,128)(2,1)S(1)} %get-tuple-element.147), channel_id=1, source_target_pairs={{0,2},{1,3},{2,0},{3,1},{4,6},{5,7},{6,4},{7,5},{8,10},{9,11},{10,... | collective-permute-start | bytes 393224 | tf_op jit(solution)/shard_map/ppermute | solution.py:13
  44.1 7.3 %collective-permute-done.11 = bf16[128,512]{1,0:T(8,128)(2,1)S(1)} collective-permute-done((bf16[128,512]{1,0:T(8,128)(2,1)S(1)}, bf16[128,512]{1,0:T(8,128)(2,1)S(1)}, u32[]{:S(2)}, u32[]{:S(2)}) %collective-permute-start.11) | collective-permute-done | bytes 131104 | tf_op jit(solution)/shard_map/ppermute | solution.py:13
  51.4 0.5 fusion.4
  52.2 1.6 %collective-permute-start.14 = (bf16[128,512]{0,1:T(8,128)(2,1)S(1)}, bf16[128,512]{0,1:T(8,128)(2,1)S(1)}, u32[]{:S(2)}, u32[]{:S(2)}) collective-permute-start(bf16[128,512]{0,1:T(8,128)(2,1)S(1)} %pad_maximum_fusion.24), channel_id=1, source_target_pairs={{0,8},{4,12},{8,0},{12,4},{16,24},{20,28},{24,16},{28,20},{1,9},{5... | collective-permute-start | bytes 393224 | tf_op jit(solution)/shard_map/ppermute | solution.py:13
  53.7 0.2 constant_dynamic-slice_fusion
  53.9 3.3 %collective-permute-done.14 = bf16[128,512]{0,1:T(8,128)(2,1)S(1)} collective-permute-done((bf16[128,512]{0,1:T(8,128)(2,1)S(1)}, bf16[128,512]{0,1:T(8,128)(2,1)S(1)}, u32[]{:S(2)}, u32[]{:S(2)}) %collective-permute-start.14) | collective-permute-done | bytes 131104 | tf_op jit(solution)/shard_map/ppermute | solution.py:13
  57.3 1.8 %collective-permute-start.15 = (bf16[128,512]{0,1:T(8,128)(2,1)S(1)}, bf16[128,512]{0,1:T(8,128)(2,1)S(1)}, u32[]{:S(2)}, u32[]{:S(2)}) collective-permute-start(bf16[128,512]{0,1:T(8,128)(2,1)S(1)} %fusion.11), channel_id=1, source_target_pairs={{0,1},{1,0},{2,3},{3,2},{4,5},{5,4},{6,7},{7,6},{8,9},{9,8},{10,11... | collective-permute-start | bytes 393224 | tf_op jit(solution)/shard_map/ppermute | solution.py:13
  59.2 3.1 %collective-permute-done.15 = bf16[128,512]{0,1:T(8,128)(2,1)S(1)} collective-permute-done((bf16[128,512]{0,1:T(8,128)(2,1)S(1)}, bf16[128,512]{0,1:T(8,128)(2,1)S(1)}, u32[]{:S(2)}, u32[]{:S(2)}) %collective-permute-start.15) | collective-permute-done | bytes 131104 | tf_op jit(solution)/shard_map/ppermute | solution.py:13
  62.5 0.4 fusion.101
  62.9 0.4 fusion.102
  63.4 1.3 %collective-permute-done.16 = bf16[128,512]{1,0:T(8,128)(2,1)S(1)} collective-permute-done((bf16[128,512]{1,0:T(8,128)(2,1)S(1)}, bf16[128,512]{1,0:T(8,128)(2,1)S(1)}, u32[]{:S(2)}, u32[]{:S(2)}) %collective-permute-start.16) | collective-permute-done | bytes 131104 | tf_op jit(solution)/shard_map/ppermute | solution.py:13
  64.7 0.3 fusion.35
  65.0 0.3 fusion.103
  65.6 1.8 %collective-permute-start.17 = (bf16[128,512]{0,1:T(8,128)(2,1)S(1)}, bf16[128,512]{0,1:T(8,128)(2,1)S(1)}, u32[]{:S(2)}, u32[]{:S(2)}) collective-permute-start(bf16[128,512]{0,1:T(8,128)(2,1)S(1)} %pad_maximum_fusion.26), channel_id=1, source_target_pairs={{0,1},{1,0},{2,3},{3,2},{4,5},{5,4},{6,7},{7,6},{8,9},{9,8},{10,11... | collective-permute-start | bytes 393224 | tf_op jit(solution)/shard_map/ppermute | solution.py:13
  67.4 3.8 %collective-permute-done.17 = bf16[128,512]{0,1:T(8,128)(2,1)S(1)} collective-permute-done((bf16[128,512]{0,1:T(8,128)(2,1)S(1)}, bf16[128,512]{0,1:T(8,128)(2,1)S(1)}, u32[]{:S(2)}, u32[]{:S(2)}) %collective-permute-start.17) | collective-permute-done | bytes 131104 | tf_op jit(solution)/shard_map/ppermute | solution.py:13
  71.3 0.9 collective-permute-start.18
  72.3 0.4 fusion.2
  72.7 7.1 %collective-permute-done.18 = bf16[128,512]{0,1:T(8,128)(2,1)S(1)} collective-permute-done((bf16[128,512]{0,1:T(8,128)(2,1)S(1)}, bf16[128,512]{0,1:T(8,128)(2,1)S(1)}, u32[]{:S(2)}, u32[]{:S(2)}) %collective-permute-start.18) | collective-permute-done | bytes 131104 | tf_op jit(solution)/shard_map/ppermute | solution.py:13
  79.9 1.6 %collective-permute-start.19 = (bf16[128,512]{0,1:T(8,128)(2,1)S(1)}, bf16[128,512]{0,1:T(8,128)(2,1)S(1)}, u32[]{:S(2)}, u32[]{:S(2)}) collective-permute-start(bf16[128,512]{0,1:T(8,128)(2,1)S(1)} %add_convert_fusion.2), channel_id=1, source_target_pairs={{0,8},{4,12},{8,0},{12,4},{16,24},{20,28},{24,16},{28,20},{1,9},{5... | collective-permute-start | bytes 393224 | tf_op jit(solution)/shard_map/ppermute | solution.py:13
  81.5 3.3 %collective-permute-done.19 = bf16[128,512]{0,1:T(8,128)(2,1)S(1)} collective-permute-done((bf16[128,512]{0,1:T(8,128)(2,1)S(1)}, bf16[128,512]{0,1:T(8,128)(2,1)S(1)}, u32[]{:S(2)}, u32[]{:S(2)}) %collective-permute-start.19) | collective-permute-done | bytes 131104 | tf_op jit(solution)/shard_map/ppermute | solution.py:13
  85.3 0.4 convolution_convert_fusion.1
  85.8 0.3 fusion.44
  86.0 0.3 fusion.36
  86.3 0.8 collective-permute-done.20
  87.1 0.3 fusion.7
  87.4 0.3 fusion.50
  87.7 0.3 convolution_add_fusion
  88.0 0.2 collective-permute-start.21
  88.2 1.2 %collective-permute-done.21 = bf16[128,512]{0,1:T(8,128)(2,1)S(1)} collective-permute-done((bf16[128,512]{0,1:T(8,128)(2,1)S(1)}, bf16[128,512]{0,1:T(8,128)(2,1)S(1)}, u32[]{:S(2)}, u32[]{:S(2)}) %collective-permute-start.21) | collective-permute-done | bytes 131104 | tf_op jit(solution)/shard_map/ppermute | solution.py:13
  89.5 0.4 fusion.3
  90.0 8.2 %collective-permute-done.22 = bf16[128,512]{0,1:T(8,128)(2,1)S(1)} collective-permute-done((bf16[128,512]{0,1:T(8,128)(2,1)S(1)}, bf16[128,512]{0,1:T(8,128)(2,1)S(1)}, u32[]{:S(2)}, u32[]{:S(2)}) %collective-permute-start.22) | collective-permute-done | bytes 131104 | tf_op jit(solution)/shard_map/ppermute | solution.py:13
  98.4 1.3 %collective-permute-done.23 = bf16[128,512]{0,1:T(8,128)(2,1)S(1)} collective-permute-done((bf16[128,512]{0,1:T(8,128)(2,1)S(1)}, bf16[128,512]{0,1:T(8,128)(2,1)S(1)}, u32[]{:S(2)}, u32[]{:S(2)}) %collective-permute-start.23) | collective-permute-done | bytes 131104 | tf_op jit(solution)/shard_map/ppermute | solution.py:13
  99.7 0.5 fusion.8
  100.2 0.2 fusion.47
  100.4 0.2 convolution_add_fusion.2
  100.8 2.1 %collective-permute-start.25 = (bf16[128,128]{0,1:T(8,128)(2,1)S(1)}, bf16[128,128]{0,1:T(8,128)(2,1)S(1)}, u32[]{:S(2)}, u32[]{:S(2)}) collective-permute-start(bf16[128,128]{0,1:T(8,128)(2,1)S(1)} %get-tuple-element.83), channel_id=1, source_target_pairs={{0,1},{1,0},{2,3},{3,2},{4,5},{5,4},{6,7},{7,6},{8,9},{9,8},{10,11... | collective-permute-start | bytes 98312 | tf_op jit(solution)/shard_map/ppermute | solution.py:13
  102.9 0.4 collective-permute-start.26
  103.3 2.1 %collective-permute-start.27 = (bf16[128,128]{0,1:T(8,128)(2,1)S(1)}, bf16[128,128]{0,1:T(8,128)(2,1)S(1)}, u32[]{:S(2)}, u32[]{:S(2)}) collective-permute-start(bf16[128,128]{0,1:T(8,128)(2,1)S(1)} %get-tuple-element.81), channel_id=1, source_target_pairs={{0,3},{1,2},{2,1},{3,0},{4,7},{5,6},{6,5},{7,4},{8,11},{9,10},{10,... | collective-permute-start | bytes 98312 | tf_op jit(solution)/shard_map/ppermute | solution.py:13
  105.3 0.3 collective-permute-done.25
  105.6 2.3 %collective-permute-done.26 = bf16[128,128]{0,1:T(8,128)(2,1)S(1)} collective-permute-done((bf16[128,128]{0,1:T(8,128)(2,1)S(1)}, bf16[128,128]{0,1:T(8,128)(2,1)S(1)}, u32[]{:S(2)}, u32[]{:S(2)}) %collective-permute-start.26) | collective-permute-done | bytes 32800 | tf_op jit(solution)/shard_map/ppermute | solution.py:13
  108.0 1.0 collective-permute-done.27
  109.1 0.8 pad_maximum_fusion.1
  (133 shorter events, 4.1 us)
Async XLA Ops:
  0.0 2.3 %slice-start.1 = ((bf16[128,1536]{1,0:T(8,128)(2,1)}), bf16[128,512]{1,0:T(8,128)(2,1)S(1)}, s32[]{:S(2)}) async-start(bf16[128,1536]{1,0:T(8,128)(2,1)} %param.7), calls=%async_computation.1 | async-start | bytes 262144 | tf_op jit(solution)/shard_map/slice | solution.py:111
  0.0 2.1 %copy-start.5 = (s32[2,128]{1,0:T(2,128)S(1)}, s32[2,128]{1,0:T(2,128)}, u32[]{:S(2)}) copy-start(s32[2,128]{1,0:T(2,128)} %param.9) | copy-start | bytes 3076
  0.0 2.1 %copy-start.6 = (s32[2,128,1]{1,2,0:T(1,128)S(1)}, s32[2,128,1]{1,2,0:T(1,128)}, u32[]{:S(2)}) copy-start(s32[2,128,1]{1,2,0:T(1,128)} %param.8) | copy-start | bytes 3076
  0.0 2.1 %copy-start = (bf16[3,128,256]{2,1,0:T(8,128)(2,1)S(1)}, bf16[3,128,256]{2,1,0:T(8,128)(2,1)}, u32[]{:S(2)}) copy-start(bf16[3,128,256]{2,1,0:T(8,128)(2,1)} %param.5) | copy-start | bytes 589828
  2.3 22.3 %collective-permute-start = (bf16[136,640]{1,0:T(8,128)(2,1)S(1)}, bf16[136,640]{1,0:T(8,128)(2,1)S(1)}, u32[]{:S(2)}, u32[]{:S(2)}) collective-permute-start(bf16[136,640]{1,0:T(8,128)(2,1)S(1)} %get-tuple-element.130), channel_id=1, source_target_pairs={{0,1},{1,0},{2,3},{3,2},{4,5},{5,4},{6,7},{7,6},{8,9},{9,8},{10,11... | collective-permute-start | bytes 522248 | tf_op jit(solution)/shard_map/ppermute | solution.py:13
  5.5 3.6 %slice-start = ((bf16[128,3584]{1,0:T(8,128)(2,1)}), bf16[128,2048]{1,0:T(8,128)(2,1)S(1)}, s32[]{:S(2)}) async-start(bf16[128,3584]{1,0:T(8,128)(2,1)} %param.6), calls=%async_computation | async-start | bytes 1048576 | tf_op jit(solution)/shard_map/slice | solution.py:110
  5.5 19.1 %collective-permute-start.1 = (bf16[136,640]{1,0:T(8,128)(2,1)S(1)}, bf16[136,640]{1,0:T(8,128)(2,1)S(1)}, u32[]{:S(2)}, u32[]{:S(2)}) collective-permute-start(bf16[136,640]{1,0:T(8,128)(2,1)S(1)} %get-tuple-element.131), channel_id=1, source_target_pairs={{0,2},{1,3},{2,0},{3,1},{4,6},{5,7},{6,4},{7,5},{8,10},{9,11},{10,... | collective-permute-start | bytes 522248 | tf_op jit(solution)/shard_map/ppermute | solution.py:13
  8.2 16.5 %collective-permute-start.2 = (bf16[136,640]{1,0:T(8,128)(2,1)S(1)}, bf16[136,640]{1,0:T(8,128)(2,1)S(1)}, u32[]{:S(2)}, u32[]{:S(2)}) collective-permute-start(bf16[136,640]{1,0:T(8,128)(2,1)S(1)} %get-tuple-element.129), channel_id=1, source_target_pairs={{0,3},{1,2},{2,1},{3,0},{4,7},{5,6},{6,5},{7,4},{8,11},{9,10},{10,... | collective-permute-start | bytes 522248 | tf_op jit(solution)/shard_map/ppermute | solution.py:13
  8.2 11.3 %collective-permute-start.3 = (bf16[128,512]{1,0:T(8,128)(2,1)S(1)}, bf16[128,512]{1,0:T(8,128)(2,1)S(1)}, u32[]{:S(2)}, u32[]{:S(2)}) collective-permute-start(bf16[128,512]{1,0:T(8,128)(2,1)S(1)} %slice.273), channel_id=1, source_target_pairs={{0,1},{1,0},{2,3},{3,2},{4,5},{5,4},{6,7},{7,6},{8,9},{9,8},{10,11... | collective-permute-start | bytes 393224 | tf_op jit(solution)/shard_map/ppermute | solution.py:13
  9.1 0.9 slice-start.2
  10.0 11.9 %collective-permute-start.5 = (bf16[128,512]{1,0:T(8,128)(2,1)S(1)}, bf16[128,512]{1,0:T(8,128)(2,1)S(1)}, u32[]{:S(2)}, u32[]{:S(2)}) collective-permute-start(bf16[128,512]{1,0:T(8,128)(2,1)S(1)} %get-tuple-element.94), channel_id=1, source_target_pairs={{0,4},{4,0},{8,12},{12,8},{16,20},{20,16},{24,28},{28,24},{1,5},{5... | collective-permute-start | bytes 393224 | tf_op jit(solution)/shard_map/ppermute | solution.py:13
  19.5 15.8 %collective-permute-start.6 = (bf16[128,1024]{1,0:T(8,128)(2,1)S(1)}, bf16[128,1024]{1,0:T(8,128)(2,1)S(1)}, u32[]{:S(2)}, u32[]{:S(2)}) collective-permute-start(bf16[128,1024]{1,0:T(8,128)(2,1)S(1)} %slice.274), channel_id=1, source_target_pairs={{0,1},{1,0},{2,3},{3,2},{4,5},{5,4},{6,7},{7,6},{8,9},{9,8},{10,11... | collective-permute-start | bytes 786440 | tf_op jit(solution)/shard_map/ppermute | solution.py:13
  22.0 9.1 %collective-permute-start.8 = (bf16[256,256]{1,0:T(8,128)(2,1)S(1)}, bf16[256,256]{1,0:T(8,128)(2,1)S(1)}, u32[]{:S(2)}, u32[]{:S(2)}) collective-permute-start(bf16[256,256]{1,0:T(8,128)(2,1)S(1)} %get-tuple-element.92), channel_id=1, source_target_pairs={{0,2},{1,3},{2,0},{3,1},{4,6},{5,7},{6,4},{7,5},{8,10},{9,11},{10,... | collective-permute-start | bytes 393224 | tf_op jit(solution)/shard_map/ppermute | solution.py:13
  25.3 1.1 copy-start.1
  25.6 9.7 %collective-permute-start.4 = (bf16[128,512]{1,0:T(8,128)(2,1)S(1)}, bf16[128,512]{1,0:T(8,128)(2,1)S(1)}, u32[]{:S(2)}, u32[]{:S(2)}) collective-permute-start(bf16[128,512]{1,0:T(8,128)(2,1)S(1)} %get-tuple-element.143), channel_id=1, source_target_pairs={{0,2},{1,3},{2,0},{3,1},{4,6},{5,7},{6,4},{7,5},{8,10},{9,11},{10,... | collective-permute-start | bytes 393224 | tf_op jit(solution)/shard_map/ppermute | solution.py:13
  26.3 9.6 %collective-permute-start.12 = (bf16[128,1024]{0,1:T(8,128)(2,1)S(1)}, bf16[128,1024]{0,1:T(8,128)(2,1)S(1)}, u32[]{:S(2)}, u32[]{:S(2)}) collective-permute-start(bf16[128,1024]{0,1:T(8,128)(2,1)S(1)} %get-tuple-element.76), channel_id=1, source_target_pairs={{0,4},{4,0},{8,12},{12,8},{16,20},{20,16},{24,28},{28,24},{1,5},{5... | collective-permute-start | bytes 786440 | tf_op jit(solution)/shard_map/ppermute | solution.py:13
  31.1 8.4 %collective-permute-start.9 = (bf16[512,256]{1,0:T(8,128)(2,1)S(1)}, bf16[512,256]{1,0:T(8,128)(2,1)S(1)}, u32[]{:S(2)}, u32[]{:S(2)}) collective-permute-start(bf16[512,256]{1,0:T(8,128)(2,1)S(1)} %pad_maximum_fusion.9), channel_id=1, source_target_pairs={{0,1},{1,0},{2,3},{3,2},{4,5},{5,4},{6,7},{7,6},{8,9},{9,8},{10,11... | collective-permute-start | bytes 786440 | tf_op jit(solution)/shard_map/ppermute | solution.py:13
  35.8 3.8 %collective-permute-start.7 = (bf16[128,1024]{0,1:T(8,128)(2,1)S(1)}, bf16[128,1024]{0,1:T(8,128)(2,1)S(1)}, u32[]{:S(2)}, u32[]{:S(2)}) collective-permute-start(bf16[128,1024]{0,1:T(8,128)(2,1)S(1)} %get-tuple-element.145), channel_id=1, source_target_pairs={{0,4},{4,0},{8,12},{12,8},{16,20},{20,16},{24,28},{28,24},{1,5},{5... | collective-permute-start | bytes 786440 | tf_op jit(solution)/shard_map/ppermute | solution.py:13
  36.0 15.4 %collective-permute-start.13 = (bf16[256,1024]{0,1:T(8,128)(2,1)S(1)}, bf16[256,1024]{0,1:T(8,128)(2,1)S(1)}, u32[]{:S(2)}, u32[]{:S(2)}) collective-permute-start(bf16[256,1024]{0,1:T(8,128)(2,1)S(1)} %pad_maximum_fusion), channel_id=1, source_target_pairs={{0,8},{4,12},{8,0},{12,4},{16,24},{20,28},{24,16},{28,20},{1,9},{5... | collective-permute-start | bytes 1572872 | tf_op jit(solution)/shard_map/ppermute | solution.py:13
  40.1 1.9 %copy-start.3 = (bf16[128,256]{0,1:T(8,128)(2,1)}, bf16[128,256]{0,1:T(8,128)(2,1)S(1)}, u32[]{:S(2)}) copy-start(bf16[128,256]{0,1:T(8,128)(2,1)S(1)} %fusion.30) | copy-start | bytes 196612
  40.3 1.4 %collective-permute-start.10 = (bf16[128,512]{1,0:T(8,128)(2,1)S(1)}, bf16[128,512]{1,0:T(8,128)(2,1)S(1)}, u32[]{:S(2)}, u32[]{:S(2)}) collective-permute-start(bf16[128,512]{1,0:T(8,128)(2,1)S(1)} %convolution_convert_fusion.2), channel_id=1, source_target_pairs={{0,4},{4,0},{8,12},{12,8},{16,20},{20,16},{24,28},{28,24},{1,5},{5... | collective-permute-start | bytes 393224 | tf_op jit(solution)/shard_map/ppermute | solution.py:13
  42.0 9.3 %collective-permute-start.11 = (bf16[128,512]{1,0:T(8,128)(2,1)S(1)}, bf16[128,512]{1,0:T(8,128)(2,1)S(1)}, u32[]{:S(2)}, u32[]{:S(2)}) collective-permute-start(bf16[128,512]{1,0:T(8,128)(2,1)S(1)} %get-tuple-element.147), channel_id=1, source_target_pairs={{0,2},{1,3},{2,0},{3,1},{4,6},{5,7},{6,4},{7,5},{8,10},{9,11},{10,... | collective-permute-start | bytes 393224 | tf_op jit(solution)/shard_map/ppermute | solution.py:13
  52.2 5.0 %collective-permute-start.14 = (bf16[128,512]{0,1:T(8,128)(2,1)S(1)}, bf16[128,512]{0,1:T(8,128)(2,1)S(1)}, u32[]{:S(2)}, u32[]{:S(2)}) collective-permute-start(bf16[128,512]{0,1:T(8,128)(2,1)S(1)} %pad_maximum_fusion.24), channel_id=1, source_target_pairs={{0,8},{4,12},{8,0},{12,4},{16,24},{20,28},{24,16},{28,20},{1,9},{5... | collective-permute-start | bytes 393224 | tf_op jit(solution)/shard_map/ppermute | solution.py:13
  57.3 5.0 %collective-permute-start.15 = (bf16[128,512]{0,1:T(8,128)(2,1)S(1)}, bf16[128,512]{0,1:T(8,128)(2,1)S(1)}, u32[]{:S(2)}, u32[]{:S(2)}) collective-permute-start(bf16[128,512]{0,1:T(8,128)(2,1)S(1)} %fusion.11), channel_id=1, source_target_pairs={{0,1},{1,0},{2,3},{3,2},{4,5},{5,4},{6,7},{7,6},{8,9},{9,8},{10,11... | collective-permute-start | bytes 393224 | tf_op jit(solution)/shard_map/ppermute | solution.py:13
  63.3 1.4 %collective-permute-start.16 = (bf16[128,512]{1,0:T(8,128)(2,1)S(1)}, bf16[128,512]{1,0:T(8,128)(2,1)S(1)}, u32[]{:S(2)}, u32[]{:S(2)}) collective-permute-start(bf16[128,512]{1,0:T(8,128)(2,1)S(1)} %pad_maximum_fusion.25), channel_id=1, source_target_pairs={{0,4},{4,0},{8,12},{12,8},{16,20},{20,16},{24,28},{28,24},{1,5},{5... | collective-permute-start | bytes 393224 | tf_op jit(solution)/shard_map/ppermute | solution.py:13
  65.6 5.6 %collective-permute-start.17 = (bf16[128,512]{0,1:T(8,128)(2,1)S(1)}, bf16[128,512]{0,1:T(8,128)(2,1)S(1)}, u32[]{:S(2)}, u32[]{:S(2)}) collective-permute-start(bf16[128,512]{0,1:T(8,128)(2,1)S(1)} %pad_maximum_fusion.26), channel_id=1, source_target_pairs={{0,1},{1,0},{2,3},{3,2},{4,5},{5,4},{6,7},{7,6},{8,9},{9,8},{10,11... | collective-permute-start | bytes 393224 | tf_op jit(solution)/shard_map/ppermute | solution.py:13
  71.3 8.5 %collective-permute-start.18 = (bf16[128,512]{0,1:T(8,128)(2,1)S(1)}, bf16[128,512]{0,1:T(8,128)(2,1)S(1)}, u32[]{:S(2)}, u32[]{:S(2)}) collective-permute-start(bf16[128,512]{0,1:T(8,128)(2,1)S(1)} %get-tuple-element.67), channel_id=1, source_target_pairs={{0,2},{1,3},{2,0},{3,1},{4,6},{5,7},{6,4},{7,5},{8,10},{9,11},{10,... | collective-permute-start | bytes 393224 | tf_op jit(solution)/shard_map/ppermute | solution.py:13
  79.9 5.0 %collective-permute-start.19 = (bf16[128,512]{0,1:T(8,128)(2,1)S(1)}, bf16[128,512]{0,1:T(8,128)(2,1)S(1)}, u32[]{:S(2)}, u32[]{:S(2)}) collective-permute-start(bf16[128,512]{0,1:T(8,128)(2,1)S(1)} %add_convert_fusion.2), channel_id=1, source_target_pairs={{0,8},{4,12},{8,0},{12,4},{16,24},{20,28},{24,16},{28,20},{1,9},{5... | collective-permute-start | bytes 393224 | tf_op jit(solution)/shard_map/ppermute | solution.py:13
  85.7 1.4 %copy-start.4 = (bf16[128,256]{0,1:T(8,128)(2,1)S(1)}, bf16[128,256]{0,1:T(8,128)(2,1)}, u32[]{:S(2)}) copy-start(bf16[128,256]{0,1:T(8,128)(2,1)} %copy-done.3) | copy-start | bytes 196612
  85.7 1.4 %collective-permute-start.20 = (bf16[128,512]{1,0:T(8,128)(2,1)S(1)}, bf16[128,512]{1,0:T(8,128)(2,1)S(1)}, u32[]{:S(2)}, u32[]{:S(2)}) collective-permute-start(bf16[128,512]{1,0:T(8,128)(2,1)S(1)} %convolution_convert_fusion.1), channel_id=1, source_target_pairs={{0,4},{4,0},{8,12},{12,8},{16,20},{20,16},{24,28},{28,24},{1,5},{5... | collective-permute-start | bytes 393224 | tf_op jit(solution)/shard_map/ppermute | solution.py:13
  88.0 1.4 %collective-permute-start.21 = (bf16[128,512]{0,1:T(8,128)(2,1)S(1)}, bf16[128,512]{0,1:T(8,128)(2,1)S(1)}, u32[]{:S(2)}, u32[]{:S(2)}) collective-permute-start(bf16[128,512]{0,1:T(8,128)(2,1)S(1)} %dynamic-slice_convert_fusion.1), channel_id=1, source_target_pairs={{0,4},{4,0},{8,12},{12,8},{16,20},{20,16},{24,28},{28,24},{1,5},{5... | collective-permute-start | bytes 393224 | tf_op jit(solution)/shard_map/ppermute | solution.py:13
  89.4 8.8 %collective-permute-start.22 = (bf16[128,512]{0,1:T(8,128)(2,1)S(1)}, bf16[128,512]{0,1:T(8,128)(2,1)S(1)}, u32[]{:S(2)}, u32[]{:S(2)}) collective-permute-start(bf16[128,512]{0,1:T(8,128)(2,1)S(1)} %fusion.25), channel_id=1, source_target_pairs={{0,2},{1,3},{2,0},{3,1},{4,6},{5,7},{6,4},{7,5},{8,10},{9,11},{10,... | collective-permute-start | bytes 393224 | tf_op jit(solution)/shard_map/ppermute | solution.py:13
  89.5 10.1 %copy-start.2 = (bf16[128,256]{0,1:T(8,128)(2,1)S(1)}, bf16[128,256]{0,1:T(8,128)(2,1)}, u32[]{:S(2)}) copy-start(bf16[128,256]{0,1:T(8,128)(2,1)} %copy-done.1) | copy-start | bytes 196612
  98.2 1.4 %collective-permute-start.23 = (bf16[128,512]{0,1:T(8,128)(2,1)S(1)}, bf16[128,512]{0,1:T(8,128)(2,1)S(1)}, u32[]{:S(2)}, u32[]{:S(2)}) collective-permute-start(bf16[128,512]{0,1:T(8,128)(2,1)S(1)} %add_convert_fusion.1), channel_id=1, source_target_pairs={{0,4},{4,0},{8,12},{12,8},{16,20},{20,16},{24,28},{28,24},{1,5},{5... | collective-permute-start | bytes 393224 | tf_op jit(solution)/shard_map/ppermute | solution.py:13
  100.7 8.3 %collective-permute-start.24 = (bf16[256,128]{0,1:T(8,128)(2,1)S(1)}, bf16[256,128]{0,1:T(8,128)(2,1)S(1)}, u32[]{:S(2)}, u32[]{:S(2)}) collective-permute-start(bf16[256,128]{0,1:T(8,128)(2,1)S(1)} %constant_dynamic-slice_fusion.1), channel_id=1, source_target_pairs={{0,1},{1,0},{2,3},{3,2},{4,5},{5,4},{6,7},{7,6},{8,9},{9,8},{10,11... | collective-permute-start | bytes 196616 | tf_op jit(solution)/shard_map/ppermute | solution.py:13
  100.8 4.8 %collective-permute-start.25 = (bf16[128,128]{0,1:T(8,128)(2,1)S(1)}, bf16[128,128]{0,1:T(8,128)(2,1)S(1)}, u32[]{:S(2)}, u32[]{:S(2)}) collective-permute-start(bf16[128,128]{0,1:T(8,128)(2,1)S(1)} %get-tuple-element.83), channel_id=1, source_target_pairs={{0,1},{1,0},{2,3},{3,2},{4,5},{5,4},{6,7},{7,6},{8,9},{9,8},{10,11... | collective-permute-start | bytes 98312 | tf_op jit(solution)/shard_map/ppermute | solution.py:13
  102.9 5.1 %collective-permute-start.26 = (bf16[128,128]{0,1:T(8,128)(2,1)S(1)}, bf16[128,128]{0,1:T(8,128)(2,1)S(1)}, u32[]{:S(2)}, u32[]{:S(2)}) collective-permute-start(bf16[128,128]{0,1:T(8,128)(2,1)S(1)} %get-tuple-element.82), channel_id=1, source_target_pairs={{0,2},{1,3},{2,0},{3,1},{4,6},{5,7},{6,4},{7,5},{8,10},{9,11},{10,... | collective-permute-start | bytes 98312 | tf_op jit(solution)/shard_map/ppermute | solution.py:13
  103.3 5.7 %collective-permute-start.27 = (bf16[128,128]{0,1:T(8,128)(2,1)S(1)}, bf16[128,128]{0,1:T(8,128)(2,1)S(1)}, u32[]{:S(2)}, u32[]{:S(2)}) collective-permute-start(bf16[128,128]{0,1:T(8,128)(2,1)S(1)} %get-tuple-element.81), channel_id=1, source_target_pairs={{0,3},{1,2},{2,1},{3,0},{4,7},{5,6},{6,5},{7,4},{8,11},{9,10},{10,... | collective-permute-start | bytes 98312 | tf_op jit(solution)/shard_map/ppermute | solution.py:13

commit v10 on v9

--- a/solution.py
+++ b/solution.py
@@ -191,13 +191,13 @@
         return (jnp.arange(2 * leaf_rows)[:, None] == target).astype(BF16)
 
     select0 = selector(lists, 0)
-    select1 = selector(lists, 1)
     pivots1 = ordered(rhs1, jnp.zeros_like(rhs1), side, 1).astype(F32) - forward(updated0, select0)
     pivots1 = (pivots1 + traded(pivots1.astype(BF16), "leaf", 1).astype(F32)).astype(BF16)
 
     solved1_pair = pair_forward(pivots1, inverse1, inverse1_pair)
     updated1 = forward(solved1_pair, columns1_side).astype(BF16)
     updated1 = forward(solved1_pair, columns1) + traded(updated1, "leaf", 1).astype(F32)
+    select1 = lax.optimization_barrier(selector(after(lists, solved1_pair), 1))
     updated1 = high_sum(updated1).astype(BF16)
     updated1, wing2 = together(updated1, wing2)
 

time: 110 us -> 111 us (level)
  waiting for transfers between devices: 61.4 us -> 64 us
  starting transfers between devices: 33.1 us -> 31.3 us
    ppermute x28, waiting for transfers between devices: 61.4 us -> 64 us  [traded(): lax.ppermute(shard, axis, [(i, i ^ mask) for i in range(lax.axis_size(axi...]
    ppermute x28, starting transfers between devices: 33.1 us -> 31.3 us  [traded(): lax.ppermute(shard, axis, [(i, i ^ mask) for i in range(lax.axis_size(axi...]
  transfers between devices with their start and end apart: 28 -> 28, of which waited for: 19 -> 20; matrix products, arithmetic and copies ran while one was open for 5% -> 5% of each run, Pallas kernels for 0% -> 0%
where the time goes in v10:
time: 111 us
  waiting for transfers between devices  64 us (58%)
  starting transfers between devices  31.3 us (28%)
  matrix products  6.31 us (6%)
  local copies, waits for them, and re-layouts  4.2 us (4%)
  other arithmetic  4.18 us (4%)
    ppermute x28, waiting for transfers between devices, traded(): lax.ppermute(shard, axis, [(i, i ^ mask) for i in range(lax.axis_size(axi...  64 us
    ppermute x28, starting transfers between devices, traded(): lax.ppermute(shard, axis, [(i, i ^ mask) for i in range(lax.axis_size(axi...  31.3 us
    dot_general x21, matrix products, product(): lax.dot_general(left, right, (((left_dim,), (right_dim,)), ((), ())), pre...  6.31 us
  transfers between devices with their start and end apart: 28, of which 20 were waited for; matrix products, arithmetic and copies ran while one was open for 5% of the time, Pallas kernels for 0%

profile of v10, /device:TPU:0, one launch (start us, length us, event | category | flops | bytes accessed | tf_op | source)
XLA Modules:
  0.0 111.1 jit_solution(15614029248307749396)
XLA Ops:
  0.0 1.0 slice.274
  1.0 0.9 slice.273
  2.2 3.2 %collective-permute-start = (bf16[136,640]{1,0:T(8,128)(2,1)S(1)}, bf16[136,640]{1,0:T(8,128)(2,1)S(1)}, u32[]{:S(2)}, u32[]{:S(2)}) collective-permute-start(bf16[136,640]{1,0:T(8,128)(2,1)S(1)} %get-tuple-element.132), channel_id=1, source_target_pairs={{0,1},{1,0},{2,3},{3,2},{4,5},{5,4},{6,7},{7,6},{8,9},{9,8},{10,11... | collective-permute-start | bytes 522248 | tf_op jit(solution)/shard_map/ppermute | solution.py:13
  5.4 2.5 %collective-permute-start.2 = (bf16[136,640]{1,0:T(8,128)(2,1)S(1)}, bf16[136,640]{1,0:T(8,128)(2,1)S(1)}, u32[]{:S(2)}, u32[]{:S(2)}) collective-permute-start(bf16[136,640]{1,0:T(8,128)(2,1)S(1)} %get-tuple-element.131), channel_id=1, source_target_pairs={{0,3},{1,2},{2,1},{3,0},{4,7},{5,6},{6,5},{7,4},{8,11},{9,10},{10,... | collective-permute-start | bytes 522248 | tf_op jit(solution)/shard_map/ppermute | solution.py:13
  8.1 1.8 %collective-permute-start.3 = (bf16[128,512]{1,0:T(8,128)(2,1)S(1)}, bf16[128,512]{1,0:T(8,128)(2,1)S(1)}, u32[]{:S(2)}, u32[]{:S(2)}) collective-permute-start(bf16[128,512]{1,0:T(8,128)(2,1)S(1)} %slice.273), channel_id=1, source_target_pairs={{0,1},{1,0},{2,3},{3,2},{4,5},{5,4},{6,7},{7,6},{8,9},{9,8},{10,11... | collective-permute-start | bytes 393224 | tf_op jit(solution)/shard_map/ppermute | solution.py:13
  9.9 0.3 copy.30
  10.2 0.7 slice-done.2
  11.2 8.3 %collective-permute-done.3 = bf16[128,512]{1,0:T(8,128)(2,1)S(1)} collective-permute-done((bf16[128,512]{1,0:T(8,128)(2,1)S(1)}, bf16[128,512]{1,0:T(8,128)(2,1)S(1)}, u32[]{:S(2)}, u32[]{:S(2)}) %collective-permute-start.3) | collective-permute-done | bytes 131104 | tf_op jit(solution)/shard_map/ppermute | solution.py:13
  19.4 2.5 %collective-permute-start.6 = (bf16[128,1024]{1,0:T(8,128)(2,1)S(1)}, bf16[128,1024]{1,0:T(8,128)(2,1)S(1)}, u32[]{:S(2)}, u32[]{:S(2)}) collective-permute-start(bf16[128,1024]{1,0:T(8,128)(2,1)S(1)} %slice.274), channel_id=1, source_target_pairs={{0,1},{1,0},{2,3},{3,2},{4,5},{5,4},{6,7},{7,6},{8,9},{9,8},{10,11... | collective-permute-start | bytes 786440 | tf_op jit(solution)/shard_map/ppermute | solution.py:13
  21.9 1.1 collective-permute-start.8
  23.1 0.4 collective-permute-done.1
  24.1 0.2 fusion.97
  24.5 1.6 %collective-permute-start.4 = (bf16[128,512]{1,0:T(8,128)(2,1)S(1)}, bf16[128,512]{1,0:T(8,128)(2,1)S(1)}, u32[]{:S(2)}, u32[]{:S(2)}) collective-permute-start(bf16[128,512]{1,0:T(8,128)(2,1)S(1)} %get-tuple-element.143), channel_id=1, source_target_pairs={{0,2},{1,3},{2,0},{3,1},{4,6},{5,7},{6,4},{7,5},{8,10},{9,11},{10,... | collective-permute-start | bytes 393224 | tf_op jit(solution)/shard_map/ppermute | solution.py:13
  26.4 4.5 %collective-permute-done.8 = bf16[256,256]{1,0:T(8,128)(2,1)S(1)} collective-permute-done((bf16[256,256]{1,0:T(8,128)(2,1)S(1)}, bf16[256,256]{1,0:T(8,128)(2,1)S(1)}, u32[]{:S(2)}, u32[]{:S(2)}) %collective-permute-start.8) | collective-permute-done | bytes 131104 | tf_op jit(solution)/shard_map/ppermute | solution.py:13
  30.9 4.2 %collective-permute-start.9 = (bf16[512,256]{1,0:T(8,128)(2,1)S(1)}, bf16[512,256]{1,0:T(8,128)(2,1)S(1)}, u32[]{:S(2)}, u32[]{:S(2)}) collective-permute-start(bf16[512,256]{1,0:T(8,128)(2,1)S(1)} %pad_maximum_fusion.9), channel_id=1, source_target_pairs={{0,1},{1,0},{2,3},{3,2},{4,5},{5,4},{6,7},{7,6},{8,9},{9,8},{10,11... | collective-permute-start | bytes 786440 | tf_op jit(solution)/shard_map/ppermute | solution.py:13
  35.1 0.6 collective-permute-done.4
  35.7 0.5 fusion.98
  36.3 1.6 %collective-permute-start.13 = (bf16[256,1024]{0,1:T(8,128)(2,1)S(1)}, bf16[256,1024]{0,1:T(8,128)(2,1)S(1)}, u32[]{:S(2)}, u32[]{:S(2)}) collective-permute-start(bf16[256,1024]{0,1:T(8,128)(2,1)S(1)} %pad_maximum_fusion), channel_id=1, source_target_pairs={{0,8},{4,12},{8,0},{12,4},{16,24},{20,28},{24,16},{28,20},{1,9},{5... | collective-permute-start | bytes 1572872 | tf_op jit(solution)/shard_map/ppermute | solution.py:13
  37.9 2.3 %collective-permute-done.9 = bf16[512,256]{1,0:T(8,128)(2,1)S(1)} collective-permute-done((bf16[512,256]{1,0:T(8,128)(2,1)S(1)}, bf16[512,256]{1,0:T(8,128)(2,1)S(1)}, u32[]{:S(2)}, u32[]{:S(2)}) %collective-permute-start.9) | collective-permute-done | bytes 262176 | tf_op jit(solution)/shard_map/ppermute | solution.py:13
  40.4 0.3 fusion.75
  40.6 0.3 fusion.74
  40.9 0.2 convolution_convert_fusion.2
  41.3 1.3 %collective-permute-done.10 = bf16[128,512]{1,0:T(8,128)(2,1)S(1)} collective-permute-done((bf16[128,512]{1,0:T(8,128)(2,1)S(1)}, bf16[128,512]{1,0:T(8,128)(2,1)S(1)}, u32[]{:S(2)}, u32[]{:S(2)}) %collective-permute-start.10) | collective-permute-done | bytes 131104 | tf_op jit(solution)/shard_map/ppermute | solution.py:13
  42.6 0.2 fusion.22
  42.8 1.2 %collective-permute-start.11 = (bf16[128,512]{1,0:T(8,128)(2,1)S(1)}, bf16[128,512]{1,0:T(8,128)(2,1)S(1)}, u32[]{:S(2)}, u32[]{:S(2)}) collective-permute-start(bf16[128,512]{1,0:T(8,128)(2,1)S(1)} %get-tuple-element.147), channel_id=1, source_target_pairs={{0,2},{1,3},{2,0},{3,1},{4,6},{5,7},{6,4},{7,5},{8,10},{9,11},{10,... | collective-permute-start | bytes 393224 | tf_op jit(solution)/shard_map/ppermute | solution.py:13
  44.0 0.4 fusion.1
  44.4 7.7 %collective-permute-done.11 = bf16[128,512]{1,0:T(8,128)(2,1)S(1)} collective-permute-done((bf16[128,512]{1,0:T(8,128)(2,1)S(1)}, bf16[128,512]{1,0:T(8,128)(2,1)S(1)}, u32[]{:S(2)}, u32[]{:S(2)}) %collective-permute-start.11) | collective-permute-done | bytes 131104 | tf_op jit(solution)/shard_map/ppermute | solution.py:13
  52.2 0.4 convolution_subtract_fusion
  52.9 1.6 %collective-permute-start.14 = (bf16[128,512]{0,1:T(8,128)(2,1)S(1)}, bf16[128,512]{0,1:T(8,128)(2,1)S(1)}, u32[]{:S(2)}, u32[]{:S(2)}) collective-permute-start(bf16[128,512]{0,1:T(8,128)(2,1)S(1)} %pad_maximum_fusion.24), channel_id=1, source_target_pairs={{0,8},{4,12},{8,0},{12,4},{16,24},{20,28},{24,16},{28,20},{1,9},{5... | collective-permute-start | bytes 393224 | tf_op jit(solution)/shard_map/ppermute | solution.py:13
  54.7 3.3 %collective-permute-done.14 = bf16[128,512]{0,1:T(8,128)(2,1)S(1)} collective-permute-done((bf16[128,512]{0,1:T(8,128)(2,1)S(1)}, bf16[128,512]{0,1:T(8,128)(2,1)S(1)}, u32[]{:S(2)}, u32[]{:S(2)}) %collective-permute-start.14) | collective-permute-done | bytes 131104 | tf_op jit(solution)/shard_map/ppermute | solution.py:13
  58.1 0.9 collective-permute-start.15
  59.1 4.0 %collective-permute-done.15 = bf16[128,512]{0,1:T(8,128)(2,1)S(1)} collective-permute-done((bf16[128,512]{0,1:T(8,128)(2,1)S(1)}, bf16[128,512]{0,1:T(8,128)(2,1)S(1)}, u32[]{:S(2)}, u32[]{:S(2)}) %collective-permute-start.15) | collective-permute-done | bytes 131104 | tf_op jit(solution)/shard_map/ppermute | solution.py:13
  63.2 0.4 fusion.99
  63.6 0.4 fusion.100
  64.2 1.3 %collective-permute-done.16 = bf16[128,512]{1,0:T(8,128)(2,1)S(1)} collective-permute-done((bf16[128,512]{1,0:T(8,128)(2,1)S(1)}, bf16[128,512]{1,0:T(8,128)(2,1)S(1)}, u32[]{:S(2)}, u32[]{:S(2)}) %collective-permute-start.16) | collective-permute-done | bytes 131104 | tf_op jit(solution)/shard_map/ppermute | solution.py:13
  65.5 0.3 fusion.33
  65.8 0.3 fusion.101
  66.3 0.9 collective-permute-start.17
  67.3 4.7 %collective-permute-done.17 = bf16[128,512]{0,1:T(8,128)(2,1)S(1)} collective-permute-done((bf16[128,512]{0,1:T(8,128)(2,1)S(1)}, bf16[128,512]{0,1:T(8,128)(2,1)S(1)}, u32[]{:S(2)}, u32[]{:S(2)}) %collective-permute-start.17) | collective-permute-done | bytes 131104 | tf_op jit(solution)/shard_map/ppermute | solution.py:13
  72.1 1.4 %collective-permute-start.18 = (bf16[128,512]{0,1:T(8,128)(2,1)S(1)}, bf16[128,512]{0,1:T(8,128)(2,1)S(1)}, u32[]{:S(2)}, u32[]{:S(2)}) collective-permute-start(bf16[128,512]{0,1:T(8,128)(2,1)S(1)} %get-tuple-element.69), channel_id=1, source_target_pairs={{0,2},{1,3},{2,0},{3,1},{4,6},{5,7},{6,4},{7,5},{8,10},{9,11},{10,... | collective-permute-start | bytes 393224 | tf_op jit(solution)/shard_map/ppermute | solution.py:13
  73.5 0.4 fusion.2
  73.9 6.7 %collective-permute-done.18 = bf16[128,512]{0,1:T(8,128)(2,1)S(1)} collective-permute-done((bf16[128,512]{0,1:T(8,128)(2,1)S(1)}, bf16[128,512]{0,1:T(8,128)(2,1)S(1)}, u32[]{:S(2)}, u32[]{:S(2)}) %collective-permute-start.18) | collective-permute-done | bytes 131104 | tf_op jit(solution)/shard_map/ppermute | solution.py:13
  80.7 1.5 %collective-permute-start.19 = (bf16[128,512]{0,1:T(8,128)(2,1)S(1)}, bf16[128,512]{0,1:T(8,128)(2,1)S(1)}, u32[]{:S(2)}, u32[]{:S(2)}) collective-permute-start(bf16[128,512]{0,1:T(8,128)(2,1)S(1)} %add_convert_fusion.2), channel_id=1, source_target_pairs={{0,8},{4,12},{8,0},{12,4},{16,24},{20,28},{24,16},{28,20},{1,9},{5... | collective-permute-start | bytes 393224 | tf_op jit(solution)/shard_map/ppermute | solution.py:13
  82.3 3.5 %collective-permute-done.19 = bf16[128,512]{0,1:T(8,128)(2,1)S(1)} collective-permute-done((bf16[128,512]{0,1:T(8,128)(2,1)S(1)}, bf16[128,512]{0,1:T(8,128)(2,1)S(1)}, u32[]{:S(2)}, u32[]{:S(2)}) %collective-permute-start.19) | collective-permute-done | bytes 131104 | tf_op jit(solution)/shard_map/ppermute | solution.py:13
  86.3 0.3 convolution_convert_fusion.1
  86.7 0.3 fusion.42
  87.0 0.3 fusion.34
  87.2 0.8 collective-permute-done.20
  88.0 0.3 fusion.6
  88.3 0.3 fusion.48
  88.6 0.3 convolution_add_fusion
  89.1 1.2 %collective-permute-done.21 = bf16[128,512]{0,1:T(8,128)(2,1)S(1)} collective-permute-done((bf16[128,512]{0,1:T(8,128)(2,1)S(1)}, bf16[128,512]{0,1:T(8,128)(2,1)S(1)}, u32[]{:S(2)}, u32[]{:S(2)}) %collective-permute-start.21) | collective-permute-done | bytes 131104 | tf_op jit(solution)/shard_map/ppermute | solution.py:13
  90.4 0.4 fusion.3
  90.9 8.8 %collective-permute-done.22 = bf16[128,512]{0,1:T(8,128)(2,1)S(1)} collective-permute-done((bf16[128,512]{0,1:T(8,128)(2,1)S(1)}, bf16[128,512]{0,1:T(8,128)(2,1)S(1)}, u32[]{:S(2)}, u32[]{:S(2)}) %collective-permute-start.22) | collective-permute-done | bytes 131104 | tf_op jit(solution)/shard_map/ppermute | solution.py:13
  99.9 1.3 %collective-permute-done.23 = bf16[128,512]{0,1:T(8,128)(2,1)S(1)} collective-permute-done((bf16[128,512]{0,1:T(8,128)(2,1)S(1)}, bf16[128,512]{0,1:T(8,128)(2,1)S(1)}, u32[]{:S(2)}, u32[]{:S(2)}) %collective-permute-start.23) | collective-permute-done | bytes 131104 | tf_op jit(solution)/shard_map/ppermute | solution.py:13
  101.2 0.5 fusion.7
  101.7 0.2 fusion.45
  101.9 0.2 convolution_add_fusion.2
  102.3 2.1 %collective-permute-start.25 = (bf16[128,128]{0,1:T(8,128)(2,1)S(1)}, bf16[128,128]{0,1:T(8,128)(2,1)S(1)}, u32[]{:S(2)}, u32[]{:S(2)}) collective-permute-start(bf16[128,128]{0,1:T(8,128)(2,1)S(1)} %get-tuple-element.85), channel_id=1, source_target_pairs={{0,1},{1,0},{2,3},{3,2},{4,5},{5,4},{6,7},{7,6},{8,9},{9,8},{10,11... | collective-permute-start | bytes 98312 | tf_op jit(solution)/shard_map/ppermute | solution.py:13
  104.4 2.4 %collective-permute-start.27 = (bf16[128,128]{0,1:T(8,128)(2,1)S(1)}, bf16[128,128]{0,1:T(8,128)(2,1)S(1)}, u32[]{:S(2)}, u32[]{:S(2)}) collective-permute-start(bf16[128,128]{0,1:T(8,128)(2,1)S(1)} %get-tuple-element.83), channel_id=1, source_target_pairs={{0,3},{1,2},{2,1},{3,0},{4,7},{5,6},{6,5},{7,4},{8,11},{9,10},{10,... | collective-permute-start | bytes 98312 | tf_op jit(solution)/shard_map/ppermute | solution.py:13
  106.8 0.3 collective-permute-done.25
  107.1 2.3 %collective-permute-done.26 = bf16[128,128]{0,1:T(8,128)(2,1)S(1)} collective-permute-done((bf16[128,128]{0,1:T(8,128)(2,1)S(1)}, bf16[128,128]{0,1:T(8,128)(2,1)S(1)}, u32[]{:S(2)}, u32[]{:S(2)}) %collective-permute-start.26) | collective-permute-done | bytes 32800 | tf_op jit(solution)/shard_map/ppermute | solution.py:13
  109.5 0.7 collective-permute-done.27
  110.3 0.8 pad_maximum_fusion.1
  (128 shorter events, 4.6 us)
Async XLA Ops:
  0.0 2.2 %slice-start.1 = ((bf16[128,1536]{1,0:T(8,128)(2,1)}), bf16[128,512]{1,0:T(8,128)(2,1)S(1)}, s32[]{:S(2)}) async-start(bf16[128,1536]{1,0:T(8,128)(2,1)} %param.7), calls=%async_computation.1 | async-start | bytes 262144 | tf_op jit(solution)/shard_map/slice | solution.py:111
  0.0 2.0 %copy-start = (bf16[3,128,256]{2,1,0:T(8,128)(2,1)S(1)}, bf16[3,128,256]{2,1,0:T(8,128)(2,1)}, u32[]{:S(2)}) copy-start(bf16[3,128,256]{2,1,0:T(8,128)(2,1)} %param.5) | copy-start | bytes 589828
  0.0 2.0 %copy-start.1 = (s32[2,128]{1,0:T(2,128)S(1)}, s32[2,128]{1,0:T(2,128)}, u32[]{:S(2)}) copy-start(s32[2,128]{1,0:T(2,128)} %param.9) | copy-start | bytes 3076
  0.0 2.0 %copy-start.2 = (s32[2,128,1]{1,2,0:T(1,128)S(1)}, s32[2,128,1]{1,2,0:T(1,128)}, u32[]{:S(2)}) copy-start(s32[2,128,1]{1,2,0:T(1,128)} %param.8) | copy-start | bytes 3076
  2.2 20.8 %collective-permute-start = (bf16[136,640]{1,0:T(8,128)(2,1)S(1)}, bf16[136,640]{1,0:T(8,128)(2,1)S(1)}, u32[]{:S(2)}, u32[]{:S(2)}) collective-permute-start(bf16[136,640]{1,0:T(8,128)(2,1)S(1)} %get-tuple-element.132), channel_id=1, source_target_pairs={{0,1},{1,0},{2,3},{3,2},{4,5},{5,4},{6,7},{7,6},{8,9},{9,8},{10,11... | collective-permute-start | bytes 522248 | tf_op jit(solution)/shard_map/ppermute | solution.py:13
  5.4 17.6 %collective-permute-start.2 = (bf16[136,640]{1,0:T(8,128)(2,1)S(1)}, bf16[136,640]{1,0:T(8,128)(2,1)S(1)}, u32[]{:S(2)}, u32[]{:S(2)}) collective-permute-start(bf16[136,640]{1,0:T(8,128)(2,1)S(1)} %get-tuple-element.131), channel_id=1, source_target_pairs={{0,3},{1,2},{2,1},{3,0},{4,7},{5,6},{6,5},{7,4},{8,11},{9,10},{10,... | collective-permute-start | bytes 522248 | tf_op jit(solution)/shard_map/ppermute | solution.py:13
  7.9 2.0 %slice-start = ((bf16[128,3584]{1,0:T(8,128)(2,1)}), bf16[128,2048]{1,0:T(8,128)(2,1)S(1)}, s32[]{:S(2)}) async-start(bf16[128,3584]{1,0:T(8,128)(2,1)} %param.6), calls=%async_computation | async-start | bytes 1048576 | tf_op jit(solution)/shard_map/slice | solution.py:110
  7.9 15.5 %collective-permute-start.1 = (bf16[136,640]{1,0:T(8,128)(2,1)S(1)}, bf16[136,640]{1,0:T(8,128)(2,1)S(1)}, u32[]{:S(2)}, u32[]{:S(2)}) collective-permute-start(bf16[136,640]{1,0:T(8,128)(2,1)S(1)} %get-tuple-element.133), channel_id=1, source_target_pairs={{0,2},{1,3},{2,0},{3,1},{4,6},{5,7},{6,4},{7,5},{8,10},{9,11},{10,... | collective-permute-start | bytes 522248 | tf_op jit(solution)/shard_map/ppermute | solution.py:13
  8.1 11.3 %collective-permute-start.3 = (bf16[128,512]{1,0:T(8,128)(2,1)S(1)}, bf16[128,512]{1,0:T(8,128)(2,1)S(1)}, u32[]{:S(2)}, u32[]{:S(2)}) collective-permute-start(bf16[128,512]{1,0:T(8,128)(2,1)S(1)} %slice.273), channel_id=1, source_target_pairs={{0,1},{1,0},{2,3},{3,2},{4,5},{5,4},{6,7},{7,6},{8,9},{9,8},{10,11... | collective-permute-start | bytes 393224 | tf_op jit(solution)/shard_map/ppermute | solution.py:13
  9.9 0.9 slice-start.2
  10.9 11.0 %collective-permute-start.5 = (bf16[128,512]{1,0:T(8,128)(2,1)S(1)}, bf16[128,512]{1,0:T(8,128)(2,1)S(1)}, u32[]{:S(2)}, u32[]{:S(2)}) collective-permute-start(bf16[128,512]{1,0:T(8,128)(2,1)S(1)} %get-tuple-element.96), channel_id=1, source_target_pairs={{0,4},{4,0},{8,12},{12,8},{16,20},{20,16},{24,28},{28,24},{1,5},{5... | collective-permute-start | bytes 393224 | tf_op jit(solution)/shard_map/ppermute | solution.py:13
  19.4 16.2 %collective-permute-start.6 = (bf16[128,1024]{1,0:T(8,128)(2,1)S(1)}, bf16[128,1024]{1,0:T(8,128)(2,1)S(1)}, u32[]{:S(2)}, u32[]{:S(2)}) collective-permute-start(bf16[128,1024]{1,0:T(8,128)(2,1)S(1)} %slice.274), channel_id=1, source_target_pairs={{0,1},{1,0},{2,3},{3,2},{4,5},{5,4},{6,7},{7,6},{8,9},{9,8},{10,11... | collective-permute-start | bytes 786440 | tf_op jit(solution)/shard_map/ppermute | solution.py:13
  21.9 8.9 %collective-permute-start.8 = (bf16[256,256]{1,0:T(8,128)(2,1)S(1)}, bf16[256,256]{1,0:T(8,128)(2,1)S(1)}, u32[]{:S(2)}, u32[]{:S(2)}) collective-permute-start(bf16[256,256]{1,0:T(8,128)(2,1)S(1)} %get-tuple-element.94), channel_id=1, source_target_pairs={{0,2},{1,3},{2,0},{3,1},{4,6},{5,7},{6,4},{7,5},{8,10},{9,11},{10,... | collective-permute-start | bytes 393224 | tf_op jit(solution)/shard_map/ppermute | solution.py:13
  24.5 11.8 %collective-permute-start.12 = (bf16[128,1024]{0,1:T(8,128)(2,1)S(1)}, bf16[128,1024]{0,1:T(8,128)(2,1)S(1)}, u32[]{:S(2)}, u32[]{:S(2)}) collective-permute-start(bf16[128,1024]{0,1:T(8,128)(2,1)S(1)} %get-tuple-element.78), channel_id=1, source_target_pairs={{0,4},{4,0},{8,12},{12,8},{16,20},{20,16},{24,28},{28,24},{1,5},{5... | collective-permute-start | bytes 786440 | tf_op jit(solution)/shard_map/ppermute | solution.py:13
  24.5 11.1 %collective-permute-start.4 = (bf16[128,512]{1,0:T(8,128)(2,1)S(1)}, bf16[128,512]{1,0:T(8,128)(2,1)S(1)}, u32[]{:S(2)}, u32[]{:S(2)}) collective-permute-start(bf16[128,512]{1,0:T(8,128)(2,1)S(1)} %get-tuple-element.143), channel_id=1, source_target_pairs={{0,2},{1,3},{2,0},{3,1},{4,6},{5,7},{6,4},{7,5},{8,10},{9,11},{10,... | collective-permute-start | bytes 393224 | tf_op jit(solution)/shard_map/ppermute | solution.py:13
  30.9 9.3 %collective-permute-start.9 = (bf16[512,256]{1,0:T(8,128)(2,1)S(1)}, bf16[512,256]{1,0:T(8,128)(2,1)S(1)}, u32[]{:S(2)}, u32[]{:S(2)}) collective-permute-start(bf16[512,256]{1,0:T(8,128)(2,1)S(1)} %pad_maximum_fusion.9), channel_id=1, source_target_pairs={{0,1},{1,0},{2,3},{3,2},{4,5},{5,4},{6,7},{7,6},{8,9},{9,8},{10,11... | collective-permute-start | bytes 786440 | tf_op jit(solution)/shard_map/ppermute | solution.py:13
  36.2 4.2 %collective-permute-start.7 = (bf16[128,1024]{0,1:T(8,128)(2,1)S(1)}, bf16[128,1024]{0,1:T(8,128)(2,1)S(1)}, u32[]{:S(2)}, u32[]{:S(2)}) collective-permute-start(bf16[128,1024]{0,1:T(8,128)(2,1)S(1)} %get-tuple-element.145), channel_id=1, source_target_pairs={{0,4},{4,0},{8,12},{12,8},{16,20},{20,16},{24,28},{28,24},{1,5},{5... | collective-permute-start | bytes 786440 | tf_op jit(solution)/shard_map/ppermute | solution.py:13
  36.3 15.8 %collective-permute-start.13 = (bf16[256,1024]{0,1:T(8,128)(2,1)S(1)}, bf16[256,1024]{0,1:T(8,128)(2,1)S(1)}, u32[]{:S(2)}, u32[]{:S(2)}) collective-permute-start(bf16[256,1024]{0,1:T(8,128)(2,1)S(1)} %pad_maximum_fusion), channel_id=1, source_target_pairs={{0,8},{4,12},{8,0},{12,4},{16,24},{20,28},{24,16},{28,20},{1,9},{5... | collective-permute-start | bytes 1572872 | tf_op jit(solution)/shard_map/ppermute | solution.py:13
  41.2 1.4 %collective-permute-start.10 = (bf16[128,512]{1,0:T(8,128)(2,1)S(1)}, bf16[128,512]{1,0:T(8,128)(2,1)S(1)}, u32[]{:S(2)}, u32[]{:S(2)}) collective-permute-start(bf16[128,512]{1,0:T(8,128)(2,1)S(1)} %convolution_convert_fusion.2), channel_id=1, source_target_pairs={{0,4},{4,0},{8,12},{12,8},{16,20},{20,16},{24,28},{28,24},{1,5},{5... | collective-permute-start | bytes 393224 | tf_op jit(solution)/shard_map/ppermute | solution.py:13
  42.8 9.3 %collective-permute-start.11 = (bf16[128,512]{1,0:T(8,128)(2,1)S(1)}, bf16[128,512]{1,0:T(8,128)(2,1)S(1)}, u32[]{:S(2)}, u32[]{:S(2)}) collective-permute-start(bf16[128,512]{1,0:T(8,128)(2,1)S(1)} %get-tuple-element.147), channel_id=1, source_target_pairs={{0,2},{1,3},{2,0},{3,1},{4,6},{5,7},{6,4},{7,5},{8,10},{9,11},{10,... | collective-permute-start | bytes 393224 | tf_op jit(solution)/shard_map/ppermute | solution.py:13
  52.9 5.0 %collective-permute-start.14 = (bf16[128,512]{0,1:T(8,128)(2,1)S(1)}, bf16[128,512]{0,1:T(8,128)(2,1)S(1)}, u32[]{:S(2)}, u32[]{:S(2)}) collective-permute-start(bf16[128,512]{0,1:T(8,128)(2,1)S(1)} %pad_maximum_fusion.24), channel_id=1, source_target_pairs={{0,8},{4,12},{8,0},{12,4},{16,24},{20,28},{24,16},{28,20},{1,9},{5... | collective-permute-start | bytes 393224 | tf_op jit(solution)/shard_map/ppermute | solution.py:13
  58.1 5.0 %collective-permute-start.15 = (bf16[128,512]{0,1:T(8,128)(2,1)S(1)}, bf16[128,512]{0,1:T(8,128)(2,1)S(1)}, u32[]{:S(2)}, u32[]{:S(2)}) collective-permute-start(bf16[128,512]{0,1:T(8,128)(2,1)S(1)} %fusion.9), channel_id=1, source_target_pairs={{0,1},{1,0},{2,3},{3,2},{4,5},{5,4},{6,7},{7,6},{8,9},{9,8},{10,11... | collective-permute-start | bytes 393224 | tf_op jit(solution)/shard_map/ppermute | solution.py:13
  64.0 1.4 %collective-permute-start.16 = (bf16[128,512]{1,0:T(8,128)(2,1)S(1)}, bf16[128,512]{1,0:T(8,128)(2,1)S(1)}, u32[]{:S(2)}, u32[]{:S(2)}) collective-permute-start(bf16[128,512]{1,0:T(8,128)(2,1)S(1)} %pad_maximum_fusion.25), channel_id=1, source_target_pairs={{0,4},{4,0},{8,12},{12,8},{16,20},{20,16},{24,28},{28,24},{1,5},{5... | collective-permute-start | bytes 393224 | tf_op jit(solution)/shard_map/ppermute | solution.py:13
  66.3 5.6 %collective-permute-start.17 = (bf16[128,512]{0,1:T(8,128)(2,1)S(1)}, bf16[128,512]{0,1:T(8,128)(2,1)S(1)}, u32[]{:S(2)}, u32[]{:S(2)}) collective-permute-start(bf16[128,512]{0,1:T(8,128)(2,1)S(1)} %pad_maximum_fusion.26), channel_id=1, source_target_pairs={{0,1},{1,0},{2,3},{3,2},{4,5},{5,4},{6,7},{7,6},{8,9},{9,8},{10,11... | collective-permute-start | bytes 393224 | tf_op jit(solution)/shard_map/ppermute | solution.py:13
  72.1 8.5 %collective-permute-start.18 = (bf16[128,512]{0,1:T(8,128)(2,1)S(1)}, bf16[128,512]{0,1:T(8,128)(2,1)S(1)}, u32[]{:S(2)}, u32[]{:S(2)}) collective-permute-start(bf16[128,512]{0,1:T(8,128)(2,1)S(1)} %get-tuple-element.69), channel_id=1, source_target_pairs={{0,2},{1,3},{2,0},{3,1},{4,6},{5,7},{6,4},{7,5},{8,10},{9,11},{10,... | collective-permute-start | bytes 393224 | tf_op jit(solution)/shard_map/ppermute | solution.py:13
  80.7 5.2 %collective-permute-start.19 = (bf16[128,512]{0,1:T(8,128)(2,1)S(1)}, bf16[128,512]{0,1:T(8,128)(2,1)S(1)}, u32[]{:S(2)}, u32[]{:S(2)}) collective-permute-start(bf16[128,512]{0,1:T(8,128)(2,1)S(1)} %add_convert_fusion.2), channel_id=1, source_target_pairs={{0,8},{4,12},{8,0},{12,4},{16,24},{20,28},{24,16},{28,20},{1,9},{5... | collective-permute-start | bytes 393224 | tf_op jit(solution)/shard_map/ppermute | solution.py:13
  86.6 1.4 %collective-permute-start.20 = (bf16[128,512]{1,0:T(8,128)(2,1)S(1)}, bf16[128,512]{1,0:T(8,128)(2,1)S(1)}, u32[]{:S(2)}, u32[]{:S(2)}) collective-permute-start(bf16[128,512]{1,0:T(8,128)(2,1)S(1)} %convolution_convert_fusion.1), channel_id=1, source_target_pairs={{0,4},{4,0},{8,12},{12,8},{16,20},{20,16},{24,28},{28,24},{1,5},{5... | collective-permute-start | bytes 393224 | tf_op jit(solution)/shard_map/ppermute | solution.py:13
  88.9 1.4 %collective-permute-start.21 = (bf16[128,512]{0,1:T(8,128)(2,1)S(1)}, bf16[128,512]{0,1:T(8,128)(2,1)S(1)}, u32[]{:S(2)}, u32[]{:S(2)}) collective-permute-start(bf16[128,512]{0,1:T(8,128)(2,1)S(1)} %dynamic-slice_convert_fusion.1), channel_id=1, source_target_pairs={{0,4},{4,0},{8,12},{12,8},{16,20},{20,16},{24,28},{28,24},{1,5},{5... | collective-permute-start | bytes 393224 | tf_op jit(solution)/shard_map/ppermute | solution.py:13
  90.4 9.3 %collective-permute-start.22 = (bf16[128,512]{0,1:T(8,128)(2,1)S(1)}, bf16[128,512]{0,1:T(8,128)(2,1)S(1)}, u32[]{:S(2)}, u32[]{:S(2)}) collective-permute-start(bf16[128,512]{0,1:T(8,128)(2,1)S(1)} %fusion.23), channel_id=1, source_target_pairs={{0,2},{1,3},{2,0},{3,1},{4,6},{5,7},{6,4},{7,5},{8,10},{9,11},{10,... | collective-permute-start | bytes 393224 | tf_op jit(solution)/shard_map/ppermute | solution.py:13
  99.7 1.4 %collective-permute-start.23 = (bf16[128,512]{0,1:T(8,128)(2,1)S(1)}, bf16[128,512]{0,1:T(8,128)(2,1)S(1)}, u32[]{:S(2)}, u32[]{:S(2)}) collective-permute-start(bf16[128,512]{0,1:T(8,128)(2,1)S(1)} %add_convert_fusion.1), channel_id=1, source_target_pairs={{0,4},{4,0},{8,12},{12,8},{16,20},{20,16},{24,28},{28,24},{1,5},{5... | collective-permute-start | bytes 393224 | tf_op jit(solution)/shard_map/ppermute | solution.py:13
  102.2 8.0 %collective-permute-start.24 = (bf16[256,128]{0,1:T(8,128)(2,1)S(1)}, bf16[256,128]{0,1:T(8,128)(2,1)S(1)}, u32[]{:S(2)}, u32[]{:S(2)}) collective-permute-start(bf16[256,128]{0,1:T(8,128)(2,1)S(1)} %constant_dynamic-slice_fusion.1), channel_id=1, source_target_pairs={{0,1},{1,0},{2,3},{3,2},{4,5},{5,4},{6,7},{7,6},{8,9},{9,8},{10,11... | collective-permute-start | bytes 196616 | tf_op jit(solution)/shard_map/ppermute | solution.py:13
  102.3 4.8 %collective-permute-start.25 = (bf16[128,128]{0,1:T(8,128)(2,1)S(1)}, bf16[128,128]{0,1:T(8,128)(2,1)S(1)}, u32[]{:S(2)}, u32[]{:S(2)}) collective-permute-start(bf16[128,128]{0,1:T(8,128)(2,1)S(1)} %get-tuple-element.85), channel_id=1, source_target_pairs={{0,1},{1,0},{2,3},{3,2},{4,5},{5,4},{6,7},{7,6},{8,9},{9,8},{10,11... | collective-permute-start | bytes 98312 | tf_op jit(solution)/shard_map/ppermute | solution.py:13
  104.4 5.1 %collective-permute-start.26 = (bf16[128,128]{0,1:T(8,128)(2,1)S(1)}, bf16[128,128]{0,1:T(8,128)(2,1)S(1)}, u32[]{:S(2)}, u32[]{:S(2)}) collective-permute-start(bf16[128,128]{0,1:T(8,128)(2,1)S(1)} %get-tuple-element.84), channel_id=1, source_target_pairs={{0,2},{1,3},{2,0},{3,1},{4,6},{5,7},{6,4},{7,5},{8,10},{9,11},{10,... | collective-permute-start | bytes 98312 | tf_op jit(solution)/shard_map/ppermute | solution.py:13
  104.4 5.8 %collective-permute-start.27 = (bf16[128,128]{0,1:T(8,128)(2,1)S(1)}, bf16[128,128]{0,1:T(8,128)(2,1)S(1)}, u32[]{:S(2)}, u32[]{:S(2)}) collective-permute-start(bf16[128,128]{0,1:T(8,128)(2,1)S(1)} %get-tuple-element.83), channel_id=1, source_target_pairs={{0,3},{1,2},{2,1},{3,0},{4,7},{5,6},{6,5},{7,4},{8,11},{9,10},{10,... | collective-permute-start | bytes 98312 | tf_op jit(solution)/shard_map/ppermute | solution.py:13
